TPU v7x, 512 devices: a whole 4x8x8 slice. The times are simulated.
512 devices in a mesh: dp: 16 (over z, y_hi), tensor: 32 (over y_lo, x, core).
Axes of the slice: x: 4, y: 8 (y_hi: 2, y_lo: 4; y = y_hi * 4 + y_lo), z: 8, core: 2. Of those that a mesh axis runs over, the one named last changes fastest.
Arguments:
- activations: bfloat16 [65536, 8192], P(('dp', 'tensor')), may hold values from -6 to 6
- key_cotangent: bfloat16 [65536, 768], P(('dp', 'tensor')), may hold values from -16 to 16
- doc_lengths: int32 [16, 8], P('dp'), may hold values from 1 to 2048, 4096 in all within a row
- weight_codes: int32 [8192, 768], P('tensor'), may hold values from 0 to 3
- zero_points: int32 [128, 768], P('tensor'), may hold values from 0 to 3
- step_sizes: float32 [128, 768], P('tensor'), may hold values from 0.004 to 0.016
Outputs:
- input_grad: bfloat16 [65536, 8192], P(('dp', 'tensor'))
- step_grad: float32 [128, 768], P('tensor')
Inputs may be any that keep to these rules, and one draw needn't show every extreme that they name: `doc_lengths`: each row sums to 4096; its longest document has exactly 2048 tokens.
All inputs are finite; a program needn't handle non-finite values.
Results may differ from a plain program's by a relative error of at most 0.0057.
Values may be sent and summed in bfloat16 or wider, within the bound.
No kernel may reach another device: no remote copies, remote signals or barrier semaphores. Data moves between devices by JAX's collectives and lax.ppermute only.
A program may use at most 64 MiB of HBM per device.

v0:
```python
import math

import jax
import jax.numpy as jnp
from jax import lax
from jax.sharding import PartitionSpec as P

HEAD = 128
GROUP = 64


def token_positions(ends, indices):
    starts = jnp.where(ends[None, :] <= indices[:, None], ends[None, :], 0)
    return indices - jnp.max(starts, axis=1)


def rope_back(cotangent, positions):
    count = cotangent.shape[0]
    split = cotangent.astype(jnp.float32).reshape(count, -1, HEAD)
    middle = HEAD // 2
    freqs = jnp.exp(jnp.arange(middle, dtype=jnp.float32) * (-2.0 * math.log(10000.0) / HEAD))
    angles = positions.astype(jnp.float32)[:, None] * freqs[None, :]
    cosine = jnp.cos(angles)[:, None, :]
    sine = jnp.sin(angles)[:, None, :]
    first = split[..., :middle]
    second = split[..., middle:]
    lower = first * cosine + second * sine
    upper = second * cosine - first * sine
    return jnp.concatenate([lower, upper], axis=-1).reshape(count, -1).astype(jnp.bfloat16)


def per_device(activations, key_cotangent, doc_lengths, weight_codes, zero_points, step_sizes):
    tok_count = activations.shape[0]
    key_cols = weight_codes.shape[1]
    ends = jnp.cumsum(doc_lengths[0], dtype=jnp.int32)
    offset = lax.axis_index("tensor") * tok_count
    indices = offset + jnp.arange(tok_count, dtype=jnp.int32)
    rotated = rope_back(key_cotangent, token_positions(ends, indices))
    levels = (weight_codes - jnp.repeat(zero_points, GROUP, axis=0)).astype(jnp.float32)
    weight = (jnp.repeat(step_sizes, GROUP, axis=0) * levels).astype(jnp.bfloat16)
    token_columns = lax.all_to_all(activations, "tensor", split_axis=1, concat_axis=0, tiled=True)
    seq_tokens = token_columns.shape[0]
    weight_grad = lax.dot_general(
        token_columns,
        lax.all_gather(rotated, "tensor", axis=0, tiled=True),
        (((0,), (0,)), ((), ())),
        preferred_element_type=jnp.float32,
    )
    input_grad = lax.dot_general(
        rotated,
        lax.all_gather(weight, "tensor", axis=0, tiled=True),
        (((1,), (1,)), ((), ())),
        preferred_element_type=jnp.float32,
    ).astype(jnp.bfloat16)
    partial_grad = (weight_grad * levels).reshape(-1, GROUP, key_cols).sum(axis=1) / seq_tokens
    step_grad = lax.psum(partial_grad, "dp")
    return (input_grad, step_grad)


def solution(mesh):
    in_specs = (
        P(("dp", "tensor"), None),
        P(("dp", "tensor"), None),
        P("dp", None),
        P("tensor", None),
        P("tensor", None),
        P("tensor", None),
    )
    out_specs = (P(("dp", "tensor"), None), P("tensor", None))
    return jax.shard_map(
        per_device, mesh=mesh, in_specs=in_specs, out_specs=out_specs, check_vma=False
    )
```

profile of v0, /device:TPU:8, one launch (start us, length us, event | category | flops | bytes accessed | tf_op | source)
XLA Modules:
  0.0 246.2 jit_solution(1297412576108415106)
XLA Ops:
  7.2 0.0 copy-start.1
  7.2 0.0 all-gather.5.cloned.1.call-start
  7.3 1.0 reduce-window.8
  8.2 0.1 select_reduce_fusion
  8.3 1.1 copy.12
  9.4 0.2 multiply_cosine_fusion
  9.6 0.1 add_convert_fusion
  9.7 0.7 pad_maximum_fusion
  10.4 0.0 all-gather.5.cloned.1.call-update
  10.4 0.0 all-gather.3.cloned.1.call-start
  10.5 2.0 fusion.2
  12.5 0.0 all-gather.3.cloned.1.call-update
  12.5 0.0 copy-done.1
  12.5 2.4 copy.13
  14.9 73.0 %all_to_all.19 = bf16[128,32,256]{0,2,1:T(8,128)(2,1)S(1)} all-to-all(bf16[128,32,256]{0,2,1:T(8,128)(2,1)} %bitcast.28), channel_id=1, replica_groups=mesh['dp'=16,'tensor'=32] {'tensor'}, dimensions={1} | all-to-all | bytes 4194304 | tf_op jit(solution)/shard_map/all_to_all | solution.py:41
  87.9 2.9 %copy.14 = bf16[32,128,256]{2,1,0:T(8,128)(2,1)} copy(bf16[32,128,256]{1,2,0:T(8,128)(2,1)S(1)} %bitcast.27) | data formatting | bytes 4194304 | tf_op jit(solution)/shard_map/all_to_all | solution.py:41
  90.8 29.3 %all-gather.5.cloned.1.call-done = bf16[4096,768]{0,1:T(8,128)(2,1)} async-done(((bf16[128,768]{0,1:T(8,128)(2,1)}), bf16[4096,768]{0,1:T(8,128)(2,1)}) %all-gather.5.cloned.1.call-update) | async-done | bytes 6291472 | tf_op jit(solution)/shard_map/all_gather | solution.py:45
  120.1 0.0 copy-start
  120.1 5.3 %bitcast_reduce_fusion = f32[4,768]{1,0:T(4,128)S(1)} fusion(f32[256,768]{1,0:T(8,128)S(1)} %get-tuple-element.3, bf16[4096,768]{0,1:T(8,128)(2,1)} %all-gather.5.cloned.1.call-done, bf16[4096,256]{1,0:T(8,128)(2,1)} %bitcast.31), kind=kOutput, calls=%fused_computation.3 | convolution fusion | flops 1611002880 | bytes 9187328 | tf_op jit(solution)/shard_map/dot_general | solution.py:43
  125.4 103.8 %psum.7 = f32[4,768]{1,0:T(4,128)} all-reduce(f32[4,768]{1,0:T(4,128)S(1)} %broadcast_multiply_fusion), channel_id=1, replica_groups=mesh['dp'=16,'tensor'=32] {'dp'}, use_global_device_ids=true, to_apply=%region_3.4 | all-reduce | flops 3072 | bytes 24576 | tf_op jit(solution)/shard_map/psum | solution.py:56
  229.2 0.0 all-gather.3.cloned.1.call-done
  229.2 0.0 copy-done
  229.2 10.1 %convolution_convert_fusion = bf16[128,8192]{1,0:T(8,128)(2,1)} fusion(bf16[128,768]{0,1:T(8,128)(2,1)S(1)} %bitcast.30, bf16[8192,768]{1,0:T(8,128)(2,1)} %all-gather.3.cloned.1.call-done), kind=kOutput, calls=%fused_computation | convolution fusion | flops 1611661312 | bytes 14876672 | tf_op jit(solution)/shard_map/dot_general | solution.py:49
  (5 shorter events, 0.1 us)
Async XLA Ops:
  7.2 5.3 %copy-start.1 = (bf16[128,8192]{1,0:T(8,128)(2,1)S(1)}, bf16[128,8192]{1,0:T(8,128)(2,1)}, u32[]{:S(2)}) copy-start(bf16[128,8192]{1,0:T(8,128)(2,1)} %param.6) | copy-start | bytes 6291460
  7.2 113.0 %all-gather.5.cloned.1.call-start = ((), (), s32[]{:S(2)}) async-start(), calls=%async_computation.2 | async-start | bytes 6488064 | tf_op jit(solution)/shard_map/all_gather | solution.py:45
  10.4 218.8 %all-gather.3.cloned.1.call-start = ((), (), s32[]{:S(2)}) async-start(), calls=%async_computation.1 | async-start | bytes 12976128 | tf_op jit(solution)/shard_map/all_gather | solution.py:51
  120.1 109.1 %copy-start = (bf16[128,6,128]{0,2,1:T(8,128)(2,1)S(1)}, bf16[128,6,128]{0,2,1:T(8,128)(2,1)}, u32[]{:S(2)}) copy-start(bf16[128,6,128]{0,2,1:T(8,128)(2,1)} %pad_maximum_fusion) | copy-start | bytes 589828
Sparse Core Ops, SparseCore 0:
  10.5 109.5 all-gather.4
  122.3 85.2 all-gather.2
where the time goes:
time: 246 us
  blocking collectives  177 us (72%)
  waiting for transfers between devices  29.4 us (12%)
  matrix products  15.4 us (6%)
  between operations  14.1 us (6%)
  local copies, waits for them, and re-layouts  6.41 us (3%)
  other arithmetic  4.03 us (2%)
    psum x1, blocking collectives, per_device(): step_grad = lax.psum(partial_grad, 'dp')  104 us
    all_to_all x1, blocking collectives, per_device(): lax.all_to_all(activations, 'tensor', split_axis=1, concat_axis=0, tiled=...  73 us
    all_gather x1, waiting for transfers between devices, per_device(): lax.all_gather(rotated, 'tensor', axis=0, tiled=True)  29.3 us
    dot_general x1, matrix products, per_device(): lax.dot_general(rotated, lax.all_gather(weight, 'tensor', axis=0, tiled=T...  10.1 us
    dot_general x1, matrix products, per_device(): lax.dot_general(token_columns, lax.all_gather(rotated, 'tensor', axis=0,...  5.28 us
  transfers between devices with their start and end apart: 2, of which 1 were waited for; matrix products, arithmetic and copies ran while one was open for 5% of the time, Pallas kernels for 0%

commit v1 on v0

v1 whole, which is shorter than its diff:
```python
import functools
import math

import jax
import jax.numpy as jnp
from jax import lax
from jax.experimental import pallas as pl
from jax.experimental.pallas import tpu as pltpu
from jax.sharding import PartitionSpec as P

HEAD = 128
GROUP = 64
AXES = ("dp", "tensor")
NX, NY, NYL, NZ = 4, 8, 4, 8
VMEM = 48 * 1024 * 1024


def device_at(x, y, z, core):
    x, y, z = x % NX, y % NY, z % NZ
    dp = z * (NY // NYL) + y // NYL
    return dp * (NX * NYL * 2) + ((y % NYL) * NX + x) * 2 + core


def permutation(target):
    return [
        (device_at(x, y, z, core), device_at(*target(x, y, z, core)))
        for x in range(NX)
        for y in range(NY)
        for z in range(NZ)
        for core in range(2)
    ]


def send(value, dx, dy, cross=False):
    def target(x, y, z, core):
        sign = 1 if (core == 0) != cross else -1
        return x + sign * dx, y + sign * dy, z, core ^ int(cross)

    return lax.ppermute(value, AXES, permutation(target))


def swap(value):
    return lax.ppermute(value, AXES, permutation(lambda x, y, z, core: (x, y, z, core ^ 1)))


def token_positions(lengths, indices):
    count = lengths.shape[0]
    order = jnp.arange(count, dtype=jnp.int32)
    ends = jnp.sum(jnp.where(order[:, None] <= order[None, :], lengths[:, None], 0), axis=0)
    starts = jnp.where(ends[None, :] <= indices[:, None], ends[None, :], 0)
    return indices - jnp.max(starts, axis=1)


def rope_back(cotangent, positions):
    count = cotangent.shape[0]
    split = cotangent.astype(jnp.float32).reshape(count, -1, HEAD)
    middle = HEAD // 2
    freqs = jnp.exp(jnp.arange(middle, dtype=jnp.float32) * (-2.0 * math.log(10000.0) / HEAD))
    angles = positions.astype(jnp.float32)[:, None] * freqs[None, :]
    cosine = jnp.cos(angles)[:, None, :]
    sine = jnp.sin(angles)[:, None, :]
    first = split[..., :middle]
    second = split[..., middle:]
    lower = first * cosine + second * sine
    upper = second * cosine - first * sine
    return jnp.concatenate([lower, upper], axis=-1).reshape(count, -1).astype(jnp.bfloat16)


def dequant_kernel(codes_ref, zeros_ref, steps_ref, weight_ref):
    for group in range(zeros_ref.shape[0]):
        rows = pl.ds(group * GROUP, GROUP)
        levels = (codes_ref[rows, :] - zeros_ref[group : group + 1, :]).astype(jnp.float32)
        weight_ref[rows, :] = (steps_ref[group : group + 1, :] * levels).astype(jnp.bfloat16)


def dequant(codes, zeros, steps):
    return pl.pallas_call(
        dequant_kernel,
        out_shape=jax.ShapeDtypeStruct(codes.shape, jnp.bfloat16),
        compiler_params=pltpu.CompilerParams(vmem_limit_bytes=VMEM),
        name="dequant",
    )(codes, zeros, steps)


def shards_kernel(counts, aliased, table, mine_ref, other_ref, rot_ref, *refs):
    weights = refs[: len(counts)]
    grad_ref, sent_ref, sums_ref = refs[len(counts) + int(aliased) :]
    at = pl.program_id(0)
    half = mine_ref.shape[0]

    def unit(weight_ref):
        weight = weight_ref[...]
        rot = rot_ref[...]
        grad = lax.dot_general(
            rot, weight, (((1,), (1,)), ((), ())), preferred_element_type=jnp.float32
        ).astype(jnp.bfloat16)
        grad_ref[...] = grad[:half]
        sent_ref[...] = grad[half:]
        feats = jnp.concatenate([mine_ref[...], other_ref[...]], axis=0)
        weight_grad = lax.dot_general(
            feats, rot, (((0,), (0,)), ((), ())), preferred_element_type=jnp.float32
        )
        product = weight_grad * weight.astype(jnp.float32)
        groups = product.shape[0] // GROUP
        sums_ref[0] = product.reshape(groups, GROUP, product.shape[1]).sum(axis=1)

    first = 0
    for count, weight_ref in zip(counts, weights):
        if len(counts) == 1:
            unit(weight_ref)
        else:
            inside = jnp.logical_and(at >= first, at < first + count)
            pl.when(inside)(functools.partial(unit, weight_ref))
        first += count


def shards(table, mine, other, rot, weights, rows, grad=None):
    tokens, width = mine.shape
    cols = rot.shape[1]
    counts = tuple(weight.shape[0] // rows for weight in weights)
    total = sum(counts)

    def weight_spec(first, count):
        return pl.BlockSpec((rows, cols), lambda i, t: (jnp.clip(i - first, 0, count - 1), 0))

    firsts = [sum(counts[:k]) for k in range(len(counts))]
    in_specs = [
        pl.BlockSpec((tokens, rows), lambda i, t: (0, t[i])),
        pl.BlockSpec((tokens, rows), lambda i, t: (0, t[i])),
        pl.BlockSpec(rot.shape, lambda i, t: (0, 0)),
    ] + [weight_spec(first, count) for first, count in zip(firsts, counts)]
    operands = [mine, other, rot, *weights]
    aliases = {}
    if grad is not None:
        aliases = {1 + len(operands): 0}
        in_specs.append(pl.BlockSpec(memory_space=pl.ANY))
        operands.append(grad)
    groups = rows // GROUP
    return pl.pallas_call(
        functools.partial(shards_kernel, counts, grad is not None),
        out_shape=(
            jax.ShapeDtypeStruct((tokens, width), jnp.bfloat16),
            jax.ShapeDtypeStruct((tokens, total * rows), jnp.bfloat16),
            jax.ShapeDtypeStruct((total, groups, cols), jnp.float32),
        ),
        grid_spec=pltpu.PrefetchScalarGridSpec(
            num_scalar_prefetch=1,
            grid=(total,),
            in_specs=in_specs,
            out_specs=(
                pl.BlockSpec((tokens, rows), lambda i, t: (0, t[i])),
                pl.BlockSpec((tokens, rows), lambda i, t: (0, i)),
                pl.BlockSpec((1, groups, cols), lambda i, t: (i, 0, 0)),
            ),
        ),
        input_output_aliases=aliases,
        cost_estimate=pl.CostEstimate(
            flops=8 * total * rows * cols * tokens,
            bytes_accessed=total * rows * (cols * 2 + tokens * 8),
            transcendentals=0,
        ),
        compiler_params=pltpu.CompilerParams(vmem_limit_bytes=VMEM),
        name="shards",
    )(table, *operands)


def place_kernel(table, block_ref, grad_in, grad_ref):
    grad_ref[...] = block_ref[...]


def place(table, blocks, grad, rows):
    tokens = grad.shape[0]
    return pl.pallas_call(
        place_kernel,
        out_shape=jax.ShapeDtypeStruct(grad.shape, grad.dtype),
        grid_spec=pltpu.PrefetchScalarGridSpec(
            num_scalar_prefetch=1,
            grid=(blocks.shape[1] // rows,),
            in_specs=[
                pl.BlockSpec((tokens, rows), lambda i, t: (0, i)),
                pl.BlockSpec(memory_space=pl.ANY),
            ],
            out_specs=pl.BlockSpec((tokens, rows), lambda i, t: (0, t[i])),
        ),
        input_output_aliases={2: 0},
        cost_estimate=pl.CostEstimate(
            flops=0, bytes_accessed=2 * blocks.size * 2, transcendentals=0
        ),
        compiler_params=pltpu.CompilerParams(vmem_limit_bytes=VMEM),
        name="place",
    )(table, blocks, grad)


def spread_kernel(table, *refs):
    *sums, all_ref = refs
    all_ref[...] = jnp.zeros_like(all_ref)
    unit = 0
    for ref in sums:
        for row in range(ref.shape[0]):
            all_ref[table[unit]] = ref[row].astype(all_ref.dtype)
            unit += 1


def spread(table, sums, devices):
    return pl.pallas_call(
        spread_kernel,
        out_shape=jax.ShapeDtypeStruct((devices, *sums[0].shape[1:]), jnp.bfloat16),
        in_specs=[pl.BlockSpec(memory_space=pltpu.SMEM)]
        + [pl.BlockSpec(memory_space=pltpu.VMEM)] * len(sums),
        out_specs=pl.BlockSpec(memory_space=pltpu.VMEM),
        compiler_params=pltpu.CompilerParams(vmem_limit_bytes=VMEM),
        name="spread",
    )(table, *sums)


def unit_table(x, y, core):
    sign = 2 * core - 1

    def owner(dx, dy, half):
        return (((y + sign * dy) % NYL) * NX + (x + sign * dx) % NX) * 2 + half

    return (
        [owner(0, 0, core)]
        + [owner(1, 0, 0), owner(1, 0, 1)]
        + [owner(0, 1, 0), owner(0, 1, 1)]
        + [owner(1, 1, 0), owner(1, 1, 1)]
        + [owner(-1, 1, 0), owner(-1, 1, 1)]
        + [owner(2, 1, 0), owner(2, 1, 1), owner(2, 0, core)]
        + [owner(1, 2, 0), owner(1, 2, 1), owner(0, 2, core)]
        + [owner(2, 2, core)]
    )


def per_device(activations, key_cotangent, doc_lengths, weight_codes, zero_points, step_sizes):
    tokens = activations.shape[0]
    rows = weight_codes.shape[0]
    place_in = lax.axis_index("tensor")
    devices = NX * NYL * 2
    core = place_in % 2
    x = (place_in // 2) % NX
    y = place_in // (2 * NX)
    table = jnp.stack(unit_table(x, y, core)).astype(jnp.int32)
    theirs = jnp.stack(unit_table(x, y, 1 - core)).astype(jnp.int32)

    weight = dequant(weight_codes, zero_points, step_sizes)
    pairs = [[2 * chip, 2 * chip + 1] for chip in range(NX * NYL)]
    chip_weight = lax.all_gather(weight, "tensor", axis=0, tiled=True, axis_index_groups=pairs)

    from_x = send(chip_weight, 1, 0)
    from_y = send(chip_weight, 0, 1)

    indices = place_in * tokens + jnp.arange(tokens, dtype=jnp.int32)
    mine = rope_back(key_cotangent, token_positions(doc_lengths[0], indices))
    rot = jnp.concatenate([mine, swap(mine)], axis=0)
    others = swap(activations)

    from_xy = send(from_y, 1, 0)
    from_yx = send(from_x, 0, 1, cross=True)

    grad, sent_near, sums_near = shards(
        table[:5], activations, others, rot, [weight, from_x, from_y], rows
    )
    got_near = swap(sent_near)

    def my_half(value):
        return lax.dynamic_slice_in_dim(value, core * rows, rows, axis=0)

    far_x = send(jnp.concatenate([from_xy, my_half(from_x)], axis=0), 1, 0)
    far_y = send(jnp.concatenate([from_xy, my_half(from_y)], axis=0), 0, 1)
    far = send(my_half(from_xy), 1, 1)

    grad, sent_mid, sums_mid = shards(
        table[5:9], activations, others, rot, [from_xy, from_yx], rows, grad
    )
    got_mid = swap(sent_mid)
    grad = place(theirs[:5], got_near, grad, rows)
    grad = place(theirs[5:9], got_mid, grad, rows)

    grad, sent_far, sums_far = shards(
        table[9:], activations, others, rot, [far_x, far_y, far], rows, grad
    )
    got_far = swap(sent_far)

    sums = spread(table, [sums_near, sums_mid, sums_far], devices)
    shares = lax.all_to_all(sums, "tensor", split_axis=0, concat_axis=0, tiled=True)
    share = jnp.sum(shares.astype(jnp.float32), axis=0).astype(jnp.bfloat16)
    copies = lax.axis_size("dp")
    totals = lax.all_to_all(
        jnp.broadcast_to(share[None], (copies, *share.shape)),
        "dp",
        split_axis=0,
        concat_axis=0,
        tiled=True,
    )
    seq_tokens = tokens * devices
    total = jnp.sum(totals.astype(jnp.float32), axis=0)
    step_grad = total / (seq_tokens * step_sizes)
    grad = place(theirs[9:], got_far, grad, rows)
    return (grad, step_grad)


def solution(mesh):
    in_specs = (
        P(("dp", "tensor"), None),
        P(("dp", "tensor"), None),
        P("dp", None),
        P("tensor", None),
        P("tensor", None),
        P("tensor", None),
    )
    out_specs = (P(("dp", "tensor"), None), P("tensor", None))
    return jax.shard_map(
        per_device, mesh=mesh, in_specs=in_specs, out_specs=out_specs, check_vma=False
    )
```

time: 246 us -> 130 us (0.53)
  the two profiles are of different devices: /device:TPU:8 before, /device:TPU:1 now
where the time goes in v1:
time: 130 us; the launch traced here: 129 us
  starting transfers between devices  48.5 us (37%)
  waiting for transfers between devices  30 us (23%)
  Pallas kernels  28 us (22%)
  blocking collectives  9.01 us (7%)
  local copies, waits for them, and re-layouts  7.96 us (6%)
  other arithmetic  3.94 us (3%)
    ppermute x7, starting transfers between devices, send(): return lax.ppermute(value, AXES, permutation(target))  22.1 us
    pallas_call x3, Pallas kernels, shards(): pl.pallas_call(functools.partial(shards_kernel, counts, grad is not None)...  17.8 us
    ppermute x7, waiting for transfers between devices, send(): return lax.ppermute(value, AXES, permutation(target))  13.1 us
    ppermute x5, starting transfers between devices, swap(): lax.ppermute(value, AXES, permutation(lambda x, y, z, core: (x, y, z, cor...  12.7 us
    all_to_all x1, starting transfers between devices, per_device(): lax.all_to_all(jnp.broadcast_to(share[None], (copies, *share.shape)), 'dp...  10 us
    all_gather x1, blocking collectives, per_device(): lax.all_gather(weight, 'tensor', axis=0, tiled=True, axis_index_groups=pa...  9.01 us
    pallas_call x3, Pallas kernels, place(): pl.pallas_call(place_kernel, out_shape=jax.ShapeDtypeStruct(grad.shape, g...  8.82 us
    all_to_all x1, waiting for transfers between devices, per_device(): lax.all_to_all(jnp.broadcast_to(share[None], (copies, *share.shape)), 'dp...  8.55 us
  transfers between devices with their start and end apart: 14, of which 5 were waited for; matrix products, arithmetic and copies ran while one was open for 6% of the time, Pallas kernels for 15%

profile of v1, /device:TPU:1, one launch (start us, length us, event | category | flops | bytes accessed | tf_op | source)
XLA Modules:
  0.0 128.8 jit_solution(8612904098794860793)
XLA Ops:
  0.7 1.3 copy-done.3
  1.9 0.7 copy-done.4
  2.6 0.7 copy-done.6
  3.3 0.1 dequant.1.refs_0_
  3.5 9.0 %all_gather.3 = bf16[512,768]{1,0:T(8,128)(2,1)} all-gather(bf16[256,768]{1,0:T(8,128)(2,1)S(1)} %dequant.1.refs_0_), channel_id=1, replica_groups={{0,1},{2,3},{4,5},{6,7},{8,9},{10,11},{12,13},{14,15},{16,17},{18,19},{..., dimensions={0}, use_global_device_ids=true | all-gather | bytes 1179648 | tf_op jit(solution)/shard_map/all_gather | solution.py:247
  12.5 1.9 %collective-permute-start.2 = (bf16[512,768]{1,0:T(8,128)(2,1)}, bf16[512,768]{1,0:T(8,128)(2,1)}, u32[]{:S(2)}, u32[]{:S(2)}) collective-permute-start(bf16[512,768]{1,0:T(8,128)(2,1)} %all_gather.3), channel_id=1, source_target_pairs={{0,8},{1,57},{64,72},{65,121},{128,136},{129,185},{192,200},{193,2... | collective-permute-start | bytes 2359304 | tf_op jit(solution)/shard_map/ppermute | solution.py:39
  14.4 2.2 %collective-permute-start.4 = (bf16[512,768]{1,0:T(8,128)(2,1)}, bf16[512,768]{1,0:T(8,128)(2,1)}, u32[]{:S(2)}, u32[]{:S(2)}) collective-permute-start(bf16[512,768]{1,0:T(8,128)(2,1)} %all_gather.3), channel_id=1, source_target_pairs={{0,2},{1,7},{64,66},{65,71},{128,130},{129,135},{192,194},{193,199... | collective-permute-start | bytes 2359304 | tf_op jit(solution)/shard_map/ppermute | solution.py:39
  16.6 2.0 %collective-permute-start = (bf16[128,8192]{1,0:T(8,128)(2,1)S(1)}, bf16[128,8192]{1,0:T(8,128)(2,1)}, u32[]{:S(2)}, u32[]{:S(2)}) collective-permute-start(bf16[128,8192]{1,0:T(8,128)(2,1)S(1)} %copy-done), channel_id=1, source_target_pairs={{0,1},{1,0},{64,65},{65,64},{128,129},{129,128},{192,193},{193,192... | collective-permute-start | bytes 6291464 | tf_op jit(solution)/shard_map/ppermute | solution.py:43
  18.6 0.2 copy.23
  19.0 0.1 select_reduce_fusion
  19.0 6.8 %collective-permute-done.2.refs_2_ = bf16[512,768]{1,0:T(8,128)(2,1)} collective-permute-done((bf16[512,768]{1,0:T(8,128)(2,1)}, bf16[512,768]{1,0:T(8,128)(2,1)}, u32[]{:S(2)}, u32[]{:S(2)}) %collective-permute-start.2) | collective-permute-done | bytes 786464 | tf_op jit(solution)/shard_map/ppermute | solution.py:39
  25.8 1.9 %collective-permute-start.3 = (bf16[512,768]{1,0:T(8,128)(2,1)}, bf16[512,768]{1,0:T(8,128)(2,1)S(1)}, u32[]{:S(2)}, u32[]{:S(2)}) collective-permute-start(bf16[512,768]{1,0:T(8,128)(2,1)} %collective-permute-done.2.refs_2_), channel_id=1, source_target_pairs={{0,2},{1,7},{64,66},{65,71},{128,130},{129,135},{192,194},{193,199... | collective-permute-start | bytes 2359304 | tf_op jit(solution)/shard_map/ppermute | solution.py:39
  27.7 0.2 multiply_cosine_fusion
  28.0 2.8 %collective-permute-start.8 = (bf16[512,768]{1,0:T(8,128)(2,1)}, bf16[512,768]{1,0:T(8,128)(2,1)}, u32[]{:S(2)}, u32[]{:S(2)}) collective-permute-start(bf16[512,768]{1,0:T(8,128)(2,1)} %collective-permute-done.4.refs_1_), channel_id=1, source_target_pairs={{0,57},{1,8},{64,121},{65,72},{128,185},{129,136},{192,249},{193,2... | collective-permute-start | bytes 2359304 | tf_op jit(solution)/shard_map/ppermute | solution.py:39
  30.7 1.0 constant_dynamic-slice_fusion.1
  31.7 1.0 constant_dynamic-slice_fusion.2
  32.8 6.3 %collective-permute-done.3.refs_0_ = bf16[512,768]{1,0:T(8,128)(2,1)S(1)} collective-permute-done((bf16[512,768]{1,0:T(8,128)(2,1)}, bf16[512,768]{1,0:T(8,128)(2,1)S(1)}, u32[]{:S(2)}, u32[]{:S(2)}) %collective-permute-start.3) | collective-permute-done | bytes 786464 | tf_op jit(solution)/shard_map/ppermute | solution.py:39
  39.1 1.6 %pad_maximum_fusion = (bf16[768,768]{1,0:T(8,128)(2,1)}, bf16[768,768]{1,0:T(8,128)(2,1)}) fusion(bf16[512,768]{1,0:T(8,128)(2,1)S(1)} %collective-permute-done.3.refs_0_, bf16[256,768]{1,0:T(8,128)(2,1)S(1)} %constant_dynamic-slice_fusion.1, bf16[256,768]{1,0:T(8,128)(2,1)S(1)} %constant_dynamic-slice_fusion.2), kind=kLoop, calls=%fused_computation | loop fusion | flops 4128768 | bytes 3932160 | tf_op jit(solution)/shard_map/concatenate | solution.py:269
  40.7 3.1 %collective-permute-start.5 = (bf16[768,768]{1,0:T(8,128)(2,1)}, bf16[768,768]{1,0:T(8,128)(2,1)}, u32[]{:S(2)}, u32[]{:S(2)}) collective-permute-start(bf16[768,768]{1,0:T(8,128)(2,1)} %get-tuple-element.21), channel_id=1, source_target_pairs={{0,2},{1,7},{64,66},{65,71},{128,130},{129,135},{192,194},{193,199... | collective-permute-start | bytes 3538952 | tf_op jit(solution)/shard_map/ppermute | solution.py:39
  43.9 2.7 %collective-permute-start.6 = (bf16[768,768]{1,0:T(8,128)(2,1)}, bf16[768,768]{1,0:T(8,128)(2,1)}, u32[]{:S(2)}, u32[]{:S(2)}) collective-permute-start(bf16[768,768]{1,0:T(8,128)(2,1)} %get-tuple-element.20), channel_id=1, source_target_pairs={{0,8},{1,57},{64,72},{65,121},{128,136},{129,185},{192,200},{193,2... | collective-permute-start | bytes 3538952 | tf_op jit(solution)/shard_map/ppermute | solution.py:39
  46.7 0.1 copy.25
  46.8 4.3 %collective-permute-start.1 = (bf16[128,768]{1,0:T(8,128)(2,1)S(1)}, bf16[128,768]{1,0:T(8,128)(2,1)}, u32[]{:S(2)}, u32[]{:S(2)}) collective-permute-start(bf16[128,768]{1,0:T(8,128)(2,1)S(1)} %copy.25), channel_id=1, source_target_pairs={{0,1},{1,0},{64,65},{65,64},{128,129},{129,128},{192,193},{193,192... | collective-permute-start | bytes 589832 | tf_op jit(solution)/shard_map/ppermute | solution.py:43
  51.4 0.9 collective-permute-done.1
  52.3 1.0 pad_maximum_fusion.2.rot_ref
  53.3 0.8 constant_dynamic-slice_fusion
  54.1 7.5 %collective-permute-start.7 = (bf16[256,768]{1,0:T(8,128)(2,1)}, bf16[256,768]{1,0:T(8,128)(2,1)}, u32[]{:S(2)}, u32[]{:S(2)}) collective-permute-start(bf16[256,768]{1,0:T(8,128)(2,1)} %constant_dynamic-slice_fusion), channel_id=1, source_target_pairs={{0,10},{1,63},{64,74},{65,127},{128,138},{129,191},{192,202},{193,... | collective-permute-start | bytes 1179656 | tf_op jit(solution)/shard_map/ppermute | solution.py:39
  61.6 1.0 copy-done.2
  62.6 5.8 %shards.3 = (bf16[128,8192]{1,0:T(8,128)(2,1)}, bf16[128,1280]{1,0:T(8,128)(2,1)}, f32[5,4,768]{2,1,0:T(4,128)S(1)}) custom-call(s32[5]{0:T(128)S(1)} %stack.143.table, bf16[128,8192]{1,0:T(8,128)(2,1)S(1)} %copy-done, bf16[128,8192]{1,0:T(8,128)(2,1)} %collective-permute-done.other_ref, bf16[256,768]{1,0:T(8,128)(2,1)S(1)} %pad_maximum_fusion.2.rot_ref, ...), custom_call_target="tpu_custom_call" | custom-call | flops 1006632960 | bytes 3276800 | tf_op jit(solution)/shard_map/shards/pallas_call | solution.py:139
  68.4 1.9 %collective-permute-start.10 = (bf16[128,1280]{1,0:T(8,128)(2,1)}, bf16[128,1280]{1,0:T(8,128)(2,1)}, u32[]{:S(2)}, u32[]{:S(2)}) collective-permute-start(bf16[128,1280]{1,0:T(8,128)(2,1)} %get-tuple-element.13), channel_id=1, source_target_pairs={{0,1},{1,0},{64,65},{65,64},{128,129},{129,128},{192,193},{193,192... | collective-permute-start | bytes 983048 | tf_op jit(solution)/shard_map/ppermute | solution.py:43
  70.3 4.8 %shards.4 = (bf16[128,8192]{1,0:T(8,128)(2,1)}, bf16[128,1024]{1,0:T(8,128)(2,1)}, f32[4,4,768]{2,1,0:T(4,128)S(1)}) custom-call(s32[4]{0:T(128)S(1)} %pad_add_fusion.1.table, bf16[128,8192]{1,0:T(8,128)(2,1)S(1)} %copy-done, bf16[128,8192]{1,0:T(8,128)(2,1)} %collective-permute-done.other_ref, ...), custom_call_target="tpu_custom_call", output_to_operand_aliasing={{0}: (6, {})} | custom-call | flops 805306368 | bytes 2621440 | tf_op jit(solution)/shard_map/shards/pallas_call | solution.py:139
  75.1 2.4 %collective-permute-start.9 = (bf16[128,1024]{1,0:T(8,128)(2,1)}, bf16[128,1024]{1,0:T(8,128)(2,1)S(1)}, u32[]{:S(2)}, u32[]{:S(2)}) collective-permute-start(bf16[128,1024]{1,0:T(8,128)(2,1)} %get-tuple-element.12), channel_id=1, source_target_pairs={{0,1},{1,0},{64,65},{65,64},{128,129},{129,128},{192,193},{193,192... | collective-permute-start | bytes 786440 | tf_op jit(solution)/shard_map/ppermute | solution.py:43
  77.6 0.1 stack.127.table
  77.7 0.1 stack.150.table
  77.8 0.1 stack.149.table
  78.0 3.8 %place.3.grad_in = bf16[128,8192]{1,0:T(8,128)(2,1)} custom-call(s32[5]{0:T(128)S(1)} %stack.149.table, bf16[128,1280]{1,0:T(8,128)(2,1)} %collective-permute-done.10.block_ref, bf16[128,8192]{1,0:T(8,128)(2,1)} %get-tuple-element.14.grad_in), custom_call_target="tpu_custom_call", output_to_operand_aliasing={{}: (2, {})} | custom-call | bytes 655360 | tf_op jit(solution)/shard_map/place/pallas_call | solution.py:173
  81.8 1.9 %place.4.refs_3_ = bf16[128,8192]{1,0:T(8,128)(2,1)} custom-call(s32[4]{0:T(128)S(1)} %pad_add_fusion.table, bf16[128,1024]{1,0:T(8,128)(2,1)S(1)} %collective-permute-done.9.block_ref, bf16[128,8192]{1,0:T(8,128)(2,1)} %place.3.grad_in), custom_call_target="tpu_custom_call", output_to_operand_aliasing={{}: (2, {})} | custom-call | bytes 524288 | tf_op jit(solution)/shard_map/place/pallas_call | solution.py:173
  83.7 7.2 %shards.5 = (bf16[128,8192]{1,0:T(8,128)(2,1)}, bf16[128,1792]{1,0:T(8,128)(2,1)S(1)}, f32[7,4,768]{2,1,0:T(4,128)S(1)}) custom-call(s32[7]{0:T(128)S(1)} %stack.127.table, bf16[128,8192]{1,0:T(8,128)(2,1)S(1)} %copy-done, bf16[128,8192]{1,0:T(8,128)(2,1)} %collective-permute-done.other_ref, ...), custom_call_target="tpu_custom_call", output_to_operand_aliasing={{0}: (7, {})} | custom-call | flops 1409286144 | bytes 4587520 | tf_op jit(solution)/shard_map/shards/pallas_call | solution.py:139
  90.9 1.2 spread.1
  92.2 3.6 %all-to-all-start = ((bf16[32,4,768]{2,1,0:T(4,128)(2,1)}), bf16[32,4,768]{2,1,0:T(4,128)(2,1)S(1)}, u32[]{:S(2)}, u32[]{:S(2)}) async-start(bf16[32,4,768]{2,1,0:T(4,128)(2,1)} %spread.1), calls=%async_computation | async-start | bytes 393216 | tf_op jit(solution)/shard_map/all_to_all | solution.py:285
  95.8 2.1 %collective-permute-start.11 = (bf16[128,1792]{1,0:T(8,128)(2,1)S(1)}, bf16[128,1792]{1,0:T(8,128)(2,1)S(1)}, u32[]{:S(2)}, u32[]{:S(2)}) collective-permute-start(bf16[128,1792]{1,0:T(8,128)(2,1)S(1)} %get-tuple-element.15), channel_id=1, source_target_pairs={{0,1},{1,0},{64,65},{65,64},{128,129},{129,128},{192,193},{193,192... | collective-permute-start | bytes 1376264 | tf_op jit(solution)/shard_map/ppermute | solution.py:43
  98.0 7.5 %all-to-all-done = bf16[32,4,768]{2,1,0:T(4,128)(2,1)S(1)} async-done(((bf16[32,4,768]{2,1,0:T(4,128)(2,1)}), bf16[32,4,768]{2,1,0:T(4,128)(2,1)S(1)}, u32[]{:S(2)}, u32[]{:S(2)}) %all-to-all-start) | async-done | bytes 196640 | tf_op jit(solution)/shard_map/all_to_all | solution.py:285
  105.5 0.1 reduce_sum.31
  105.6 0.7 broadcast_in_dim.43
  106.2 10.0 %all-to-all-start.1 = ((bf16[16,4,768]{2,1,0:T(4,128)(2,1)}), bf16[16,4,768]{2,1,0:T(4,128)(2,1)S(1)}, u32[]{:S(2)}, u32[]{:S(2)}) async-start(bf16[16,4,768]{2,1,0:T(4,128)(2,1)} %broadcast_in_dim.43), calls=%async_computation.1 | async-start | bytes 196608 | tf_op jit(solution)/shard_map/all_to_all | solution.py:288
  116.3 0.1 stack.119.table
  116.4 3.1 %place.5 = bf16[128,8192]{1,0:T(8,128)(2,1)} custom-call(s32[7]{0:T(128)S(1)} %stack.119.table, bf16[128,1792]{1,0:T(8,128)(2,1)S(1)} %collective-permute-done.11.block_ref, bf16[128,8192]{1,0:T(8,128)(2,1)} %get-tuple-element.16.grad_in), custom_call_target="tpu_custom_call", output_to_operand_aliasing={{}: (2, {})} | custom-call | bytes 917504 | tf_op jit(solution)/shard_map/place/pallas_call | solution.py:173
  119.5 8.5 %all-to-all-done.1 = bf16[16,4,768]{2,1,0:T(4,128)(2,1)S(1)} async-done(((bf16[16,4,768]{2,1,0:T(4,128)(2,1)}), bf16[16,4,768]{2,1,0:T(4,128)(2,1)S(1)}, u32[]{:S(2)}, u32[]{:S(2)}) %all-to-all-start.1) | async-done | bytes 98336 | tf_op jit(solution)/shard_map/all_to_all | solution.py:288
  128.1 0.6 multiply_divide_fusion
  (34 shorter events, 0.5 us)
Async XLA Ops:
  0.6 16.0 %copy-start = (bf16[128,8192]{1,0:T(8,128)(2,1)S(1)}, bf16[128,8192]{1,0:T(8,128)(2,1)}, u32[]{:S(2)}) copy-start(bf16[128,8192]{1,0:T(8,128)(2,1)} %mine_ref.5) | copy-start | bytes 6291460
  0.6 1.3 copy-start.3
  1.9 0.7 copy-start.4
  2.6 0.7 copy-start.6
  3.3 15.3 %copy-start.7 = (bf16[128,768]{1,0:T(8,128)(2,1)S(1)}, bf16[128,768]{1,0:T(8,128)(2,1)}, u32[]{:S(2)}) copy-start(bf16[128,768]{1,0:T(8,128)(2,1)} %param.7) | copy-start | bytes 589828
  3.3 15.5 %copy-start.8 = (s32[1,8]{1,0:T(1,128)S(1)}, s32[1,8]{1,0:T(1,128)}, u32[]{:S(2)}) copy-start(s32[1,8]{1,0:T(1,128)} %param.8) | copy-start | bytes 100
  3.4 10.9 %copy-start.1 = (bf16[256,768]{1,0:T(8,128)(2,1)}, bf16[256,768]{1,0:T(8,128)(2,1)S(1)}, u32[]{:S(2)}) copy-start(bf16[256,768]{1,0:T(8,128)(2,1)S(1)} %dequant.1.refs_0_) | copy-start | bytes 1179652
  12.5 13.3 %collective-permute-start.2 = (bf16[512,768]{1,0:T(8,128)(2,1)}, bf16[512,768]{1,0:T(8,128)(2,1)}, u32[]{:S(2)}, u32[]{:S(2)}) collective-permute-start(bf16[512,768]{1,0:T(8,128)(2,1)} %all_gather.3), channel_id=1, source_target_pairs={{0,8},{1,57},{64,72},{65,121},{128,136},{129,185},{192,200},{193,2... | collective-permute-start | bytes 2359304 | tf_op jit(solution)/shard_map/ppermute | solution.py:39
  14.4 13.6 %collective-permute-start.4 = (bf16[512,768]{1,0:T(8,128)(2,1)}, bf16[512,768]{1,0:T(8,128)(2,1)}, u32[]{:S(2)}, u32[]{:S(2)}) collective-permute-start(bf16[512,768]{1,0:T(8,128)(2,1)} %all_gather.3), channel_id=1, source_target_pairs={{0,2},{1,7},{64,66},{65,71},{128,130},{129,135},{192,194},{193,199... | collective-permute-start | bytes 2359304 | tf_op jit(solution)/shard_map/ppermute | solution.py:39
  16.6 45.0 %collective-permute-start = (bf16[128,8192]{1,0:T(8,128)(2,1)S(1)}, bf16[128,8192]{1,0:T(8,128)(2,1)}, u32[]{:S(2)}, u32[]{:S(2)}) collective-permute-start(bf16[128,8192]{1,0:T(8,128)(2,1)S(1)} %copy-done), channel_id=1, source_target_pairs={{0,1},{1,0},{64,65},{65,64},{128,129},{129,128},{192,193},{193,192... | collective-permute-start | bytes 6291464 | tf_op jit(solution)/shard_map/ppermute | solution.py:43
  25.8 13.3 %collective-permute-start.3 = (bf16[512,768]{1,0:T(8,128)(2,1)}, bf16[512,768]{1,0:T(8,128)(2,1)S(1)}, u32[]{:S(2)}, u32[]{:S(2)}) collective-permute-start(bf16[512,768]{1,0:T(8,128)(2,1)} %collective-permute-done.2.refs_2_), channel_id=1, source_target_pairs={{0,2},{1,7},{64,66},{65,71},{128,130},{129,135},{192,194},{193,199... | collective-permute-start | bytes 2359304 | tf_op jit(solution)/shard_map/ppermute | solution.py:39
  28.0 42.3 %collective-permute-start.8 = (bf16[512,768]{1,0:T(8,128)(2,1)}, bf16[512,768]{1,0:T(8,128)(2,1)}, u32[]{:S(2)}, u32[]{:S(2)}) collective-permute-start(bf16[512,768]{1,0:T(8,128)(2,1)} %collective-permute-done.4.refs_1_), channel_id=1, source_target_pairs={{0,57},{1,8},{64,121},{65,72},{128,185},{129,136},{192,249},{193,2... | collective-permute-start | bytes 2359304 | tf_op jit(solution)/shard_map/ppermute | solution.py:39
  40.7 43.0 %collective-permute-start.5 = (bf16[768,768]{1,0:T(8,128)(2,1)}, bf16[768,768]{1,0:T(8,128)(2,1)}, u32[]{:S(2)}, u32[]{:S(2)}) collective-permute-start(bf16[768,768]{1,0:T(8,128)(2,1)} %get-tuple-element.21), channel_id=1, source_target_pairs={{0,2},{1,7},{64,66},{65,71},{128,130},{129,135},{192,194},{193,199... | collective-permute-start | bytes 3538952 | tf_op jit(solution)/shard_map/ppermute | solution.py:39
  43.9 39.8 %collective-permute-start.6 = (bf16[768,768]{1,0:T(8,128)(2,1)}, bf16[768,768]{1,0:T(8,128)(2,1)}, u32[]{:S(2)}, u32[]{:S(2)}) collective-permute-start(bf16[768,768]{1,0:T(8,128)(2,1)} %get-tuple-element.20), channel_id=1, source_target_pairs={{0,8},{1,57},{64,72},{65,121},{128,136},{129,185},{192,200},{193,2... | collective-permute-start | bytes 3538952 | tf_op jit(solution)/shard_map/ppermute | solution.py:39
  46.8 5.5 %collective-permute-start.1 = (bf16[128,768]{1,0:T(8,128)(2,1)S(1)}, bf16[128,768]{1,0:T(8,128)(2,1)}, u32[]{:S(2)}, u32[]{:S(2)}) collective-permute-start(bf16[128,768]{1,0:T(8,128)(2,1)S(1)} %copy.25), channel_id=1, source_target_pairs={{0,1},{1,0},{64,65},{65,64},{128,129},{129,128},{192,193},{193,192... | collective-permute-start | bytes 589832 | tf_op jit(solution)/shard_map/ppermute | solution.py:43
  54.1 29.6 %collective-permute-start.7 = (bf16[256,768]{1,0:T(8,128)(2,1)}, bf16[256,768]{1,0:T(8,128)(2,1)}, u32[]{:S(2)}, u32[]{:S(2)}) collective-permute-start(bf16[256,768]{1,0:T(8,128)(2,1)} %constant_dynamic-slice_fusion), channel_id=1, source_target_pairs={{0,10},{1,63},{64,74},{65,127},{128,138},{129,191},{192,202},{193,... | collective-permute-start | bytes 1179656 | tf_op jit(solution)/shard_map/ppermute | solution.py:39
  61.6 1.0 copy-start.2
  68.4 9.6 %collective-permute-start.10 = (bf16[128,1280]{1,0:T(8,128)(2,1)}, bf16[128,1280]{1,0:T(8,128)(2,1)}, u32[]{:S(2)}, u32[]{:S(2)}) collective-permute-start(bf16[128,1280]{1,0:T(8,128)(2,1)} %get-tuple-element.13), channel_id=1, source_target_pairs={{0,1},{1,0},{64,65},{65,64},{128,129},{129,128},{192,193},{193,192... | collective-permute-start | bytes 983048 | tf_op jit(solution)/shard_map/ppermute | solution.py:43
  75.1 6.7 %collective-permute-start.9 = (bf16[128,1024]{1,0:T(8,128)(2,1)}, bf16[128,1024]{1,0:T(8,128)(2,1)S(1)}, u32[]{:S(2)}, u32[]{:S(2)}) collective-permute-start(bf16[128,1024]{1,0:T(8,128)(2,1)} %get-tuple-element.12), channel_id=1, source_target_pairs={{0,1},{1,0},{64,65},{65,64},{128,129},{129,128},{192,193},{193,192... | collective-permute-start | bytes 786440 | tf_op jit(solution)/shard_map/ppermute | solution.py:43
  92.2 13.3 %all-to-all-start = ((bf16[32,4,768]{2,1,0:T(4,128)(2,1)}), bf16[32,4,768]{2,1,0:T(4,128)(2,1)S(1)}, u32[]{:S(2)}, u32[]{:S(2)}) async-start(bf16[32,4,768]{2,1,0:T(4,128)(2,1)} %spread.1), calls=%async_computation | async-start | bytes 393216 | tf_op jit(solution)/shard_map/all_to_all | solution.py:285
  95.8 20.6 %collective-permute-start.11 = (bf16[128,1792]{1,0:T(8,128)(2,1)S(1)}, bf16[128,1792]{1,0:T(8,128)(2,1)S(1)}, u32[]{:S(2)}, u32[]{:S(2)}) collective-permute-start(bf16[128,1792]{1,0:T(8,128)(2,1)S(1)} %get-tuple-element.15), channel_id=1, source_target_pairs={{0,1},{1,0},{64,65},{65,64},{128,129},{129,128},{192,193},{193,192... | collective-permute-start | bytes 1376264 | tf_op jit(solution)/shard_map/ppermute | solution.py:43
  106.2 21.9 %all-to-all-start.1 = ((bf16[16,4,768]{2,1,0:T(4,128)(2,1)}), bf16[16,4,768]{2,1,0:T(4,128)(2,1)S(1)}, u32[]{:S(2)}, u32[]{:S(2)}) async-start(bf16[16,4,768]{2,1,0:T(4,128)(2,1)} %broadcast_in_dim.43), calls=%async_computation.1 | async-start | bytes 196608 | tf_op jit(solution)/shard_map/all_to_all | solution.py:288
  116.4 11.7 %copy-start.5 = (f32[4,768]{1,0:T(4,128)S(1)}, f32[4,768]{1,0:T(4,128)}, u32[]{:S(2)}) copy-start(f32[4,768]{1,0:T(4,128)} %steps_ref.1) | copy-start | bytes 36868

commit v2 on v1

v2 whole, which is shorter than its diff:
```python
import functools
import math

import jax
import jax.numpy as jnp
from jax import lax
from jax.experimental import pallas as pl
from jax.experimental.pallas import tpu as pltpu
from jax.sharding import PartitionSpec as P

HEAD = 128
GROUP = 64
AXES = ("dp", "tensor")
NX, NY, NYL, NZ = 4, 8, 4, 8
VMEM = 24 * 1024 * 1024
DEQUANT_VMEM = 56 * 1024 * 1024


def device_at(x, y, z, core):
    x, y, z = x % NX, y % NY, z % NZ
    dp = z * (NY // NYL) + y // NYL
    return dp * (NX * NYL * 2) + ((y % NYL) * NX + x) * 2 + core


def permutation(target):
    return [
        (device_at(x, y, z, core), device_at(*target(x, y, z, core)))
        for x in range(NX)
        for y in range(NY)
        for z in range(NZ)
        for core in range(2)
    ]


def send(value, dx, dy, cross=False):
    def target(x, y, z, core):
        sign = 1 if (core == 0) != cross else -1
        return x + sign * dx, y + sign * dy, z, core ^ int(cross)

    return lax.ppermute(value, AXES, permutation(target))


def swap(value):
    return lax.ppermute(value, AXES, permutation(lambda x, y, z, core: (x, y, z, core ^ 1)))


def token_positions(lengths, indices):
    count = lengths.shape[0]
    order = jnp.arange(count, dtype=jnp.int32)
    ends = jnp.sum(jnp.where(order[:, None] <= order[None, :], lengths[:, None], 0), axis=0)
    starts = jnp.where(ends[None, :] <= indices[:, None], ends[None, :], 0)
    return indices - jnp.max(starts, axis=1)


def rope_back(cotangent, positions):
    count = cotangent.shape[0]
    split = cotangent.astype(jnp.float32).reshape(count, -1, HEAD)
    middle = HEAD // 2
    freqs = jnp.exp(jnp.arange(middle, dtype=jnp.float32) * (-2.0 * math.log(10000.0) / HEAD))
    angles = positions.astype(jnp.float32)[:, None] * freqs[None, :]
    cosine = jnp.cos(angles)[:, None, :]
    sine = jnp.sin(angles)[:, None, :]
    first = split[..., :middle]
    second = split[..., middle:]
    lower = first * cosine + second * sine
    upper = second * cosine - first * sine
    return jnp.concatenate([lower, upper], axis=-1).reshape(count, -1).astype(jnp.bfloat16)


def dequant_kernel(codes_hbm, zeros_hbm, steps_hbm, weight_ref, codes, zeros, steps, sems):
    groups = zeros.shape[0]
    copies = [
        pltpu.make_async_copy(zeros_hbm, zeros, sems.at[0]),
        pltpu.make_async_copy(steps_hbm, steps, sems.at[1]),
    ]
    for group in range(groups):
        rows = pl.ds(group * GROUP, GROUP)
        copies.append(pltpu.make_async_copy(codes_hbm.at[rows], codes.at[rows], sems.at[2 + group]))
    for copy in copies:
        copy.start()
    copies[0].wait()
    copies[1].wait()
    for group in range(groups):
        rows = pl.ds(group * GROUP, GROUP)
        copies[2 + group].wait()
        levels = (codes[rows, :] - zeros[group : group + 1, :]).astype(jnp.float32)
        weight_ref[rows, :] = (steps[group : group + 1, :] * levels).astype(jnp.bfloat16)


def dequant(codes, zeros, steps):
    return pl.pallas_call(
        dequant_kernel,
        out_shape=jax.ShapeDtypeStruct(codes.shape, jnp.bfloat16),
        in_specs=[pl.BlockSpec(memory_space=pl.ANY)] * 3,
        out_specs=pl.BlockSpec(memory_space=pltpu.VMEM),
        scratch_shapes=[
            pltpu.VMEM(codes.shape, codes.dtype),
            pltpu.VMEM(zeros.shape, zeros.dtype),
            pltpu.VMEM(steps.shape, steps.dtype),
            pltpu.SemaphoreType.DMA((2 + zeros.shape[0],)),
        ],
        compiler_params=pltpu.CompilerParams(vmem_limit_bytes=DEQUANT_VMEM),
        name="dequant",
    )(codes, zeros, steps)


def units_of(weights, rows):
    return [(ref, at) for ref in weights for at in range(0, ref.shape[0], rows)]


def columns_of(table, unit, rows):
    return pl.ds(pl.multiple_of(table[unit] * rows, rows), rows)


def group_sums(table, unit, weight, mine_ref, other_ref, rot_ref):
    rows, cols = weight.shape
    columns = columns_of(table, unit, rows)
    feats = jnp.concatenate([mine_ref[:, columns], other_ref[:, columns]], axis=0)
    weight_grad = lax.dot_general(
        feats, rot_ref[...], (((0,), (0,)), ((), ())), preferred_element_type=jnp.float32
    )
    product = weight_grad * weight.astype(jnp.float32)
    return product.reshape(rows // GROUP, GROUP, cols).sum(axis=1)


def put_grad(table, unit, weight, rot_ref, own, sent_ref, grad_ref, sems):
    rows = weight.shape[0]
    tokens = own.shape[0]
    grad = lax.dot_general(
        rot_ref[...], weight, (((1,), (1,)), ((), ())), preferred_element_type=jnp.float32
    ).astype(jnp.bfloat16)
    block = pl.ds(unit * rows, rows)
    own[:, block] = grad[:tokens]
    sent_ref[:, block] = grad[tokens:]
    copy = pltpu.make_async_copy(
        own.at[:, block], grad_ref.at[:, columns_of(table, unit, rows)], sems.at[unit]
    )
    copy.start()
    return copy


def near_kernel(rows, count, table, mine_ref, other_ref, rot_ref, *refs):
    weights, (grad_ref, sent_ref, sums_ref, own, sems) = refs[:count], refs[count:]
    copies = []
    for unit, (ref, at) in enumerate(units_of(weights, rows)):
        weight = ref[at : at + rows, :]
        copies.append(put_grad(table, unit, weight, rot_ref, own, sent_ref, grad_ref, sems))
        sums_ref[unit] = group_sums(table, unit, weight, mine_ref, other_ref, rot_ref)
    for copy in copies:
        copy.wait()


def far_sums_kernel(rows, count, near, table, mine_ref, other_ref, rot_ref, *refs):
    weights, (near_ref, all_ref) = refs[:count], refs[count:]
    all_ref[...] = jnp.zeros_like(all_ref)
    for unit in range(near):
        all_ref[table[unit]] = near_ref[unit].astype(all_ref.dtype)
    for unit, (ref, at) in enumerate(units_of(weights, rows), near):
        weight = ref[at : at + rows, :]
        sums = group_sums(table, unit, weight, mine_ref, other_ref, rot_ref)
        all_ref[table[unit]] = sums.astype(all_ref.dtype)


def far_grad_kernel(rows, count, table, rot_ref, *refs):
    weights, (_, grad_ref, sent_ref, own, sems) = refs[:count], refs[count:]
    copies = []
    for unit, (ref, at) in enumerate(units_of(weights, rows)):
        weight = ref[at : at + rows, :]
        copies.append(put_grad(table, unit, weight, rot_ref, own, sent_ref, grad_ref, sems))
    for copy in copies:
        copy.wait()


def place_kernel(count, table, blocks_ref, grad_in, grad_ref, sems):
    rows = blocks_ref.shape[1] // count
    copies = [
        pltpu.make_async_copy(
            blocks_ref.at[:, pl.ds(unit * rows, rows)],
            grad_ref.at[:, columns_of(table, unit, rows)],
            sems.at[unit],
        )
        for unit in range(count)
    ]
    for copy in copies:
        copy.start()
    for copy in copies:
        copy.wait()


SMEM_SPEC = pl.BlockSpec(memory_space=pltpu.SMEM)
VMEM_SPEC = pl.BlockSpec(memory_space=pltpu.VMEM)
ANY_SPEC = pl.BlockSpec(memory_space=pl.ANY)


def cost(units, rows, cols, tokens, dots):
    return pl.CostEstimate(
        flops=4 * dots * units * rows * cols * tokens,
        bytes_accessed=units * rows * (cols * 2 + tokens * 4),
        transcendentals=0,
    )


def near_shards(table, mine, other, rot, weights, rows):
    tokens, width = mine.shape
    cols = rot.shape[1]
    total = sum(weight.shape[0] for weight in weights) // rows
    return pl.pallas_call(
        functools.partial(near_kernel, rows, len(weights)),
        out_shape=(
            jax.ShapeDtypeStruct((tokens, width), jnp.bfloat16),
            jax.ShapeDtypeStruct((tokens, total * rows), jnp.bfloat16),
            jax.ShapeDtypeStruct((total, rows // GROUP, cols), jnp.float32),
        ),
        in_specs=[SMEM_SPEC] + [VMEM_SPEC] * (3 + len(weights)),
        out_specs=(ANY_SPEC, VMEM_SPEC, VMEM_SPEC),
        scratch_shapes=[
            pltpu.VMEM((tokens, total * rows), jnp.bfloat16),
            pltpu.SemaphoreType.DMA((total,)),
        ],
        cost_estimate=cost(total, rows, cols, tokens, 2),
        compiler_params=pltpu.CompilerParams(vmem_limit_bytes=VMEM),
        name="near_shards",
    )(table, mine, other, rot, *weights)


def far_sums(table, mine, other, rot, weights, near_sums, rows, devices):
    tokens = mine.shape[0]
    groups, cols = near_sums.shape[1:]
    return pl.pallas_call(
        functools.partial(far_sums_kernel, rows, len(weights), near_sums.shape[0]),
        out_shape=jax.ShapeDtypeStruct((devices, groups, cols), jnp.bfloat16),
        in_specs=[SMEM_SPEC] + [VMEM_SPEC] * (4 + len(weights)),
        out_specs=VMEM_SPEC,
        cost_estimate=cost(devices // 4, rows, cols, tokens, 1),
        compiler_params=pltpu.CompilerParams(vmem_limit_bytes=VMEM),
        name="far_sums",
    )(table, mine, other, rot, *weights, near_sums)


def far_grad(table, rot, weights, grad, rows):
    tokens = grad.shape[0]
    cols = rot.shape[1]
    total = sum(weight.shape[0] for weight in weights) // rows
    return pl.pallas_call(
        functools.partial(far_grad_kernel, rows, len(weights)),
        out_shape=(
            jax.ShapeDtypeStruct(grad.shape, grad.dtype),
            jax.ShapeDtypeStruct((tokens, total * rows), jnp.bfloat16),
        ),
        in_specs=[SMEM_SPEC] + [VMEM_SPEC] * (1 + len(weights)) + [ANY_SPEC],
        out_specs=(ANY_SPEC, VMEM_SPEC),
        scratch_shapes=[
            pltpu.VMEM((tokens, total * rows), jnp.bfloat16),
            pltpu.SemaphoreType.DMA((total,)),
        ],
        input_output_aliases={2 + len(weights): 0},
        cost_estimate=cost(total, rows, cols, tokens, 1),
        compiler_params=pltpu.CompilerParams(vmem_limit_bytes=VMEM),
        name="far_grad",
    )(table, rot, *weights, grad)


def place(table, blocks, grad, rows):
    count = blocks.shape[1] // rows
    return pl.pallas_call(
        functools.partial(place_kernel, count),
        out_shape=jax.ShapeDtypeStruct(grad.shape, grad.dtype),
        in_specs=[SMEM_SPEC, ANY_SPEC, ANY_SPEC],
        out_specs=ANY_SPEC,
        scratch_shapes=[pltpu.SemaphoreType.DMA((count,))],
        input_output_aliases={2: 0},
        cost_estimate=pl.CostEstimate(
            flops=0, bytes_accessed=2 * blocks.size * 2, transcendentals=0
        ),
        compiler_params=pltpu.CompilerParams(vmem_limit_bytes=VMEM),
        name="place",
    )(table, blocks, grad)


def unit_table(x, y, core):
    sign = 2 * core - 1

    def owner(dx, dy, half):
        return (((y + sign * dy) % NYL) * NX + (x + sign * dx) % NX) * 2 + half

    return (
        [owner(0, 0, core)]
        + [owner(1, 0, 0), owner(1, 0, 1)]
        + [owner(0, 1, 0), owner(0, 1, 1)]
        + [owner(1, 1, 0), owner(1, 1, 1)]
        + [owner(-1, 1, 0), owner(-1, 1, 1)]
        + [owner(2, 0, core), owner(0, 2, core)]
        + [owner(2, 1, 0), owner(2, 1, 1)]
        + [owner(1, 2, 0), owner(1, 2, 1)]
        + [owner(2, 2, core)]
    )


def per_device(activations, key_cotangent, doc_lengths, weight_codes, zero_points, step_sizes):
    tokens = activations.shape[0]
    rows = weight_codes.shape[0]
    place_in = lax.axis_index("tensor")
    devices = NX * NYL * 2
    core = place_in % 2
    x = (place_in // 2) % NX
    y = place_in // (2 * NX)
    table = jnp.stack(unit_table(x, y, core)).astype(jnp.int32)
    theirs = jnp.stack(unit_table(x, y, 1 - core)).astype(jnp.int32)

    weight = dequant(weight_codes, zero_points, step_sizes)
    pairs = [[2 * chip, 2 * chip + 1] for chip in range(NX * NYL)]
    chip_weight = lax.all_gather(weight, "tensor", axis=0, tiled=True, axis_index_groups=pairs)

    from_x = send(chip_weight, 1, 0)
    from_y = send(chip_weight, 0, 1)

    indices = place_in * tokens + jnp.arange(tokens, dtype=jnp.int32)
    mine = rope_back(key_cotangent, token_positions(doc_lengths[0], indices))
    rot = jnp.concatenate([mine, swap(mine)], axis=0)
    others = swap(activations)
    from_x, from_y, rot = lax.optimization_barrier((from_x, from_y, rot))

    def my_half(value):
        return lax.dynamic_slice_in_dim(value, core * rows, rows, axis=0)

    from_xy = send(from_y, 1, 0)
    from_yx = send(from_x, 0, 1, cross=True)
    half_x, half_y = my_half(from_x), my_half(from_y)
    far_xx = send(half_x, 1, 0)
    far_yy = send(half_y, 0, 1)
    from_xy, far_xx, _ = lax.optimization_barrier((from_xy, far_xx, half_y))

    far_x = send(from_xy, 1, 0)
    far_y = send(from_xy, 0, 1)
    far = send(my_half(from_xy), 1, 1)

    near = [weight, from_x, from_y, from_xy, from_yx]
    grad, sent_near, sums_near = near_shards(table[:9], activations, others, rot, near, rows)
    got_near = swap(sent_near)
    grad = place(theirs[:9], got_near, grad, rows)

    fars = [far_xx, far_yy, far_x, far_y, far]
    sums = far_sums(table, activations, others, rot, fars, sums_near, rows, devices)
    shares = lax.all_to_all(sums, "tensor", split_axis=0, concat_axis=0, tiled=True)

    grad, sent_far = far_grad(table[9:], rot, fars, grad, rows)
    got_far = swap(sent_far)

    share = jnp.sum(shares.astype(jnp.float32), axis=0).astype(jnp.bfloat16)
    copies = lax.axis_size("dp")
    totals = lax.all_to_all(
        jnp.broadcast_to(share[None], (copies, *share.shape)),
        "dp",
        split_axis=0,
        concat_axis=0,
        tiled=True,
    )
    seq_tokens = tokens * devices
    total = jnp.sum(totals.astype(jnp.float32), axis=0)
    step_grad = total / (seq_tokens * step_sizes)
    grad = place(theirs[9:], got_far, grad, rows)
    return (grad, step_grad)


def solution(mesh):
    in_specs = (
        P(("dp", "tensor"), None),
        P(("dp", "tensor"), None),
        P("dp", None),
        P("tensor", None),
        P("tensor", None),
        P("tensor", None),
    )
    out_specs = (P(("dp", "tensor"), None), P("tensor", None))
    return jax.shard_map(
        per_device, mesh=mesh, in_specs=in_specs, out_specs=out_specs, check_vma=False
    )
```

time: 130 us -> 138 us (1.062)
  Pallas kernels: 28 us -> 36.2 us
  starting transfers between devices: 48.5 us -> 55.1 us
  waiting for transfers between devices: 30 us -> 24.2 us
  other arithmetic: 3.94 us -> 1.27 us
  blocking collectives: 9.01 us -> 10.8 us
    all_to_all x1, waiting for transfers between devices: 8.55 us -> 0.01 us  [per_device(): lax.all_to_all(jnp.broadcast_to(share[None], (copies, *share.shape)), 'dp...]
    all_to_all x1, starting transfers between devices: 3.65 us -> 11.3 us  [per_device(): lax.all_to_all(sums, 'tensor', split_axis=0, concat_axis=0, tiled=True)]
    pallas_call x7 -> x5, Pallas kernels: 27.9 us -> 34 us  [the longest x2 21 us: place(): pl.pallas_call(functools.partial(place_kernel, count), out_shape=jax.Shap...]
    ppermute x5 -> x4, starting transfers between devices: 12.7 us -> 10.2 us  [swap(): lax.ppermute(value, AXES, permutation(lambda x, y, z, core: (x, y, z, cor...]
    all_to_all x1, waiting for transfers between devices: 7.48 us -> 9.71 us  [per_device(): lax.all_to_all(sums, 'tensor', split_axis=0, concat_axis=0, tiled=True)]
    pallas_call x1, Pallas kernels: 0.1 us -> 2.23 us  [dequant(): pl.pallas_call(dequant_kernel, out_shape=jax.ShapeDtypeStruct(codes.shape...]
    all_gather x1, blocking collectives: 9.01 us -> 10.8 us  [per_device(): lax.all_gather(weight, 'tensor', axis=0, tiled=True, axis_index_groups=pa...]
    dynamic_slice x3, local copies, waits for them, and re-layouts: 2.85 us -> 4.63 us  [my_half(): return lax.dynamic_slice_in_dim(value, core * rows, rows, axis=0)]
  transfers between devices with their start and end apart: 14 -> 15, of which waited for: 5 -> 7; matrix products, arithmetic and copies ran while one was open for 6% -> 5% of each run, Pallas kernels for 15% -> 24%
where the time goes in v2:
time: 138 us; the launch traced here: 137 us
  starting transfers between devices  55.1 us (40%)
  Pallas kernels  36.2 us (26%)
  waiting for transfers between devices  24.2 us (18%)
  blocking collectives  10.8 us (8%)
  local copies, waits for them, and re-layouts  8.08 us (6%)
    ppermute x9, starting transfers between devices, send(): return lax.ppermute(value, AXES, permutation(target))  22 us
    pallas_call x2, Pallas kernels, place(): pl.pallas_call(functools.partial(place_kernel, count), out_shape=jax.Shap...  21 us
    ppermute x9, waiting for transfers between devices, send(): return lax.ppermute(value, AXES, permutation(target))  12.8 us
    all_to_all x1, starting transfers between devices, per_device(): lax.all_to_all(jnp.broadcast_to(share[None], (copies, *share.shape)), 'dp...  11.5 us
    all_to_all x1, starting transfers between devices, per_device(): lax.all_to_all(sums, 'tensor', split_axis=0, concat_axis=0, tiled=True)  11.3 us
    all_gather x1, blocking collectives, per_device(): lax.all_gather(weight, 'tensor', axis=0, tiled=True, axis_index_groups=pa...  10.8 us
    ppermute x4, starting transfers between devices, swap(): lax.ppermute(value, AXES, permutation(lambda x, y, z, core: (x, y, z, cor...  10.2 us
    all_to_all x1, waiting for transfers between devices, per_device(): lax.all_to_all(sums, 'tensor', split_axis=0, concat_axis=0, tiled=True)  9.71 us
  transfers between devices with their start and end apart: 15, of which 7 were waited for; matrix products, arithmetic and copies ran while one was open for 5% of the time, Pallas kernels for 24%

profile of v2, /device:TPU:1, one launch (start us, length us, event | category | flops | bytes accessed | tf_op | source)
XLA Modules:
  0.0 136.9 jit_solution(7242024283666882139)
XLA Ops:
  0.7 2.2 %dequant.1.refs_0_ = bf16[256,768]{1,0:T(8,128)(2,1)} custom-call(s32[256,768]{1,0:T(8,128)} %codes_hbm.1, s32[4,768]{1,0:T(4,128)} %zeros_hbm.1, f32[4,768]{1,0:T(4,128)} %steps_hbm.1), custom_call_target="tpu_custom_call" | custom-call | tf_op jit(solution)/shard_map/dequant/pallas_call | solution.py:91
  2.9 10.8 %all_gather.3 = bf16[512,768]{1,0:T(8,128)(2,1)} all-gather(bf16[256,768]{1,0:T(8,128)(2,1)} %dequant.1.refs_0_), channel_id=1, replica_groups={{0,1},{2,3},{4,5},{6,7},{8,9},{10,11},{12,13},{14,15},{16,17},{18,19},{..., dimensions={0}, use_global_device_ids=true | all-gather | bytes 1179648 | tf_op jit(solution)/shard_map/all_gather | solution.py:312
  13.7 1.9 %collective-permute-start = (bf16[512,768]{1,0:T(8,128)(2,1)}, bf16[512,768]{1,0:T(8,128)(2,1)}, u32[]{:S(2)}, u32[]{:S(2)}) collective-permute-start(bf16[512,768]{1,0:T(8,128)(2,1)} %all_gather.3), channel_id=1, source_target_pairs={{0,2},{1,7},{64,66},{65,71},{128,130},{129,135},{192,194},{193,199... | collective-permute-start | bytes 2359304 | tf_op jit(solution)/shard_map/ppermute | solution.py:40
  15.6 2.2 %collective-permute-start.1 = (bf16[512,768]{1,0:T(8,128)(2,1)}, bf16[512,768]{1,0:T(8,128)(2,1)}, u32[]{:S(2)}, u32[]{:S(2)}) collective-permute-start(bf16[512,768]{1,0:T(8,128)(2,1)} %all_gather.3), channel_id=1, source_target_pairs={{0,8},{1,57},{64,72},{65,121},{128,136},{129,185},{192,200},{193,2... | collective-permute-start | bytes 2359304 | tf_op jit(solution)/shard_map/ppermute | solution.py:40
  17.8 1.9 %collective-permute-start.9 = (bf16[128,8192]{1,0:T(8,128)(2,1)S(1)}, bf16[128,8192]{1,0:T(8,128)(2,1)}, u32[]{:S(2)}, u32[]{:S(2)}) collective-permute-start(bf16[128,8192]{1,0:T(8,128)(2,1)S(1)} %copy-done), channel_id=1, source_target_pairs={{0,1},{1,0},{64,65},{65,64},{128,129},{129,128},{192,193},{193,192... | collective-permute-start | bytes 6291464 | tf_op jit(solution)/shard_map/ppermute | solution.py:44
  19.8 0.1 select_reduce_fusion.1
  19.9 0.1 select_reduce_fusion
  20.0 0.2 copy.21
  20.2 0.2 multiply_cosine_fusion
  20.4 0.1 add_convert_fusion
  20.5 0.1 copy.23
  20.6 2.4 %collective-permute-start.2 = (bf16[128,768]{1,0:T(8,128)(2,1)S(1)}, bf16[128,768]{1,0:T(8,128)(2,1)S(1)}, u32[]{:S(2)}, u32[]{:S(2)}) collective-permute-start(bf16[128,768]{1,0:T(8,128)(2,1)S(1)} %copy.23), channel_id=1, source_target_pairs={{0,1},{1,0},{64,65},{65,64},{128,129},{129,128},{192,193},{193,192... | collective-permute-start | bytes 589832 | tf_op jit(solution)/shard_map/ppermute | solution.py:44
  23.0 1.1 collective-permute-done.2
  24.2 2.8 %collective-permute-done.refs_1_ = bf16[512,768]{1,0:T(8,128)(2,1)} collective-permute-done((bf16[512,768]{1,0:T(8,128)(2,1)}, bf16[512,768]{1,0:T(8,128)(2,1)}, u32[]{:S(2)}, u32[]{:S(2)}) %collective-permute-start) | collective-permute-done | bytes 786464 | tf_op jit(solution)/shard_map/ppermute | solution.py:40
  27.0 1.9 %collective-permute-done.1.refs_2_ = bf16[512,768]{1,0:T(8,128)(2,1)} collective-permute-done((bf16[512,768]{1,0:T(8,128)(2,1)}, bf16[512,768]{1,0:T(8,128)(2,1)}, u32[]{:S(2)}, u32[]{:S(2)}) %collective-permute-start.1) | collective-permute-done | bytes 786464 | tf_op jit(solution)/shard_map/ppermute | solution.py:40
  29.0 1.9 %collective-permute-start.3 = (bf16[512,768]{1,0:T(8,128)(2,1)}, bf16[512,768]{1,0:T(8,128)(2,1)}, u32[]{:S(2)}, u32[]{:S(2)}) collective-permute-start(bf16[512,768]{1,0:T(8,128)(2,1)} %collective-permute-done.1.refs_2_), channel_id=1, source_target_pairs={{0,2},{1,7},{64,66},{65,71},{128,130},{129,135},{192,194},{193,199... | collective-permute-start | bytes 2359304 | tf_op jit(solution)/shard_map/ppermute | solution.py:40
  30.9 1.0 constant_dynamic-slice_fusion.2
  31.9 1.9 %collective-permute-start.4 = (bf16[256,768]{1,0:T(8,128)(2,1)S(1)}, bf16[256,768]{1,0:T(8,128)(2,1)S(1)}, u32[]{:S(2)}, u32[]{:S(2)}) collective-permute-start(bf16[256,768]{1,0:T(8,128)(2,1)S(1)} %constant_dynamic-slice_fusion.2), channel_id=1, source_target_pairs={{0,2},{1,7},{64,66},{65,71},{128,130},{129,135},{192,194},{193,199... | collective-permute-start | bytes 1179656 | tf_op jit(solution)/shard_map/ppermute | solution.py:40
  33.9 2.9 %collective-permute-start.10 = (bf16[512,768]{1,0:T(8,128)(2,1)}, bf16[512,768]{1,0:T(8,128)(2,1)S(1)}, u32[]{:S(2)}, u32[]{:S(2)}) collective-permute-start(bf16[512,768]{1,0:T(8,128)(2,1)} %collective-permute-done.refs_1_), channel_id=1, source_target_pairs={{0,57},{1,8},{64,121},{65,72},{128,185},{129,136},{192,249},{193,2... | collective-permute-start | bytes 2359304 | tf_op jit(solution)/shard_map/ppermute | solution.py:40
  36.7 1.8 %constant_dynamic-slice_fusion.1 = bf16[256,768]{1,0:T(8,128)(2,1)} fusion(bf16[512,768]{1,0:T(8,128)(2,1)} %collective-permute-done.1.refs_2_, s32[]{:T(128)S(6)} %select_n.199), kind=kLoop, calls=%fused_computation.12 | loop fusion | bytes 786436 | tf_op jit(solution)/shard_map/dynamic_slice | solution.py:324
  38.5 7.9 %collective-permute-done.4.refs_0_ = bf16[256,768]{1,0:T(8,128)(2,1)S(1)} collective-permute-done((bf16[256,768]{1,0:T(8,128)(2,1)S(1)}, bf16[256,768]{1,0:T(8,128)(2,1)S(1)}, u32[]{:S(2)}, u32[]{:S(2)}) %collective-permute-start.4) | collective-permute-done | bytes 393248 | tf_op jit(solution)/shard_map/ppermute | solution.py:40
  46.4 3.1 %collective-permute-start.6 = (bf16[512,768]{1,0:T(8,128)(2,1)}, bf16[512,768]{1,0:T(8,128)(2,1)}, u32[]{:S(2)}, u32[]{:S(2)}) collective-permute-start(bf16[512,768]{1,0:T(8,128)(2,1)} %collective-permute-done.3.refs_3_), channel_id=1, source_target_pairs={{0,2},{1,7},{64,66},{65,71},{128,130},{129,135},{192,194},{193,199... | collective-permute-start | bytes 2359304 | tf_op jit(solution)/shard_map/ppermute | solution.py:40
  49.5 3.3 %collective-permute-start.7 = (bf16[512,768]{1,0:T(8,128)(2,1)}, bf16[512,768]{1,0:T(8,128)(2,1)}, u32[]{:S(2)}, u32[]{:S(2)}) collective-permute-start(bf16[512,768]{1,0:T(8,128)(2,1)} %collective-permute-done.3.refs_3_), channel_id=1, source_target_pairs={{0,8},{1,57},{64,72},{65,121},{128,136},{129,185},{192,200},{193,2... | collective-permute-start | bytes 2359304 | tf_op jit(solution)/shard_map/ppermute | solution.py:40
  52.9 2.1 %collective-permute-start.5 = (bf16[256,768]{1,0:T(8,128)(2,1)}, bf16[256,768]{1,0:T(8,128)(2,1)}, u32[]{:S(2)}, u32[]{:S(2)}) collective-permute-start(bf16[256,768]{1,0:T(8,128)(2,1)} %constant_dynamic-slice_fusion.1), channel_id=1, source_target_pairs={{0,8},{1,57},{64,72},{65,121},{128,136},{129,185},{192,200},{193,2... | collective-permute-start | bytes 1179656 | tf_op jit(solution)/shard_map/ppermute | solution.py:40
  55.0 1.8 %constant_dynamic-slice_fusion = bf16[256,768]{1,0:T(8,128)(2,1)} fusion(bf16[512,768]{1,0:T(8,128)(2,1)} %collective-permute-done.3.refs_3_, s32[]{:T(128)S(6)} %select_n.199), kind=kLoop, calls=%fused_computation.11 | loop fusion | bytes 786436 | tf_op jit(solution)/shard_map/dynamic_slice | solution.py:324
  56.8 0.9 copy-done.2
  57.7 2.7 %collective-permute-start.8 = (bf16[256,768]{1,0:T(8,128)(2,1)}, bf16[256,768]{1,0:T(8,128)(2,1)}, u32[]{:S(2)}, u32[]{:S(2)}) collective-permute-start(bf16[256,768]{1,0:T(8,128)(2,1)} %constant_dynamic-slice_fusion), channel_id=1, source_target_pairs={{0,10},{1,63},{64,74},{65,127},{128,138},{129,191},{192,202},{193,... | collective-permute-start | bytes 1179656 | tf_op jit(solution)/shard_map/ppermute | solution.py:40
  60.5 0.1 stack.143.table
  60.6 1.1 copy-done.3
  61.7 5.8 %near_shards.1 = (bf16[128,8192]{1,0:T(8,128)(2,1)}, bf16[128,2304]{1,0:T(8,128)(2,1)}, f32[9,4,768]{2,1,0:T(4,128)S(1)}) custom-call(s32[9]{0:T(128)S(1)} %stack.143.table, bf16[128,8192]{1,0:T(8,128)(2,1)S(1)} %copy-done, bf16[128,8192]{1,0:T(8,128)(2,1)} %collective-permute-done.9.other_ref, bf16[256,768]{1,0:T(8,128)(2,1)S(1)} %pad_maximum_fusion.rot_ref, ...), custom_call_target="tpu_custom_call" | custom-call | flops 1811939328 | bytes 4718592 | tf_op jit(solution)/shard_map/near_shards/pallas_call | solution.py:207
  67.6 3.4 %collective-permute-start.11 = (bf16[128,2304]{1,0:T(8,128)(2,1)}, bf16[128,2304]{1,0:T(8,128)(2,1)}, u32[]{:S(2)}, u32[]{:S(2)}) collective-permute-start(bf16[128,2304]{1,0:T(8,128)(2,1)} %get-tuple-element.17), channel_id=1, source_target_pairs={{0,1},{1,0},{64,65},{65,64},{128,129},{129,128},{192,193},{193,192... | collective-permute-start | bytes 1769480 | tf_op jit(solution)/shard_map/ppermute | solution.py:44
  71.1 0.1 stack.144.table
  71.2 0.1 collective-permute-done.8.refs_4_
  71.3 4.0 %far_sums.1 = bf16[32,4,768]{2,1,0:T(4,128)(2,1)} custom-call(s32[16]{0:T(128)S(1)} %stack.144.table, bf16[128,8192]{1,0:T(8,128)(2,1)S(1)} %copy-done, bf16[128,8192]{1,0:T(8,128)(2,1)} %collective-permute-done.9.other_ref, bf16[256,768]{1,0:T(8,128)(2,1)S(1)} %pad_maximum_fusion.rot_ref, bf16[256,768]{1,0:T(8,128)(2,1)S(1)} %collective-permute-done.4.refs_0_, ...), custom_call_target="tpu_custom_call" | custom-call | flops 805306368 | bytes 4194304 | tf_op jit(solution)/shard_map/far_sums/pallas_call | solution.py:229
  75.2 11.3 %all-to-all-start = ((bf16[32,4,768]{2,1,0:T(4,128)(2,1)}), bf16[32,4,768]{2,1,0:T(4,128)(2,1)S(1)}, u32[]{:S(2)}, u32[]{:S(2)}) async-start(bf16[32,4,768]{2,1,0:T(4,128)(2,1)} %far_sums.1), calls=%async_computation | async-start | bytes 393216 | tf_op jit(solution)/shard_map/all_to_all | solution.py:344
  86.6 9.7 %all-to-all-done = bf16[32,4,768]{2,1,0:T(4,128)(2,1)S(1)} async-done(((bf16[32,4,768]{2,1,0:T(4,128)(2,1)}), bf16[32,4,768]{2,1,0:T(4,128)(2,1)S(1)}, u32[]{:S(2)}, u32[]{:S(2)}) %all-to-all-start) | async-done | bytes 196640 | tf_op jit(solution)/shard_map/all_to_all | solution.py:344
  96.3 0.1 reduce_sum.31
  96.4 0.7 broadcast_in_dim.43
  97.1 11.5 %all-to-all-start.1 = ((bf16[16,4,768]{2,1,0:T(4,128)(2,1)}), bf16[16,4,768]{2,1,0:T(4,128)(2,1)S(1)}, u32[]{:S(2)}, u32[]{:S(2)}) async-start(bf16[16,4,768]{2,1,0:T(4,128)(2,1)} %broadcast_in_dim.43), calls=%async_computation.1 | async-start | bytes 196608 | tf_op jit(solution)/shard_map/all_to_all | solution.py:351
  108.6 0.1 stack.123.table
  108.7 0.1 stack.133.table
  108.8 19.6 %place.2.refs_5_ = bf16[128,8192]{1,0:T(8,128)(2,1)} custom-call(s32[9]{0:T(128)S(1)} %stack.133.table, bf16[128,2304]{1,0:T(8,128)(2,1)} %collective-permute-done.11.blocks_ref, bf16[128,8192]{1,0:T(8,128)(2,1)} %get-tuple-element.18.grad_in), custom_call_target="tpu_custom_call", output_to_operand_aliasing={{}: (2, {})} | custom-call | bytes 1179648 | tf_op jit(solution)/shard_map/place/pallas_call | solution.py:265
  128.4 3.2 %far_grad.1 = (bf16[128,8192]{1,0:T(8,128)(2,1)}, bf16[128,1792]{1,0:T(8,128)(2,1)S(1)}) custom-call(s32[7]{0:T(128)S(1)} %stack.123.table, bf16[256,768]{1,0:T(8,128)(2,1)S(1)} %pad_maximum_fusion.rot_ref, bf16[256,768]{1,0:T(8,128)(2,1)S(1)} %collective-permute-done.4.refs_0_, ...), custom_call_target="tpu_custom_call", output_to_operand_aliasing={{0}: (7, {})} | custom-call | flops 704643072 | bytes 3670016 | tf_op jit(solution)/shard_map/far_grad/pallas_call | solution.py:244
  131.6 2.5 %collective-permute-start.12 = (bf16[128,1792]{1,0:T(8,128)(2,1)S(1)}, bf16[128,1792]{1,0:T(8,128)(2,1)S(1)}, u32[]{:S(2)}, u32[]{:S(2)}) collective-permute-start(bf16[128,1792]{1,0:T(8,128)(2,1)S(1)} %get-tuple-element.19), channel_id=1, source_target_pairs={{0,1},{1,0},{64,65},{65,64},{128,129},{129,128},{192,193},{193,192... | collective-permute-start | bytes 1376264 | tf_op jit(solution)/shard_map/ppermute | solution.py:44
  134.2 0.1 stack.115.table
  134.4 0.6 multiply_divide_fusion
  135.0 0.6 collective-permute-done.12.blocks_ref
  135.6 1.4 place.3
  (27 shorter events, 0.2 us)
Async XLA Ops:
  0.6 17.2 %copy-start = (bf16[128,8192]{1,0:T(8,128)(2,1)S(1)}, bf16[128,8192]{1,0:T(8,128)(2,1)}, u32[]{:S(2)}) copy-start(bf16[128,8192]{1,0:T(8,128)(2,1)} %mine_ref.3) | copy-start | bytes 6291460
  0.6 19.1 %copy-start.6 = (s32[1,8]{1,0:T(1,128)S(1)}, s32[1,8]{1,0:T(1,128)}, u32[]{:S(2)}) copy-start(s32[1,8]{1,0:T(1,128)} %param.8) | copy-start | bytes 100
  0.7 19.3 %copy-start.4 = (bf16[128,768]{1,0:T(8,128)(2,1)S(1)}, bf16[128,768]{1,0:T(8,128)(2,1)}, u32[]{:S(2)}) copy-start(bf16[128,768]{1,0:T(8,128)(2,1)} %param.7) | copy-start | bytes 589828
  13.7 13.3 %collective-permute-start = (bf16[512,768]{1,0:T(8,128)(2,1)}, bf16[512,768]{1,0:T(8,128)(2,1)}, u32[]{:S(2)}, u32[]{:S(2)}) collective-permute-start(bf16[512,768]{1,0:T(8,128)(2,1)} %all_gather.3), channel_id=1, source_target_pairs={{0,2},{1,7},{64,66},{65,71},{128,130},{129,135},{192,194},{193,199... | collective-permute-start | bytes 2359304 | tf_op jit(solution)/shard_map/ppermute | solution.py:40
  15.6 13.3 %collective-permute-start.1 = (bf16[512,768]{1,0:T(8,128)(2,1)}, bf16[512,768]{1,0:T(8,128)(2,1)}, u32[]{:S(2)}, u32[]{:S(2)}) collective-permute-start(bf16[512,768]{1,0:T(8,128)(2,1)} %all_gather.3), channel_id=1, source_target_pairs={{0,8},{1,57},{64,72},{65,121},{128,136},{129,185},{192,200},{193,2... | collective-permute-start | bytes 2359304 | tf_op jit(solution)/shard_map/ppermute | solution.py:40
  17.8 42.8 %collective-permute-start.9 = (bf16[128,8192]{1,0:T(8,128)(2,1)S(1)}, bf16[128,8192]{1,0:T(8,128)(2,1)}, u32[]{:S(2)}, u32[]{:S(2)}) collective-permute-start(bf16[128,8192]{1,0:T(8,128)(2,1)S(1)} %copy-done), channel_id=1, source_target_pairs={{0,1},{1,0},{64,65},{65,64},{128,129},{129,128},{192,193},{193,192... | collective-permute-start | bytes 6291464 | tf_op jit(solution)/shard_map/ppermute | solution.py:44
  20.4 40.2 %copy-start.1 = (bf16[256,768]{1,0:T(8,128)(2,1)S(1)}, bf16[256,768]{1,0:T(8,128)(2,1)}, u32[]{:S(2)}) copy-start(bf16[256,768]{1,0:T(8,128)(2,1)} %dequant.1.refs_0_) | copy-start | bytes 1179652
  20.6 3.5 %collective-permute-start.2 = (bf16[128,768]{1,0:T(8,128)(2,1)S(1)}, bf16[128,768]{1,0:T(8,128)(2,1)S(1)}, u32[]{:S(2)}, u32[]{:S(2)}) collective-permute-start(bf16[128,768]{1,0:T(8,128)(2,1)S(1)} %copy.23), channel_id=1, source_target_pairs={{0,1},{1,0},{64,65},{65,64},{128,129},{129,128},{192,193},{193,192... | collective-permute-start | bytes 589832 | tf_op jit(solution)/shard_map/ppermute | solution.py:44
  29.0 17.4 %collective-permute-start.3 = (bf16[512,768]{1,0:T(8,128)(2,1)}, bf16[512,768]{1,0:T(8,128)(2,1)}, u32[]{:S(2)}, u32[]{:S(2)}) collective-permute-start(bf16[512,768]{1,0:T(8,128)(2,1)} %collective-permute-done.1.refs_2_), channel_id=1, source_target_pairs={{0,2},{1,7},{64,66},{65,71},{128,130},{129,135},{192,194},{193,199... | collective-permute-start | bytes 2359304 | tf_op jit(solution)/shard_map/ppermute | solution.py:40
  31.9 14.5 %collective-permute-start.4 = (bf16[256,768]{1,0:T(8,128)(2,1)S(1)}, bf16[256,768]{1,0:T(8,128)(2,1)S(1)}, u32[]{:S(2)}, u32[]{:S(2)}) collective-permute-start(bf16[256,768]{1,0:T(8,128)(2,1)S(1)} %constant_dynamic-slice_fusion.2), channel_id=1, source_target_pairs={{0,2},{1,7},{64,66},{65,71},{128,130},{129,135},{192,194},{193,199... | collective-permute-start | bytes 1179656 | tf_op jit(solution)/shard_map/ppermute | solution.py:40
  33.9 22.9 %collective-permute-start.10 = (bf16[512,768]{1,0:T(8,128)(2,1)}, bf16[512,768]{1,0:T(8,128)(2,1)S(1)}, u32[]{:S(2)}, u32[]{:S(2)}) collective-permute-start(bf16[512,768]{1,0:T(8,128)(2,1)} %collective-permute-done.refs_1_), channel_id=1, source_target_pairs={{0,57},{1,8},{64,121},{65,72},{128,185},{129,136},{192,249},{193,2... | collective-permute-start | bytes 2359304 | tf_op jit(solution)/shard_map/ppermute | solution.py:40
  46.4 24.9 %collective-permute-start.6 = (bf16[512,768]{1,0:T(8,128)(2,1)}, bf16[512,768]{1,0:T(8,128)(2,1)}, u32[]{:S(2)}, u32[]{:S(2)}) collective-permute-start(bf16[512,768]{1,0:T(8,128)(2,1)} %collective-permute-done.3.refs_3_), channel_id=1, source_target_pairs={{0,2},{1,7},{64,66},{65,71},{128,130},{129,135},{192,194},{193,199... | collective-permute-start | bytes 2359304 | tf_op jit(solution)/shard_map/ppermute | solution.py:40
  49.5 21.7 %collective-permute-start.7 = (bf16[512,768]{1,0:T(8,128)(2,1)}, bf16[512,768]{1,0:T(8,128)(2,1)}, u32[]{:S(2)}, u32[]{:S(2)}) collective-permute-start(bf16[512,768]{1,0:T(8,128)(2,1)} %collective-permute-done.3.refs_3_), channel_id=1, source_target_pairs={{0,8},{1,57},{64,72},{65,121},{128,136},{129,185},{192,200},{193,2... | collective-permute-start | bytes 2359304 | tf_op jit(solution)/shard_map/ppermute | solution.py:40
  52.9 18.3 %collective-permute-start.5 = (bf16[256,768]{1,0:T(8,128)(2,1)}, bf16[256,768]{1,0:T(8,128)(2,1)}, u32[]{:S(2)}, u32[]{:S(2)}) collective-permute-start(bf16[256,768]{1,0:T(8,128)(2,1)} %constant_dynamic-slice_fusion.1), channel_id=1, source_target_pairs={{0,8},{1,57},{64,72},{65,121},{128,136},{129,185},{192,200},{193,2... | collective-permute-start | bytes 1179656 | tf_op jit(solution)/shard_map/ppermute | solution.py:40
  56.8 0.9 copy-start.2
  57.7 13.6 %collective-permute-start.8 = (bf16[256,768]{1,0:T(8,128)(2,1)}, bf16[256,768]{1,0:T(8,128)(2,1)}, u32[]{:S(2)}, u32[]{:S(2)}) collective-permute-start(bf16[256,768]{1,0:T(8,128)(2,1)} %constant_dynamic-slice_fusion), channel_id=1, source_target_pairs={{0,10},{1,63},{64,74},{65,127},{128,138},{129,191},{192,202},{193,... | collective-permute-start | bytes 1179656 | tf_op jit(solution)/shard_map/ppermute | solution.py:40
  60.6 1.1 copy-start.3
  67.6 41.2 %collective-permute-start.11 = (bf16[128,2304]{1,0:T(8,128)(2,1)}, bf16[128,2304]{1,0:T(8,128)(2,1)}, u32[]{:S(2)}, u32[]{:S(2)}) collective-permute-start(bf16[128,2304]{1,0:T(8,128)(2,1)} %get-tuple-element.17), channel_id=1, source_target_pairs={{0,1},{1,0},{64,65},{65,64},{128,129},{129,128},{192,193},{193,192... | collective-permute-start | bytes 1769480 | tf_op jit(solution)/shard_map/ppermute | solution.py:44
  75.2 21.1 %all-to-all-start = ((bf16[32,4,768]{2,1,0:T(4,128)(2,1)}), bf16[32,4,768]{2,1,0:T(4,128)(2,1)S(1)}, u32[]{:S(2)}, u32[]{:S(2)}) async-start(bf16[32,4,768]{2,1,0:T(4,128)(2,1)} %far_sums.1), calls=%async_computation | async-start | bytes 393216 | tf_op jit(solution)/shard_map/all_to_all | solution.py:344
  97.1 37.2 %all-to-all-start.1 = ((bf16[16,4,768]{2,1,0:T(4,128)(2,1)}), bf16[16,4,768]{2,1,0:T(4,128)(2,1)S(1)}, u32[]{:S(2)}, u32[]{:S(2)}) async-start(bf16[16,4,768]{2,1,0:T(4,128)(2,1)} %broadcast_in_dim.43), calls=%async_computation.1 | async-start | bytes 196608 | tf_op jit(solution)/shard_map/all_to_all | solution.py:351
  128.4 5.9 %copy-start.5 = (f32[4,768]{1,0:T(4,128)S(1)}, f32[4,768]{1,0:T(4,128)}, u32[]{:S(2)}) copy-start(f32[4,768]{1,0:T(4,128)} %steps_hbm.1) | copy-start | bytes 36868
  131.6 3.9 %collective-permute-start.12 = (bf16[128,1792]{1,0:T(8,128)(2,1)S(1)}, bf16[128,1792]{1,0:T(8,128)(2,1)S(1)}, u32[]{:S(2)}, u32[]{:S(2)}) collective-permute-start(bf16[128,1792]{1,0:T(8,128)(2,1)S(1)} %get-tuple-element.19), channel_id=1, source_target_pairs={{0,1},{1,0},{64,65},{65,64},{128,129},{129,128},{192,193},{193,192... | collective-permute-start | bytes 1376264 | tf_op jit(solution)/shard_map/ppermute | solution.py:44

commit v3 on v2

v3 whole, which is shorter than its diff:
```python
import functools
import math

import jax
import jax.numpy as jnp
from jax import lax
from jax.experimental import pallas as pl
from jax.experimental.pallas import tpu as pltpu
from jax.sharding import PartitionSpec as P

HEAD = 128
GROUP = 64
AXES = ("dp", "tensor")
NX, NY, NYL, NZ = 4, 8, 4, 8
VMEM = 12 * 1024 * 1024


def device_at(x, y, z, core):
    x, y, z = x % NX, y % NY, z % NZ
    dp = z * (NY // NYL) + y // NYL
    return dp * (NX * NYL * 2) + ((y % NYL) * NX + x) * 2 + core


def permutation(target):
    return [
        (device_at(x, y, z, core), device_at(*target(x, y, z, core)))
        for x in range(NX)
        for y in range(NY)
        for z in range(NZ)
        for core in range(2)
    ]


def send(value, dx, dy, cross=False):
    def target(x, y, z, core):
        sign = 1 if (core == 0) != cross else -1
        return x + sign * dx, y + sign * dy, z, core ^ int(cross)

    return lax.ppermute(value, AXES, permutation(target))


def swap(value):
    return lax.ppermute(value, AXES, permutation(lambda x, y, z, core: (x, y, z, core ^ 1)))


def token_positions(lengths, indices):
    count = lengths.shape[0]
    order = jnp.arange(count, dtype=jnp.int32)
    ends = jnp.sum(jnp.where(order[:, None] <= order[None, :], lengths[:, None], 0), axis=0)
    starts = jnp.where(ends[None, :] <= indices[:, None], ends[None, :], 0)
    return indices - jnp.max(starts, axis=1)


def rope_back(cotangent, positions):
    count = cotangent.shape[0]
    split = cotangent.astype(jnp.float32).reshape(count, -1, HEAD)
    middle = HEAD // 2
    freqs = jnp.exp(jnp.arange(middle, dtype=jnp.float32) * (-2.0 * math.log(10000.0) / HEAD))
    angles = positions.astype(jnp.float32)[:, None] * freqs[None, :]
    cosine = jnp.cos(angles)[:, None, :]
    sine = jnp.sin(angles)[:, None, :]
    first = split[..., :middle]
    second = split[..., middle:]
    lower = first * cosine + second * sine
    upper = second * cosine - first * sine
    return jnp.concatenate([lower, upper], axis=-1).reshape(count, -1).astype(jnp.bfloat16)


def dequant(codes, zeros, steps):
    groups, cols = zeros.shape
    levels = (codes.reshape(groups, GROUP, cols) - zeros[:, None, :]).astype(jnp.float32)
    return (steps[:, None, :] * levels).astype(jnp.bfloat16).reshape(codes.shape)


def columns_of(table, unit, rows):
    return pl.ds(pl.multiple_of(table[unit] * rows, rows), rows)


class Units:
    def __init__(self, rows, table, weights, held, sems, first=0):
        self.rows, self.table, self.held, self.first = rows, table, held, first
        self.copies = []
        for ref in weights:
            for at in range(0, ref.shape[0], rows):
                unit = len(self.copies)
                copy = pltpu.make_async_copy(
                    ref.at[pl.ds(at, rows)], held.at[pl.ds(unit * rows, rows)], sems.at[unit]
                )
                copy.start()
                self.copies.append(copy)
        self.count = len(self.copies)

    def load_features(self, mine, other, feats, sems):
        self.feats, self.feat_copies = feats, []
        tokens = mine.shape[0]
        for unit in range(self.count):
            columns = columns_of(self.table, self.first + unit, self.rows)
            block = pl.ds(unit * self.rows, self.rows)
            pair = [
                pltpu.make_async_copy(
                    ref.at[:, columns],
                    feats.at[pl.ds(core * tokens, tokens), block],
                    sems.at[2 * unit + core],
                )
                for core, ref in enumerate((mine, other))
            ]
            for copy in pair:
                copy.start()
            self.feat_copies.append(pair)

    def weight(self, unit):
        self.copies[unit].wait()
        return self.held[pl.ds(unit * self.rows, self.rows), :]

    def group_sums(self, unit, weight, rot):
        for copy in self.feat_copies[unit]:
            copy.wait()
        feats = self.feats[:, pl.ds(unit * self.rows, self.rows)]
        weight_grad = lax.dot_general(
            feats, rot, (((0,), (0,)), ((), ())), preferred_element_type=jnp.float32
        )
        product = weight_grad * weight.astype(jnp.float32)
        return product.reshape(self.rows // GROUP, GROUP, rot.shape[1]).sum(axis=1)

    def put_grad(self, unit, weight, rot, own, sent_ref, grad_ref, sems):
        tokens = own.shape[0]
        grad = lax.dot_general(
            rot, weight, (((1,), (1,)), ((), ())), preferred_element_type=jnp.float32
        ).astype(jnp.bfloat16)
        block = pl.ds(unit * self.rows, self.rows)
        own[:, block] = grad[:tokens]
        sent_ref[:, block] = grad[tokens:]
        columns = columns_of(self.table, self.first + unit, self.rows)
        copy = pltpu.make_async_copy(own.at[:, block], grad_ref.at[:, columns], sems.at[unit])
        copy.start()
        return copy


def near_kernel(rows, count, table, rot_ref, mine_ref, other_ref, *refs):
    weights, refs = refs[:count], refs[count:]
    grad_ref, sent_ref, sums_ref, held, feats, own, held_sems, feat_sems, own_sems = refs
    units = Units(rows, table, weights, held, held_sems)
    units.load_features(mine_ref, other_ref, feats, feat_sems)
    rot = rot_ref[...]
    copies = []
    for unit in range(units.count):
        weight = units.weight(unit)
        copies.append(units.put_grad(unit, weight, rot, own, sent_ref, grad_ref, own_sems))
        sums_ref[unit] = units.group_sums(unit, weight, rot)
    for copy in copies:
        copy.wait()


def far_sums_kernel(rows, count, near, table, rot_ref, near_ref, mine_ref, other_ref, *refs):
    weights, (all_ref, held, feats, held_sems, feat_sems) = refs[:count], refs[count:]
    units = Units(rows, table, weights, held, held_sems, near)
    units.load_features(mine_ref, other_ref, feats, feat_sems)
    all_ref[...] = jnp.zeros_like(all_ref)
    for unit in range(near):
        all_ref[table[unit]] = near_ref[unit].astype(all_ref.dtype)
    rot = rot_ref[...]
    for unit in range(units.count):
        sums = units.group_sums(unit, units.weight(unit), rot)
        all_ref[table[near + unit]] = sums.astype(all_ref.dtype)


def far_grad_kernel(rows, count, near, table, rot_ref, *refs):
    weights, refs = refs[:count], refs[count:]
    _, grad_ref, sent_ref, held, own, held_sems, own_sems = refs
    units = Units(rows, table, weights, held, held_sems, near)
    rot = rot_ref[...]
    copies = [
        units.put_grad(unit, units.weight(unit), rot, own, sent_ref, grad_ref, own_sems)
        for unit in range(units.count)
    ]
    for copy in copies:
        copy.wait()


SMEM_SPEC = pl.BlockSpec(memory_space=pltpu.SMEM)
VMEM_SPEC = pl.BlockSpec(memory_space=pltpu.VMEM)
ANY_SPEC = pl.BlockSpec(memory_space=pl.ANY)


def cost(units, rows, cols, tokens, dots):
    return pl.CostEstimate(
        flops=4 * dots * units * rows * cols * tokens,
        bytes_accessed=units * rows * (cols * 2 + tokens * 4),
        transcendentals=0,
    )


def scratch(units, rows, cols, tokens, feats, own):
    held = pltpu.VMEM((units * rows, cols), jnp.bfloat16)
    of_feats = pltpu.VMEM((2 * tokens, units * rows), jnp.bfloat16)
    of_own = pltpu.VMEM((tokens, units * rows), jnp.bfloat16)
    buffers = [held] + [of_feats] * feats + [of_own] * own
    sems = [units] + [2 * units] * feats + [units] * own
    return buffers + [pltpu.SemaphoreType.DMA((count,)) for count in sems]


def near_shards(table, mine, other, rot, weights, rows):
    tokens, width = mine.shape
    cols = rot.shape[1]
    total = sum(weight.shape[0] for weight in weights) // rows
    return pl.pallas_call(
        functools.partial(near_kernel, rows, len(weights)),
        out_shape=(
            jax.ShapeDtypeStruct((tokens, width), jnp.bfloat16),
            jax.ShapeDtypeStruct((tokens, total * rows), jnp.bfloat16),
            jax.ShapeDtypeStruct((total, rows // GROUP, cols), jnp.float32),
        ),
        in_specs=[SMEM_SPEC, VMEM_SPEC] + [ANY_SPEC] * (2 + len(weights)),
        out_specs=(ANY_SPEC, VMEM_SPEC, VMEM_SPEC),
        scratch_shapes=scratch(total, rows, cols, tokens, 1, 1),
        cost_estimate=cost(total, rows, cols, tokens, 2),
        compiler_params=pltpu.CompilerParams(vmem_limit_bytes=VMEM),
        name="near_shards",
    )(table, rot, mine, other, *weights)


def far_sums(table, mine, other, rot, weights, near_sums, rows, devices):
    tokens = mine.shape[0]
    near, groups, cols = near_sums.shape
    total = sum(weight.shape[0] for weight in weights) // rows
    return pl.pallas_call(
        functools.partial(far_sums_kernel, rows, len(weights), near),
        out_shape=jax.ShapeDtypeStruct((devices, groups, cols), jnp.bfloat16),
        in_specs=[SMEM_SPEC, VMEM_SPEC, VMEM_SPEC] + [ANY_SPEC] * (2 + len(weights)),
        out_specs=VMEM_SPEC,
        scratch_shapes=scratch(total, rows, cols, tokens, 1, 0),
        cost_estimate=cost(total, rows, cols, tokens, 1),
        compiler_params=pltpu.CompilerParams(vmem_limit_bytes=VMEM),
        name="far_sums",
    )(table, rot, near_sums, mine, other, *weights)


def far_grad(table, rot, weights, grad, rows, near):
    tokens = grad.shape[0]
    cols = rot.shape[1]
    total = sum(weight.shape[0] for weight in weights) // rows
    return pl.pallas_call(
        functools.partial(far_grad_kernel, rows, len(weights), near),
        out_shape=(
            jax.ShapeDtypeStruct(grad.shape, grad.dtype),
            jax.ShapeDtypeStruct((tokens, total * rows), jnp.bfloat16),
        ),
        in_specs=[SMEM_SPEC, VMEM_SPEC] + [ANY_SPEC] * (len(weights) + 1),
        out_specs=(ANY_SPEC, VMEM_SPEC),
        scratch_shapes=scratch(total, rows, cols, tokens, 0, 1),
        input_output_aliases={2 + len(weights): 0},
        cost_estimate=cost(total, rows, cols, tokens, 1),
        compiler_params=pltpu.CompilerParams(vmem_limit_bytes=VMEM),
        name="far_grad",
    )(table, rot, *weights, grad)


def place_kernel(count, first, table, blocks_ref, grad_in, grad_ref, sems):
    rows = blocks_ref.shape[1] // count
    copies = [
        pltpu.make_async_copy(
            blocks_ref.at[:, pl.ds(unit * rows, rows)],
            grad_ref.at[:, columns_of(table, first + unit, rows)],
            sems.at[unit],
        )
        for unit in range(count)
    ]
    for copy in copies:
        copy.start()
    for copy in copies:
        copy.wait()


def place(table, blocks, grad, rows, first):
    count = blocks.shape[1] // rows
    return pl.pallas_call(
        functools.partial(place_kernel, count, first),
        out_shape=jax.ShapeDtypeStruct(grad.shape, grad.dtype),
        in_specs=[SMEM_SPEC, VMEM_SPEC, ANY_SPEC],
        out_specs=ANY_SPEC,
        scratch_shapes=[pltpu.SemaphoreType.DMA((count,))],
        input_output_aliases={2: 0},
        cost_estimate=pl.CostEstimate(
            flops=0, bytes_accessed=2 * blocks.size * 2, transcendentals=0
        ),
        compiler_params=pltpu.CompilerParams(vmem_limit_bytes=VMEM),
        name="place",
    )(table, blocks, grad)


def unit_table(x, y, core):
    sign = 2 * core - 1

    def owner(dx, dy, half):
        return (((y + sign * dy) % NYL) * NX + (x + sign * dx) % NX) * 2 + half

    return (
        [owner(0, 0, core)]
        + [owner(1, 0, 0), owner(1, 0, 1)]
        + [owner(0, 1, 0), owner(0, 1, 1)]
        + [owner(1, 1, 0), owner(1, 1, 1)]
        + [owner(-1, 1, 0), owner(-1, 1, 1)]
        + [owner(2, 0, core), owner(0, 2, core)]
        + [owner(2, 1, 0), owner(2, 1, 1)]
        + [owner(-1, 2, 0), owner(-1, 2, 1)]
        + [owner(2, 2, core)]
    )


def per_device(activations, key_cotangent, doc_lengths, weight_codes, zero_points, step_sizes):
    tokens = activations.shape[0]
    rows = weight_codes.shape[0]
    place_in = lax.axis_index("tensor")
    devices = NX * NYL * 2
    core = place_in % 2
    x = (place_in // 2) % NX
    y = place_in // (2 * NX)
    table = jnp.stack(unit_table(x, y, core)).astype(jnp.int32)
    theirs = jnp.stack(unit_table(x, y, 1 - core)).astype(jnp.int32)

    weight = dequant(weight_codes, zero_points, step_sizes)
    pairs = [[2 * chip, 2 * chip + 1] for chip in range(NX * NYL)]
    chip_weight = lax.all_gather(weight, "tensor", axis=0, tiled=True, axis_index_groups=pairs)

    from_x = send(chip_weight, 1, 0)
    from_y = send(chip_weight, 0, 1)

    indices = place_in * tokens + jnp.arange(tokens, dtype=jnp.int32)
    mine = rope_back(key_cotangent, token_positions(doc_lengths[0], indices))
    rot = jnp.concatenate([mine, swap(mine)], axis=0)
    others = swap(activations)
    from_x, from_y, rot = lax.optimization_barrier((from_x, from_y, rot))

    def my_half(value):
        return lax.dynamic_slice_in_dim(value, core * rows, rows, axis=0)

    from_xy = send(from_y, 1, 0)
    from_yx = send(from_x, 0, 1, cross=True)
    far_xx = send(my_half(from_x), 1, 0)
    far_yy = send(my_half(from_y), 0, 1)
    from_xy, from_yx, _, _ = lax.optimization_barrier((from_xy, from_yx, far_xx, far_yy))

    far_x = send(from_xy, 1, 0)
    far_y = send(from_yx, 0, 1)
    far = send(my_half(from_xy), 1, 1)

    near = [weight, from_x, from_y, from_xy, from_yx]
    grad, sent_near, sums_near = near_shards(table, activations, others, rot, near, rows)
    got_near = swap(sent_near)
    grad = place(theirs, got_near, grad, rows, 0)

    fars = [far_xx, far_yy, far_x, far_y, far]
    at_hand = sums_near.shape[0]
    sums = far_sums(table, activations, others, rot, fars, sums_near, rows, devices)
    shares = lax.all_to_all(sums, "tensor", split_axis=0, concat_axis=0, tiled=True)

    grad, sent_far = far_grad(table, rot, fars, grad, rows, at_hand)
    got_far = swap(sent_far)

    share = jnp.sum(shares.astype(jnp.float32), axis=0).astype(jnp.bfloat16)
    copies = lax.axis_size("dp")
    totals = lax.all_to_all(
        jnp.broadcast_to(share[None], (copies, *share.shape)),
        "dp",
        split_axis=0,
        concat_axis=0,
        tiled=True,
    )
    seq_tokens = tokens * devices
    total = jnp.sum(totals.astype(jnp.float32), axis=0)
    step_grad = total / (seq_tokens * step_sizes)
    grad = place(theirs, got_far, grad, rows, at_hand)
    return (grad, step_grad)


def solution(mesh):
    in_specs = (
        P(("dp", "tensor"), None),
        P(("dp", "tensor"), None),
        P("dp", None),
        P("tensor", None),
        P("tensor", None),
        P("tensor", None),
    )
    out_specs = (P(("dp", "tensor"), None), P("tensor", None))
    return jax.shard_map(
        per_device, mesh=mesh, in_specs=in_specs, out_specs=out_specs, check_vma=False
    )
```

time: 138 us -> 122 us (0.88)
  Pallas kernels: 36.2 us -> 24.2 us
  local copies, waits for them, and re-layouts: 8.08 us -> 5.84 us
  blocking collectives: 10.8 us -> 9.01 us
  waiting for transfers between devices: 24.2 us -> 22.7 us
  other arithmetic: 1.27 us -> 2.66 us
    pallas_call x4 -> x3, Pallas kernels: 26.4 us -> 7.94 us  [the longest x1 4.57 us: far_grad(): pl.pallas_call(functools.partial(far_grad_kernel, rows, len(weights), nea...]
    ppermute x9, starting transfers between devices: 22 us -> 30.3 us  [send(): return lax.ppermute(value, AXES, permutation(target))]
    all_to_all x1, starting transfers between devices: 11.3 us -> 5.53 us  [per_device(): lax.all_to_all(sums, 'tensor', split_axis=0, concat_axis=0, tiled=True)]
    pallas_call x1, Pallas kernels: 5.83 us -> 10.5 us  [near_shards(): pl.pallas_call(functools.partial(near_kernel, rows, len(weights)), out_sh...]
    ppermute x9, waiting for transfers between devices: 12.8 us -> 9.48 us  [send(): return lax.ppermute(value, AXES, permutation(target))]
    all_to_all x1, waiting for transfers between devices: 0.01 us -> 2.55 us  [per_device(): lax.all_to_all(jnp.broadcast_to(share[None], (copies, *share.shape)), 'dp...]
    pallas_call x1, Pallas kernels: 3.97 us -> 5.8 us  [far_sums(): pl.pallas_call(functools.partial(far_sums_kernel, rows, len(weights), nea...]
    all_gather x1, blocking collectives: 10.8 us -> 9.01 us  [per_device(): lax.all_gather(weight, 'tensor', axis=0, tiled=True, axis_index_groups=pa...]
  transfers between devices with their start and end apart: 15 -> 15, of which waited for: 7 -> 7; matrix products, arithmetic and copies ran while one was open for 5% -> 5% of each run, Pallas kernels for 24% -> 19%
where the time goes in v3:
time: 122 us; the launch traced here: 121 us
  starting transfers between devices  55.5 us (45%)
  Pallas kernels  24.2 us (20%)
  waiting for transfers between devices  22.7 us (19%)
  blocking collectives  9.01 us (7%)
  local copies, waits for them, and re-layouts  5.84 us (5%)
  other arithmetic  2.66 us (2%)
  between operations  1.31 us (1%)
    ppermute x9, starting transfers between devices, send(): return lax.ppermute(value, AXES, permutation(target))  30.3 us
    all_to_all x1, starting transfers between devices, per_device(): lax.all_to_all(jnp.broadcast_to(share[None], (copies, *share.shape)), 'dp...  10.9 us
    pallas_call x1, Pallas kernels, near_shards(): pl.pallas_call(functools.partial(near_kernel, rows, len(weights)), out_sh...  10.5 us
    all_to_all x1, waiting for transfers between devices, per_device(): lax.all_to_all(sums, 'tensor', split_axis=0, concat_axis=0, tiled=True)  9.55 us
    ppermute x9, waiting for transfers between devices, send(): return lax.ppermute(value, AXES, permutation(target))  9.48 us
    all_gather x1, blocking collectives, per_device(): lax.all_gather(weight, 'tensor', axis=0, tiled=True, axis_index_groups=pa...  9.01 us
    ppermute x4, starting transfers between devices, swap(): lax.ppermute(value, AXES, permutation(lambda x, y, z, core: (x, y, z, cor...  8.75 us
    pallas_call x1, Pallas kernels, far_sums(): pl.pallas_call(functools.partial(far_sums_kernel, rows, len(weights), nea...  5.8 us
  transfers between devices with their start and end apart: 15, of which 7 were waited for; matrix products, arithmetic and copies ran while one was open for 5% of the time, Pallas kernels for 19%

profile of v3, /device:TPU:1, one launch (start us, length us, event | category | flops | bytes accessed | tf_op | source)
XLA Modules:
  0.0 121.2 jit_solution(17660827891936542200)
XLA Ops:
  0.7 1.4 %fusion.2.refs_0_ = bf16[256,768]{1,0:T(8,128)(2,1)S(1)} fusion(s32[256,768]{1,0:T(8,128)} %param.9, s32[4,768]{1,0:T(4,128)} %param.10, f32[4,768]{1,0:T(4,128)} %param.11), kind=kLoop, calls=%fused_computation.3 | loop fusion | flops 786432 | bytes 1204224 | tf_op jit(solution)/shard_map/convert_element_type | solution.py:72
  2.1 9.0 %all_gather.3 = bf16[512,768]{1,0:T(8,128)(2,1)} all-gather(bf16[256,768]{1,0:T(8,128)(2,1)S(1)} %fusion.2.refs_0_), channel_id=1, replica_groups={{0,1},{2,3},{4,5},{6,7},{8,9},{10,11},{12,13},{14,15},{16,17},{18,19},{..., dimensions={0}, use_global_device_ids=true | all-gather | bytes 1179648 | tf_op jit(solution)/shard_map/all_gather | solution.py:323
  11.1 1.9 %collective-permute-start = (bf16[512,768]{1,0:T(8,128)(2,1)}, bf16[512,768]{1,0:T(8,128)(2,1)}, u32[]{:S(2)}, u32[]{:S(2)}) collective-permute-start(bf16[512,768]{1,0:T(8,128)(2,1)} %all_gather.3), channel_id=1, source_target_pairs={{0,2},{1,7},{64,66},{65,71},{128,130},{129,135},{192,194},{193,199... | collective-permute-start | bytes 2359304 | tf_op jit(solution)/shard_map/ppermute | solution.py:39
  13.0 2.2 %collective-permute-start.1 = (bf16[512,768]{1,0:T(8,128)(2,1)}, bf16[512,768]{1,0:T(8,128)(2,1)}, u32[]{:S(2)}, u32[]{:S(2)}) collective-permute-start(bf16[512,768]{1,0:T(8,128)(2,1)} %all_gather.3), channel_id=1, source_target_pairs={{0,8},{1,57},{64,72},{65,121},{128,136},{129,185},{192,200},{193,2... | collective-permute-start | bytes 2359304 | tf_op jit(solution)/shard_map/ppermute | solution.py:39
  15.2 2.0 %collective-permute-start.10 = (bf16[128,8192]{1,0:T(8,128)(2,1)S(1)}, bf16[128,8192]{1,0:T(8,128)(2,1)}, u32[]{:S(2)}, u32[]{:S(2)}) collective-permute-start(bf16[128,8192]{1,0:T(8,128)(2,1)S(1)} %copy-done), channel_id=1, source_target_pairs={{0,1},{1,0},{64,65},{65,64},{128,129},{129,128},{192,193},{193,192... | collective-permute-start | bytes 6291464 | tf_op jit(solution)/shard_map/ppermute | solution.py:43
  17.3 0.1 select_reduce_fusion.1
  17.3 0.1 select_reduce_fusion
  17.4 0.2 copy.21
  17.6 0.2 multiply_cosine_fusion
  17.8 0.1 add_convert_fusion
  17.9 0.1 copy.23
  18.1 2.3 %collective-permute-start.2 = (bf16[128,768]{1,0:T(8,128)(2,1)S(1)}, bf16[128,768]{1,0:T(8,128)(2,1)S(1)}, u32[]{:S(2)}, u32[]{:S(2)}) collective-permute-start(bf16[128,768]{1,0:T(8,128)(2,1)S(1)} %copy.23), channel_id=1, source_target_pairs={{0,1},{1,0},{64,65},{65,64},{128,129},{129,128},{192,193},{193,192... | collective-permute-start | bytes 589832 | tf_op jit(solution)/shard_map/ppermute | solution.py:43
  20.4 1.1 collective-permute-done.2
  21.6 2.8 %collective-permute-done.refs_1_ = bf16[512,768]{1,0:T(8,128)(2,1)} collective-permute-done((bf16[512,768]{1,0:T(8,128)(2,1)}, bf16[512,768]{1,0:T(8,128)(2,1)}, u32[]{:S(2)}, u32[]{:S(2)}) %collective-permute-start) | collective-permute-done | bytes 786464 | tf_op jit(solution)/shard_map/ppermute | solution.py:39
  24.4 1.9 %collective-permute-done.1.refs_2_ = bf16[512,768]{1,0:T(8,128)(2,1)} collective-permute-done((bf16[512,768]{1,0:T(8,128)(2,1)}, bf16[512,768]{1,0:T(8,128)(2,1)}, u32[]{:S(2)}, u32[]{:S(2)}) %collective-permute-start.1) | collective-permute-done | bytes 786464 | tf_op jit(solution)/shard_map/ppermute | solution.py:39
  26.3 1.9 %collective-permute-start.5 = (bf16[512,768]{1,0:T(8,128)(2,1)}, bf16[512,768]{1,0:T(8,128)(2,1)}, u32[]{:S(2)}, u32[]{:S(2)}) collective-permute-start(bf16[512,768]{1,0:T(8,128)(2,1)} %collective-permute-done.1.refs_2_), channel_id=1, source_target_pairs={{0,2},{1,7},{64,66},{65,71},{128,130},{129,135},{192,194},{193,199... | collective-permute-start | bytes 2359304 | tf_op jit(solution)/shard_map/ppermute | solution.py:39
  28.2 2.8 %collective-permute-start.6 = (bf16[512,768]{1,0:T(8,128)(2,1)}, bf16[512,768]{1,0:T(8,128)(2,1)}, u32[]{:S(2)}, u32[]{:S(2)}) collective-permute-start(bf16[512,768]{1,0:T(8,128)(2,1)} %collective-permute-done.refs_1_), channel_id=1, source_target_pairs={{0,57},{1,8},{64,121},{65,72},{128,185},{129,136},{192,249},{193,2... | collective-permute-start | bytes 2359304 | tf_op jit(solution)/shard_map/ppermute | solution.py:39
  31.0 1.0 constant_dynamic-slice_fusion
  32.1 1.0 constant_dynamic-slice_fusion.1
  33.1 6.1 %collective-permute-start.4 = (bf16[256,768]{1,0:T(8,128)(2,1)S(1)}, bf16[256,768]{1,0:T(8,128)(2,1)S(1)}, u32[]{:S(2)}, u32[]{:S(2)}) collective-permute-start(bf16[256,768]{1,0:T(8,128)(2,1)S(1)} %constant_dynamic-slice_fusion), channel_id=1, source_target_pairs={{0,8},{1,57},{64,72},{65,121},{128,136},{129,185},{192,200},{193,2... | collective-permute-start | bytes 1179656 | tf_op jit(solution)/shard_map/ppermute | solution.py:39
  39.2 4.9 %collective-permute-start.3 = (bf16[256,768]{1,0:T(8,128)(2,1)S(1)}, bf16[256,768]{1,0:T(8,128)(2,1)S(1)}, u32[]{:S(2)}, u32[]{:S(2)}) collective-permute-start(bf16[256,768]{1,0:T(8,128)(2,1)S(1)} %constant_dynamic-slice_fusion.1), channel_id=1, source_target_pairs={{0,2},{1,7},{64,66},{65,71},{128,130},{129,135},{192,194},{193,199... | collective-permute-start | bytes 1179656 | tf_op jit(solution)/shard_map/ppermute | solution.py:39
  44.0 2.3 %collective-permute-done.4.refs_1_ = bf16[256,768]{1,0:T(8,128)(2,1)S(1)} collective-permute-done((bf16[256,768]{1,0:T(8,128)(2,1)S(1)}, bf16[256,768]{1,0:T(8,128)(2,1)S(1)}, u32[]{:S(2)}, u32[]{:S(2)}) %collective-permute-start.4) | collective-permute-done | bytes 393248 | tf_op jit(solution)/shard_map/ppermute | solution.py:39
  46.3 2.4 %collective-permute-done.3.refs_0_ = bf16[256,768]{1,0:T(8,128)(2,1)S(1)} collective-permute-done((bf16[256,768]{1,0:T(8,128)(2,1)S(1)}, bf16[256,768]{1,0:T(8,128)(2,1)S(1)}, u32[]{:S(2)}, u32[]{:S(2)}) %collective-permute-start.3) | collective-permute-done | bytes 393248 | tf_op jit(solution)/shard_map/ppermute | solution.py:39
  48.7 0.8 copy-done.1
  49.5 0.0 collective-permute-done.5.refs_3_
  49.5 0.0 collective-permute-done.6.refs_4_
  49.5 5.3 %collective-permute-start.7 = (bf16[512,768]{1,0:T(8,128)(2,1)}, bf16[512,768]{1,0:T(8,128)(2,1)}, u32[]{:S(2)}, u32[]{:S(2)}) collective-permute-start(bf16[512,768]{1,0:T(8,128)(2,1)} %collective-permute-done.5.refs_3_), channel_id=1, source_target_pairs={{0,2},{1,7},{64,66},{65,71},{128,130},{129,135},{192,194},{193,199... | collective-permute-start | bytes 2359304 | tf_op jit(solution)/shard_map/ppermute | solution.py:39
  54.8 2.0 %collective-permute-start.8 = (bf16[512,768]{1,0:T(8,128)(2,1)}, bf16[512,768]{1,0:T(8,128)(2,1)}, u32[]{:S(2)}, u32[]{:S(2)}) collective-permute-start(bf16[512,768]{1,0:T(8,128)(2,1)} %collective-permute-done.6.refs_4_), channel_id=1, source_target_pairs={{0,8},{1,57},{64,72},{65,121},{128,136},{129,185},{192,200},{193,2... | collective-permute-start | bytes 2359304 | tf_op jit(solution)/shard_map/ppermute | solution.py:39
  56.8 1.8 %constant_dynamic-slice_fusion.2 = bf16[256,768]{1,0:T(8,128)(2,1)} fusion(bf16[512,768]{1,0:T(8,128)(2,1)} %collective-permute-done.5.refs_3_, s32[]{:T(128)S(6)} %select_n.201), kind=kLoop, calls=%fused_computation.17 | loop fusion | bytes 786436 | tf_op jit(solution)/shard_map/dynamic_slice | solution.py:335
  58.6 3.4 %collective-permute-start.9 = (bf16[256,768]{1,0:T(8,128)(2,1)}, bf16[256,768]{1,0:T(8,128)(2,1)}, u32[]{:S(2)}, u32[]{:S(2)}) collective-permute-start(bf16[256,768]{1,0:T(8,128)(2,1)} %constant_dynamic-slice_fusion.2), channel_id=1, source_target_pairs={{0,10},{1,63},{64,74},{65,127},{128,138},{129,191},{192,202},{193,... | collective-permute-start | bytes 1179656 | tf_op jit(solution)/shard_map/ppermute | solution.py:39
  62.2 0.1 stack.135.table
  62.3 10.5 %near_shards.1 = (bf16[128,8192]{1,0:T(8,128)(2,1)}, bf16[128,2304]{1,0:T(8,128)(2,1)}, f32[9,4,768]{2,1,0:T(4,128)S(1)}) custom-call(s32[16]{0:T(128)S(1)} %stack.135.table, bf16[256,768]{1,0:T(8,128)(2,1)S(1)} %pad_maximum_fusion.rot_ref, bf16[128,8192]{1,0:T(8,128)(2,1)S(1)} %copy-done, bf16[128,8192]{1,0:T(8,128)(2,1)} %collective-permute-done.10.other_ref, ...), custom_call_target="tpu_custom_call" | custom-call | flops 1811939328 | bytes 4718592 | tf_op jit(solution)/shard_map/near_shards/pallas_call | solution.py:206
  72.7 1.9 %collective-permute-start.11 = (bf16[128,2304]{1,0:T(8,128)(2,1)}, bf16[128,2304]{1,0:T(8,128)(2,1)}, u32[]{:S(2)}, u32[]{:S(2)}) collective-permute-start(bf16[128,2304]{1,0:T(8,128)(2,1)} %get-tuple-element.17), channel_id=1, source_target_pairs={{0,1},{1,0},{64,65},{65,64},{128,129},{129,128},{192,193},{193,192... | collective-permute-start | bytes 1769480 | tf_op jit(solution)/shard_map/ppermute | solution.py:43
  74.7 0.0 collective-permute-done.8.refs_3_
  74.7 5.8 %far_sums.1 = bf16[32,4,768]{2,1,0:T(4,128)(2,1)} custom-call(s32[16]{0:T(128)S(1)} %stack.135.table, bf16[256,768]{1,0:T(8,128)(2,1)S(1)} %pad_maximum_fusion.rot_ref, f32[9,4,768]{2,1,0:T(4,128)S(1)} %get-tuple-element.21.near_ref, bf16[128,8192]{1,0:T(8,128)(2,1)S(1)} %copy-done, bf16[128,8192]{1,0:T(8,128)(2,1)} %collective-permute-done.10.other_ref, ...), custom_call_target="tpu_custom_call" | custom-call | flops 704643072 | bytes 3670016 | tf_op jit(solution)/shard_map/far_sums/pallas_call | solution.py:226
  80.5 5.5 %all-to-all-start = ((bf16[32,4,768]{2,1,0:T(4,128)(2,1)}), bf16[32,4,768]{2,1,0:T(4,128)(2,1)S(1)}, u32[]{:S(2)}, u32[]{:S(2)}) async-start(bf16[32,4,768]{2,1,0:T(4,128)(2,1)} %far_sums.1), calls=%async_computation | async-start | bytes 393216 | tf_op jit(solution)/shard_map/all_to_all | solution.py:355
  86.1 9.6 %all-to-all-done = bf16[32,4,768]{2,1,0:T(4,128)(2,1)S(1)} async-done(((bf16[32,4,768]{2,1,0:T(4,128)(2,1)}), bf16[32,4,768]{2,1,0:T(4,128)(2,1)S(1)}, u32[]{:S(2)}, u32[]{:S(2)}) %all-to-all-start) | async-done | bytes 196640 | tf_op jit(solution)/shard_map/all_to_all | solution.py:355
  95.7 0.1 reduce_sum.31
  95.8 0.7 broadcast_in_dim.30
  96.5 10.9 %all-to-all-start.1 = ((bf16[16,4,768]{2,1,0:T(4,128)(2,1)}), bf16[16,4,768]{2,1,0:T(4,128)(2,1)S(1)}, u32[]{:S(2)}, u32[]{:S(2)}) async-start(bf16[16,4,768]{2,1,0:T(4,128)(2,1)} %broadcast_in_dim.30), calls=%async_computation.1 | async-start | bytes 196608 | tf_op jit(solution)/shard_map/all_to_all | solution.py:362
  107.4 0.1 stack.118.table
  107.5 2.0 %place.2.refs_5_ = bf16[128,8192]{1,0:T(8,128)(2,1)} custom-call(s32[16]{0:T(128)S(1)} %stack.118.table, bf16[128,2304]{1,0:T(8,128)(2,1)} %collective-permute-done.11.blocks_ref, bf16[128,8192]{1,0:T(8,128)(2,1)} %get-tuple-element.18.grad_in), custom_call_target="tpu_custom_call", output_to_operand_aliasing={{}: (2, {})} | custom-call | bytes 1179648 | tf_op jit(solution)/shard_map/place/pallas_call | solution.py:276
  109.6 0.0 copy-start.5
  109.6 4.6 %far_grad.1 = (bf16[128,8192]{1,0:T(8,128)(2,1)}, bf16[128,1792]{1,0:T(8,128)(2,1)S(1)}) custom-call(s32[16]{0:T(128)S(1)} %stack.135.table, bf16[256,768]{1,0:T(8,128)(2,1)S(1)} %pad_maximum_fusion.rot_ref, bf16[256,768]{1,0:T(8,128)(2,1)S(1)} %copy-done.3, bf16[256,768]{1,0:T(8,128)(2,1)S(1)} %collective-permute-done.4.refs_1_, ...), custom_call_target="tpu_custom_call", output_to_operand_aliasing={{0}: (7, {})} | custom-call | flops 704643072 | bytes 3670016 | tf_op jit(solution)/shard_map/far_grad/pallas_call | solution.py:242
  114.1 2.5 %collective-permute-start.12 = (bf16[128,1792]{1,0:T(8,128)(2,1)S(1)}, bf16[128,1792]{1,0:T(8,128)(2,1)S(1)}, u32[]{:S(2)}, u32[]{:S(2)}) collective-permute-start(bf16[128,1792]{1,0:T(8,128)(2,1)S(1)} %get-tuple-element.19), channel_id=1, source_target_pairs={{0,1},{1,0},{64,65},{65,64},{128,129},{129,128},{192,193},{193,192... | collective-permute-start | bytes 1376264 | tf_op jit(solution)/shard_map/ppermute | solution.py:43
  116.7 2.6 %all-to-all-done.1 = bf16[16,4,768]{2,1,0:T(4,128)(2,1)S(1)} async-done(((bf16[16,4,768]{2,1,0:T(4,128)(2,1)}), bf16[16,4,768]{2,1,0:T(4,128)(2,1)S(1)}, u32[]{:S(2)}, u32[]{:S(2)}) %all-to-all-start.1) | async-done | bytes 98336 | tf_op jit(solution)/shard_map/all_to_all | solution.py:362
  119.3 0.6 multiply_divide_fusion
  119.9 1.4 %place.3 = bf16[128,8192]{1,0:T(8,128)(2,1)} custom-call(s32[16]{0:T(128)S(1)} %stack.118.table, bf16[128,1792]{1,0:T(8,128)(2,1)S(1)} %collective-permute-done.12.blocks_ref, bf16[128,8192]{1,0:T(8,128)(2,1)} %get-tuple-element.20.grad_in), custom_call_target="tpu_custom_call", output_to_operand_aliasing={{}: (2, {})} | custom-call | bytes 917504 | tf_op jit(solution)/shard_map/place/pallas_call | solution.py:276
  (24 shorter events, 0.2 us)
Async XLA Ops:
  0.6 14.6 %copy-start = (bf16[128,8192]{1,0:T(8,128)(2,1)S(1)}, bf16[128,8192]{1,0:T(8,128)(2,1)}, u32[]{:S(2)}) copy-start(bf16[128,8192]{1,0:T(8,128)(2,1)} %mine_ref.3) | copy-start | bytes 6291460
  0.6 16.6 %copy-start.6 = (s32[1,8]{1,0:T(1,128)S(1)}, s32[1,8]{1,0:T(1,128)}, u32[]{:S(2)}) copy-start(s32[1,8]{1,0:T(1,128)} %param.8) | copy-start | bytes 100
  0.7 16.8 %copy-start.4 = (bf16[128,768]{1,0:T(8,128)(2,1)S(1)}, bf16[128,768]{1,0:T(8,128)(2,1)}, u32[]{:S(2)}) copy-start(bf16[128,768]{1,0:T(8,128)(2,1)} %param.7) | copy-start | bytes 589828
  11.1 13.3 %collective-permute-start = (bf16[512,768]{1,0:T(8,128)(2,1)}, bf16[512,768]{1,0:T(8,128)(2,1)}, u32[]{:S(2)}, u32[]{:S(2)}) collective-permute-start(bf16[512,768]{1,0:T(8,128)(2,1)} %all_gather.3), channel_id=1, source_target_pairs={{0,2},{1,7},{64,66},{65,71},{128,130},{129,135},{192,194},{193,199... | collective-permute-start | bytes 2359304 | tf_op jit(solution)/shard_map/ppermute | solution.py:39
  13.0 13.3 %collective-permute-start.1 = (bf16[512,768]{1,0:T(8,128)(2,1)}, bf16[512,768]{1,0:T(8,128)(2,1)}, u32[]{:S(2)}, u32[]{:S(2)}) collective-permute-start(bf16[512,768]{1,0:T(8,128)(2,1)} %all_gather.3), channel_id=1, source_target_pairs={{0,8},{1,57},{64,72},{65,121},{128,136},{129,185},{192,200},{193,2... | collective-permute-start | bytes 2359304 | tf_op jit(solution)/shard_map/ppermute | solution.py:39
  15.2 47.1 %collective-permute-start.10 = (bf16[128,8192]{1,0:T(8,128)(2,1)S(1)}, bf16[128,8192]{1,0:T(8,128)(2,1)}, u32[]{:S(2)}, u32[]{:S(2)}) collective-permute-start(bf16[128,8192]{1,0:T(8,128)(2,1)S(1)} %copy-done), channel_id=1, source_target_pairs={{0,1},{1,0},{64,65},{65,64},{128,129},{129,128},{192,193},{193,192... | collective-permute-start | bytes 6291464 | tf_op jit(solution)/shard_map/ppermute | solution.py:43
  18.1 3.4 %collective-permute-start.2 = (bf16[128,768]{1,0:T(8,128)(2,1)S(1)}, bf16[128,768]{1,0:T(8,128)(2,1)S(1)}, u32[]{:S(2)}, u32[]{:S(2)}) collective-permute-start(bf16[128,768]{1,0:T(8,128)(2,1)S(1)} %copy.23), channel_id=1, source_target_pairs={{0,1},{1,0},{64,65},{65,64},{128,129},{129,128},{192,193},{193,192... | collective-permute-start | bytes 589832 | tf_op jit(solution)/shard_map/ppermute | solution.py:43
  26.3 23.2 %collective-permute-start.5 = (bf16[512,768]{1,0:T(8,128)(2,1)}, bf16[512,768]{1,0:T(8,128)(2,1)}, u32[]{:S(2)}, u32[]{:S(2)}) collective-permute-start(bf16[512,768]{1,0:T(8,128)(2,1)} %collective-permute-done.1.refs_2_), channel_id=1, source_target_pairs={{0,2},{1,7},{64,66},{65,71},{128,130},{129,135},{192,194},{193,199... | collective-permute-start | bytes 2359304 | tf_op jit(solution)/shard_map/ppermute | solution.py:39
  28.2 21.2 %collective-permute-start.6 = (bf16[512,768]{1,0:T(8,128)(2,1)}, bf16[512,768]{1,0:T(8,128)(2,1)}, u32[]{:S(2)}, u32[]{:S(2)}) collective-permute-start(bf16[512,768]{1,0:T(8,128)(2,1)} %collective-permute-done.refs_1_), channel_id=1, source_target_pairs={{0,57},{1,8},{64,121},{65,72},{128,185},{129,136},{192,249},{193,2... | collective-permute-start | bytes 2359304 | tf_op jit(solution)/shard_map/ppermute | solution.py:39
  33.1 13.2 %collective-permute-start.4 = (bf16[256,768]{1,0:T(8,128)(2,1)S(1)}, bf16[256,768]{1,0:T(8,128)(2,1)S(1)}, u32[]{:S(2)}, u32[]{:S(2)}) collective-permute-start(bf16[256,768]{1,0:T(8,128)(2,1)S(1)} %constant_dynamic-slice_fusion), channel_id=1, source_target_pairs={{0,8},{1,57},{64,72},{65,121},{128,136},{129,185},{192,200},{193,2... | collective-permute-start | bytes 1179656 | tf_op jit(solution)/shard_map/ppermute | solution.py:39
  39.2 9.6 %collective-permute-start.3 = (bf16[256,768]{1,0:T(8,128)(2,1)S(1)}, bf16[256,768]{1,0:T(8,128)(2,1)S(1)}, u32[]{:S(2)}, u32[]{:S(2)}) collective-permute-start(bf16[256,768]{1,0:T(8,128)(2,1)S(1)} %constant_dynamic-slice_fusion.1), channel_id=1, source_target_pairs={{0,2},{1,7},{64,66},{65,71},{128,130},{129,135},{192,194},{193,199... | collective-permute-start | bytes 1179656 | tf_op jit(solution)/shard_map/ppermute | solution.py:39
  48.7 0.8 copy-start.1
  49.5 25.2 %collective-permute-start.7 = (bf16[512,768]{1,0:T(8,128)(2,1)}, bf16[512,768]{1,0:T(8,128)(2,1)}, u32[]{:S(2)}, u32[]{:S(2)}) collective-permute-start(bf16[512,768]{1,0:T(8,128)(2,1)} %collective-permute-done.5.refs_3_), channel_id=1, source_target_pairs={{0,2},{1,7},{64,66},{65,71},{128,130},{129,135},{192,194},{193,199... | collective-permute-start | bytes 2359304 | tf_op jit(solution)/shard_map/ppermute | solution.py:39
  54.8 19.9 %collective-permute-start.8 = (bf16[512,768]{1,0:T(8,128)(2,1)}, bf16[512,768]{1,0:T(8,128)(2,1)}, u32[]{:S(2)}, u32[]{:S(2)}) collective-permute-start(bf16[512,768]{1,0:T(8,128)(2,1)} %collective-permute-done.6.refs_4_), channel_id=1, source_target_pairs={{0,8},{1,57},{64,72},{65,121},{128,136},{129,185},{192,200},{193,2... | collective-permute-start | bytes 2359304 | tf_op jit(solution)/shard_map/ppermute | solution.py:39
  58.6 16.1 %collective-permute-start.9 = (bf16[256,768]{1,0:T(8,128)(2,1)}, bf16[256,768]{1,0:T(8,128)(2,1)}, u32[]{:S(2)}, u32[]{:S(2)}) collective-permute-start(bf16[256,768]{1,0:T(8,128)(2,1)} %constant_dynamic-slice_fusion.2), channel_id=1, source_target_pairs={{0,10},{1,63},{64,74},{65,127},{128,138},{129,191},{192,202},{193,... | collective-permute-start | bytes 1179656 | tf_op jit(solution)/shard_map/ppermute | solution.py:39
  62.3 12.4 %copy-start.2 = (bf16[256,768]{1,0:T(8,128)(2,1)S(1)}, bf16[256,768]{1,0:T(8,128)(2,1)}, u32[]{:S(2)}) copy-start(bf16[256,768]{1,0:T(8,128)(2,1)} %copy-done.1) | copy-start | bytes 1179652
  72.7 34.8 %collective-permute-start.11 = (bf16[128,2304]{1,0:T(8,128)(2,1)}, bf16[128,2304]{1,0:T(8,128)(2,1)}, u32[]{:S(2)}, u32[]{:S(2)}) collective-permute-start(bf16[128,2304]{1,0:T(8,128)(2,1)} %get-tuple-element.17), channel_id=1, source_target_pairs={{0,1},{1,0},{64,65},{65,64},{128,129},{129,128},{192,193},{193,192... | collective-permute-start | bytes 1769480 | tf_op jit(solution)/shard_map/ppermute | solution.py:43
  80.5 15.2 %all-to-all-start = ((bf16[32,4,768]{2,1,0:T(4,128)(2,1)}), bf16[32,4,768]{2,1,0:T(4,128)(2,1)S(1)}, u32[]{:S(2)}, u32[]{:S(2)}) async-start(bf16[32,4,768]{2,1,0:T(4,128)(2,1)} %far_sums.1), calls=%async_computation | async-start | bytes 393216 | tf_op jit(solution)/shard_map/all_to_all | solution.py:355
  96.5 22.7 %all-to-all-start.1 = ((bf16[16,4,768]{2,1,0:T(4,128)(2,1)}), bf16[16,4,768]{2,1,0:T(4,128)(2,1)S(1)}, u32[]{:S(2)}, u32[]{:S(2)}) async-start(bf16[16,4,768]{2,1,0:T(4,128)(2,1)} %broadcast_in_dim.30), calls=%async_computation.1 | async-start | bytes 196608 | tf_op jit(solution)/shard_map/all_to_all | solution.py:362
  107.5 2.0 %copy-start.3 = (bf16[256,768]{1,0:T(8,128)(2,1)S(1)}, bf16[256,768]{1,0:T(8,128)(2,1)}, u32[]{:S(2)}) copy-start(bf16[256,768]{1,0:T(8,128)(2,1)} %copy-done.1) | copy-start | bytes 1179652
  109.6 9.7 %copy-start.5 = (f32[4,768]{1,0:T(4,128)S(1)}, f32[4,768]{1,0:T(4,128)}, u32[]{:S(2)}) copy-start(f32[4,768]{1,0:T(4,128)} %param.11) | copy-start | bytes 36868
  114.1 5.7 %collective-permute-start.12 = (bf16[128,1792]{1,0:T(8,128)(2,1)S(1)}, bf16[128,1792]{1,0:T(8,128)(2,1)S(1)}, u32[]{:S(2)}, u32[]{:S(2)}) collective-permute-start(bf16[128,1792]{1,0:T(8,128)(2,1)S(1)} %get-tuple-element.19), channel_id=1, source_target_pairs={{0,1},{1,0},{64,65},{65,64},{128,129},{129,128},{192,193},{193,192... | collective-permute-start | bytes 1376264 | tf_op jit(solution)/shard_map/ppermute | solution.py:43

commit v4 on v3

--- a/solution.py
+++ b/solution.py
@@ -90,32 +90,13 @@
                 self.copies.append(copy)
         self.count = len(self.copies)
 
-    def load_features(self, mine, other, feats, sems):
-        self.feats, self.feat_copies = feats, []
-        tokens = mine.shape[0]
-        for unit in range(self.count):
-            columns = columns_of(self.table, self.first + unit, self.rows)
-            block = pl.ds(unit * self.rows, self.rows)
-            pair = [
-                pltpu.make_async_copy(
-                    ref.at[:, columns],
-                    feats.at[pl.ds(core * tokens, tokens), block],
-                    sems.at[2 * unit + core],
-                )
-                for core, ref in enumerate((mine, other))
-            ]
-            for copy in pair:
-                copy.start()
-            self.feat_copies.append(pair)
-
     def weight(self, unit):
         self.copies[unit].wait()
         return self.held[pl.ds(unit * self.rows, self.rows), :]
 
-    def group_sums(self, unit, weight, rot):
-        for copy in self.feat_copies[unit]:
-            copy.wait()
-        feats = self.feats[:, pl.ds(unit * self.rows, self.rows)]
+    def group_sums(self, unit, weight, rot, mine, other):
+        block = pl.ds((self.first + unit) * self.rows, self.rows)
+        feats = jnp.concatenate([mine[:, block], other[:, block]], axis=0)
         weight_grad = lax.dot_general(
             feats, rot, (((0,), (0,)), ((), ())), preferred_element_type=jnp.float32
         )
@@ -136,31 +117,36 @@
         return copy
 
 
+def pack_kernel(rows, table, theirs, feats_ref, mine_ref, sent_ref):
+    for unit in range(mine_ref.shape[1] // rows):
+        block = pl.ds(unit * rows, rows)
+        mine_ref[:, block] = feats_ref[:, columns_of(table, unit, rows)]
+        sent_ref[:, block] = feats_ref[:, columns_of(theirs, unit, rows)]
+
+
 def near_kernel(rows, count, table, rot_ref, mine_ref, other_ref, *refs):
     weights, refs = refs[:count], refs[count:]
-    grad_ref, sent_ref, sums_ref, held, feats, own, held_sems, feat_sems, own_sems = refs
+    grad_ref, sent_ref, sums_ref, held, own, held_sems, own_sems = refs
     units = Units(rows, table, weights, held, held_sems)
-    units.load_features(mine_ref, other_ref, feats, feat_sems)
     rot = rot_ref[...]
     copies = []
     for unit in range(units.count):
         weight = units.weight(unit)
         copies.append(units.put_grad(unit, weight, rot, own, sent_ref, grad_ref, own_sems))
-        sums_ref[unit] = units.group_sums(unit, weight, rot)
+        sums_ref[unit] = units.group_sums(unit, weight, rot, mine_ref, other_ref)
     for copy in copies:
         copy.wait()
 
 
 def far_sums_kernel(rows, count, near, table, rot_ref, near_ref, mine_ref, other_ref, *refs):
-    weights, (all_ref, held, feats, held_sems, feat_sems) = refs[:count], refs[count:]
+    weights, (all_ref, held, held_sems) = refs[:count], refs[count:]
     units = Units(rows, table, weights, held, held_sems, near)
-    units.load_features(mine_ref, other_ref, feats, feat_sems)
     all_ref[...] = jnp.zeros_like(all_ref)
     for unit in range(near):
         all_ref[table[unit]] = near_ref[unit].astype(all_ref.dtype)
     rot = rot_ref[...]
     for unit in range(units.count):
-        sums = units.group_sums(unit, units.weight(unit), rot)
+        sums = units.group_sums(unit, units.weight(unit), rot, mine_ref, other_ref)
         all_ref[table[near + unit]] = sums.astype(all_ref.dtype)
 
 
@@ -190,17 +176,29 @@
     )
 
 
-def scratch(units, rows, cols, tokens, feats, own):
-    held = pltpu.VMEM((units * rows, cols), jnp.bfloat16)
-    of_feats = pltpu.VMEM((2 * tokens, units * rows), jnp.bfloat16)
-    of_own = pltpu.VMEM((tokens, units * rows), jnp.bfloat16)
-    buffers = [held] + [of_feats] * feats + [of_own] * own
-    sems = [units] + [2 * units] * feats + [units] * own
-    return buffers + [pltpu.SemaphoreType.DMA((count,)) for count in sems]
-
-
-def near_shards(table, mine, other, rot, weights, rows):
-    tokens, width = mine.shape
+def scratch(units, rows, cols, tokens, own):
+    buffers = [pltpu.VMEM((units * rows, cols), jnp.bfloat16)]
+    buffers += [pltpu.VMEM((tokens, units * rows), jnp.bfloat16)] * own
+    return buffers + [pltpu.SemaphoreType.DMA((units,))] * (1 + own)
+
+
+def pack(table, theirs, feats, rows):
+    packed = jax.ShapeDtypeStruct((feats.shape[0], table.shape[0] * rows), feats.dtype)
+    return pl.pallas_call(
+        functools.partial(pack_kernel, rows),
+        out_shape=(packed, packed),
+        in_specs=[SMEM_SPEC, SMEM_SPEC, VMEM_SPEC],
+        out_specs=(VMEM_SPEC, VMEM_SPEC),
+        cost_estimate=pl.CostEstimate(
+            flops=0, bytes_accessed=3 * feats.size * 2, transcendentals=0
+        ),
+        compiler_params=pltpu.CompilerParams(vmem_limit_bytes=VMEM),
+        name="pack",
+    )(table, theirs, feats)
+
+
+def near_shards(table, mine, other, rot, weights, rows, width):
+    tokens = mine.shape[0]
     cols = rot.shape[1]
     total = sum(weight.shape[0] for weight in weights) // rows
     return pl.pallas_call(
@@ -210,9 +208,9 @@
             jax.ShapeDtypeStruct((tokens, total * rows), jnp.bfloat16),
             jax.ShapeDtypeStruct((total, rows // GROUP, cols), jnp.float32),
         ),
-        in_specs=[SMEM_SPEC, VMEM_SPEC] + [ANY_SPEC] * (2 + len(weights)),
+        in_specs=[SMEM_SPEC] + [VMEM_SPEC] * 3 + [ANY_SPEC] * len(weights),
         out_specs=(ANY_SPEC, VMEM_SPEC, VMEM_SPEC),
-        scratch_shapes=scratch(total, rows, cols, tokens, 1, 1),
+        scratch_shapes=scratch(total, rows, cols, tokens, 1),
         cost_estimate=cost(total, rows, cols, tokens, 2),
         compiler_params=pltpu.CompilerParams(vmem_limit_bytes=VMEM),
         name="near_shards",
@@ -226,9 +224,9 @@
     return pl.pallas_call(
         functools.partial(far_sums_kernel, rows, len(weights), near),
         out_shape=jax.ShapeDtypeStruct((devices, groups, cols), jnp.bfloat16),
-        in_specs=[SMEM_SPEC, VMEM_SPEC, VMEM_SPEC] + [ANY_SPEC] * (2 + len(weights)),
+        in_specs=[SMEM_SPEC] + [VMEM_SPEC] * 4 + [ANY_SPEC] * len(weights),
         out_specs=VMEM_SPEC,
-        scratch_shapes=scratch(total, rows, cols, tokens, 1, 0),
+        scratch_shapes=scratch(total, rows, cols, tokens, 0),
         cost_estimate=cost(total, rows, cols, tokens, 1),
         compiler_params=pltpu.CompilerParams(vmem_limit_bytes=VMEM),
         name="far_sums",
@@ -247,7 +245,7 @@
         ),
         in_specs=[SMEM_SPEC, VMEM_SPEC] + [ANY_SPEC] * (len(weights) + 1),
         out_specs=(ANY_SPEC, VMEM_SPEC),
-        scratch_shapes=scratch(total, rows, cols, tokens, 0, 1),
+        scratch_shapes=scratch(total, rows, cols, tokens, 1),
         input_output_aliases={2 + len(weights): 0},
         cost_estimate=cost(total, rows, cols, tokens, 1),
         compiler_params=pltpu.CompilerParams(vmem_limit_bytes=VMEM),
@@ -328,8 +326,9 @@
     indices = place_in * tokens + jnp.arange(tokens, dtype=jnp.int32)
     mine = rope_back(key_cotangent, token_positions(doc_lengths[0], indices))
     rot = jnp.concatenate([mine, swap(mine)], axis=0)
-    others = swap(activations)
-    from_x, from_y, rot = lax.optimization_barrier((from_x, from_y, rot))
+    mine_feats, their_feats = pack(table, theirs, activations, rows)
+    feats = (mine_feats, swap(their_feats))
+    from_x, from_y, rot, _ = lax.optimization_barrier((from_x, from_y, rot, their_feats))
 
     def my_half(value):
         return lax.dynamic_slice_in_dim(value, core * rows, rows, axis=0)
@@ -345,18 +344,17 @@
     far = send(my_half(from_xy), 1, 1)
 
     near = [weight, from_x, from_y, from_xy, from_yx]
-    grad, sent_near, sums_near = near_shards(table, activations, others, rot, near, rows)
+    grad, sent_near, sums_near = near_shards(table, *feats, rot, near, rows, activations.shape[1])
     got_near = swap(sent_near)
     grad = place(theirs, got_near, grad, rows, 0)
 
     fars = [far_xx, far_yy, far_x, far_y, far]
     at_hand = sums_near.shape[0]
-    sums = far_sums(table, activations, others, rot, fars, sums_near, rows, devices)
+    sums = far_sums(table, *feats, rot, fars, sums_near, rows, devices)
     shares = lax.all_to_all(sums, "tensor", split_axis=0, concat_axis=0, tiled=True)
 
     grad, sent_far = far_grad(table, rot, fars, grad, rows, at_hand)
-    got_far = swap(sent_far)
-
+    shares, grad, sent_far = lax.optimization_barrier((shares, grad, sent_far))
     share = jnp.sum(shares.astype(jnp.float32), axis=0).astype(jnp.bfloat16)
     copies = lax.axis_size("dp")
     totals = lax.all_to_all(
@@ -366,10 +364,11 @@
         concat_axis=0,
         tiled=True,
     )
+    grad = place(theirs, swap(sent_far), grad, rows, at_hand)
+    totals, grad = lax.optimization_barrier((totals, grad))
     seq_tokens = tokens * devices
     total = jnp.sum(totals.astype(jnp.float32), axis=0)
     step_grad = total / (seq_tokens * step_sizes)
-    grad = place(theirs, got_far, grad, rows, at_hand)
     return (grad, step_grad)
 
 

time: 122 us -> 124 us (1.016)
  starting transfers between devices: 55.5 us -> 57.1 us
    all_to_all x1, waiting for transfers between devices: 9.55 us -> 1.57 us  [per_device(): lax.all_to_all(sums, 'tensor', split_axis=0, concat_axis=0, tiled=True)]
    all_to_all x1, waiting for transfers between devices: 2.55 us -> 10.4 us  [per_device(): lax.all_to_all(jnp.broadcast_to(share[None], (copies, *share.shape)), 'dp...]
    pallas_call x1, Pallas kernels: 10.5 us -> 7.27 us  [near_shards(): pl.pallas_call(functools.partial(near_kernel, rows, len(weights)), out_sh...]
    all_to_all x1, starting transfers between devices: 10.9 us -> 12.9 us  [per_device(): lax.all_to_all(jnp.broadcast_to(share[None], (copies, *share.shape)), 'dp...]
    pallas_call x0 -> x1, Pallas kernels: none -> 1.8 us  [pack(): pl.pallas_call(functools.partial(pack_kernel, rows), out_shape=(packed, p...]
    unnamed x15 -> x19, local copies, waits for them, and re-layouts: 0.94 us -> 2.67 us
    ppermute x9, starting transfers between devices: 30.3 us -> 28.7 us  [send(): return lax.ppermute(value, AXES, permutation(target))]
    ppermute x9, waiting for transfers between devices: 9.48 us -> 10.8 us  [send(): return lax.ppermute(value, AXES, permutation(target))]
  transfers between devices with their start and end apart: 15 -> 15, of which waited for: 7 -> 7; matrix products, arithmetic and copies ran while one was open for 5% -> 4% of each run, Pallas kernels for 19% -> 19%
where the time goes in v4:
time: 124 us; the launch traced here: 123 us
  starting transfers between devices  57.1 us (46%)
  Pallas kernels  23.4 us (19%)
  waiting for transfers between devices  22.8 us (18%)
  blocking collectives  9.14 us (7%)
  local copies, waits for them, and re-layouts  6.85 us (6%)
  other arithmetic  2.57 us (2%)
  between operations  1.28 us (1%)
    ppermute x9, starting transfers between devices, send(): return lax.ppermute(value, AXES, permutation(target))  28.7 us
    all_to_all x1, starting transfers between devices, per_device(): lax.all_to_all(jnp.broadcast_to(share[None], (copies, *share.shape)), 'dp...  12.9 us
    ppermute x9, waiting for transfers between devices, send(): return lax.ppermute(value, AXES, permutation(target))  10.8 us
    all_to_all x1, waiting for transfers between devices, per_device(): lax.all_to_all(jnp.broadcast_to(share[None], (copies, *share.shape)), 'dp...  10.4 us
    ppermute x4, starting transfers between devices, swap(): lax.ppermute(value, AXES, permutation(lambda x, y, z, core: (x, y, z, cor...  9.66 us
    all_gather x1, blocking collectives, per_device(): lax.all_gather(weight, 'tensor', axis=0, tiled=True, axis_index_groups=pa...  9.14 us
    pallas_call x1, Pallas kernels, near_shards(): pl.pallas_call(functools.partial(near_kernel, rows, len(weights)), out_sh...  7.27 us
    all_to_all x1, starting transfers between devices, per_device(): lax.all_to_all(sums, 'tensor', split_axis=0, concat_axis=0, tiled=True)  5.87 us
  transfers between devices with their start and end apart: 15, of which 7 were waited for; matrix products, arithmetic and copies ran while one was open for 4% of the time, Pallas kernels for 19%

profile of v4, /device:TPU:1, one launch (start us, length us, event | category | flops | bytes accessed | tf_op | source)
XLA Modules:
  0.0 123.1 jit_solution(4202902063927884262)
XLA Ops:
  0.7 1.3 %fusion.2.refs_0_ = bf16[256,768]{1,0:T(8,128)(2,1)S(1)} fusion(s32[256,768]{1,0:T(8,128)} %param.9, s32[4,768]{1,0:T(4,128)} %param.10, f32[4,768]{1,0:T(4,128)} %param.11), kind=kLoop, calls=%fused_computation.3 | loop fusion | flops 786432 | bytes 1204224 | tf_op jit(solution)/shard_map/convert_element_type | solution.py:72
  1.9 9.1 %all_gather.3 = bf16[512,768]{1,0:T(8,128)(2,1)} all-gather(bf16[256,768]{1,0:T(8,128)(2,1)S(1)} %fusion.2.refs_0_), channel_id=1, replica_groups={{0,1},{2,3},{4,5},{6,7},{8,9},{10,11},{12,13},{14,15},{16,17},{18,19},{..., dimensions={0}, use_global_device_ids=true | all-gather | bytes 1179648 | tf_op jit(solution)/shard_map/all_gather | solution.py:321
  11.1 1.9 %collective-permute-start = (bf16[512,768]{1,0:T(8,128)(2,1)}, bf16[512,768]{1,0:T(8,128)(2,1)}, u32[]{:S(2)}, u32[]{:S(2)}) collective-permute-start(bf16[512,768]{1,0:T(8,128)(2,1)} %all_gather.3), channel_id=1, source_target_pairs={{0,2},{1,7},{64,66},{65,71},{128,130},{129,135},{192,194},{193,199... | collective-permute-start | bytes 2359304 | tf_op jit(solution)/shard_map/ppermute | solution.py:39
  13.0 2.2 %collective-permute-start.1 = (bf16[512,768]{1,0:T(8,128)(2,1)}, bf16[512,768]{1,0:T(8,128)(2,1)}, u32[]{:S(2)}, u32[]{:S(2)}) collective-permute-start(bf16[512,768]{1,0:T(8,128)(2,1)} %all_gather.3), channel_id=1, source_target_pairs={{0,8},{1,57},{64,72},{65,121},{128,136},{129,185},{192,200},{193,2... | collective-permute-start | bytes 2359304 | tf_op jit(solution)/shard_map/ppermute | solution.py:39
  15.2 0.2 copy.17
  15.5 0.1 select_reduce_fusion.1
  15.5 0.1 select_reduce_fusion
  15.6 0.2 multiply_cosine_fusion
  15.8 0.1 add_convert_fusion
  15.9 0.1 copy.19
  16.1 2.0 %collective-permute-start.2 = (bf16[128,768]{1,0:T(8,128)(2,1)S(1)}, bf16[128,768]{1,0:T(8,128)(2,1)S(1)}, u32[]{:S(2)}, u32[]{:S(2)}) collective-permute-start(bf16[128,768]{1,0:T(8,128)(2,1)S(1)} %copy.19), channel_id=1, source_target_pairs={{0,1},{1,0},{64,65},{65,64},{128,129},{129,128},{192,193},{193,192... | collective-permute-start | bytes 589832 | tf_op jit(solution)/shard_map/ppermute | solution.py:43
  18.4 0.1 stack.118.table
  18.5 0.1 stack.135.theirs.table
  18.6 1.8 %pack.1 = (bf16[128,4096]{1,0:T(8,128)(2,1)S(1)}, bf16[128,4096]{1,0:T(8,128)(2,1)}) custom-call(s32[16]{0:T(128)S(1)} %stack.118.table, s32[16]{0:T(128)S(1)} %stack.135.theirs.table, bf16[128,8192]{1,0:T(8,128)(2,1)S(1)} %copy-done), custom_call_target="tpu_custom_call" | custom-call | bytes 6291456 | tf_op jit(solution)/shard_map/pack/pallas_call | solution.py:187
  20.4 1.0 copy-done.3
  21.4 3.0 %collective-permute-done.refs_1_ = bf16[512,768]{1,0:T(8,128)(2,1)} collective-permute-done((bf16[512,768]{1,0:T(8,128)(2,1)}, bf16[512,768]{1,0:T(8,128)(2,1)}, u32[]{:S(2)}, u32[]{:S(2)}) %collective-permute-start) | collective-permute-done | bytes 786464 | tf_op jit(solution)/shard_map/ppermute | solution.py:39
  24.4 1.9 %collective-permute-done.1.refs_2_ = bf16[512,768]{1,0:T(8,128)(2,1)} collective-permute-done((bf16[512,768]{1,0:T(8,128)(2,1)}, bf16[512,768]{1,0:T(8,128)(2,1)}, u32[]{:S(2)}, u32[]{:S(2)}) %collective-permute-start.1) | collective-permute-done | bytes 786464 | tf_op jit(solution)/shard_map/ppermute | solution.py:39
  26.4 1.9 %collective-permute-start.4 = (bf16[512,768]{1,0:T(8,128)(2,1)}, bf16[512,768]{1,0:T(8,128)(2,1)}, u32[]{:S(2)}, u32[]{:S(2)}) collective-permute-start(bf16[512,768]{1,0:T(8,128)(2,1)} %collective-permute-done.1.refs_2_), channel_id=1, source_target_pairs={{0,2},{1,7},{64,66},{65,71},{128,130},{129,135},{192,194},{193,199... | collective-permute-start | bytes 2359304 | tf_op jit(solution)/shard_map/ppermute | solution.py:39
  28.3 2.8 %collective-permute-start.5 = (bf16[512,768]{1,0:T(8,128)(2,1)}, bf16[512,768]{1,0:T(8,128)(2,1)}, u32[]{:S(2)}, u32[]{:S(2)}) collective-permute-start(bf16[512,768]{1,0:T(8,128)(2,1)} %collective-permute-done.refs_1_), channel_id=1, source_target_pairs={{0,57},{1,8},{64,121},{65,72},{128,185},{129,136},{192,249},{193,2... | collective-permute-start | bytes 2359304 | tf_op jit(solution)/shard_map/ppermute | solution.py:39
  31.0 3.5 %collective-permute-start.3 = (bf16[128,4096]{1,0:T(8,128)(2,1)}, bf16[128,4096]{1,0:T(8,128)(2,1)}, u32[]{:S(2)}, u32[]{:S(2)}) collective-permute-start(bf16[128,4096]{1,0:T(8,128)(2,1)} %get-tuple-element.19), channel_id=1, source_target_pairs={{0,1},{1,0},{64,65},{65,64},{128,129},{129,128},{192,193},{193,192... | collective-permute-start | bytes 3145736 | tf_op jit(solution)/shard_map/ppermute | solution.py:43
  34.6 1.1 constant_dynamic-slice_fusion.1
  35.7 1.0 constant_dynamic-slice_fusion
  36.7 4.9 %collective-permute-start.6 = (bf16[256,768]{1,0:T(8,128)(2,1)S(1)}, bf16[256,768]{1,0:T(8,128)(2,1)S(1)}, u32[]{:S(2)}, u32[]{:S(2)}) collective-permute-start(bf16[256,768]{1,0:T(8,128)(2,1)S(1)} %constant_dynamic-slice_fusion.1), channel_id=1, source_target_pairs={{0,2},{1,7},{64,66},{65,71},{128,130},{129,135},{192,194},{193,199... | collective-permute-start | bytes 1179656 | tf_op jit(solution)/shard_map/ppermute | solution.py:39
  41.6 4.5 %collective-permute-start.7 = (bf16[256,768]{1,0:T(8,128)(2,1)S(1)}, bf16[256,768]{1,0:T(8,128)(2,1)S(1)}, u32[]{:S(2)}, u32[]{:S(2)}) collective-permute-start(bf16[256,768]{1,0:T(8,128)(2,1)S(1)} %constant_dynamic-slice_fusion), channel_id=1, source_target_pairs={{0,8},{1,57},{64,72},{65,121},{128,136},{129,185},{192,200},{193,2... | collective-permute-start | bytes 1179656 | tf_op jit(solution)/shard_map/ppermute | solution.py:39
  46.1 0.2 collective-permute-done.6.refs_0_
  46.3 4.5 %collective-permute-done.7.refs_1_ = bf16[256,768]{1,0:T(8,128)(2,1)S(1)} collective-permute-done((bf16[256,768]{1,0:T(8,128)(2,1)S(1)}, bf16[256,768]{1,0:T(8,128)(2,1)S(1)}, u32[]{:S(2)}, u32[]{:S(2)}) %collective-permute-start.7) | collective-permute-done | bytes 393248 | tf_op jit(solution)/shard_map/ppermute | solution.py:39
  50.8 3.6 %collective-permute-start.8 = (bf16[512,768]{1,0:T(8,128)(2,1)}, bf16[512,768]{1,0:T(8,128)(2,1)S(1)}, u32[]{:S(2)}, u32[]{:S(2)}) collective-permute-start(bf16[512,768]{1,0:T(8,128)(2,1)} %collective-permute-done.4.refs_3_), channel_id=1, source_target_pairs={{0,2},{1,7},{64,66},{65,71},{128,130},{129,135},{192,194},{193,199... | collective-permute-start | bytes 2359304 | tf_op jit(solution)/shard_map/ppermute | solution.py:39
  54.4 5.0 %collective-permute-start.9 = (bf16[512,768]{1,0:T(8,128)(2,1)}, bf16[512,768]{1,0:T(8,128)(2,1)S(1)}, u32[]{:S(2)}, u32[]{:S(2)}) collective-permute-start(bf16[512,768]{1,0:T(8,128)(2,1)} %collective-permute-done.5.refs_4_), channel_id=1, source_target_pairs={{0,8},{1,57},{64,72},{65,121},{128,136},{129,185},{192,200},{193,2... | collective-permute-start | bytes 2359304 | tf_op jit(solution)/shard_map/ppermute | solution.py:39
  59.4 1.0 constant_dynamic-slice_fusion.2
  60.5 1.9 %collective-permute-start.10 = (bf16[256,768]{1,0:T(8,128)(2,1)S(1)}, bf16[256,768]{1,0:T(8,128)(2,1)S(1)}, u32[]{:S(2)}, u32[]{:S(2)}) collective-permute-start(bf16[256,768]{1,0:T(8,128)(2,1)S(1)} %constant_dynamic-slice_fusion.2), channel_id=1, source_target_pairs={{0,10},{1,63},{64,74},{65,127},{128,138},{129,191},{192,202},{193,... | collective-permute-start | bytes 1179656 | tf_op jit(solution)/shard_map/ppermute | solution.py:39
  62.4 7.3 %near_shards.1 = (bf16[128,8192]{1,0:T(8,128)(2,1)}, bf16[128,2304]{1,0:T(8,128)(2,1)}, f32[9,4,768]{2,1,0:T(4,128)S(1)}) custom-call(s32[16]{0:T(128)S(1)} %stack.118.table, bf16[256,768]{1,0:T(8,128)(2,1)S(1)} %pad_maximum_fusion.rot_ref, bf16[128,4096]{1,0:T(8,128)(2,1)S(1)} %copy-done.4, bf16[128,4096]{1,0:T(8,128)(2,1)} %collective-permute-done.3.other_ref, ...), custom_call_target="tpu_custom_call" | custom-call | flops 1811939328 | bytes 4718592 | tf_op jit(solution)/shard_map/near_shards/pallas_call | solution.py:204
  69.7 1.9 %collective-permute-start.11 = (bf16[128,2304]{1,0:T(8,128)(2,1)}, bf16[128,2304]{1,0:T(8,128)(2,1)}, u32[]{:S(2)}, u32[]{:S(2)}) collective-permute-start(bf16[128,2304]{1,0:T(8,128)(2,1)} %get-tuple-element.27), channel_id=1, source_target_pairs={{0,1},{1,0},{64,65},{65,64},{128,129},{129,128},{192,193},{193,192... | collective-permute-start | bytes 1769480 | tf_op jit(solution)/shard_map/ppermute | solution.py:43
  71.6 1.1 collective-permute-done.10.refs_4_
  72.8 5.7 %far_sums.1 = bf16[32,4,768]{2,1,0:T(4,128)(2,1)} custom-call(s32[16]{0:T(128)S(1)} %stack.118.table, bf16[256,768]{1,0:T(8,128)(2,1)S(1)} %pad_maximum_fusion.rot_ref, f32[9,4,768]{2,1,0:T(4,128)S(1)} %get-tuple-element.26.near_ref, bf16[128,4096]{1,0:T(8,128)(2,1)S(1)} %copy-done.4, bf16[128,4096]{1,0:T(8,128)(2,1)} %collective-permute-done.3.other_ref, ...), custom_call_target="tpu_custom_call" | custom-call | flops 704643072 | bytes 3670016 | tf_op jit(solution)/shard_map/far_sums/pallas_call | solution.py:224
  78.5 0.7 copy-done.1
  79.2 5.9 %all-to-all-start = ((bf16[32,4,768]{2,1,0:T(4,128)(2,1)}), bf16[32,4,768]{2,1,0:T(4,128)(2,1)S(1)}, u32[]{:S(2)}, u32[]{:S(2)}) async-start(bf16[32,4,768]{2,1,0:T(4,128)(2,1)} %far_sums.1), calls=%async_computation | async-start | bytes 393216 | tf_op jit(solution)/shard_map/all_to_all | solution.py:354
  85.1 2.0 %place.2.refs_5_ = bf16[128,8192]{1,0:T(8,128)(2,1)} custom-call(s32[16]{0:T(128)S(1)} %stack.135.theirs.table, bf16[128,2304]{1,0:T(8,128)(2,1)} %collective-permute-done.11.blocks_ref, bf16[128,8192]{1,0:T(8,128)(2,1)} %get-tuple-element.28.grad_in), custom_call_target="tpu_custom_call", output_to_operand_aliasing={{}: (2, {})} | custom-call | bytes 1179648 | tf_op jit(solution)/shard_map/place/pallas_call | solution.py:274
  87.2 5.2 %far_grad.1 = (bf16[128,8192]{1,0:T(8,128)(2,1)}, bf16[128,1792]{1,0:T(8,128)(2,1)S(1)}) custom-call(s32[16]{0:T(128)S(1)} %stack.118.table, bf16[256,768]{1,0:T(8,128)(2,1)S(1)} %pad_maximum_fusion.rot_ref, bf16[256,768]{1,0:T(8,128)(2,1)S(1)} %collective-permute-done.6.refs_0_, ...), custom_call_target="tpu_custom_call", output_to_operand_aliasing={{0}: (7, {})} | custom-call | flops 704643072 | bytes 3670016 | tf_op jit(solution)/shard_map/far_grad/pallas_call | solution.py:240
  92.4 0.8 copy-done.5
  93.2 1.6 %all-to-all-done = bf16[32,4,768]{2,1,0:T(4,128)(2,1)S(1)} async-done(((bf16[32,4,768]{2,1,0:T(4,128)(2,1)}), bf16[32,4,768]{2,1,0:T(4,128)(2,1)S(1)}, u32[]{:S(2)}, u32[]{:S(2)}) %all-to-all-start) | async-done | bytes 196640 | tf_op jit(solution)/shard_map/all_to_all | solution.py:354
  94.7 2.2 %collective-permute-start.12 = (bf16[128,1792]{1,0:T(8,128)(2,1)}, bf16[128,1792]{1,0:T(8,128)(2,1)S(1)}, u32[]{:S(2)}, u32[]{:S(2)}) collective-permute-start(bf16[128,1792]{1,0:T(8,128)(2,1)} %copy-done.5), channel_id=1, source_target_pairs={{0,1},{1,0},{64,65},{65,64},{128,129},{129,128},{192,193},{193,192... | collective-permute-start | bytes 1376264 | tf_op jit(solution)/shard_map/ppermute | solution.py:43
  97.0 0.1 reduce_sum.31
  97.1 0.7 broadcast_in_dim.30
  97.7 12.9 %all-to-all-start.1 = ((bf16[16,4,768]{2,1,0:T(4,128)(2,1)}), bf16[16,4,768]{2,1,0:T(4,128)(2,1)S(1)}, u32[]{:S(2)}, u32[]{:S(2)}) async-start(bf16[16,4,768]{2,1,0:T(4,128)(2,1)} %broadcast_in_dim.30), calls=%async_computation.1 | async-start | bytes 196608 | tf_op jit(solution)/shard_map/all_to_all | solution.py:360
  110.7 1.4 %place.3 = bf16[128,8192]{1,0:T(8,128)(2,1)} custom-call(s32[16]{0:T(128)S(1)} %stack.135.theirs.table, bf16[128,1792]{1,0:T(8,128)(2,1)S(1)} %collective-permute-done.12.blocks_ref, bf16[128,8192]{1,0:T(8,128)(2,1)} %get-tuple-element.33.grad_in), custom_call_target="tpu_custom_call", output_to_operand_aliasing={{}: (2, {})} | custom-call | bytes 917504 | tf_op jit(solution)/shard_map/place/pallas_call | solution.py:274
  112.0 10.4 %all-to-all-done.1 = bf16[16,4,768]{2,1,0:T(4,128)(2,1)S(1)} async-done(((bf16[16,4,768]{2,1,0:T(4,128)(2,1)}), bf16[16,4,768]{2,1,0:T(4,128)(2,1)S(1)}, u32[]{:S(2)}, u32[]{:S(2)}) %all-to-all-start.1) | async-done | bytes 98336 | tf_op jit(solution)/shard_map/all_to_all | solution.py:360
  122.4 0.1 convert_reduce_fusion
  122.5 0.6 multiply_divide_fusion
  (29 shorter events, 0.1 us)
Async XLA Ops:
  0.6 14.6 %copy-start.6 = (bf16[128,768]{1,0:T(8,128)(2,1)S(1)}, bf16[128,768]{1,0:T(8,128)(2,1)}, u32[]{:S(2)}) copy-start(bf16[128,768]{1,0:T(8,128)(2,1)} %param.7) | copy-start | bytes 589828
  0.6 14.8 %copy-start.8 = (s32[1,8]{1,0:T(1,128)S(1)}, s32[1,8]{1,0:T(1,128)}, u32[]{:S(2)}) copy-start(s32[1,8]{1,0:T(1,128)} %param.8) | copy-start | bytes 100
  1.9 16.6 %copy-start = (bf16[128,8192]{1,0:T(8,128)(2,1)S(1)}, bf16[128,8192]{1,0:T(8,128)(2,1)}, u32[]{:S(2)}) copy-start(bf16[128,8192]{1,0:T(8,128)(2,1)} %feats_ref.1) | copy-start | bytes 6291460
  11.1 13.3 %collective-permute-start = (bf16[512,768]{1,0:T(8,128)(2,1)}, bf16[512,768]{1,0:T(8,128)(2,1)}, u32[]{:S(2)}, u32[]{:S(2)}) collective-permute-start(bf16[512,768]{1,0:T(8,128)(2,1)} %all_gather.3), channel_id=1, source_target_pairs={{0,2},{1,7},{64,66},{65,71},{128,130},{129,135},{192,194},{193,199... | collective-permute-start | bytes 2359304 | tf_op jit(solution)/shard_map/ppermute | solution.py:39
  13.0 13.3 %collective-permute-start.1 = (bf16[512,768]{1,0:T(8,128)(2,1)}, bf16[512,768]{1,0:T(8,128)(2,1)}, u32[]{:S(2)}, u32[]{:S(2)}) collective-permute-start(bf16[512,768]{1,0:T(8,128)(2,1)} %all_gather.3), channel_id=1, source_target_pairs={{0,8},{1,57},{64,72},{65,121},{128,136},{129,185},{192,200},{193,2... | collective-permute-start | bytes 2359304 | tf_op jit(solution)/shard_map/ppermute | solution.py:39
  16.1 5.3 %collective-permute-start.2 = (bf16[128,768]{1,0:T(8,128)(2,1)S(1)}, bf16[128,768]{1,0:T(8,128)(2,1)S(1)}, u32[]{:S(2)}, u32[]{:S(2)}) collective-permute-start(bf16[128,768]{1,0:T(8,128)(2,1)S(1)} %copy.19), channel_id=1, source_target_pairs={{0,1},{1,0},{64,65},{65,64},{128,129},{129,128},{192,193},{193,192... | collective-permute-start | bytes 589832 | tf_op jit(solution)/shard_map/ppermute | solution.py:43
  20.4 1.0 copy-start.3
  26.4 24.4 %collective-permute-start.4 = (bf16[512,768]{1,0:T(8,128)(2,1)}, bf16[512,768]{1,0:T(8,128)(2,1)}, u32[]{:S(2)}, u32[]{:S(2)}) collective-permute-start(bf16[512,768]{1,0:T(8,128)(2,1)} %collective-permute-done.1.refs_2_), channel_id=1, source_target_pairs={{0,2},{1,7},{64,66},{65,71},{128,130},{129,135},{192,194},{193,199... | collective-permute-start | bytes 2359304 | tf_op jit(solution)/shard_map/ppermute | solution.py:39
  28.3 22.5 %collective-permute-start.5 = (bf16[512,768]{1,0:T(8,128)(2,1)}, bf16[512,768]{1,0:T(8,128)(2,1)}, u32[]{:S(2)}, u32[]{:S(2)}) collective-permute-start(bf16[512,768]{1,0:T(8,128)(2,1)} %collective-permute-done.refs_1_), channel_id=1, source_target_pairs={{0,57},{1,8},{64,121},{65,72},{128,185},{129,136},{192,249},{193,2... | collective-permute-start | bytes 2359304 | tf_op jit(solution)/shard_map/ppermute | solution.py:39
  31.0 31.4 %collective-permute-start.3 = (bf16[128,4096]{1,0:T(8,128)(2,1)}, bf16[128,4096]{1,0:T(8,128)(2,1)}, u32[]{:S(2)}, u32[]{:S(2)}) collective-permute-start(bf16[128,4096]{1,0:T(8,128)(2,1)} %get-tuple-element.19), channel_id=1, source_target_pairs={{0,1},{1,0},{64,65},{65,64},{128,129},{129,128},{192,193},{193,192... | collective-permute-start | bytes 3145736 | tf_op jit(solution)/shard_map/ppermute | solution.py:43
  34.6 27.8 %copy-start.4 = (bf16[128,4096]{1,0:T(8,128)(2,1)S(1)}, bf16[128,4096]{1,0:T(8,128)(2,1)}, u32[]{:S(2)}) copy-start(bf16[128,4096]{1,0:T(8,128)(2,1)} %copy-done.3) | copy-start | bytes 3145732
  36.7 9.6 %collective-permute-start.6 = (bf16[256,768]{1,0:T(8,128)(2,1)S(1)}, bf16[256,768]{1,0:T(8,128)(2,1)S(1)}, u32[]{:S(2)}, u32[]{:S(2)}) collective-permute-start(bf16[256,768]{1,0:T(8,128)(2,1)S(1)} %constant_dynamic-slice_fusion.1), channel_id=1, source_target_pairs={{0,2},{1,7},{64,66},{65,71},{128,130},{129,135},{192,194},{193,199... | collective-permute-start | bytes 1179656 | tf_op jit(solution)/shard_map/ppermute | solution.py:39
  41.6 9.2 %collective-permute-start.7 = (bf16[256,768]{1,0:T(8,128)(2,1)S(1)}, bf16[256,768]{1,0:T(8,128)(2,1)S(1)}, u32[]{:S(2)}, u32[]{:S(2)}) collective-permute-start(bf16[256,768]{1,0:T(8,128)(2,1)S(1)} %constant_dynamic-slice_fusion), channel_id=1, source_target_pairs={{0,8},{1,57},{64,72},{65,121},{128,136},{129,185},{192,200},{193,2... | collective-permute-start | bytes 1179656 | tf_op jit(solution)/shard_map/ppermute | solution.py:39
  50.8 22.0 %collective-permute-start.8 = (bf16[512,768]{1,0:T(8,128)(2,1)}, bf16[512,768]{1,0:T(8,128)(2,1)S(1)}, u32[]{:S(2)}, u32[]{:S(2)}) collective-permute-start(bf16[512,768]{1,0:T(8,128)(2,1)} %collective-permute-done.4.refs_3_), channel_id=1, source_target_pairs={{0,2},{1,7},{64,66},{65,71},{128,130},{129,135},{192,194},{193,199... | collective-permute-start | bytes 2359304 | tf_op jit(solution)/shard_map/ppermute | solution.py:39
  54.4 18.4 %collective-permute-start.9 = (bf16[512,768]{1,0:T(8,128)(2,1)}, bf16[512,768]{1,0:T(8,128)(2,1)S(1)}, u32[]{:S(2)}, u32[]{:S(2)}) collective-permute-start(bf16[512,768]{1,0:T(8,128)(2,1)} %collective-permute-done.5.refs_4_), channel_id=1, source_target_pairs={{0,8},{1,57},{64,72},{65,121},{128,136},{129,185},{192,200},{193,2... | collective-permute-start | bytes 2359304 | tf_op jit(solution)/shard_map/ppermute | solution.py:39
  60.5 12.3 %collective-permute-start.10 = (bf16[256,768]{1,0:T(8,128)(2,1)S(1)}, bf16[256,768]{1,0:T(8,128)(2,1)S(1)}, u32[]{:S(2)}, u32[]{:S(2)}) collective-permute-start(bf16[256,768]{1,0:T(8,128)(2,1)S(1)} %constant_dynamic-slice_fusion.2), channel_id=1, source_target_pairs={{0,10},{1,63},{64,74},{65,127},{128,138},{129,191},{192,202},{193,... | collective-permute-start | bytes 1179656 | tf_op jit(solution)/shard_map/ppermute | solution.py:39
  69.7 15.4 %collective-permute-start.11 = (bf16[128,2304]{1,0:T(8,128)(2,1)}, bf16[128,2304]{1,0:T(8,128)(2,1)}, u32[]{:S(2)}, u32[]{:S(2)}) collective-permute-start(bf16[128,2304]{1,0:T(8,128)(2,1)} %get-tuple-element.27), channel_id=1, source_target_pairs={{0,1},{1,0},{64,65},{65,64},{128,129},{129,128},{192,193},{193,192... | collective-permute-start | bytes 1769480 | tf_op jit(solution)/shard_map/ppermute | solution.py:43
  78.5 0.7 copy-start.1
  79.2 15.5 %all-to-all-start = ((bf16[32,4,768]{2,1,0:T(4,128)(2,1)}), bf16[32,4,768]{2,1,0:T(4,128)(2,1)S(1)}, u32[]{:S(2)}, u32[]{:S(2)}) async-start(bf16[32,4,768]{2,1,0:T(4,128)(2,1)} %far_sums.1), calls=%async_computation | async-start | bytes 393216 | tf_op jit(solution)/shard_map/all_to_all | solution.py:354
  85.1 2.0 %copy-start.2 = (bf16[256,768]{1,0:T(8,128)(2,1)S(1)}, bf16[256,768]{1,0:T(8,128)(2,1)}, u32[]{:S(2)}) copy-start(bf16[256,768]{1,0:T(8,128)(2,1)} %copy-done.1) | copy-start | bytes 1179652
  92.4 0.8 copy-start.5
  94.7 15.9 %collective-permute-start.12 = (bf16[128,1792]{1,0:T(8,128)(2,1)}, bf16[128,1792]{1,0:T(8,128)(2,1)S(1)}, u32[]{:S(2)}, u32[]{:S(2)}) collective-permute-start(bf16[128,1792]{1,0:T(8,128)(2,1)} %copy-done.5), channel_id=1, source_target_pairs={{0,1},{1,0},{64,65},{65,64},{128,129},{129,128},{192,193},{193,192... | collective-permute-start | bytes 1376264 | tf_op jit(solution)/shard_map/ppermute | solution.py:43
  97.7 24.7 %all-to-all-start.1 = ((bf16[16,4,768]{2,1,0:T(4,128)(2,1)}), bf16[16,4,768]{2,1,0:T(4,128)(2,1)S(1)}, u32[]{:S(2)}, u32[]{:S(2)}) async-start(bf16[16,4,768]{2,1,0:T(4,128)(2,1)} %broadcast_in_dim.30), calls=%async_computation.1 | async-start | bytes 196608 | tf_op jit(solution)/shard_map/all_to_all | solution.py:360
  110.6 11.9 %copy-start.7 = (f32[4,768]{1,0:T(4,128)S(1)}, f32[4,768]{1,0:T(4,128)}, u32[]{:S(2)}) copy-start(f32[4,768]{1,0:T(4,128)} %param.11) | copy-start | bytes 36868

commit v5 on v0

v5 whole, which is shorter than its diff:
```python
import functools
import math

import jax
import jax.numpy as jnp
from jax import lax
from jax.experimental import pallas as pl
from jax.experimental.pallas import tpu as pltpu
from jax.sharding import PartitionSpec as P

HEAD = 128
GROUP = 64
AXES = ("dp", "tensor")
NX, NY, NYL, NZ = 4, 8, 4, 8
HALF = 128
DEVICES = 4
VMEM = 16 * 1024 * 1024


def device_at(x, y, z, core):
    x, y, z = x % NX, y % NY, z % NZ
    dp = z * (NY // NYL) + y // NYL
    return dp * (NX * NYL * 2) + ((y % NYL) * NX + x) * 2 + core


def permutation(target):
    return [
        (device_at(x, y, z, core), device_at(*target(x, y, z, core)))
        for x in range(NX)
        for y in range(NY)
        for z in range(NZ)
        for core in range(2)
    ]


def send(value, dx, dy, cross=False):
    def target(x, y, z, core):
        sign = 1 if (core == 0) != cross else -1
        return x + sign * dx, y + sign * dy, z, core ^ int(cross)

    return lax.ppermute(value, AXES, permutation(target))


def swap(value, core, plane):
    def target(x, y, z, own):
        return x, y, z ^ plane, own ^ core

    return lax.ppermute(value, AXES, permutation(target))


def token_positions(lengths, indices):
    count = lengths.shape[0]
    order = jnp.arange(count, dtype=jnp.int32)
    ends = jnp.sum(jnp.where(order[:, None] <= order[None, :], lengths[:, None], 0), axis=0)
    starts = jnp.where(ends[None, :] <= indices[:, None], ends[None, :], 0)
    return indices - jnp.max(starts, axis=1)


def rope_back(cotangent, positions):
    count = cotangent.shape[0]
    split = cotangent.astype(jnp.float32).reshape(count, -1, HEAD)
    middle = HEAD // 2
    freqs = jnp.exp(jnp.arange(middle, dtype=jnp.float32) * (-2.0 * math.log(10000.0) / HEAD))
    angles = positions.astype(jnp.float32)[:, None] * freqs[None, :]
    cosine = jnp.cos(angles)[:, None, :]
    sine = jnp.sin(angles)[:, None, :]
    first = split[..., :middle]
    second = split[..., middle:]
    lower = first * cosine + second * sine
    upper = second * cosine - first * sine
    return jnp.concatenate([lower, upper], axis=-1).reshape(count, -1).astype(jnp.bfloat16)


def dequant(codes, zeros, steps):
    groups, cols = zeros.shape
    levels = (codes.reshape(groups, GROUP, cols) - zeros[:, None, :]).astype(jnp.float32)
    return (steps[:, None, :] * levels).astype(jnp.bfloat16).reshape(codes.shape)


def columns_of(tables, device, unit, rows):
    return pl.ds(pl.multiple_of(tables[device, unit] * HALF, HALF), rows)


def blocks_of(sizes):
    return [pl.ds(sum(sizes[:unit]), size) for unit, size in enumerate(sizes)]


def load(weights, held, sems):
    blocks = blocks_of([ref.shape[0] for ref in weights])
    copies = [
        pltpu.make_async_copy(ref, held.at[block], sems.at[unit])
        for unit, (ref, block) in enumerate(zip(weights, blocks))
    ]
    for copy in copies:
        copy.start()
    for copy in copies:
        copy.wait()
    return blocks


def group_sums(feats, weight, rot):
    weight_grad = lax.dot_general(
        feats, rot, (((0,), (0,)), ((), ())), preferred_element_type=jnp.float32
    )
    product = weight_grad * weight.astype(jnp.float32)
    rows, cols = weight.shape
    return product.reshape(rows // HALF, HALF // GROUP, GROUP, cols).sum(axis=2)


def put_grads(tables, first, blocks, held, rot, grads, sent, grad_ref, sems):
    for block in blocks:
        grads[:, block] = lax.dot_general(
            rot, held[block, :], (((1,), (1,)), ((), ())), preferred_element_type=jnp.float32
        ).astype(jnp.bfloat16)
    tokens = grad_ref.shape[0]
    copies = [
        pltpu.make_async_copy(
            grads.at[pl.ds(0, tokens), block],
            grad_ref.at[:, columns_of(tables, 0, first + unit, block.size)],
            sems.at[unit],
        )
        for unit, block in enumerate(blocks)
    ]
    copies += [
        pltpu.make_async_copy(
            grads.at[pl.ds(part * tokens, tokens)], ref, sems.at[len(blocks) + part - 1]
        )
        for part, ref in enumerate(sent, 1)
    ]
    for copy in copies:
        copy.start()
    return copies


def pack_kernel(sizes, tables, feats_ref, rot_ref, mine_ref, core_ref, plane_ref):
    width = sum(sizes)
    outs = ((mine_ref, 0), (core_ref, 0), (plane_ref, 0), (plane_ref, width))
    for device, (ref, at) in enumerate(outs):
        for unit, block in enumerate(blocks_of(sizes)):
            columns = columns_of(tables, device, unit, block.size)
            ref[:, pl.ds(at + block.start, block.size)] = feats_ref[:, columns]
    core_ref[:, width:] = rot_ref[...]
    plane_ref[:, 2 * width :] = rot_ref[...]


def near_kernel(count, tables, *refs):
    feats = refs[:1] + refs[2 : DEVICES + 1]
    rots, refs = refs[1 : DEVICES + 1], refs[DEVICES + 1 :]
    weights, refs = refs[:count], refs[count:]
    grad_ref, sums_ref, rot_ref, feats_ref, *sent, held, grads, held_sems, grad_sems = refs
    blocks = load(weights, held, held_sems)
    cols = held.shape[1]
    rot = jnp.concatenate([ref[:, ref.shape[1] - cols :] for ref in rots], axis=0)
    near, far = held.shape[0], feats_ref.shape[1]
    copies = put_grads(tables, 0, blocks, held, rot, grads, sent, grad_ref, grad_sems)
    for block in blocks:
        columns = jnp.concatenate([ref[:, block] for ref in feats], axis=0)
        at = block.start // HALF
        sums_ref[at : at + block.size // HALF] = group_sums(columns, held[block, :], rot)
    rot_ref[...] = rot
    for part, ref in enumerate(feats):
        tokens = pl.ds(part * ref.shape[0], ref.shape[0])
        feats_ref[tokens, :] = ref[:, near : near + far]
    for copy in copies:
        copy.wait()


def far_sums_kernel(near, count, tables, rot_ref, feats_ref, near_ref, *refs):
    weights, (all_ref, held, sems) = refs[:count], refs[count:]
    blocks = load(weights, held, sems)
    all_ref[...] = jnp.zeros_like(all_ref)
    rot = rot_ref[...]
    sums = [near_ref[...]]
    sums += [group_sums(feats_ref[:, block], held[block, :], rot) for block in blocks]
    sizes = near + tuple(block.size for block in blocks)
    sums = jnp.concatenate(sums, axis=0).astype(all_ref.dtype)
    at = 0
    for unit, size in enumerate(sizes):
        for half in range(size // HALF):
            all_ref[tables[0, unit] + half] = sums[at]
            at += 1


def far_grad_kernel(near, count, tables, rot_ref, *refs):
    weights, refs = refs[:count], refs[count:]
    _, grad_ref, *sent, held, grads, held_sems, grad_sems = refs
    blocks = load(weights, held, held_sems)
    rot = rot_ref[...]
    copies = put_grads(tables, near, blocks, held, rot, grads, sent, grad_ref, grad_sems)
    for copy in copies:
        copy.wait()


def place_kernel(sizes, first, tables, *refs):
    *parts, _, grad_ref, sems = refs
    copies = [
        pltpu.make_async_copy(
            ref.at[:, block],
            grad_ref.at[:, columns_of(tables, device, first + unit, block.size)],
            sems.at[device - 1, unit],
        )
        for device, ref in enumerate(parts, 1)
        for unit, block in enumerate(blocks_of(sizes))
    ]
    for copy in copies:
        copy.start()
    for copy in copies:
        copy.wait()


SMEM_SPEC = pl.BlockSpec(memory_space=pltpu.SMEM)
VMEM_SPEC = pl.BlockSpec(memory_space=pltpu.VMEM)
ANY_SPEC = pl.BlockSpec(memory_space=pl.ANY)
PARAMS = pltpu.CompilerParams(vmem_limit_bytes=VMEM)


def cost(rows, cols, tokens, dots):
    return pl.CostEstimate(
        flops=2 * DEVICES * dots * rows * cols * tokens,
        bytes_accessed=rows * (cols * 2 + tokens * 2 * DEVICES),
        transcendentals=0,
    )


def scratch(weights, tokens, own):
    rows, cols = sum(weight.shape[0] for weight in weights), weights[0].shape[1]
    buffers = [pltpu.VMEM((rows, cols), jnp.bfloat16)]
    sems = [pltpu.SemaphoreType.DMA((len(weights),))]
    if own:
        buffers.append(pltpu.VMEM((DEVICES * tokens, rows), jnp.bfloat16))
        sems.append(pltpu.SemaphoreType.DMA((len(weights) + DEVICES - 1,)))
    return buffers + sems


def pack(tables, feats, rot, sizes):
    tokens, width, cols = feats.shape[0], sum(sizes), rot.shape[1]
    widths = (width, width + cols, 2 * width + cols)
    return pl.pallas_call(
        functools.partial(pack_kernel, sizes),
        out_shape=tuple(jax.ShapeDtypeStruct((tokens, size), feats.dtype) for size in widths),
        in_specs=[SMEM_SPEC, VMEM_SPEC, VMEM_SPEC],
        out_specs=(VMEM_SPEC,) * 3,
        cost_estimate=pl.CostEstimate(
            flops=0, bytes_accessed=2 * feats.size * 2, transcendentals=0
        ),
        compiler_params=PARAMS,
        name="pack",
    )(tables, feats, rot)


def near_shards(tables, feats, rot, weights, width, far):
    tokens, cols = rot.shape
    rows = sum(weight.shape[0] for weight in weights)
    return pl.pallas_call(
        functools.partial(near_kernel, len(weights)),
        out_shape=(
            jax.ShapeDtypeStruct((tokens, width), jnp.bfloat16),
            jax.ShapeDtypeStruct((rows // HALF, HALF // GROUP, cols), jnp.float32),
            jax.ShapeDtypeStruct((DEVICES * tokens, cols), jnp.bfloat16),
            jax.ShapeDtypeStruct((DEVICES * tokens, far), jnp.bfloat16),
        )
        + (jax.ShapeDtypeStruct((tokens, rows), jnp.bfloat16),) * (DEVICES - 1),
        in_specs=[SMEM_SPEC] + [VMEM_SPEC] * (DEVICES + 1) + [ANY_SPEC] * len(weights),
        out_specs=(ANY_SPEC,) + (VMEM_SPEC,) * 3 + (ANY_SPEC,) * (DEVICES - 1),
        scratch_shapes=scratch(weights, tokens, 1),
        cost_estimate=cost(rows, cols, tokens, 2),
        compiler_params=PARAMS,
        name="near_shards",
    )(tables, feats[0], rot, *feats[1:], *weights)


def far_sums(tables, rot, feats, weights, near_sums, near_sizes, halves):
    tokens, cols = rot.shape
    rows = feats.shape[1]
    return pl.pallas_call(
        functools.partial(far_sums_kernel, near_sizes, len(weights)),
        out_shape=jax.ShapeDtypeStruct((halves, HALF // GROUP, cols), jnp.bfloat16),
        in_specs=[SMEM_SPEC] + [VMEM_SPEC] * 3 + [ANY_SPEC] * len(weights),
        out_specs=VMEM_SPEC,
        scratch_shapes=scratch(weights, tokens, 0),
        cost_estimate=cost(rows, cols, tokens // DEVICES, 1),
        compiler_params=PARAMS,
        name="far_sums",
    )(tables, rot, feats, near_sums, *weights)


def far_grad(tables, rot, weights, grad, near):
    tokens, cols = grad.shape[0], rot.shape[1]
    rows = sum(weight.shape[0] for weight in weights)
    return pl.pallas_call(
        functools.partial(far_grad_kernel, near, len(weights)),
        out_shape=(jax.ShapeDtypeStruct(grad.shape, grad.dtype),)
        + (jax.ShapeDtypeStruct((tokens, rows), jnp.bfloat16),) * (DEVICES - 1),
        in_specs=[SMEM_SPEC, VMEM_SPEC] + [ANY_SPEC] * (len(weights) + 1),
        out_specs=(ANY_SPEC,) * DEVICES,
        scratch_shapes=scratch(weights, tokens, 1),
        input_output_aliases={2 + len(weights): 0},
        cost_estimate=cost(rows, cols, tokens, 1),
        compiler_params=PARAMS,
        name="far_grad",
    )(tables, rot, *weights, grad)


def place(tables, blocks, grad, sizes, first):
    return pl.pallas_call(
        functools.partial(place_kernel, sizes, first),
        out_shape=jax.ShapeDtypeStruct(grad.shape, grad.dtype),
        in_specs=[SMEM_SPEC] + [VMEM_SPEC] * len(blocks) + [ANY_SPEC],
        out_specs=ANY_SPEC,
        scratch_shapes=[pltpu.SemaphoreType.DMA((len(blocks), len(sizes)))],
        input_output_aliases={1 + len(blocks): 0},
        cost_estimate=pl.CostEstimate(
            flops=0, bytes_accessed=4 * len(blocks) * blocks[0].size, transcendentals=0
        ),
        compiler_params=PARAMS,
        name="place",
    )(tables, *blocks, grad)


def unit_table(x, y, core, plane):
    sign = 2 * core - 1

    def owner(dx, dy, half=0):
        chip = ((y + sign * dy) % NYL) * NX + (x + sign * dx) % NX
        return (chip * 2 + plane) * 2 + half

    near = [owner(0, 0, core), owner(1, 0), owner(0, 1), owner(1, 1), owner(-1, 1)]
    far = [owner(2, 0, core), owner(0, 2, core), owner(2, 1), owner(-1, 2), owner(2, 2, core)]
    return jnp.stack(near + far).astype(jnp.int32)


def per_device(activations, key_cotangent, doc_lengths, weight_codes, zero_points, step_sizes):
    tokens, width = activations.shape
    rows = weight_codes.shape[0]
    devices = NX * NYL * 2
    place_in = lax.axis_index("tensor")
    core = place_in % 2
    x = (place_in // 2) % NX
    y = place_in // (2 * NX)
    plane = (lax.axis_index("dp") // (NY // NYL)) % 2
    others = [(core, plane), (1 - core, plane), (core, 1 - plane), (1 - core, 1 - plane)]
    tables = jnp.stack([unit_table(x, y, *at) for at in others])
    near_sizes = (HALF, rows, rows, rows, rows)
    far_sizes = (HALF, HALF, rows, rows, HALF)
    sizes = near_sizes + far_sizes

    weight = dequant(weight_codes, zero_points, step_sizes)
    pairs = [[2 * chip, 2 * chip + 1] for chip in range(NX * NYL)]
    both = lax.all_gather(weight, "tensor", axis=0, tiled=True, axis_index_groups=pairs)
    chip_weight = lax.dynamic_slice_in_dim(both, plane * rows, rows, axis=0)

    def my_half(value):
        return lax.dynamic_slice_in_dim(value, core * HALF, HALF, axis=0)

    chip_weight, key_cotangent, activations = lax.optimization_barrier(
        (chip_weight, key_cotangent, activations)
    )
    from_x = send(chip_weight, 1, 0)
    from_y = send(chip_weight, 0, 1)

    indices = place_in * tokens + jnp.arange(tokens, dtype=jnp.int32)
    mine = rope_back(key_cotangent, token_positions(doc_lengths[0], indices))
    feats, for_core, for_plane = pack(tables, activations, mine, sizes)
    from_plane = swap(for_plane, 0, 1)
    from_core = swap(for_core, 1, 0)
    from_x, from_y, _ = lax.optimization_barrier((from_x, from_y, for_plane))

    from_xy = send(from_y, 1, 0)
    from_yx = send(from_x, 0, 1, cross=True)
    far_xx = send(my_half(from_x), 1, 0)
    far_yy = send(my_half(from_y), 0, 1)
    from_xy, from_yx, _, _ = lax.optimization_barrier((from_xy, from_yx, far_xx, far_yy))

    far_x = send(from_xy, 1, 0)
    far_y = send(from_yx, 0, 1)
    half_xy = my_half(from_xy)
    far = send(half_xy, 1, 1)

    for_both, _, _ = lax.optimization_barrier((from_plane, half_xy, from_yx))
    from_both = swap(for_both[:, sum(sizes) :], 1, 0)
    tokens_feats = [feats, from_core, from_plane, from_both]
    near = [my_half(chip_weight), from_x, from_y, from_xy, from_yx]
    grad, near_sums, rot, far_feats, *near_sent = near_shards(
        tables, tokens_feats, mine, near, width, sum(far_sizes)
    )
    near_got = [swap(near_sent[0], 1, 0), swap(near_sent[1], 0, 1), swap(near_sent[2], 1, 1)]
    grad = place(tables, near_got, grad, near_sizes, 0)

    fars = [far_xx, far_yy, far_x, far_y, far]
    halves = devices * rows // HALF
    sums = far_sums(tables, rot, far_feats, fars, near_sums, near_sizes, halves)
    shares = lax.all_to_all(sums, "tensor", split_axis=0, concat_axis=0, tiled=True)

    grad, *far_sent = far_grad(tables, rot, fars, grad, len(near))
    shares, grad, *far_sent = lax.optimization_barrier((shares, grad, *far_sent))
    shares = shares.astype(jnp.float32).reshape(devices, rows // GROUP, -1)
    share = jnp.sum(shares, axis=0).astype(jnp.bfloat16)
    copies = lax.axis_size("dp")
    totals = lax.all_to_all(
        jnp.broadcast_to(share[None], (copies, *share.shape)),
        "dp",
        split_axis=0,
        concat_axis=0,
        tiled=True,
    )
    far_got = [swap(far_sent[0], 1, 0), swap(far_sent[1], 0, 1), swap(far_sent[2], 1, 1)]
    grad = place(tables, far_got, grad, far_sizes, len(near))
    totals, grad = lax.optimization_barrier((totals, grad))
    seq_tokens = tokens * devices
    total = jnp.sum(totals.astype(jnp.float32), axis=0)
    step_grad = total / (seq_tokens * step_sizes)
    return (grad, step_grad)


def solution(mesh):
    in_specs = (
        P(("dp", "tensor"), None),
        P(("dp", "tensor"), None),
        P("dp", None),
        P("tensor", None),
        P("tensor", None),
        P("tensor", None),
    )
    out_specs = (P(("dp", "tensor"), None), P("tensor", None))
    return jax.shard_map(
        per_device, mesh=mesh, in_specs=in_specs, out_specs=out_specs, check_vma=False
    )
```

time: 246 us -> 139 us (0.57)
  the two profiles are of different devices: /device:TPU:8 before, /device:TPU:1 now
where the time goes in v5:
time: 139 us; the launch traced here: 137 us
  starting transfers between devices  71.8 us (52%)
  waiting for transfers between devices  26.5 us (19%)
  Pallas kernels  17 us (12%)
  blocking collectives  9.01 us (6%)
  local copies, waits for them, and re-layouts  8.64 us (6%)
  other arithmetic  2.52 us (2%)
  between operations  1.58 us (1%)
    ppermute x9, starting transfers between devices, send(): return lax.ppermute(value, AXES, permutation(target))  30.4 us
    ppermute x9, starting transfers between devices, swap(): return lax.ppermute(value, AXES, permutation(target))  23.8 us
    ppermute x9, waiting for transfers between devices, swap(): return lax.ppermute(value, AXES, permutation(target))  11.4 us
    all_to_all x1, starting transfers between devices, per_device(): lax.all_to_all(jnp.broadcast_to(share[None], (copies, *share.shape)), 'dp...  10.6 us
    all_to_all x1, waiting for transfers between devices, per_device(): lax.all_to_all(jnp.broadcast_to(share[None], (copies, *share.shape)), 'dp...  10.1 us
    all_gather x1, blocking collectives, per_device(): lax.all_gather(weight, 'tensor', axis=0, tiled=True, axis_index_groups=pa...  9.01 us
    all_to_all x1, starting transfers between devices, per_device(): lax.all_to_all(sums, 'tensor', split_axis=0, concat_axis=0, tiled=True)  7.02 us
    unnamed x22, local copies, waits for them, and re-layouts  5.38 us
  transfers between devices with their start and end apart: 20, of which 5 were waited for; matrix products, arithmetic and copies ran while one was open for 1% of the time, Pallas kernels for 8%

profile of v5, /device:TPU:1, one launch (start us, length us, event | category | flops | bytes accessed | tf_op | source)
XLA Modules:
  0.0 137.1 jit_solution(483639836734214898)
XLA Ops:
  1.0 1.2 fusion.2
  2.3 9.0 %all_gather.3 = bf16[512,768]{1,0:T(8,128)(2,1)S(1)} all-gather(bf16[256,768]{1,0:T(8,128)(2,1)S(1)} %fusion.2), channel_id=1, replica_groups={{0,1},{2,3},{4,5},{6,7},{8,9},{10,11},{12,13},{14,15},{16,17},{18,19},{..., dimensions={0}, use_global_device_ids=true | all-gather | bytes 1179648 | tf_op jit(solution)/shard_map/all_gather | solution.py:349
  11.3 0.8 constant_dynamic-slice_fusion.4
  12.1 0.2 copy.17
  12.5 0.2 multiply_cosine_fusion
  12.7 0.1 copy.18.rot_ref.refs_1_
  13.0 0.1 stack.157
  13.4 2.0 %pack.1 = (bf16[128,2048]{1,0:T(8,128)(2,1)S(1)}, bf16[128,2816]{1,0:T(8,128)(2,1)S(1)}, bf16[128,4864]{1,0:T(8,128)(2,1)}) custom-call(s32[4,10]{1,0:T(4,128)S(1)} %pad_add_fusion.tables, bf16[128,8192]{1,0:T(8,128)(2,1)S(1)} %copy-done, bf16[128,768]{1,0:T(8,128)(2,1)S(1)} %copy.18.rot_ref.refs_1_), custom_call_target="tpu_custom_call" | custom-call | bytes 4194304 | tf_op jit(solution)/shard_map/pack/pallas_call | solution.py:238
  15.4 0.9 copy-done.3
  16.2 0.8 copy-done.4
  17.0 1.9 %collective-permute-start.1 = (bf16[128,4864]{1,0:T(8,128)(2,1)}, bf16[128,4864]{1,0:T(8,128)(2,1)S(1)}, u32[]{:S(2)}, u32[]{:S(2)}) collective-permute-start(bf16[128,4864]{1,0:T(8,128)(2,1)} %get-tuple-element.35), channel_id=1, source_target_pairs={{0,64},{1,65},{64,0},{65,1},{128,192},{129,193},{192,128},{193,129... | collective-permute-start | bytes 3735560 | tf_op jit(solution)/shard_map/ppermute | solution.py:48
  18.9 1.9 %collective-permute-start.2 = (bf16[256,768]{1,0:T(8,128)(2,1)}, bf16[256,768]{1,0:T(8,128)(2,1)S(1)}, u32[]{:S(2)}, u32[]{:S(2)}) collective-permute-start(bf16[256,768]{1,0:T(8,128)(2,1)} %constant_dynamic-slice_fusion.4), channel_id=1, source_target_pairs={{0,2},{1,7},{64,66},{65,71},{128,130},{129,135},{192,194},{193,199... | collective-permute-start | bytes 1179656 | tf_op jit(solution)/shard_map/ppermute | solution.py:41
  20.9 4.3 %collective-permute-start.3 = (bf16[256,768]{1,0:T(8,128)(2,1)}, bf16[256,768]{1,0:T(8,128)(2,1)S(1)}, u32[]{:S(2)}, u32[]{:S(2)}) collective-permute-start(bf16[256,768]{1,0:T(8,128)(2,1)} %constant_dynamic-slice_fusion.4), channel_id=1, source_target_pairs={{0,8},{1,57},{64,72},{65,121},{128,136},{129,185},{192,200},{193,2... | collective-permute-start | bytes 1179656 | tf_op jit(solution)/shard_map/ppermute | solution.py:41
  25.2 2.8 %collective-permute-done.2.refs_6_ = bf16[256,768]{1,0:T(8,128)(2,1)S(1)} collective-permute-done((bf16[256,768]{1,0:T(8,128)(2,1)}, bf16[256,768]{1,0:T(8,128)(2,1)S(1)}, u32[]{:S(2)}, u32[]{:S(2)}) %collective-permute-start.2) | collective-permute-done | bytes 393248 | tf_op jit(solution)/shard_map/ppermute | solution.py:41
  28.0 2.2 %collective-permute-done.3.refs_7_ = bf16[256,768]{1,0:T(8,128)(2,1)S(1)} collective-permute-done((bf16[256,768]{1,0:T(8,128)(2,1)}, bf16[256,768]{1,0:T(8,128)(2,1)S(1)}, u32[]{:S(2)}, u32[]{:S(2)}) %collective-permute-start.3) | collective-permute-done | bytes 393248 | tf_op jit(solution)/shard_map/ppermute | solution.py:41
  30.2 2.5 %collective-permute-start.4 = (bf16[256,768]{1,0:T(8,128)(2,1)S(1)}, bf16[256,768]{1,0:T(8,128)(2,1)S(1)}, u32[]{:S(2)}, u32[]{:S(2)}) collective-permute-start(bf16[256,768]{1,0:T(8,128)(2,1)S(1)} %collective-permute-done.3.refs_7_), channel_id=1, source_target_pairs={{0,2},{1,7},{64,66},{65,71},{128,130},{129,135},{192,194},{193,199... | collective-permute-start | bytes 1179656 | tf_op jit(solution)/shard_map/ppermute | solution.py:41
  32.6 3.5 %collective-permute-start.5 = (bf16[256,768]{1,0:T(8,128)(2,1)S(1)}, bf16[256,768]{1,0:T(8,128)(2,1)S(1)}, u32[]{:S(2)}, u32[]{:S(2)}) collective-permute-start(bf16[256,768]{1,0:T(8,128)(2,1)S(1)} %collective-permute-done.2.refs_6_), channel_id=1, source_target_pairs={{0,57},{1,8},{64,121},{65,72},{128,185},{129,136},{192,249},{193,2... | collective-permute-start | bytes 1179656 | tf_op jit(solution)/shard_map/ppermute | solution.py:41
  36.1 3.4 %collective-permute-start.6 = (bf16[128,768]{1,0:T(8,128)(2,1)S(1)}, bf16[128,768]{1,0:T(8,128)(2,1)S(1)}, u32[]{:S(2)}, u32[]{:S(2)}) collective-permute-start(bf16[128,768]{1,0:T(8,128)(2,1)S(1)} %constant_dynamic-slice_fusion.3), channel_id=1, source_target_pairs={{0,2},{1,7},{64,66},{65,71},{128,130},{129,135},{192,194},{193,199... | collective-permute-start | bytes 589832 | tf_op jit(solution)/shard_map/ppermute | solution.py:41
  39.5 6.0 %collective-permute-start.7 = (bf16[128,768]{1,0:T(8,128)(2,1)S(1)}, bf16[128,768]{1,0:T(8,128)(2,1)S(1)}, u32[]{:S(2)}, u32[]{:S(2)}) collective-permute-start(bf16[128,768]{1,0:T(8,128)(2,1)S(1)} %constant_dynamic-slice_fusion.2), channel_id=1, source_target_pairs={{0,8},{1,57},{64,72},{65,121},{128,136},{129,185},{192,200},{193,2... | collective-permute-start | bytes 589832 | tf_op jit(solution)/shard_map/ppermute | solution.py:41
  45.6 3.1 %collective-permute-start = (bf16[128,2816]{1,0:T(8,128)(2,1)}, bf16[128,2816]{1,0:T(8,128)(2,1)S(1)}, u32[]{:S(2)}, u32[]{:S(2)}) collective-permute-start(bf16[128,2816]{1,0:T(8,128)(2,1)} %copy-done.3), channel_id=1, source_target_pairs={{0,1},{1,0},{64,65},{65,64},{128,129},{129,128},{192,193},{193,192... | collective-permute-start | bytes 2162696 | tf_op jit(solution)/shard_map/ppermute | solution.py:48
  48.8 1.0 copy-done.1
  49.8 3.1 %collective-permute-start.8 = (bf16[128,2816]{1,0:T(8,128)(2,1)S(1)}, bf16[128,2816]{1,0:T(8,128)(2,1)S(1)}, u32[]{:S(2)}, u32[]{:S(2)}) collective-permute-start(bf16[128,2816]{1,0:T(8,128)(2,1)S(1)} %slice.11), channel_id=1, source_target_pairs={{0,1},{1,0},{64,65},{65,64},{128,129},{129,128},{192,193},{193,192... | collective-permute-start | bytes 2162696 | tf_op jit(solution)/shard_map/ppermute | solution.py:48
  52.9 3.3 %collective-permute-start.10 = (bf16[256,768]{1,0:T(8,128)(2,1)S(1)}, bf16[256,768]{1,0:T(8,128)(2,1)S(1)}, u32[]{:S(2)}, u32[]{:S(2)}) collective-permute-start(bf16[256,768]{1,0:T(8,128)(2,1)S(1)} %collective-permute-done.5.refs_9_), channel_id=1, source_target_pairs={{0,8},{1,57},{64,72},{65,121},{128,136},{129,185},{192,200},{193,2... | collective-permute-start | bytes 1179656 | tf_op jit(solution)/shard_map/ppermute | solution.py:41
  56.2 3.6 %collective-permute-start.9 = (bf16[256,768]{1,0:T(8,128)(2,1)S(1)}, bf16[256,768]{1,0:T(8,128)(2,1)S(1)}, u32[]{:S(2)}, u32[]{:S(2)}) collective-permute-start(bf16[256,768]{1,0:T(8,128)(2,1)S(1)} %collective-permute-done.4.refs_8_), channel_id=1, source_target_pairs={{0,2},{1,7},{64,66},{65,71},{128,130},{129,135},{192,194},{193,199... | collective-permute-start | bytes 1179656 | tf_op jit(solution)/shard_map/ppermute | solution.py:41
  59.9 1.9 %collective-permute-start.11 = (bf16[128,768]{1,0:T(8,128)(2,1)S(1)}, bf16[128,768]{1,0:T(8,128)(2,1)S(1)}, u32[]{:S(2)}, u32[]{:S(2)}) collective-permute-start(bf16[128,768]{1,0:T(8,128)(2,1)S(1)} %constant_dynamic-slice_fusion.1), channel_id=1, source_target_pairs={{0,10},{1,63},{64,74},{65,127},{128,138},{129,191},{192,202},{193,... | collective-permute-start | bytes 589832 | tf_op jit(solution)/shard_map/ppermute | solution.py:41
  61.8 0.9 constant_dynamic-slice_fusion.refs_5_
  62.8 1.3 copy-done.2
  64.1 4.6 %near_shards.1 = (bf16[128,8192]{1,0:T(8,128)(2,1)}, f32[9,2,768]{2,1,0:T(2,128)S(1)}, bf16[512,768]{1,0:T(8,128)(2,1)S(1)}, bf16[512,896]{1,0:T(8,128)(2,1)S(1)...) custom-call(s32[4,10]{1,0:T(4,128)S(1)} %pad_add_fusion.tables, ...), custom_call_target="tpu_custom_call" | custom-call | flops 1811939328 | bytes 2949120 | tf_op jit(solution)/shard_map/near_shards/pallas_call | solution.py:254
  68.7 0.7 copy-done.6
  69.4 0.7 copy-done.7
  70.1 3.4 %far_sums.1 = bf16[64,2,768]{2,1,0:T(2,128)(2,1)} custom-call(s32[4,10]{1,0:T(4,128)S(1)} %pad_add_fusion.tables, bf16[512,768]{1,0:T(8,128)(2,1)S(1)} %get-tuple-element.42.rot_ref, bf16[512,896]{1,0:T(8,128)(2,1)S(1)} %get-tuple-element.43.feats_ref, f32[9,2,768]{2,1,0:T(2,128)S(1)} %get-tuple-element.44.near_ref, ...), custom_call_target="tpu_custom_call" | custom-call | flops 704643072 | bytes 2293760 | tf_op jit(solution)/shard_map/far_sums/pallas_call | solution.py:275
  73.5 7.0 %all-to-all-start = ((bf16[64,2,768]{2,1,0:T(2,128)(2,1)}), bf16[64,2,768]{2,1,0:T(2,128)(2,1)S(1)}, u32[]{:S(2)}, u32[]{:S(2)}) async-start(bf16[64,2,768]{2,1,0:T(2,128)(2,1)} %far_sums.1), calls=%async_computation | async-start | bytes 393216 | tf_op jit(solution)/shard_map/all_to_all | solution.py:392
  80.5 2.1 %collective-permute-start.12 = (bf16[128,1152]{1,0:T(8,128)(2,1)}, bf16[128,1152]{1,0:T(8,128)(2,1)S(1)}, u32[]{:S(2)}, u32[]{:S(2)}) collective-permute-start(bf16[128,1152]{1,0:T(8,128)(2,1)} %get-tuple-element.45), channel_id=1, source_target_pairs={{0,1},{1,0},{64,65},{65,64},{128,129},{129,128},{192,193},{193,192... | collective-permute-start | bytes 884744 | tf_op jit(solution)/shard_map/ppermute | solution.py:48
  82.7 1.9 %collective-permute-start.13 = (bf16[128,1152]{1,0:T(8,128)(2,1)}, bf16[128,1152]{1,0:T(8,128)(2,1)S(1)}, u32[]{:S(2)}, u32[]{:S(2)}) collective-permute-start(bf16[128,1152]{1,0:T(8,128)(2,1)} %copy-done.7), channel_id=1, source_target_pairs={{0,64},{1,65},{64,0},{65,1},{128,192},{129,193},{192,128},{193,129... | collective-permute-start | bytes 884744 | tf_op jit(solution)/shard_map/ppermute | solution.py:48
  84.6 3.8 %collective-permute-start.14 = (bf16[128,1152]{1,0:T(8,128)(2,1)}, bf16[128,1152]{1,0:T(8,128)(2,1)S(1)}, u32[]{:S(2)}, u32[]{:S(2)}) collective-permute-start(bf16[128,1152]{1,0:T(8,128)(2,1)} %copy-done.6), channel_id=1, source_target_pairs={{0,65},{1,64},{64,1},{65,0},{128,193},{129,192},{192,129},{193,128... | collective-permute-start | bytes 884744 | tf_op jit(solution)/shard_map/ppermute | solution.py:48
  88.4 4.7 %collective-permute-done.13.refs_1_ = bf16[128,1152]{1,0:T(8,128)(2,1)S(1)} collective-permute-done((bf16[128,1152]{1,0:T(8,128)(2,1)}, bf16[128,1152]{1,0:T(8,128)(2,1)S(1)}, u32[]{:S(2)}, u32[]{:S(2)}) %collective-permute-start.13) | collective-permute-done | bytes 294944 | tf_op jit(solution)/shard_map/ppermute | solution.py:48
  93.1 6.7 %collective-permute-done.14.refs_2_ = bf16[128,1152]{1,0:T(8,128)(2,1)S(1)} collective-permute-done((bf16[128,1152]{1,0:T(8,128)(2,1)}, bf16[128,1152]{1,0:T(8,128)(2,1)S(1)}, u32[]{:S(2)}, u32[]{:S(2)}) %collective-permute-start.14) | collective-permute-done | bytes 294944 | tf_op jit(solution)/shard_map/ppermute | solution.py:48
  99.9 1.6 %place.2.refs_5_ = bf16[128,8192]{1,0:T(8,128)(2,1)} custom-call(s32[4,10]{1,0:T(4,128)S(1)} %pad_add_fusion.tables, bf16[128,1152]{1,0:T(8,128)(2,1)S(1)} %collective-permute-done.12.refs_0_, bf16[128,1152]{1,0:T(8,128)(2,1)S(1)} %collective-permute-done.13.refs_1_, ...), custom_call_target="tpu_custom_call", output_to_operand_aliasing={{}: (4, {})} | custom-call | bytes 1769472 | tf_op jit(solution)/shard_map/place/pallas_call | solution.py:305
  101.5 3.9 %far_grad.1 = (bf16[128,8192]{1,0:T(8,128)(2,1)}, bf16[128,896]{1,0:T(8,128)(2,1)S(1)}, bf16[128,896]{1,0:T(8,128)(2,1)S(1)}, bf16[128,896]{1,0:T(8,128)(2,1)S(1)}) custom-call(s32[4,10]{1,0:T(4,128)S(1)} %pad_add_fusion.tables, bf16[512,768]{1,0:T(8,128)(2,1)S(1)} %get-tuple-element.42.rot_ref, ...), custom_call_target="tpu_custom_call", output_to_operand_aliasing={{0}: (7, {})} | custom-call | flops 704643072 | bytes 2293760 | tf_op jit(solution)/shard_map/far_grad/pallas_call | solution.py:290
  105.4 1.9 %collective-permute-start.15 = (bf16[128,896]{1,0:T(8,128)(2,1)S(1)}, bf16[128,896]{1,0:T(8,128)(2,1)S(1)}, u32[]{:S(2)}, u32[]{:S(2)}) collective-permute-start(bf16[128,896]{1,0:T(8,128)(2,1)S(1)} %get-tuple-element.54), channel_id=1, source_target_pairs={{0,1},{1,0},{64,65},{65,64},{128,129},{129,128},{192,193},{193,192... | collective-permute-start | bytes 688136 | tf_op jit(solution)/shard_map/ppermute | solution.py:48
  107.3 2.2 %collective-permute-start.16 = (bf16[128,896]{1,0:T(8,128)(2,1)S(1)}, bf16[128,896]{1,0:T(8,128)(2,1)S(1)}, u32[]{:S(2)}, u32[]{:S(2)}) collective-permute-start(bf16[128,896]{1,0:T(8,128)(2,1)S(1)} %get-tuple-element.55), channel_id=1, source_target_pairs={{0,64},{1,65},{64,0},{65,1},{128,192},{129,193},{192,128},{193,129... | collective-permute-start | bytes 688136 | tf_op jit(solution)/shard_map/ppermute | solution.py:48
  109.5 3.7 %collective-permute-start.17 = (bf16[128,896]{1,0:T(8,128)(2,1)S(1)}, bf16[128,896]{1,0:T(8,128)(2,1)S(1)}, u32[]{:S(2)}, u32[]{:S(2)}) collective-permute-start(bf16[128,896]{1,0:T(8,128)(2,1)S(1)} %get-tuple-element.56), channel_id=1, source_target_pairs={{0,65},{1,64},{64,1},{65,0},{128,193},{129,192},{192,129},{193,128... | collective-permute-start | bytes 688136 | tf_op jit(solution)/shard_map/ppermute | solution.py:48
  113.4 0.1 reduce
  113.5 0.7 broadcast_in_dim.30
  114.1 10.6 %all-to-all-start.1 = ((bf16[16,4,768]{2,1,0:T(4,128)(2,1)}), bf16[16,4,768]{2,1,0:T(4,128)(2,1)S(1)}, u32[]{:S(2)}, u32[]{:S(2)}) async-start(bf16[16,4,768]{2,1,0:T(4,128)(2,1)} %broadcast_in_dim.30), calls=%async_computation.1 | async-start | bytes 196608 | tf_op jit(solution)/shard_map/all_to_all | solution.py:399
  124.8 1.5 %place.3 = bf16[128,8192]{1,0:T(8,128)(2,1)} custom-call(s32[4,10]{1,0:T(4,128)S(1)} %pad_add_fusion.tables, bf16[128,896]{1,0:T(8,128)(2,1)S(1)} %collective-permute-done.15.refs_0_, bf16[128,896]{1,0:T(8,128)(2,1)S(1)} %collective-permute-done.16.refs_1_, bf16[128,896]{1,0:T(8,128)(2,1)S(1)} %collective-permute-done.17.refs_2_, ...), custom_call_target="tpu_custom_call", output_to_operand_aliasing={{}: (4, {})} | custom-call | bytes 1376256 | tf_op jit(solution)/shard_map/place/pallas_call | solution.py:305
  126.3 10.1 %all-to-all-done.1 = bf16[16,4,768]{2,1,0:T(4,128)(2,1)S(1)} async-done(((bf16[16,4,768]{2,1,0:T(4,128)(2,1)}), bf16[16,4,768]{2,1,0:T(4,128)(2,1)S(1)}, u32[]{:S(2)}, u32[]{:S(2)}) %all-to-all-start.1) | async-done | bytes 98336 | tf_op jit(solution)/shard_map/all_to_all | solution.py:399
  136.5 0.6 multiply_divide_fusion
  (49 shorter events, 0.9 us)
Async XLA Ops:
  0.6 11.4 %copy-start.8 = (bf16[128,768]{1,0:T(8,128)(2,1)S(1)}, bf16[128,768]{1,0:T(8,128)(2,1)}, u32[]{:S(2)}) copy-start(bf16[128,768]{1,0:T(8,128)(2,1)} %param.7) | copy-start | bytes 589828
  1.0 11.3 %copy-start.10 = (s32[1,8]{1,0:T(1,128)S(1)}, s32[1,8]{1,0:T(1,128)}, u32[]{:S(2)}) copy-start(s32[1,8]{1,0:T(1,128)} %param.8) | copy-start | bytes 100
  2.2 11.2 %copy-start = (bf16[128,8192]{1,0:T(8,128)(2,1)S(1)}, bf16[128,8192]{1,0:T(8,128)(2,1)}, u32[]{:S(2)}) copy-start(bf16[128,8192]{1,0:T(8,128)(2,1)} %feats_ref) | copy-start | bytes 6291460
  15.4 0.9 copy-start.3
  16.2 0.8 copy-start.4
  17.0 31.7 %collective-permute-start.1 = (bf16[128,4864]{1,0:T(8,128)(2,1)}, bf16[128,4864]{1,0:T(8,128)(2,1)S(1)}, u32[]{:S(2)}, u32[]{:S(2)}) collective-permute-start(bf16[128,4864]{1,0:T(8,128)(2,1)} %get-tuple-element.35), channel_id=1, source_target_pairs={{0,64},{1,65},{64,0},{65,1},{128,192},{129,193},{192,128},{193,129... | collective-permute-start | bytes 3735560 | tf_op jit(solution)/shard_map/ppermute | solution.py:48
  18.9 9.0 %collective-permute-start.2 = (bf16[256,768]{1,0:T(8,128)(2,1)}, bf16[256,768]{1,0:T(8,128)(2,1)S(1)}, u32[]{:S(2)}, u32[]{:S(2)}) collective-permute-start(bf16[256,768]{1,0:T(8,128)(2,1)} %constant_dynamic-slice_fusion.4), channel_id=1, source_target_pairs={{0,2},{1,7},{64,66},{65,71},{128,130},{129,135},{192,194},{193,199... | collective-permute-start | bytes 1179656 | tf_op jit(solution)/shard_map/ppermute | solution.py:41
  20.9 9.3 %collective-permute-start.3 = (bf16[256,768]{1,0:T(8,128)(2,1)}, bf16[256,768]{1,0:T(8,128)(2,1)S(1)}, u32[]{:S(2)}, u32[]{:S(2)}) collective-permute-start(bf16[256,768]{1,0:T(8,128)(2,1)} %constant_dynamic-slice_fusion.4), channel_id=1, source_target_pairs={{0,8},{1,57},{64,72},{65,121},{128,136},{129,185},{192,200},{193,2... | collective-permute-start | bytes 1179656 | tf_op jit(solution)/shard_map/ppermute | solution.py:41
  25.2 37.6 %copy-start.5 = (bf16[128,2048]{1,0:T(8,128)(2,1)S(1)}, bf16[128,2048]{1,0:T(8,128)(2,1)}, u32[]{:S(2)}) copy-start(bf16[128,2048]{1,0:T(8,128)(2,1)} %copy-done.4) | copy-start | bytes 1572868
  30.2 18.5 %collective-permute-start.4 = (bf16[256,768]{1,0:T(8,128)(2,1)S(1)}, bf16[256,768]{1,0:T(8,128)(2,1)S(1)}, u32[]{:S(2)}, u32[]{:S(2)}) collective-permute-start(bf16[256,768]{1,0:T(8,128)(2,1)S(1)} %collective-permute-done.3.refs_7_), channel_id=1, source_target_pairs={{0,2},{1,7},{64,66},{65,71},{128,130},{129,135},{192,194},{193,199... | collective-permute-start | bytes 1179656 | tf_op jit(solution)/shard_map/ppermute | solution.py:41
  32.6 16.1 %collective-permute-start.5 = (bf16[256,768]{1,0:T(8,128)(2,1)S(1)}, bf16[256,768]{1,0:T(8,128)(2,1)S(1)}, u32[]{:S(2)}, u32[]{:S(2)}) collective-permute-start(bf16[256,768]{1,0:T(8,128)(2,1)S(1)} %collective-permute-done.2.refs_6_), channel_id=1, source_target_pairs={{0,57},{1,8},{64,121},{65,72},{128,185},{129,136},{192,249},{193,2... | collective-permute-start | bytes 1179656 | tf_op jit(solution)/shard_map/ppermute | solution.py:41
  36.1 9.5 %collective-permute-start.6 = (bf16[128,768]{1,0:T(8,128)(2,1)S(1)}, bf16[128,768]{1,0:T(8,128)(2,1)S(1)}, u32[]{:S(2)}, u32[]{:S(2)}) collective-permute-start(bf16[128,768]{1,0:T(8,128)(2,1)S(1)} %constant_dynamic-slice_fusion.3), channel_id=1, source_target_pairs={{0,2},{1,7},{64,66},{65,71},{128,130},{129,135},{192,194},{193,199... | collective-permute-start | bytes 589832 | tf_op jit(solution)/shard_map/ppermute | solution.py:41
  39.5 9.1 %collective-permute-start.7 = (bf16[128,768]{1,0:T(8,128)(2,1)S(1)}, bf16[128,768]{1,0:T(8,128)(2,1)S(1)}, u32[]{:S(2)}, u32[]{:S(2)}) collective-permute-start(bf16[128,768]{1,0:T(8,128)(2,1)S(1)} %constant_dynamic-slice_fusion.2), channel_id=1, source_target_pairs={{0,8},{1,57},{64,72},{65,121},{128,136},{129,185},{192,200},{193,2... | collective-permute-start | bytes 589832 | tf_op jit(solution)/shard_map/ppermute | solution.py:41
  45.6 17.1 %collective-permute-start = (bf16[128,2816]{1,0:T(8,128)(2,1)}, bf16[128,2816]{1,0:T(8,128)(2,1)S(1)}, u32[]{:S(2)}, u32[]{:S(2)}) collective-permute-start(bf16[128,2816]{1,0:T(8,128)(2,1)} %copy-done.3), channel_id=1, source_target_pairs={{0,1},{1,0},{64,65},{65,64},{128,129},{129,128},{192,193},{193,192... | collective-permute-start | bytes 2162696 | tf_op jit(solution)/shard_map/ppermute | solution.py:48
  48.7 1.0 copy-start.1
  49.8 13.0 %collective-permute-start.8 = (bf16[128,2816]{1,0:T(8,128)(2,1)S(1)}, bf16[128,2816]{1,0:T(8,128)(2,1)S(1)}, u32[]{:S(2)}, u32[]{:S(2)}) collective-permute-start(bf16[128,2816]{1,0:T(8,128)(2,1)S(1)} %slice.11), channel_id=1, source_target_pairs={{0,1},{1,0},{64,65},{65,64},{128,129},{129,128},{192,193},{193,192... | collective-permute-start | bytes 2162696 | tf_op jit(solution)/shard_map/ppermute | solution.py:48
  52.9 17.2 %collective-permute-start.10 = (bf16[256,768]{1,0:T(8,128)(2,1)S(1)}, bf16[256,768]{1,0:T(8,128)(2,1)S(1)}, u32[]{:S(2)}, u32[]{:S(2)}) collective-permute-start(bf16[256,768]{1,0:T(8,128)(2,1)S(1)} %collective-permute-done.5.refs_9_), channel_id=1, source_target_pairs={{0,8},{1,57},{64,72},{65,121},{128,136},{129,185},{192,200},{193,2... | collective-permute-start | bytes 1179656 | tf_op jit(solution)/shard_map/ppermute | solution.py:41
  56.2 13.9 %collective-permute-start.9 = (bf16[256,768]{1,0:T(8,128)(2,1)S(1)}, bf16[256,768]{1,0:T(8,128)(2,1)S(1)}, u32[]{:S(2)}, u32[]{:S(2)}) collective-permute-start(bf16[256,768]{1,0:T(8,128)(2,1)S(1)} %collective-permute-done.4.refs_8_), channel_id=1, source_target_pairs={{0,2},{1,7},{64,66},{65,71},{128,130},{129,135},{192,194},{193,199... | collective-permute-start | bytes 1179656 | tf_op jit(solution)/shard_map/ppermute | solution.py:41
  59.9 10.2 %collective-permute-start.11 = (bf16[128,768]{1,0:T(8,128)(2,1)S(1)}, bf16[128,768]{1,0:T(8,128)(2,1)S(1)}, u32[]{:S(2)}, u32[]{:S(2)}) collective-permute-start(bf16[128,768]{1,0:T(8,128)(2,1)S(1)} %constant_dynamic-slice_fusion.1), channel_id=1, source_target_pairs={{0,10},{1,63},{64,74},{65,127},{128,138},{129,191},{192,202},{193,... | collective-permute-start | bytes 589832 | tf_op jit(solution)/shard_map/ppermute | solution.py:41
  62.8 1.3 copy-start.2
  68.6 0.7 copy-start.6
  69.4 0.7 copy-start.7
  73.5 31.9 %all-to-all-start = ((bf16[64,2,768]{2,1,0:T(2,128)(2,1)}), bf16[64,2,768]{2,1,0:T(2,128)(2,1)S(1)}, u32[]{:S(2)}, u32[]{:S(2)}) async-start(bf16[64,2,768]{2,1,0:T(2,128)(2,1)} %far_sums.1), calls=%async_computation | async-start | bytes 393216 | tf_op jit(solution)/shard_map/all_to_all | solution.py:392
  80.5 7.9 %collective-permute-start.12 = (bf16[128,1152]{1,0:T(8,128)(2,1)}, bf16[128,1152]{1,0:T(8,128)(2,1)S(1)}, u32[]{:S(2)}, u32[]{:S(2)}) collective-permute-start(bf16[128,1152]{1,0:T(8,128)(2,1)} %get-tuple-element.45), channel_id=1, source_target_pairs={{0,1},{1,0},{64,65},{65,64},{128,129},{129,128},{192,193},{193,192... | collective-permute-start | bytes 884744 | tf_op jit(solution)/shard_map/ppermute | solution.py:48
  82.7 10.4 %collective-permute-start.13 = (bf16[128,1152]{1,0:T(8,128)(2,1)}, bf16[128,1152]{1,0:T(8,128)(2,1)S(1)}, u32[]{:S(2)}, u32[]{:S(2)}) collective-permute-start(bf16[128,1152]{1,0:T(8,128)(2,1)} %copy-done.7), channel_id=1, source_target_pairs={{0,64},{1,65},{64,0},{65,1},{128,192},{129,193},{192,128},{193,129... | collective-permute-start | bytes 884744 | tf_op jit(solution)/shard_map/ppermute | solution.py:48
  84.6 15.2 %collective-permute-start.14 = (bf16[128,1152]{1,0:T(8,128)(2,1)}, bf16[128,1152]{1,0:T(8,128)(2,1)S(1)}, u32[]{:S(2)}, u32[]{:S(2)}) collective-permute-start(bf16[128,1152]{1,0:T(8,128)(2,1)} %copy-done.6), channel_id=1, source_target_pairs={{0,65},{1,64},{64,1},{65,0},{128,193},{129,192},{192,129},{193,128... | collective-permute-start | bytes 884744 | tf_op jit(solution)/shard_map/ppermute | solution.py:48
  105.4 19.3 %collective-permute-start.15 = (bf16[128,896]{1,0:T(8,128)(2,1)S(1)}, bf16[128,896]{1,0:T(8,128)(2,1)S(1)}, u32[]{:S(2)}, u32[]{:S(2)}) collective-permute-start(bf16[128,896]{1,0:T(8,128)(2,1)S(1)} %get-tuple-element.54), channel_id=1, source_target_pairs={{0,1},{1,0},{64,65},{65,64},{128,129},{129,128},{192,193},{193,192... | collective-permute-start | bytes 688136 | tf_op jit(solution)/shard_map/ppermute | solution.py:48
  107.3 17.4 %collective-permute-start.16 = (bf16[128,896]{1,0:T(8,128)(2,1)S(1)}, bf16[128,896]{1,0:T(8,128)(2,1)S(1)}, u32[]{:S(2)}, u32[]{:S(2)}) collective-permute-start(bf16[128,896]{1,0:T(8,128)(2,1)S(1)} %get-tuple-element.55), channel_id=1, source_target_pairs={{0,64},{1,65},{64,0},{65,1},{128,192},{129,193},{192,128},{193,129... | collective-permute-start | bytes 688136 | tf_op jit(solution)/shard_map/ppermute | solution.py:48
  109.5 15.2 %collective-permute-start.17 = (bf16[128,896]{1,0:T(8,128)(2,1)S(1)}, bf16[128,896]{1,0:T(8,128)(2,1)S(1)}, u32[]{:S(2)}, u32[]{:S(2)}) collective-permute-start(bf16[128,896]{1,0:T(8,128)(2,1)S(1)} %get-tuple-element.56), channel_id=1, source_target_pairs={{0,65},{1,64},{64,1},{65,0},{128,193},{129,192},{192,129},{193,128... | collective-permute-start | bytes 688136 | tf_op jit(solution)/shard_map/ppermute | solution.py:48
  114.1 22.3 %all-to-all-start.1 = ((bf16[16,4,768]{2,1,0:T(4,128)(2,1)}), bf16[16,4,768]{2,1,0:T(4,128)(2,1)S(1)}, u32[]{:S(2)}, u32[]{:S(2)}) async-start(bf16[16,4,768]{2,1,0:T(4,128)(2,1)} %broadcast_in_dim.30), calls=%async_computation.1 | async-start | bytes 196608 | tf_op jit(solution)/shard_map/all_to_all | solution.py:399
  124.7 11.7 %copy-start.9 = (f32[4,768]{1,0:T(4,128)S(1)}, f32[4,768]{1,0:T(4,128)}, u32[]{:S(2)}) copy-start(f32[4,768]{1,0:T(4,128)} %param.11) | copy-start | bytes 36868

commit v6 on v0

v6 whole, which is shorter than its diff:
```python
import functools
import math

import jax
import jax.numpy as jnp
from jax import lax
from jax.experimental import pallas as pl
from jax.experimental.pallas import tpu as pltpu
from jax.sharding import PartitionSpec as P

HEAD = 128
GROUP = 64
AXES = ("dp", "tensor")
SPLIT_Y = 2
CHUNK = 512
VMEM = 56 * 1024 * 1024
PARAMS = pltpu.CompilerParams(vmem_limit_bytes=VMEM)
SMEM_SPEC = pl.BlockSpec(memory_space=pltpu.SMEM)
VMEM_SPEC = pl.BlockSpec(memory_space=pltpu.VMEM)
ANY_SPEC = pl.BlockSpec(memory_space=pl.ANY)


def swap(value):
    count = lax.axis_size("dp")
    pairs = [(dp, (dp // SPLIT_Y ^ 1) * SPLIT_Y + dp % SPLIT_Y) for dp in range(count)]
    return lax.ppermute(value, "dp", pairs)


def token_positions(lengths, indices):
    count = lengths.shape[0]
    order = jnp.arange(count, dtype=jnp.int32)
    ends = jnp.sum(jnp.where(order[:, None] <= order[None, :], lengths[:, None], 0), axis=0)
    starts = jnp.where(ends[None, :] <= indices[:, None], ends[None, :], 0)
    return indices - jnp.max(starts, axis=1)


def rope_back(cotangent, positions):
    count = cotangent.shape[0]
    split = cotangent.astype(jnp.float32).reshape(count, -1, HEAD)
    middle = HEAD // 2
    freqs = jnp.exp(jnp.arange(middle, dtype=jnp.float32) * (-2.0 * math.log(10000.0) / HEAD))
    angles = positions.astype(jnp.float32)[:, None] * freqs[None, :]
    cosine = jnp.cos(angles)[:, None, :]
    sine = jnp.sin(angles)[:, None, :]
    first = split[..., :middle]
    second = split[..., middle:]
    lower = first * cosine + second * sine
    upper = second * cosine - first * sine
    return jnp.concatenate([lower, upper], axis=-1).reshape(count, -1).astype(jnp.bfloat16)


def dequant(codes, zeros, steps):
    groups, cols = zeros.shape
    levels = (codes.reshape(groups, GROUP, cols) - zeros[:, None, :]).astype(jnp.float32)
    return (steps[:, None, :] * levels).astype(jnp.bfloat16).reshape(codes.shape)


def columns_of(plane, unit, rows):
    return pl.ds(pl.multiple_of(unit * 2 * rows + plane * rows, rows), rows)


def pack_kernel(rows, plane_ref, feats_ref, rot_ref, mine_ref, other_ref):
    plane = plane_ref[0]
    width = mine_ref.shape[1]
    for unit in range(width // rows):
        block = pl.ds(unit * rows, rows)
        mine_ref[:, block] = feats_ref[:, columns_of(plane, unit, rows)]
        other_ref[:, block] = feats_ref[:, columns_of(1 - plane, unit, rows)]
    other_ref[:, width:] = rot_ref[...]


def pack(plane, feats, rot, rows):
    tokens, width = feats.shape
    cols = rot.shape[1]
    return pl.pallas_call(
        functools.partial(pack_kernel, rows),
        out_shape=(
            jax.ShapeDtypeStruct((tokens, width // 2), feats.dtype),
            jax.ShapeDtypeStruct((tokens, width // 2 + cols), feats.dtype),
        ),
        in_specs=[SMEM_SPEC, VMEM_SPEC, VMEM_SPEC],
        out_specs=(VMEM_SPEC, VMEM_SPEC),
        cost_estimate=pl.CostEstimate(
            flops=0, bytes_accessed=4 * feats.size, transcendentals=0
        ),
        compiler_params=PARAMS,
        name="pack",
    )(plane, feats, rot)


def load(weight_ref, held, sems):
    copies = []
    for at in range(0, held.shape[0], CHUNK):
        rows = pl.ds(at, CHUNK)
        copy = pltpu.make_async_copy(weight_ref.at[rows], held.at[rows], sems.at[at // CHUNK])
        copy.start()
        copies.append((rows, copy))
    return copies


def sums_kernel(mine_ref, rot_ref, other_ref, weight_ref, sums_ref, held, sems):
    width, cols = held.shape
    rot = jnp.concatenate([rot_ref[...], other_ref[:, width:]], axis=0)
    units, groups = sums_ref.shape[:2]
    per_chunk = CHUNK // (groups * GROUP)
    for rows, copy in load(weight_ref, held, sems):
        copy.wait()
        feats = jnp.concatenate([mine_ref[:, rows], other_ref[:, rows]], axis=0)
        weight_grad = lax.dot_general(
            feats, rot, (((0,), (0,)), ((), ())), preferred_element_type=jnp.float32
        )
        product = weight_grad * held[rows, :].astype(jnp.float32)
        sums = product.reshape(per_chunk, groups, GROUP, cols).sum(axis=2)
        first = rows.start // (groups * GROUP)
        sums_ref[first : first + per_chunk] = sums.astype(sums_ref.dtype)


def group_sums(mine, rot, other, weight, rows):
    tokens, cols = rot.shape
    width = weight.shape[0]
    return pl.pallas_call(
        sums_kernel,
        out_shape=jax.ShapeDtypeStruct((width // rows, rows // GROUP, cols), jnp.bfloat16),
        in_specs=[VMEM_SPEC] * 3 + [ANY_SPEC],
        out_specs=VMEM_SPEC,
        scratch_shapes=[
            pltpu.VMEM(weight.shape, weight.dtype),
            pltpu.SemaphoreType.DMA((width // CHUNK,)),
        ],
        cost_estimate=pl.CostEstimate(
            flops=4 * width * cols * tokens, bytes_accessed=weight.size * 2, transcendentals=0
        ),
        compiler_params=PARAMS,
        name="group_sums",
    )(mine, rot, other, weight)


def grads_kernel(rot_ref, other_ref, weight_ref, mine_ref, sent_ref, held, sems):
    width = held.shape[0]
    tokens = rot_ref.shape[0]
    rot = jnp.concatenate([rot_ref[...], other_ref[:, width:]], axis=0)
    for rows, copy in load(weight_ref, held, sems):
        copy.wait()
        grad = lax.dot_general(
            rot, held[rows, :], (((1,), (1,)), ((), ())), preferred_element_type=jnp.float32
        ).astype(jnp.bfloat16)
        mine_ref[:, rows] = grad[:tokens]
        sent_ref[:, rows] = grad[tokens:]


def grads(rot, other, weight):
    tokens, cols = rot.shape
    width = weight.shape[0]
    part = jax.ShapeDtypeStruct((tokens, width), jnp.bfloat16)
    return pl.pallas_call(
        grads_kernel,
        out_shape=(part, part),
        in_specs=[VMEM_SPEC] * 2 + [ANY_SPEC],
        out_specs=(VMEM_SPEC, VMEM_SPEC),
        scratch_shapes=[
            pltpu.VMEM(weight.shape, weight.dtype),
            pltpu.SemaphoreType.DMA((width // CHUNK,)),
        ],
        cost_estimate=pl.CostEstimate(
            flops=4 * width * cols * tokens, bytes_accessed=weight.size * 2, transcendentals=0
        ),
        compiler_params=PARAMS,
        name="grads",
    )(rot, other, weight)


def merge_kernel(rows, plane_ref, mine_ref, other_ref, grad_ref):
    plane = plane_ref[0]
    for unit in range(mine_ref.shape[1] // rows):
        block = pl.ds(unit * rows, rows)
        grad_ref[:, columns_of(plane, unit, rows)] = mine_ref[:, block]
        grad_ref[:, columns_of(1 - plane, unit, rows)] = other_ref[:, block]


def merge(plane, mine, other, rows):
    tokens, width = mine.shape
    return pl.pallas_call(
        functools.partial(merge_kernel, rows),
        out_shape=jax.ShapeDtypeStruct((tokens, 2 * width), mine.dtype),
        in_specs=[SMEM_SPEC, VMEM_SPEC, VMEM_SPEC],
        out_specs=VMEM_SPEC,
        cost_estimate=pl.CostEstimate(
            flops=0, bytes_accessed=8 * mine.size, transcendentals=0
        ),
        compiler_params=PARAMS,
        name="merge",
    )(plane, mine, other)


def per_device(activations, key_cotangent, doc_lengths, weight_codes, zero_points, step_sizes):
    tokens = activations.shape[0]
    groups, cols = step_sizes.shape
    rows = weight_codes.shape[0] // 2
    devices, copies = lax.axis_size("tensor"), lax.axis_size("dp")
    plane = (lax.axis_index("dp") // SPLIT_Y) % 2
    plane_at = plane.astype(jnp.int32).reshape(1)

    def plane_half(value):
        count = value.shape[0] // 2
        return lax.dynamic_slice_in_dim(value, plane * count, count, axis=0)

    weight = dequant(plane_half(weight_codes), plane_half(zero_points), plane_half(step_sizes))
    weight = lax.all_gather(weight, "tensor", axis=0, tiled=True)

    indices = lax.axis_index("tensor") * tokens + jnp.arange(tokens, dtype=jnp.int32)
    rot = rope_back(key_cotangent, token_positions(doc_lengths[0], indices))
    feats, to_other = pack(plane_at, activations, rot, rows)
    other = swap(to_other)

    sums = group_sums(feats, rot, other, weight, rows)
    shares = lax.all_to_all(sums, "tensor", split_axis=0, concat_axis=0, tiled=True)
    mine, sent = grads(rot, other, weight)
    got = swap(sent)
    share = jnp.sum(shares.astype(jnp.float32), axis=0).astype(jnp.bfloat16)
    totals = lax.all_to_all(
        jnp.broadcast_to(share[None], (copies, *share.shape)),
        "dp",
        split_axis=0,
        concat_axis=0,
        tiled=True,
    )
    totals = totals.astype(jnp.float32).reshape(-1, 2, SPLIT_Y, groups // 2, cols)
    total = jnp.sum(totals, axis=(0, 2)).reshape(groups, cols)
    step_grad = total / (tokens * devices * step_sizes)
    return (merge(plane_at, mine, got, rows), step_grad)


def solution(mesh):
    in_specs = (
        P(("dp", "tensor"), None),
        P(("dp", "tensor"), None),
        P("dp", None),
        P("tensor", None),
        P("tensor", None),
        P("tensor", None),
    )
    out_specs = (P(("dp", "tensor"), None), P("tensor", None))
    return jax.shard_map(
        per_device, mesh=mesh, in_specs=in_specs, out_specs=out_specs, check_vma=False
    )
```

time: 246 us -> 151 us (0.61)
  the two profiles are of different devices: /device:TPU:8 before, /device:TPU:1 now
where the time goes in v6:
time: 151 us; the launch traced here: 150 us
  waiting for transfers between devices  63.5 us (42%)
  blocking collectives  34.8 us (23%)
  Pallas kernels  21.6 us (14%)
  between operations  14.2 us (9%)
  starting transfers between devices  8.13 us (5%)
  local copies, waits for them, and re-layouts  4.3 us (3%)
  other arithmetic  3.64 us (2%)
    all_gather x1, waiting for transfers between devices, per_device(): weight = lax.all_gather(weight, 'tensor', axis=0, tiled=True)  40.2 us
    ppermute x2, waiting for transfers between devices, swap(): return lax.ppermute(value, 'dp', pairs)  23.3 us
    all_to_all x1, blocking collectives, per_device(): lax.all_to_all(jnp.broadcast_to(share[None], (copies, *share.shape)), 'dp...  21.1 us
    all_to_all x1, blocking collectives, per_device(): lax.all_to_all(sums, 'tensor', split_axis=0, concat_axis=0, tiled=True)  13.7 us
    ppermute x2, starting transfers between devices, swap(): return lax.ppermute(value, 'dp', pairs)  8.09 us
    pallas_call x1, Pallas kernels, group_sums(): pl.pallas_call(sums_kernel, out_shape=jax.ShapeDtypeStruct((width // rows...  7.51 us
    pallas_call x1, Pallas kernels, grads(): pl.pallas_call(grads_kernel, out_shape=(part, part), in_specs=[VMEM_SPEC]...  7.19 us
    pallas_call x1, Pallas kernels, pack(): pl.pallas_call(functools.partial(pack_kernel, rows), out_shape=(jax.Shape...  3.54 us
  transfers between devices with their start and end apart: 3, of which 2 were waited for; matrix products, arithmetic and copies ran while one was open for 3% of the time, Pallas kernels for 7%

profile of v6, /device:TPU:1, one launch (start us, length us, event | category | flops | bytes accessed | tf_op | source)
XLA Modules:
  0.0 150.1 jit_solution(15017825215356950569)
XLA Ops:
  7.2 0.0 copy-start
  7.2 0.0 all-gather.2.cloned.1.call-start
  7.3 0.6 copy-done
  7.9 0.7 constant_dynamic-slice_fusion
  8.6 1.7 %fusion.2 = bf16[128,768]{1,0:T(8,128)(2,1)} fusion(s32[256,768]{1,0:T(8,128)} %param.9, s32[]{:T(128)S(6)} %select_n.31, s32[2,768]{1,0:T(2,128)S(1)} %constant_dynamic-slice_fusion.1, f32[2,768]{1,0:T(2,128)S(1)} %constant_dynamic-slice_fusion), kind=kLoop, calls=%fused_computation.3 | loop fusion | flops 393216 | bytes 602116 | tf_op jit(solution)/shard_map/convert_element_type | solution.py:55
  10.3 0.0 all-gather.2.cloned.1.call-update
  10.4 1.1 copy.16
  11.5 0.7 select_reduce_fusion.1
  12.2 0.1 select_reduce_fusion
  12.3 0.2 multiply_cosine_fusion
  12.5 0.1 add_convert_fusion
  12.6 0.8 copy.18.rot_ref
  13.5 3.5 %pack.1 = (bf16[128,4096]{1,0:T(8,128)(2,1)}, bf16[128,4864]{1,0:T(8,128)(2,1)}) custom-call(s32[1]{0:T(128)} %bitcast.plane_ref, bf16[128,8192]{1,0:T(8,128)(2,1)} %feats_ref.1, bf16[128,768]{1,0:T(8,128)(2,1)} %copy.18.rot_ref), custom_call_target="tpu_custom_call" | custom-call | bytes 4194304 | tf_op jit(solution)/shard_map/pack/pallas_call | solution.py:75
  17.0 4.8 %collective-permute-start = (bf16[128,4864]{1,0:T(8,128)(2,1)}, bf16[128,4864]{1,0:T(8,128)(2,1)S(1)}, u32[]{:S(2)}, u32[]{:S(2)}) collective-permute-start(bf16[128,4864]{1,0:T(8,128)(2,1)} %get-tuple-element.6), channel_id=1, source_target_pairs={{0,64},{32,96},{64,0},{96,32},{128,192},{160,224},{192,128},{224,1... | collective-permute-start | bytes 3735560 | tf_op jit(solution)/shard_map/ppermute | solution.py:26
  21.8 23.3 %collective-permute-done.other_ref = bf16[128,4864]{1,0:T(8,128)(2,1)S(1)} collective-permute-done((bf16[128,4864]{1,0:T(8,128)(2,1)}, bf16[128,4864]{1,0:T(8,128)(2,1)S(1)}, u32[]{:S(2)}, u32[]{:S(2)}) %collective-permute-start) | collective-permute-done | bytes 1245216 | tf_op jit(solution)/shard_map/ppermute | solution.py:26
  45.1 0.0 copy-start.1
  45.1 40.2 %all-gather.2.cloned.1.call-done.weight_ref = bf16[4096,768]{1,0:T(8,128)(2,1)} async-done(((bf16[128,768]{1,0:T(8,128)(2,1)}), bf16[4096,768]{1,0:T(8,128)(2,1)}) %all-gather.2.cloned.1.call-update) | async-done | bytes 6291472 | tf_op jit(solution)/shard_map/all_gather | solution.py:208
  85.3 0.0 copy-done.1
  85.3 7.2 %grads.1 = (bf16[128,4096]{1,0:T(8,128)(2,1)}, bf16[128,4096]{1,0:T(8,128)(2,1)}) custom-call(bf16[128,768]{1,0:T(8,128)(2,1)} %copy.18.rot_ref, bf16[128,4864]{1,0:T(8,128)(2,1)} %copy-done.1, bf16[4096,768]{1,0:T(8,128)(2,1)} %all-gather.2.cloned.1.call-done.weight_ref), custom_call_target="tpu_custom_call" | custom-call | flops 1610612736 | bytes 6291456 | tf_op jit(solution)/shard_map/grads/pallas_call | solution.py:155
  92.5 3.3 %collective-permute-start.1 = (bf16[128,4096]{1,0:T(8,128)(2,1)}, bf16[128,4096]{1,0:T(8,128)(2,1)S(1)}, u32[]{:S(2)}, u32[]{:S(2)}) collective-permute-start(bf16[128,4096]{1,0:T(8,128)(2,1)} %get-tuple-element.8), channel_id=1, source_target_pairs={{0,64},{32,96},{64,0},{96,32},{128,192},{160,224},{192,128},{224,1... | collective-permute-start | bytes 3145736 | tf_op jit(solution)/shard_map/ppermute | solution.py:26
  95.8 0.0 copy-start.3
  95.8 7.5 %group_sums.1 = bf16[32,2,768]{2,1,0:T(2,128)(2,1)} custom-call(bf16[128,4096]{1,0:T(8,128)(2,1)} %get-tuple-element.9.mine_ref, bf16[128,768]{1,0:T(8,128)(2,1)} %copy.18.rot_ref, bf16[128,4864]{1,0:T(8,128)(2,1)} %copy-done.1, bf16[4096,768]{1,0:T(8,128)(2,1)} %all-gather.2.cloned.1.call-done.weight_ref), custom_call_target="tpu_custom_call" | custom-call | flops 1610612736 | bytes 6291456 | tf_op jit(solution)/shard_map/group_sums/pallas_call | solution.py:121
  103.3 13.7 %all_to_all.10 = bf16[32,2,768]{2,1,0:T(2,128)(2,1)S(1)} all-to-all(bf16[32,2,768]{2,1,0:T(2,128)(2,1)} %group_sums.1), channel_id=1, replica_groups=mesh['dp'=16,'tensor'=32] {'tensor'}, dimensions={0} | all-to-all | bytes 196608 | tf_op jit(solution)/shard_map/all_to_all | solution.py:216
  117.0 0.1 reduce_sum.31
  117.1 21.1 %all_to_all.11 = bf16[16,2,768]{2,1,0:T(2,128)(2,1)S(1)} all-to-all(bf16[16,2,768]{2,1,0:T(2,128)(2,1)S(1)} %broadcast_in_dim.30), channel_id=1, replica_groups=mesh['dp'=16,'tensor'=32] {'dp'}, dimensions={0} | all-to-all | bytes 98304 | tf_op jit(solution)/shard_map/all_to_all | solution.py:220
  138.2 0.1 convert_reduce_fusion
  138.3 0.0 copy-done.3
  138.3 0.6 multiply_divide_fusion
  138.9 0.0 collective-permute-done.1.other_ref
  138.9 0.0 copy-start.2
  138.9 1.0 copy-done.2
  139.9 3.3 %merge.1 = bf16[128,8192]{1,0:T(8,128)(2,1)} custom-call(s32[1]{0:T(128)} %bitcast.plane_ref, bf16[128,4096]{1,0:T(8,128)(2,1)} %get-tuple-element.7.mine_ref, bf16[128,4096]{1,0:T(8,128)(2,1)} %copy-done.2), custom_call_target="tpu_custom_call" | custom-call | bytes 4194304 | tf_op jit(solution)/shard_map/merge/pallas_call | solution.py:182
  (8 shorter events, 0.1 us)
Async XLA Ops:
  7.2 0.7 copy-start
  7.2 78.1 %all-gather.2.cloned.1.call-start = ((), (), s32[]{:S(2)}) async-start(), calls=%async_computation.2 | async-start | bytes 6488064 | tf_op jit(solution)/shard_map/all_gather | solution.py:208
  17.0 28.1 %collective-permute-start = (bf16[128,4864]{1,0:T(8,128)(2,1)}, bf16[128,4864]{1,0:T(8,128)(2,1)S(1)}, u32[]{:S(2)}, u32[]{:S(2)}) collective-permute-start(bf16[128,4864]{1,0:T(8,128)(2,1)} %get-tuple-element.6), channel_id=1, source_target_pairs={{0,64},{32,96},{64,0},{96,32},{128,192},{160,224},{192,128},{224,1... | collective-permute-start | bytes 3735560 | tf_op jit(solution)/shard_map/ppermute | solution.py:26
  45.1 40.2 %copy-start.1 = (bf16[128,4864]{1,0:T(8,128)(2,1)}, bf16[128,4864]{1,0:T(8,128)(2,1)S(1)}, u32[]{:S(2)}) copy-start(bf16[128,4864]{1,0:T(8,128)(2,1)S(1)} %collective-permute-done.other_ref) | copy-start | bytes 3735556
  92.5 46.4 %collective-permute-start.1 = (bf16[128,4096]{1,0:T(8,128)(2,1)}, bf16[128,4096]{1,0:T(8,128)(2,1)S(1)}, u32[]{:S(2)}, u32[]{:S(2)}) collective-permute-start(bf16[128,4096]{1,0:T(8,128)(2,1)} %get-tuple-element.8), channel_id=1, source_target_pairs={{0,64},{32,96},{64,0},{96,32},{128,192},{160,224},{192,128},{224,1... | collective-permute-start | bytes 3145736 | tf_op jit(solution)/shard_map/ppermute | solution.py:26
  95.8 42.5 %copy-start.3 = (f32[4,768]{1,0:T(4,128)S(1)}, f32[4,768]{1,0:T(4,128)}, u32[]{:S(2)}) copy-start(f32[4,768]{1,0:T(4,128)} %param.11) | copy-start | bytes 36868
  138.9 1.0 copy-start.2
Sparse Core Ops, SparseCore 0:
  10.5 74.7 all-gather.1

commit v7 on v4

--- a/solution.py
+++ b/solution.py
@@ -76,45 +76,44 @@
     return pl.ds(pl.multiple_of(table[unit] * rows, rows), rows)
 
 
-class Units:
-    def __init__(self, rows, table, weights, held, sems, first=0):
-        self.rows, self.table, self.held, self.first = rows, table, held, first
-        self.copies = []
-        for ref in weights:
-            for at in range(0, ref.shape[0], rows):
-                unit = len(self.copies)
-                copy = pltpu.make_async_copy(
-                    ref.at[pl.ds(at, rows)], held.at[pl.ds(unit * rows, rows)], sems.at[unit]
-                )
-                copy.start()
-                self.copies.append(copy)
-        self.count = len(self.copies)
-
-    def weight(self, unit):
-        self.copies[unit].wait()
-        return self.held[pl.ds(unit * self.rows, self.rows), :]
-
-    def group_sums(self, unit, weight, rot, mine, other):
-        block = pl.ds((self.first + unit) * self.rows, self.rows)
-        feats = jnp.concatenate([mine[:, block], other[:, block]], axis=0)
-        weight_grad = lax.dot_general(
-            feats, rot, (((0,), (0,)), ((), ())), preferred_element_type=jnp.float32
-        )
-        product = weight_grad * weight.astype(jnp.float32)
-        return product.reshape(self.rows // GROUP, GROUP, rot.shape[1]).sum(axis=1)
-
-    def put_grad(self, unit, weight, rot, own, sent_ref, grad_ref, sems):
-        tokens = own.shape[0]
+def load(weights, held, sems):
+    copies, at = [], 0
+    for unit, ref in enumerate(weights):
+        rows = pl.ds(at, ref.shape[0])
+        copies.append(pltpu.make_async_copy(ref, held.at[rows], sems.at[unit]))
+        at += ref.shape[0]
+    for copy in copies:
+        copy.start()
+    for copy in copies:
+        copy.wait()
+
+
+def group_sums(feats, weight, rot):
+    weight_grad = lax.dot_general(
+        feats, rot, (((0,), (0,)), ((), ())), preferred_element_type=jnp.float32
+    )
+    product = weight_grad * weight.astype(jnp.float32)
+    rows, cols = weight.shape
+    return product.reshape(rows // GROUP, GROUP, cols).sum(axis=1)
+
+
+def put_grads(table, first, rows, held, rot, own, sent_ref, grad_ref, sems):
+    tokens, width = own.shape
+    copies = []
+    for unit in range(width // rows):
+        block = pl.ds(unit * rows, rows)
         grad = lax.dot_general(
-            rot, weight, (((1,), (1,)), ((), ())), preferred_element_type=jnp.float32
+            rot, held[block, :], (((1,), (1,)), ((), ())), preferred_element_type=jnp.float32
         ).astype(jnp.bfloat16)
-        block = pl.ds(unit * self.rows, self.rows)
         own[:, block] = grad[:tokens]
         sent_ref[:, block] = grad[tokens:]
-        columns = columns_of(self.table, self.first + unit, self.rows)
-        copy = pltpu.make_async_copy(own.at[:, block], grad_ref.at[:, columns], sems.at[unit])
+        columns = columns_of(table, first + unit, rows)
+        copies.append(
+            pltpu.make_async_copy(own.at[:, block], grad_ref.at[:, columns], sems.at[unit])
+        )
+    for copy in copies:
         copy.start()
-        return copy
+    return copies
 
 
 def pack_kernel(rows, table, theirs, feats_ref, mine_ref, sent_ref):
@@ -127,38 +126,36 @@
 def near_kernel(rows, count, table, rot_ref, mine_ref, other_ref, *refs):
     weights, refs = refs[:count], refs[count:]
     grad_ref, sent_ref, sums_ref, held, own, held_sems, own_sems = refs
-    units = Units(rows, table, weights, held, held_sems)
+    load(weights, held, held_sems)
     rot = rot_ref[...]
-    copies = []
-    for unit in range(units.count):
-        weight = units.weight(unit)
-        copies.append(units.put_grad(unit, weight, rot, own, sent_ref, grad_ref, own_sems))
-        sums_ref[unit] = units.group_sums(unit, weight, rot, mine_ref, other_ref)
+    copies = put_grads(table, 0, rows, held, rot, own, sent_ref, grad_ref, own_sems)
+    for unit in range(sums_ref.shape[0]):
+        block = pl.ds(unit * rows, rows)
+        feats = jnp.concatenate([mine_ref[:, block], other_ref[:, block]], axis=0)
+        sums_ref[unit] = group_sums(feats, held[block, :], rot)
     for copy in copies:
         copy.wait()
 
 
 def far_sums_kernel(rows, count, near, table, rot_ref, near_ref, mine_ref, other_ref, *refs):
     weights, (all_ref, held, held_sems) = refs[:count], refs[count:]
-    units = Units(rows, table, weights, held, held_sems, near)
+    load(weights, held, held_sems)
+    rot = rot_ref[...]
+    sums = [near_ref[unit] for unit in range(near)]
+    for unit in range(held.shape[0] // rows):
+        block = pl.ds((near + unit) * rows, rows)
+        feats = jnp.concatenate([mine_ref[:, block], other_ref[:, block]], axis=0)
+        sums.append(group_sums(feats, held[pl.ds(unit * rows, rows), :], rot))
     all_ref[...] = jnp.zeros_like(all_ref)
-    for unit in range(near):
-        all_ref[table[unit]] = near_ref[unit].astype(all_ref.dtype)
-    rot = rot_ref[...]
-    for unit in range(units.count):
-        sums = units.group_sums(unit, units.weight(unit), rot, mine_ref, other_ref)
-        all_ref[table[near + unit]] = sums.astype(all_ref.dtype)
+    for unit, of_unit in enumerate(sums):
+        all_ref[table[unit]] = of_unit.astype(all_ref.dtype)
 
 
 def far_grad_kernel(rows, count, near, table, rot_ref, *refs):
     weights, refs = refs[:count], refs[count:]
     _, grad_ref, sent_ref, held, own, held_sems, own_sems = refs
-    units = Units(rows, table, weights, held, held_sems, near)
-    rot = rot_ref[...]
-    copies = [
-        units.put_grad(unit, units.weight(unit), rot, own, sent_ref, grad_ref, own_sems)
-        for unit in range(units.count)
-    ]
+    load(weights, held, held_sems)
+    copies = put_grads(table, near, rows, held, rot_ref[...], own, sent_ref, grad_ref, own_sems)
     for copy in copies:
         copy.wait()
 
@@ -335,26 +332,28 @@
 
     from_xy = send(from_y, 1, 0)
     from_yx = send(from_x, 0, 1, cross=True)
-    far_xx = send(my_half(from_x), 1, 0)
-    far_yy = send(my_half(from_y), 0, 1)
-    from_xy, from_yx, _, _ = lax.optimization_barrier((from_xy, from_yx, far_xx, far_yy))
+    half_x, half_y = my_half(from_x), my_half(from_y)
+    from_xy, _, _ = lax.optimization_barrier((from_xy, half_x, half_y))
 
     far_x = send(from_xy, 1, 0)
     far_y = send(from_yx, 0, 1)
-    far = send(my_half(from_xy), 1, 1)
+    half_xy = my_half(from_xy)
+    far = send(half_xy, 1, 1)
+    half_x, half_y, _ = lax.optimization_barrier((half_x, half_y, half_xy))
+    far_xx = send(half_x, 1, 0)
+    far_yy = send(half_y, 0, 1)
 
     near = [weight, from_x, from_y, from_xy, from_yx]
     grad, sent_near, sums_near = near_shards(table, *feats, rot, near, rows, activations.shape[1])
-    got_near = swap(sent_near)
-    grad = place(theirs, got_near, grad, rows, 0)
-
     fars = [far_xx, far_yy, far_x, far_y, far]
     at_hand = sums_near.shape[0]
     sums = far_sums(table, *feats, rot, fars, sums_near, rows, devices)
     shares = lax.all_to_all(sums, "tensor", split_axis=0, concat_axis=0, tiled=True)
 
     grad, sent_far = far_grad(table, rot, fars, grad, rows, at_hand)
-    shares, grad, sent_far = lax.optimization_barrier((shares, grad, sent_far))
+    sent_near, _ = lax.optimization_barrier((sent_near, sums))
+    got_near = swap(sent_near)
+    shares, sent_far = lax.optimization_barrier((shares, sent_far))
     share = jnp.sum(shares.astype(jnp.float32), axis=0).astype(jnp.bfloat16)
     copies = lax.axis_size("dp")
     totals = lax.all_to_all(
@@ -364,6 +363,7 @@
         concat_axis=0,
         tiled=True,
     )
+    grad = place(theirs, got_near, grad, rows, 0)
     grad = place(theirs, swap(sent_far), grad, rows, at_hand)
     totals, grad = lax.optimization_barrier((totals, grad))
     seq_tokens = tokens * devices

time: 124 us -> 118 us (0.952)
  waiting for transfers between devices: 22.8 us -> 14.4 us
  Pallas kernels: 23.4 us -> 17.6 us
  local copies, waits for them, and re-layouts: 6.85 us -> 10.4 us
  other arithmetic: 2.57 us -> 5.24 us
  starting transfers between devices: 57.1 us -> 59.1 us
    ppermute x9, waiting for transfers between devices: 10.8 us -> 3.25 us  [send(): return lax.ppermute(value, AXES, permutation(target))]
    unnamed x19 -> x25, local copies, waits for them, and re-layouts: 2.67 us -> 6.55 us
    all_to_all x1, starting transfers between devices: 5.87 us -> 8.3 us  [per_device(): lax.all_to_all(sums, 'tensor', split_axis=0, concat_axis=0, tiled=True)]
    pallas_call x1, Pallas kernels: 5.24 us -> 3 us  [far_grad(): pl.pallas_call(functools.partial(far_grad_kernel, rows, len(weights), nea...]
    pallas_call x1, Pallas kernels: 5.69 us -> 3.65 us  [far_sums(): pl.pallas_call(functools.partial(far_sums_kernel, rows, len(weights), nea...]
    all_to_all x1, waiting for transfers between devices: 10.4 us -> 8.39 us  [per_device(): lax.all_to_all(jnp.broadcast_to(share[None], (copies, *share.shape)), 'dp...]
    ppermute x4, starting transfers between devices: 9.66 us -> 11.6 us  [swap(): lax.ppermute(value, AXES, permutation(lambda x, y, z, core: (x, y, z, cor...]
    pallas_call x1, Pallas kernels: 7.27 us -> 5.85 us  [near_shards(): pl.pallas_call(functools.partial(near_kernel, rows, len(weights)), out_sh...]
  transfers between devices with their start and end apart: 15 -> 15, of which waited for: 7 -> 5; matrix products, arithmetic and copies ran while one was open for 4% -> 7% of each run, Pallas kernels for 19% -> 12%
where the time goes in v7:
time: 118 us; the launch traced here: 117 us
  starting transfers between devices  59.1 us (50%)
  Pallas kernels  17.6 us (15%)
  waiting for transfers between devices  14.4 us (12%)
  local copies, waits for them, and re-layouts  10.4 us (9%)
  blocking collectives  9.14 us (8%)
  other arithmetic  5.24 us (4%)
  between operations  1.27 us (1%)
    ppermute x9, starting transfers between devices, send(): return lax.ppermute(value, AXES, permutation(target))  27.7 us
    ppermute x4, starting transfers between devices, swap(): lax.ppermute(value, AXES, permutation(lambda x, y, z, core: (x, y, z, cor...  11.6 us
    all_to_all x1, starting transfers between devices, per_device(): lax.all_to_all(jnp.broadcast_to(share[None], (copies, *share.shape)), 'dp...  11.5 us
    all_gather x1, blocking collectives, per_device(): lax.all_gather(weight, 'tensor', axis=0, tiled=True, axis_index_groups=pa...  9.14 us
    all_to_all x1, waiting for transfers between devices, per_device(): lax.all_to_all(jnp.broadcast_to(share[None], (copies, *share.shape)), 'dp...  8.39 us
    all_to_all x1, starting transfers between devices, per_device(): lax.all_to_all(sums, 'tensor', split_axis=0, concat_axis=0, tiled=True)  8.3 us
    unnamed x25, local copies, waits for them, and re-layouts  6.55 us
    pallas_call x1, Pallas kernels, near_shards(): pl.pallas_call(functools.partial(near_kernel, rows, len(weights)), out_sh...  5.85 us
  transfers between devices with their start and end apart: 15, of which 5 were waited for; matrix products, arithmetic and copies ran while one was open for 7% of the time, Pallas kernels for 12%

profile of v7, /device:TPU:1, one launch (start us, length us, event | category | flops | bytes accessed | tf_op | source)
XLA Modules:
  0.0 117.1 jit_solution(13031712594057490674)
XLA Ops:
  0.6 1.2 %fusion.2.refs_0_ = bf16[256,768]{1,0:T(8,128)(2,1)S(1)} fusion(s32[256,768]{1,0:T(8,128)} %param.9, s32[4,768]{1,0:T(4,128)} %param.10, f32[4,768]{1,0:T(4,128)} %param.11), kind=kLoop, calls=%fused_computation.3 | loop fusion | flops 786432 | bytes 1204224 | tf_op jit(solution)/shard_map/convert_element_type | solution.py:72
  1.9 9.1 %all_gather.3 = bf16[512,768]{1,0:T(8,128)(2,1)} all-gather(bf16[256,768]{1,0:T(8,128)(2,1)S(1)} %fusion.2.refs_0_), channel_id=1, replica_groups={{0,1},{2,3},{4,5},{6,7},{8,9},{10,11},{12,13},{14,15},{16,17},{18,19},{..., dimensions={0}, use_global_device_ids=true | all-gather | bytes 1179648 | tf_op jit(solution)/shard_map/all_gather | solution.py:318
  11.0 1.9 %collective-permute-start = (bf16[512,768]{1,0:T(8,128)(2,1)}, bf16[512,768]{1,0:T(8,128)(2,1)S(1)}, u32[]{:S(2)}, u32[]{:S(2)}) collective-permute-start(bf16[512,768]{1,0:T(8,128)(2,1)} %all_gather.3), channel_id=1, source_target_pairs={{0,2},{1,7},{64,66},{65,71},{128,130},{129,135},{192,194},{193,199... | collective-permute-start | bytes 2359304 | tf_op jit(solution)/shard_map/ppermute | solution.py:39
  13.0 2.2 %collective-permute-start.1 = (bf16[512,768]{1,0:T(8,128)(2,1)}, bf16[512,768]{1,0:T(8,128)(2,1)}, u32[]{:S(2)}, u32[]{:S(2)}) collective-permute-start(bf16[512,768]{1,0:T(8,128)(2,1)} %all_gather.3), channel_id=1, source_target_pairs={{0,8},{1,57},{64,72},{65,121},{128,136},{129,185},{192,200},{193,2... | collective-permute-start | bytes 2359304 | tf_op jit(solution)/shard_map/ppermute | solution.py:39
  15.2 1.1 copy.17
  16.3 0.8 convert.10
  17.1 0.1 select_reduce_fusion
  17.2 0.2 multiply_cosine_fusion
  17.4 1.1 add_convert_fusion
  18.6 0.8 copy.19
  19.4 2.1 %collective-permute-start.2 = (bf16[128,768]{1,0:T(8,128)(2,1)}, bf16[128,768]{1,0:T(8,128)(2,1)}, u32[]{:S(2)}, u32[]{:S(2)}) collective-permute-start(bf16[128,768]{1,0:T(8,128)(2,1)} %copy.19), channel_id=1, source_target_pairs={{0,1},{1,0},{64,65},{65,64},{128,129},{129,128},{192,193},{193,192... | collective-permute-start | bytes 589832 | tf_op jit(solution)/shard_map/ppermute | solution.py:43
  21.8 0.1 stack.118.table
  21.9 0.1 stack.135.theirs.table
  22.0 1.8 %pack.1 = (bf16[128,4096]{1,0:T(8,128)(2,1)S(1)}, bf16[128,4096]{1,0:T(8,128)(2,1)}) custom-call(s32[16]{0:T(128)S(1)} %stack.118.table, s32[16]{0:T(128)S(1)} %stack.135.theirs.table, bf16[128,8192]{1,0:T(8,128)(2,1)S(1)} %copy-done), custom_call_target="tpu_custom_call" | custom-call | bytes 6291456 | tf_op jit(solution)/shard_map/pack/pallas_call | solution.py:184
  23.8 1.0 copy-done.3
  24.8 1.0 pad_maximum_fusion.rot_ref
  25.8 0.5 collective-permute-done.1.refs_2_
  26.3 4.3 %collective-permute-start.4 = (bf16[512,768]{1,0:T(8,128)(2,1)}, bf16[512,768]{1,0:T(8,128)(2,1)}, u32[]{:S(2)}, u32[]{:S(2)}) collective-permute-start(bf16[512,768]{1,0:T(8,128)(2,1)} %collective-permute-done.1.refs_2_), channel_id=1, source_target_pairs={{0,2},{1,7},{64,66},{65,71},{128,130},{129,135},{192,194},{193,199... | collective-permute-start | bytes 2359304 | tf_op jit(solution)/shard_map/ppermute | solution.py:39
  30.7 2.2 %collective-permute-start.5 = (bf16[512,768]{1,0:T(8,128)(2,1)S(1)}, bf16[512,768]{1,0:T(8,128)(2,1)}, u32[]{:S(2)}, u32[]{:S(2)}) collective-permute-start(bf16[512,768]{1,0:T(8,128)(2,1)S(1)} %collective-permute-done.refs_1_), channel_id=1, source_target_pairs={{0,57},{1,8},{64,121},{65,72},{128,185},{129,136},{192,249},{193,2... | collective-permute-start | bytes 2359304 | tf_op jit(solution)/shard_map/ppermute | solution.py:39
  32.8 5.0 %collective-permute-start.3 = (bf16[128,4096]{1,0:T(8,128)(2,1)}, bf16[128,4096]{1,0:T(8,128)(2,1)}, u32[]{:S(2)}, u32[]{:S(2)}) collective-permute-start(bf16[128,4096]{1,0:T(8,128)(2,1)} %get-tuple-element.20), channel_id=1, source_target_pairs={{0,1},{1,0},{64,65},{65,64},{128,129},{129,128},{192,193},{193,192... | collective-permute-start | bytes 3145736 | tf_op jit(solution)/shard_map/ppermute | solution.py:43
  37.8 1.1 constant_dynamic-slice_fusion
  39.0 0.9 collective-permute-done.4.refs_3_
  39.9 5.3 %collective-permute-start.8 = (bf16[512,768]{1,0:T(8,128)(2,1)}, bf16[512,768]{1,0:T(8,128)(2,1)S(1)}, u32[]{:S(2)}, u32[]{:S(2)}) collective-permute-start(bf16[512,768]{1,0:T(8,128)(2,1)} %collective-permute-done.4.refs_3_), channel_id=1, source_target_pairs={{0,2},{1,7},{64,66},{65,71},{128,130},{129,135},{192,194},{193,199... | collective-permute-start | bytes 2359304 | tf_op jit(solution)/shard_map/ppermute | solution.py:39
  45.2 4.9 %collective-permute-start.9 = (bf16[512,768]{1,0:T(8,128)(2,1)}, bf16[512,768]{1,0:T(8,128)(2,1)S(1)}, u32[]{:S(2)}, u32[]{:S(2)}) collective-permute-start(bf16[512,768]{1,0:T(8,128)(2,1)} %collective-permute-done.5.refs_4_), channel_id=1, source_target_pairs={{0,8},{1,57},{64,72},{65,121},{128,136},{129,185},{192,200},{193,2... | collective-permute-start | bytes 2359304 | tf_op jit(solution)/shard_map/ppermute | solution.py:39
  50.1 1.0 constant_dynamic-slice_fusion.2
  51.2 1.9 %collective-permute-start.6 = (bf16[256,768]{1,0:T(8,128)(2,1)S(1)}, bf16[256,768]{1,0:T(8,128)(2,1)S(1)}, u32[]{:S(2)}, u32[]{:S(2)}) collective-permute-start(bf16[256,768]{1,0:T(8,128)(2,1)S(1)} %get-tuple-element.27), channel_id=1, source_target_pairs={{0,2},{1,7},{64,66},{65,71},{128,130},{129,135},{192,194},{193,199... | collective-permute-start | bytes 1179656 | tf_op jit(solution)/shard_map/ppermute | solution.py:39
  53.1 1.9 %collective-permute-start.7 = (bf16[256,768]{1,0:T(8,128)(2,1)S(1)}, bf16[256,768]{1,0:T(8,128)(2,1)S(1)}, u32[]{:S(2)}, u32[]{:S(2)}) collective-permute-start(bf16[256,768]{1,0:T(8,128)(2,1)S(1)} %get-tuple-element.28), channel_id=1, source_target_pairs={{0,8},{1,57},{64,72},{65,121},{128,136},{129,185},{192,200},{193,2... | collective-permute-start | bytes 1179656 | tf_op jit(solution)/shard_map/ppermute | solution.py:39
  55.0 3.0 %collective-permute-start.10 = (bf16[256,768]{1,0:T(8,128)(2,1)S(1)}, bf16[256,768]{1,0:T(8,128)(2,1)S(1)}, u32[]{:S(2)}, u32[]{:S(2)}) collective-permute-start(bf16[256,768]{1,0:T(8,128)(2,1)S(1)} %constant_dynamic-slice_fusion.2), channel_id=1, source_target_pairs={{0,10},{1,63},{64,74},{65,127},{128,138},{129,191},{192,202},{193,... | collective-permute-start | bytes 1179656 | tf_op jit(solution)/shard_map/ppermute | solution.py:39
  58.1 1.1 copy-done.6
  59.2 5.8 %near_shards.1 = (bf16[128,8192]{1,0:T(8,128)(2,1)}, bf16[128,2304]{1,0:T(8,128)(2,1)S(1)}, f32[9,4,768]{2,1,0:T(4,128)S(1)}) custom-call(s32[16]{0:T(128)S(1)} %stack.118.table, bf16[256,768]{1,0:T(8,128)(2,1)S(1)} %pad_maximum_fusion.rot_ref, bf16[128,4096]{1,0:T(8,128)(2,1)S(1)} %copy-done.4, bf16[128,4096]{1,0:T(8,128)(2,1)} %collective-permute-done.3.other_ref, ...), custom_call_target="tpu_custom_call" | custom-call | flops 1811939328 | bytes 4718592 | tf_op jit(solution)/shard_map/near_shards/pallas_call | solution.py:201
  65.0 0.8 copy-done.7
  65.9 1.8 %collective-permute-done.10.refs_4_ = bf16[256,768]{1,0:T(8,128)(2,1)S(1)} collective-permute-done((bf16[256,768]{1,0:T(8,128)(2,1)S(1)}, bf16[256,768]{1,0:T(8,128)(2,1)S(1)}, u32[]{:S(2)}, u32[]{:S(2)}) %collective-permute-start.10) | collective-permute-done | bytes 393248 | tf_op jit(solution)/shard_map/ppermute | solution.py:39
  67.7 3.6 %far_sums.1 = bf16[32,4,768]{2,1,0:T(4,128)(2,1)} custom-call(s32[16]{0:T(128)S(1)} %stack.118.table, bf16[256,768]{1,0:T(8,128)(2,1)S(1)} %pad_maximum_fusion.rot_ref, f32[9,4,768]{2,1,0:T(4,128)S(1)} %get-tuple-element.26.near_ref, bf16[128,4096]{1,0:T(8,128)(2,1)S(1)} %copy-done.4, bf16[128,4096]{1,0:T(8,128)(2,1)} %collective-permute-done.3.other_ref, ...), custom_call_target="tpu_custom_call" | custom-call | flops 704643072 | bytes 3670016 | tf_op jit(solution)/shard_map/far_sums/pallas_call | solution.py:221
  71.4 0.7 copy-done.1
  72.1 8.3 %all-to-all-start = ((bf16[32,4,768]{2,1,0:T(4,128)(2,1)}), bf16[32,4,768]{2,1,0:T(4,128)(2,1)S(1)}, u32[]{:S(2)}, u32[]{:S(2)}) async-start(bf16[32,4,768]{2,1,0:T(4,128)(2,1)} %far_sums.1), calls=%async_computation | async-start | bytes 393216 | tf_op jit(solution)/shard_map/all_to_all | solution.py:351
  80.4 2.3 %collective-permute-start.12 = (bf16[128,2304]{1,0:T(8,128)(2,1)}, bf16[128,2304]{1,0:T(8,128)(2,1)}, u32[]{:S(2)}, u32[]{:S(2)}) collective-permute-start(bf16[128,2304]{1,0:T(8,128)(2,1)} %copy-done.7), channel_id=1, source_target_pairs={{0,1},{1,0},{64,65},{65,64},{128,129},{129,128},{192,193},{193,192... | collective-permute-start | bytes 1769480 | tf_op jit(solution)/shard_map/ppermute | solution.py:43
  82.7 1.0 copy-done.2
  83.7 3.0 %far_grad.1 = (bf16[128,8192]{1,0:T(8,128)(2,1)}, bf16[128,1792]{1,0:T(8,128)(2,1)S(1)}) custom-call(s32[16]{0:T(128)S(1)} %stack.118.table, bf16[256,768]{1,0:T(8,128)(2,1)S(1)} %pad_maximum_fusion.rot_ref, bf16[256,768]{1,0:T(8,128)(2,1)S(1)} %collective-permute-done.6.refs_0_, ...), custom_call_target="tpu_custom_call", output_to_operand_aliasing={{0}: (7, {})} | custom-call | flops 704643072 | bytes 3670016 | tf_op jit(solution)/shard_map/far_grad/pallas_call | solution.py:237
  86.7 0.8 copy-done.8
  87.5 2.7 %all-to-all-done = bf16[32,4,768]{2,1,0:T(4,128)(2,1)S(1)} async-done(((bf16[32,4,768]{2,1,0:T(4,128)(2,1)}), bf16[32,4,768]{2,1,0:T(4,128)(2,1)S(1)}, u32[]{:S(2)}, u32[]{:S(2)}) %all-to-all-start) | async-done | bytes 196640 | tf_op jit(solution)/shard_map/all_to_all | solution.py:351
  90.1 2.2 %collective-permute-start.11 = (bf16[128,1792]{1,0:T(8,128)(2,1)}, bf16[128,1792]{1,0:T(8,128)(2,1)S(1)}, u32[]{:S(2)}, u32[]{:S(2)}) collective-permute-start(bf16[128,1792]{1,0:T(8,128)(2,1)} %copy-done.8), channel_id=1, source_target_pairs={{0,1},{1,0},{64,65},{65,64},{128,129},{129,128},{192,193},{193,192... | collective-permute-start | bytes 1376264 | tf_op jit(solution)/shard_map/ppermute | solution.py:43
  92.4 0.1 reduce_sum.31
  92.5 0.7 broadcast_in_dim.30
  93.1 11.5 %all-to-all-start.1 = ((bf16[16,4,768]{2,1,0:T(4,128)(2,1)}), bf16[16,4,768]{2,1,0:T(4,128)(2,1)S(1)}, u32[]{:S(2)}, u32[]{:S(2)}) async-start(bf16[16,4,768]{2,1,0:T(4,128)(2,1)} %broadcast_in_dim.30), calls=%async_computation.1 | async-start | bytes 196608 | tf_op jit(solution)/shard_map/all_to_all | solution.py:359
  104.7 2.0 %place.2.grad_in = bf16[128,8192]{1,0:T(8,128)(2,1)} custom-call(s32[16]{0:T(128)S(1)} %stack.135.theirs.table, bf16[128,2304]{1,0:T(8,128)(2,1)} %collective-permute-done.12.blocks_ref, bf16[128,8192]{1,0:T(8,128)(2,1)} %get-tuple-element.35.grad_in), custom_call_target="tpu_custom_call", output_to_operand_aliasing={{}: (2, {})} | custom-call | bytes 1179648 | tf_op jit(solution)/shard_map/place/pallas_call | solution.py:271
  106.7 1.4 %place.3 = bf16[128,8192]{1,0:T(8,128)(2,1)} custom-call(s32[16]{0:T(128)S(1)} %stack.135.theirs.table, bf16[128,1792]{1,0:T(8,128)(2,1)S(1)} %collective-permute-done.11.blocks_ref, bf16[128,8192]{1,0:T(8,128)(2,1)} %place.2.grad_in), custom_call_target="tpu_custom_call", output_to_operand_aliasing={{}: (2, {})} | custom-call | bytes 917504 | tf_op jit(solution)/shard_map/place/pallas_call | solution.py:271
  108.0 8.4 %all-to-all-done.1 = bf16[16,4,768]{2,1,0:T(4,128)(2,1)S(1)} async-done(((bf16[16,4,768]{2,1,0:T(4,128)(2,1)}), bf16[16,4,768]{2,1,0:T(4,128)(2,1)S(1)}, u32[]{:S(2)}, u32[]{:S(2)}) %all-to-all-start.1) | async-done | bytes 98336 | tf_op jit(solution)/shard_map/all_to_all | solution.py:359
  116.5 0.6 multiply_divide_fusion
  (34 shorter events, 0.2 us)
Async XLA Ops:
  0.6 16.4 %copy-start.11 = (s32[1,8]{1,0:T(1,128)S(1)}, s32[1,8]{1,0:T(1,128)}, u32[]{:S(2)}) copy-start(s32[1,8]{1,0:T(1,128)} %param.8) | copy-start | bytes 100
  1.9 20.1 %copy-start = (bf16[128,8192]{1,0:T(8,128)(2,1)S(1)}, bf16[128,8192]{1,0:T(8,128)(2,1)}, u32[]{:S(2)}) copy-start(bf16[128,8192]{1,0:T(8,128)(2,1)} %feats_ref.1) | copy-start | bytes 6291460
  11.0 14.7 %collective-permute-start = (bf16[512,768]{1,0:T(8,128)(2,1)}, bf16[512,768]{1,0:T(8,128)(2,1)S(1)}, u32[]{:S(2)}, u32[]{:S(2)}) collective-permute-start(bf16[512,768]{1,0:T(8,128)(2,1)} %all_gather.3), channel_id=1, source_target_pairs={{0,2},{1,7},{64,66},{65,71},{128,130},{129,135},{192,194},{193,199... | collective-permute-start | bytes 2359304 | tf_op jit(solution)/shard_map/ppermute | solution.py:39
  13.0 13.3 %collective-permute-start.1 = (bf16[512,768]{1,0:T(8,128)(2,1)}, bf16[512,768]{1,0:T(8,128)(2,1)}, u32[]{:S(2)}, u32[]{:S(2)}) collective-permute-start(bf16[512,768]{1,0:T(8,128)(2,1)} %all_gather.3), channel_id=1, source_target_pairs={{0,8},{1,57},{64,72},{65,121},{128,136},{129,185},{192,200},{193,2... | collective-permute-start | bytes 2359304 | tf_op jit(solution)/shard_map/ppermute | solution.py:39
  19.4 5.4 %copy-start.9 = (bf16[128,768]{1,0:T(8,128)(2,1)S(1)}, bf16[128,768]{1,0:T(8,128)(2,1)}, u32[]{:S(2)}) copy-start(bf16[128,768]{1,0:T(8,128)(2,1)} %copy.19) | copy-start | bytes 589828
  19.4 5.4 %collective-permute-start.2 = (bf16[128,768]{1,0:T(8,128)(2,1)}, bf16[128,768]{1,0:T(8,128)(2,1)}, u32[]{:S(2)}, u32[]{:S(2)}) collective-permute-start(bf16[128,768]{1,0:T(8,128)(2,1)} %copy.19), channel_id=1, source_target_pairs={{0,1},{1,0},{64,65},{65,64},{128,129},{129,128},{192,193},{193,192... | collective-permute-start | bytes 589832 | tf_op jit(solution)/shard_map/ppermute | solution.py:43
  23.8 1.0 copy-start.3
  25.8 24.4 %copy-start.5 = (bf16[512,768]{1,0:T(8,128)(2,1)}, bf16[512,768]{1,0:T(8,128)(2,1)S(1)}, u32[]{:S(2)}) copy-start(bf16[512,768]{1,0:T(8,128)(2,1)S(1)} %collective-permute-done.refs_1_) | copy-start | bytes 2359300
  26.3 13.6 %collective-permute-start.4 = (bf16[512,768]{1,0:T(8,128)(2,1)}, bf16[512,768]{1,0:T(8,128)(2,1)}, u32[]{:S(2)}, u32[]{:S(2)}) collective-permute-start(bf16[512,768]{1,0:T(8,128)(2,1)} %collective-permute-done.1.refs_2_), channel_id=1, source_target_pairs={{0,2},{1,7},{64,66},{65,71},{128,130},{129,135},{192,194},{193,199... | collective-permute-start | bytes 2359304 | tf_op jit(solution)/shard_map/ppermute | solution.py:39
  30.7 14.5 %collective-permute-start.5 = (bf16[512,768]{1,0:T(8,128)(2,1)S(1)}, bf16[512,768]{1,0:T(8,128)(2,1)}, u32[]{:S(2)}, u32[]{:S(2)}) collective-permute-start(bf16[512,768]{1,0:T(8,128)(2,1)S(1)} %collective-permute-done.refs_1_), channel_id=1, source_target_pairs={{0,57},{1,8},{64,121},{65,72},{128,185},{129,136},{192,249},{193,2... | collective-permute-start | bytes 2359304 | tf_op jit(solution)/shard_map/ppermute | solution.py:39
  32.8 22.2 %collective-permute-start.3 = (bf16[128,4096]{1,0:T(8,128)(2,1)}, bf16[128,4096]{1,0:T(8,128)(2,1)}, u32[]{:S(2)}, u32[]{:S(2)}) collective-permute-start(bf16[128,4096]{1,0:T(8,128)(2,1)} %get-tuple-element.20), channel_id=1, source_target_pairs={{0,1},{1,0},{64,65},{65,64},{128,129},{129,128},{192,193},{193,192... | collective-permute-start | bytes 3145736 | tf_op jit(solution)/shard_map/ppermute | solution.py:43
  37.8 20.2 %copy-start.4 = (bf16[128,4096]{1,0:T(8,128)(2,1)S(1)}, bf16[128,4096]{1,0:T(8,128)(2,1)}, u32[]{:S(2)}) copy-start(bf16[128,4096]{1,0:T(8,128)(2,1)} %copy-done.3) | copy-start | bytes 3145732
  39.9 27.8 %collective-permute-start.8 = (bf16[512,768]{1,0:T(8,128)(2,1)}, bf16[512,768]{1,0:T(8,128)(2,1)S(1)}, u32[]{:S(2)}, u32[]{:S(2)}) collective-permute-start(bf16[512,768]{1,0:T(8,128)(2,1)} %collective-permute-done.4.refs_3_), channel_id=1, source_target_pairs={{0,2},{1,7},{64,66},{65,71},{128,130},{129,135},{192,194},{193,199... | collective-permute-start | bytes 2359304 | tf_op jit(solution)/shard_map/ppermute | solution.py:39
  45.2 22.5 %collective-permute-start.9 = (bf16[512,768]{1,0:T(8,128)(2,1)}, bf16[512,768]{1,0:T(8,128)(2,1)S(1)}, u32[]{:S(2)}, u32[]{:S(2)}) collective-permute-start(bf16[512,768]{1,0:T(8,128)(2,1)} %collective-permute-done.5.refs_4_), channel_id=1, source_target_pairs={{0,8},{1,57},{64,72},{65,121},{128,136},{129,185},{192,200},{193,2... | collective-permute-start | bytes 2359304 | tf_op jit(solution)/shard_map/ppermute | solution.py:39
  51.2 14.7 %collective-permute-start.6 = (bf16[256,768]{1,0:T(8,128)(2,1)S(1)}, bf16[256,768]{1,0:T(8,128)(2,1)S(1)}, u32[]{:S(2)}, u32[]{:S(2)}) collective-permute-start(bf16[256,768]{1,0:T(8,128)(2,1)S(1)} %get-tuple-element.27), channel_id=1, source_target_pairs={{0,2},{1,7},{64,66},{65,71},{128,130},{129,135},{192,194},{193,199... | collective-permute-start | bytes 1179656 | tf_op jit(solution)/shard_map/ppermute | solution.py:39
  53.1 12.8 %collective-permute-start.7 = (bf16[256,768]{1,0:T(8,128)(2,1)S(1)}, bf16[256,768]{1,0:T(8,128)(2,1)S(1)}, u32[]{:S(2)}, u32[]{:S(2)}) collective-permute-start(bf16[256,768]{1,0:T(8,128)(2,1)S(1)} %get-tuple-element.28), channel_id=1, source_target_pairs={{0,8},{1,57},{64,72},{65,121},{128,136},{129,185},{192,200},{193,2... | collective-permute-start | bytes 1179656 | tf_op jit(solution)/shard_map/ppermute | solution.py:39
  55.0 12.6 %collective-permute-start.10 = (bf16[256,768]{1,0:T(8,128)(2,1)S(1)}, bf16[256,768]{1,0:T(8,128)(2,1)S(1)}, u32[]{:S(2)}, u32[]{:S(2)}) collective-permute-start(bf16[256,768]{1,0:T(8,128)(2,1)S(1)} %constant_dynamic-slice_fusion.2), channel_id=1, source_target_pairs={{0,10},{1,63},{64,74},{65,127},{128,138},{129,191},{192,202},{193,... | collective-permute-start | bytes 1179656 | tf_op jit(solution)/shard_map/ppermute | solution.py:39
  58.0 1.1 copy-start.6
  65.0 0.8 copy-start.7
  71.3 0.8 copy-start.1
  72.1 18.1 %all-to-all-start = ((bf16[32,4,768]{2,1,0:T(4,128)(2,1)}), bf16[32,4,768]{2,1,0:T(4,128)(2,1)S(1)}, u32[]{:S(2)}, u32[]{:S(2)}) async-start(bf16[32,4,768]{2,1,0:T(4,128)(2,1)} %far_sums.1), calls=%async_computation | async-start | bytes 393216 | tf_op jit(solution)/shard_map/all_to_all | solution.py:351
  80.4 24.3 %collective-permute-start.12 = (bf16[128,2304]{1,0:T(8,128)(2,1)}, bf16[128,2304]{1,0:T(8,128)(2,1)}, u32[]{:S(2)}, u32[]{:S(2)}) collective-permute-start(bf16[128,2304]{1,0:T(8,128)(2,1)} %copy-done.7), channel_id=1, source_target_pairs={{0,1},{1,0},{64,65},{65,64},{128,129},{129,128},{192,193},{193,192... | collective-permute-start | bytes 1769480 | tf_op jit(solution)/shard_map/ppermute | solution.py:43
  82.7 1.0 copy-start.2
  86.7 0.8 copy-start.8
  90.1 16.5 %collective-permute-start.11 = (bf16[128,1792]{1,0:T(8,128)(2,1)}, bf16[128,1792]{1,0:T(8,128)(2,1)S(1)}, u32[]{:S(2)}, u32[]{:S(2)}) collective-permute-start(bf16[128,1792]{1,0:T(8,128)(2,1)} %copy-done.8), channel_id=1, source_target_pairs={{0,1},{1,0},{64,65},{65,64},{128,129},{129,128},{192,193},{193,192... | collective-permute-start | bytes 1376264 | tf_op jit(solution)/shard_map/ppermute | solution.py:43
  93.1 23.3 %all-to-all-start.1 = ((bf16[16,4,768]{2,1,0:T(4,128)(2,1)}), bf16[16,4,768]{2,1,0:T(4,128)(2,1)S(1)}, u32[]{:S(2)}, u32[]{:S(2)}) async-start(bf16[16,4,768]{2,1,0:T(4,128)(2,1)} %broadcast_in_dim.30), calls=%async_computation.1 | async-start | bytes 196608 | tf_op jit(solution)/shard_map/all_to_all | solution.py:359
  106.6 9.8 %copy-start.10 = (f32[4,768]{1,0:T(4,128)S(1)}, f32[4,768]{1,0:T(4,128)}, u32[]{:S(2)}) copy-start(f32[4,768]{1,0:T(4,128)} %param.11) | copy-start | bytes 36868

commit v8 on v7

--- a/solution.py
+++ b/solution.py
@@ -51,19 +51,13 @@
     return indices - jnp.max(starts, axis=1)
 
 
-def rope_back(cotangent, positions):
-    count = cotangent.shape[0]
-    split = cotangent.astype(jnp.float32).reshape(count, -1, HEAD)
+def rotation(positions):
     middle = HEAD // 2
     freqs = jnp.exp(jnp.arange(middle, dtype=jnp.float32) * (-2.0 * math.log(10000.0) / HEAD))
     angles = positions.astype(jnp.float32)[:, None] * freqs[None, :]
-    cosine = jnp.cos(angles)[:, None, :]
-    sine = jnp.sin(angles)[:, None, :]
-    first = split[..., :middle]
-    second = split[..., middle:]
-    lower = first * cosine + second * sine
-    upper = second * cosine - first * sine
-    return jnp.concatenate([lower, upper], axis=-1).reshape(count, -1).astype(jnp.bfloat16)
+    cosine, sine = jnp.cos(angles), jnp.sin(angles)
+    even = jnp.concatenate([cosine, cosine], axis=1)
+    return even, jnp.concatenate([sine, -sine], axis=1)
 
 
 def dequant(codes, zeros, steps):
@@ -116,8 +110,16 @@
     return copies
 
 
-def pack_kernel(rows, table, theirs, feats_ref, mine_ref, sent_ref):
-    for unit in range(mine_ref.shape[1] // rows):
+def pack_kernel(rows, table, theirs, even_ref, odd_ref, cot_ref, feats_ref, *outs):
+    rot_ref, mine_ref, sent_ref = outs
+    width = mine_ref.shape[1]
+    even, odd = even_ref[...], odd_ref[...]
+    for at in range(0, cot_ref.shape[1], HEAD):
+        head = cot_ref[:, at : at + HEAD].astype(jnp.float32)
+        turned = head * even + pltpu.roll(head, HEAD // 2, 1) * odd
+        rot_ref[:, at : at + HEAD] = turned.astype(rot_ref.dtype)
+        sent_ref[:, width + at : width + at + HEAD] = turned.astype(rot_ref.dtype)
+    for unit in range(width // rows):
         block = pl.ds(unit * rows, rows)
         mine_ref[:, block] = feats_ref[:, columns_of(table, unit, rows)]
         sent_ref[:, block] = feats_ref[:, columns_of(theirs, unit, rows)]
@@ -125,9 +127,11 @@
 
 def near_kernel(rows, count, table, rot_ref, mine_ref, other_ref, *refs):
     weights, refs = refs[:count], refs[count:]
-    grad_ref, sent_ref, sums_ref, held, own, held_sems, own_sems = refs
+    grad_ref, sent_ref, sums_ref, *both, held, own, held_sems, own_sems = refs
     load(weights, held, held_sems)
-    rot = rot_ref[...]
+    rot = jnp.concatenate([rot_ref[...], other_ref[:, mine_ref.shape[1] :]], axis=0)
+    for ref in both:
+        ref[...] = rot
     copies = put_grads(table, 0, rows, held, rot, own, sent_ref, grad_ref, own_sems)
     for unit in range(sums_ref.shape[0]):
         block = pl.ds(unit * rows, rows)
@@ -179,19 +183,23 @@
     return buffers + [pltpu.SemaphoreType.DMA((units,))] * (1 + own)
 
 
-def pack(table, theirs, feats, rows):
-    packed = jax.ShapeDtypeStruct((feats.shape[0], table.shape[0] * rows), feats.dtype)
+def pack(table, theirs, turn, cotangent, feats, rows):
+    tokens, cols = cotangent.shape
+    width = table.shape[0] * rows
     return pl.pallas_call(
         functools.partial(pack_kernel, rows),
-        out_shape=(packed, packed),
-        in_specs=[SMEM_SPEC, SMEM_SPEC, VMEM_SPEC],
-        out_specs=(VMEM_SPEC, VMEM_SPEC),
+        out_shape=tuple(
+            jax.ShapeDtypeStruct((tokens, size), feats.dtype)
+            for size in (cols, width, width + cols)
+        ),
+        in_specs=[SMEM_SPEC, SMEM_SPEC] + [VMEM_SPEC] * 4,
+        out_specs=(VMEM_SPEC,) * 3,
         cost_estimate=pl.CostEstimate(
             flops=0, bytes_accessed=3 * feats.size * 2, transcendentals=0
         ),
         compiler_params=pltpu.CompilerParams(vmem_limit_bytes=VMEM),
         name="pack",
-    )(table, theirs, feats)
+    )(table, theirs, *turn, cotangent, feats)
 
 
 def near_shards(table, mine, other, rot, weights, rows, width):
@@ -204,9 +212,10 @@
             jax.ShapeDtypeStruct((tokens, width), jnp.bfloat16),
             jax.ShapeDtypeStruct((tokens, total * rows), jnp.bfloat16),
             jax.ShapeDtypeStruct((total, rows // GROUP, cols), jnp.float32),
-        ),
+        )
+        + (jax.ShapeDtypeStruct((2 * tokens, cols), jnp.bfloat16),) * 2,
         in_specs=[SMEM_SPEC] + [VMEM_SPEC] * 3 + [ANY_SPEC] * len(weights),
-        out_specs=(ANY_SPEC, VMEM_SPEC, VMEM_SPEC),
+        out_specs=(ANY_SPEC,) + (VMEM_SPEC,) * 4,
         scratch_shapes=scratch(total, rows, cols, tokens, 1),
         cost_estimate=cost(total, rows, cols, tokens, 2),
         compiler_params=pltpu.CompilerParams(vmem_limit_bytes=VMEM),
@@ -321,11 +330,10 @@
     from_y = send(chip_weight, 0, 1)
 
     indices = place_in * tokens + jnp.arange(tokens, dtype=jnp.int32)
-    mine = rope_back(key_cotangent, token_positions(doc_lengths[0], indices))
-    rot = jnp.concatenate([mine, swap(mine)], axis=0)
-    mine_feats, their_feats = pack(table, theirs, activations, rows)
-    feats = (mine_feats, swap(their_feats))
-    from_x, from_y, rot, _ = lax.optimization_barrier((from_x, from_y, rot, their_feats))
+    turn = rotation(token_positions(doc_lengths[0], indices))
+    mine, mine_feats, to_other = pack(table, theirs, turn, key_cotangent, activations, rows)
+    feats = (mine_feats, swap(to_other))
+    from_x, from_y, _ = lax.optimization_barrier((from_x, from_y, to_other))
 
     def my_half(value):
         return lax.dynamic_slice_in_dim(value, core * rows, rows, axis=0)
@@ -337,32 +345,26 @@
 
     far_x = send(from_xy, 1, 0)
     far_y = send(from_yx, 0, 1)
-    half_xy = my_half(from_xy)
-    far = send(half_xy, 1, 1)
-    half_x, half_y, _ = lax.optimization_barrier((half_x, half_y, half_xy))
     far_xx = send(half_x, 1, 0)
     far_yy = send(half_y, 0, 1)
+    half_xy, _, _ = lax.optimization_barrier((my_half(from_xy), far_xx, far_yy))
+    far = send(half_xy, 1, 1)
 
     near = [weight, from_x, from_y, from_xy, from_yx]
-    grad, sent_near, sums_near = near_shards(table, *feats, rot, near, rows, activations.shape[1])
+    grad, sent_near, sums_near, rot, rot_again = near_shards(
+        table, *feats, mine, near, rows, activations.shape[1]
+    )
     fars = [far_xx, far_yy, far_x, far_y, far]
     at_hand = sums_near.shape[0]
     sums = far_sums(table, *feats, rot, fars, sums_near, rows, devices)
     shares = lax.all_to_all(sums, "tensor", split_axis=0, concat_axis=0, tiled=True)
 
-    grad, sent_far = far_grad(table, rot, fars, grad, rows, at_hand)
-    sent_near, _ = lax.optimization_barrier((sent_near, sums))
+    grad, sent_far = far_grad(table, rot_again, fars, grad, rows, at_hand)
     got_near = swap(sent_near)
-    shares, sent_far = lax.optimization_barrier((shares, sent_far))
     share = jnp.sum(shares.astype(jnp.float32), axis=0).astype(jnp.bfloat16)
-    copies = lax.axis_size("dp")
-    totals = lax.all_to_all(
-        jnp.broadcast_to(share[None], (copies, *share.shape)),
-        "dp",
-        split_axis=0,
-        concat_axis=0,
-        tiled=True,
-    )
+    share = jnp.broadcast_to(share[None], (lax.axis_size("dp"), *share.shape))
+    share, sent_far = lax.optimization_barrier((share, sent_far))
+    totals = lax.all_to_all(share, "dp", split_axis=0, concat_axis=0, tiled=True)
     grad = place(theirs, got_near, grad, rows, 0)
     grad = place(theirs, swap(sent_far), grad, rows, at_hand)
     totals, grad = lax.optimization_barrier((totals, grad))

time: 118 us -> 113 us (0.958)
  starting transfers between devices: 59.1 us -> 52.9 us
  waiting for transfers between devices: 14.4 us -> 20.1 us
  other arithmetic: 5.24 us -> 2.77 us
  local copies, waits for them, and re-layouts: 10.4 us -> 8.03 us
    ppermute x9, waiting for transfers between devices: 3.25 us -> 8.03 us  [send(): return lax.ppermute(value, AXES, permutation(target))]
    ppermute x4 -> x3, starting transfers between devices: 11.6 us -> 7.98 us  [swap(): lax.ppermute(value, AXES, permutation(lambda x, y, z, core: (x, y, z, cor...]
    all_to_all x1, starting transfers between devices: 8.3 us -> 5.19 us  [per_device(): lax.all_to_all(sums, 'tensor', split_axis=0, concat_axis=0, tiled=True)]
    unnamed x25 -> x24, local copies, waits for them, and re-layouts: 6.55 us -> 4 us
    dynamic_slice x2 -> x3, local copies, waits for them, and re-layouts: 2.17 us -> 3.17 us  [my_half(): return lax.dynamic_slice_in_dim(value, core * rows, rows, axis=0)]
  transfers between devices with their start and end apart: 15 -> 14, of which waited for: 5 -> 5; matrix products, arithmetic and copies ran while one was open for 7% -> 4% of each run, Pallas kernels for 12% -> 13%
where the time goes in v8:
time: 113 us; the launch traced here: 112 us
  starting transfers between devices  52.9 us (47%)
  waiting for transfers between devices  20.1 us (18%)
  Pallas kernels  18.1 us (16%)
  blocking collectives  8.87 us (8%)
  local copies, waits for them, and re-layouts  8.03 us (7%)
  other arithmetic  2.77 us (2%)
  between operations  1.32 us (1%)
    ppermute x9, starting transfers between devices, send(): return lax.ppermute(value, AXES, permutation(target))  28.2 us
    all_to_all x1, starting transfers between devices, per_device(): lax.all_to_all(share, 'dp', split_axis=0, concat_axis=0, tiled=True)  11.5 us
    all_gather x1, blocking collectives, per_device(): lax.all_gather(weight, 'tensor', axis=0, tiled=True, axis_index_groups=pa...  8.87 us
    all_to_all x1, waiting for transfers between devices, per_device(): lax.all_to_all(share, 'dp', split_axis=0, concat_axis=0, tiled=True)  8.39 us
    ppermute x9, waiting for transfers between devices, send(): return lax.ppermute(value, AXES, permutation(target))  8.03 us
    ppermute x3, starting transfers between devices, swap(): lax.ppermute(value, AXES, permutation(lambda x, y, z, core: (x, y, z, cor...  7.98 us
    pallas_call x1, Pallas kernels, near_shards(): pl.pallas_call(functools.partial(near_kernel, rows, len(weights)), out_sh...  5.95 us
    all_to_all x1, starting transfers between devices, per_device(): lax.all_to_all(sums, 'tensor', split_axis=0, concat_axis=0, tiled=True)  5.19 us
  transfers between devices with their start and end apart: 14, of which 5 were waited for; matrix products, arithmetic and copies ran while one was open for 4% of the time, Pallas kernels for 13%

profile of v8, /device:TPU:1, one launch (start us, length us, event | category | flops | bytes accessed | tf_op | source)
XLA Modules:
  0.0 112.0 jit_solution(4868381414657687002)
XLA Ops:
  0.7 1.4 %fusion.2.refs_0_ = bf16[256,768]{1,0:T(8,128)(2,1)S(1)} fusion(s32[256,768]{1,0:T(8,128)} %param.9, s32[4,768]{1,0:T(4,128)} %param.10, f32[4,768]{1,0:T(4,128)} %param.11), kind=kLoop, calls=%fused_computation.3 | loop fusion | flops 786432 | bytes 1204224 | tf_op jit(solution)/shard_map/convert_element_type | solution.py:66
  2.1 8.9 %all_gather.3 = bf16[512,768]{1,0:T(8,128)(2,1)S(1)} all-gather(bf16[256,768]{1,0:T(8,128)(2,1)S(1)} %fusion.2.refs_0_), channel_id=1, replica_groups={{0,1},{2,3},{4,5},{6,7},{8,9},{10,11},{12,13},{14,15},{16,17},{18,19},{..., dimensions={0}, use_global_device_ids=true | all-gather | bytes 1179648 | tf_op jit(solution)/shard_map/all_gather | solution.py:327
  10.9 1.9 %collective-permute-start.1 = (bf16[512,768]{1,0:T(8,128)(2,1)S(1)}, bf16[512,768]{1,0:T(8,128)(2,1)}, u32[]{:S(2)}, u32[]{:S(2)}) collective-permute-start(bf16[512,768]{1,0:T(8,128)(2,1)S(1)} %all_gather.3), channel_id=1, source_target_pairs={{0,2},{1,7},{64,66},{65,71},{128,130},{129,135},{192,194},{193,199... | collective-permute-start | bytes 2359304 | tf_op jit(solution)/shard_map/ppermute | solution.py:39
  12.9 2.2 %collective-permute-start.2 = (bf16[512,768]{1,0:T(8,128)(2,1)S(1)}, bf16[512,768]{1,0:T(8,128)(2,1)}, u32[]{:S(2)}, u32[]{:S(2)}) collective-permute-start(bf16[512,768]{1,0:T(8,128)(2,1)S(1)} %all_gather.3), channel_id=1, source_target_pairs={{0,8},{1,57},{64,72},{65,121},{128,136},{129,185},{192,200},{193,2... | collective-permute-start | bytes 2359304 | tf_op jit(solution)/shard_map/ppermute | solution.py:39
  15.4 0.1 select_reduce_fusion.1
  15.5 0.1 stack.118.table
  15.6 0.1 stack.135.theirs.table
  15.7 0.1 select_reduce_fusion
  15.8 0.3 multiply_sine_fusion
  16.1 0.1 pad_maximum_fusion
  16.2 1.9 %pack.1 = (bf16[128,768]{1,0:T(8,128)(2,1)S(1)}, bf16[128,4096]{1,0:T(8,128)(2,1)S(1)}, bf16[128,4864]{1,0:T(8,128)(2,1)}) custom-call(s32[16]{0:T(128)S(1)} %stack.118.table, s32[16]{0:T(128)S(1)} %stack.135.theirs.table, f32[128,128]{1,0:T(8,128)S(1)} %get-tuple-element.41.even_ref, f32[128,128]{1,0:T(8,128)S(1)} %get-tuple-element.42.odd_ref, ...), custom_call_target="tpu_custom_call" | custom-call | bytes 6291456 | tf_op jit(solution)/shard_map/pack/pallas_call | solution.py:189
  18.2 1.0 copy-done.1
  19.1 0.7 copy-done.8
  19.8 4.2 %collective-permute-done.1.refs_1_ = bf16[512,768]{1,0:T(8,128)(2,1)} collective-permute-done((bf16[512,768]{1,0:T(8,128)(2,1)S(1)}, bf16[512,768]{1,0:T(8,128)(2,1)}, u32[]{:S(2)}, u32[]{:S(2)}) %collective-permute-start.1) | collective-permute-done | bytes 786464 | tf_op jit(solution)/shard_map/ppermute | solution.py:39
  24.1 1.9 %collective-permute-done.2.refs_2_ = bf16[512,768]{1,0:T(8,128)(2,1)} collective-permute-done((bf16[512,768]{1,0:T(8,128)(2,1)S(1)}, bf16[512,768]{1,0:T(8,128)(2,1)}, u32[]{:S(2)}, u32[]{:S(2)}) %collective-permute-start.2) | collective-permute-done | bytes 786464 | tf_op jit(solution)/shard_map/ppermute | solution.py:39
  26.0 1.9 %collective-permute-start.3 = (bf16[512,768]{1,0:T(8,128)(2,1)}, bf16[512,768]{1,0:T(8,128)(2,1)}, u32[]{:S(2)}, u32[]{:S(2)}) collective-permute-start(bf16[512,768]{1,0:T(8,128)(2,1)} %collective-permute-done.2.refs_2_), channel_id=1, source_target_pairs={{0,2},{1,7},{64,66},{65,71},{128,130},{129,135},{192,194},{193,199... | collective-permute-start | bytes 2359304 | tf_op jit(solution)/shard_map/ppermute | solution.py:39
  27.9 2.8 %collective-permute-start.4 = (bf16[512,768]{1,0:T(8,128)(2,1)}, bf16[512,768]{1,0:T(8,128)(2,1)}, u32[]{:S(2)}, u32[]{:S(2)}) collective-permute-start(bf16[512,768]{1,0:T(8,128)(2,1)} %collective-permute-done.1.refs_1_), channel_id=1, source_target_pairs={{0,57},{1,8},{64,121},{65,72},{128,185},{129,136},{192,249},{193,2... | collective-permute-start | bytes 2359304 | tf_op jit(solution)/shard_map/ppermute | solution.py:39
  30.7 3.5 %collective-permute-start = (bf16[128,4864]{1,0:T(8,128)(2,1)}, bf16[128,4864]{1,0:T(8,128)(2,1)}, u32[]{:S(2)}, u32[]{:S(2)}) collective-permute-start(bf16[128,4864]{1,0:T(8,128)(2,1)} %get-tuple-element.22), channel_id=1, source_target_pairs={{0,1},{1,0},{64,65},{65,64},{128,129},{129,128},{192,193},{193,192... | collective-permute-start | bytes 3735560 | tf_op jit(solution)/shard_map/ppermute | solution.py:43
  34.2 1.1 constant_dynamic-slice_fusion.1
  35.3 4.9 %collective-permute-start.5 = (bf16[256,768]{1,0:T(8,128)(2,1)S(1)}, bf16[256,768]{1,0:T(8,128)(2,1)S(1)}, u32[]{:S(2)}, u32[]{:S(2)}) collective-permute-start(bf16[256,768]{1,0:T(8,128)(2,1)S(1)} %constant_dynamic-slice_fusion.1), channel_id=1, source_target_pairs={{0,2},{1,7},{64,66},{65,71},{128,130},{129,135},{192,194},{193,199... | collective-permute-start | bytes 1179656 | tf_op jit(solution)/shard_map/ppermute | solution.py:39
  40.2 1.0 constant_dynamic-slice_fusion
  41.2 4.5 %collective-permute-start.6 = (bf16[256,768]{1,0:T(8,128)(2,1)S(1)}, bf16[256,768]{1,0:T(8,128)(2,1)S(1)}, u32[]{:S(2)}, u32[]{:S(2)}) collective-permute-start(bf16[256,768]{1,0:T(8,128)(2,1)S(1)} %constant_dynamic-slice_fusion), channel_id=1, source_target_pairs={{0,8},{1,57},{64,72},{65,121},{128,136},{129,185},{192,200},{193,2... | collective-permute-start | bytes 1179656 | tf_op jit(solution)/shard_map/ppermute | solution.py:39
  45.7 0.0 collective-permute-done.3.refs_3_
  45.7 3.6 %collective-permute-start.7 = (bf16[512,768]{1,0:T(8,128)(2,1)}, bf16[512,768]{1,0:T(8,128)(2,1)S(1)}, u32[]{:S(2)}, u32[]{:S(2)}) collective-permute-start(bf16[512,768]{1,0:T(8,128)(2,1)} %collective-permute-done.3.refs_3_), channel_id=1, source_target_pairs={{0,2},{1,7},{64,66},{65,71},{128,130},{129,135},{192,194},{193,199... | collective-permute-start | bytes 2359304 | tf_op jit(solution)/shard_map/ppermute | solution.py:39
  49.4 0.0 collective-permute-done.4.refs_4_
  49.4 1.9 %collective-permute-start.8 = (bf16[512,768]{1,0:T(8,128)(2,1)}, bf16[512,768]{1,0:T(8,128)(2,1)S(1)}, u32[]{:S(2)}, u32[]{:S(2)}) collective-permute-start(bf16[512,768]{1,0:T(8,128)(2,1)} %collective-permute-done.4.refs_4_), channel_id=1, source_target_pairs={{0,8},{1,57},{64,72},{65,121},{128,136},{129,185},{192,200},{193,2... | collective-permute-start | bytes 2359304 | tf_op jit(solution)/shard_map/ppermute | solution.py:39
  51.3 1.0 constant_dynamic-slice_fusion.2
  52.3 4.5 %collective-permute-start.9 = (bf16[256,768]{1,0:T(8,128)(2,1)S(1)}, bf16[256,768]{1,0:T(8,128)(2,1)S(1)}, u32[]{:S(2)}, u32[]{:S(2)}) collective-permute-start(bf16[256,768]{1,0:T(8,128)(2,1)S(1)} %constant_dynamic-slice_fusion.2), channel_id=1, source_target_pairs={{0,10},{1,63},{64,74},{65,127},{128,138},{129,191},{192,202},{193,... | collective-permute-start | bytes 1179656 | tf_op jit(solution)/shard_map/ppermute | solution.py:39
  56.9 5.9 %near_shards.1 = (bf16[128,8192]{1,0:T(8,128)(2,1)}, bf16[128,2304]{1,0:T(8,128)(2,1)S(1)}, f32[9,4,768]{2,1,0:T(4,128)S(1)}, bf16[256,768]{1,0:T(8,128)(2,1)S(1)}, bf16[256,768]{1,0:T(8,128)(2,1)S(1)}) custom-call(s32[16]{0:T(128)S(1)} %stack.118.table, bf16[128,768]{1,0:T(8,128)(2,1)S(1)} %copy-done.9, bf16[128,4096]{1,0:T(8,128)(2,1)S(1)} %copy-done.2, ...), custom_call_target="tpu_custom_call" | custom-call | flops 1811939328 | bytes 4718592 | tf_op jit(solution)/shard_map/near_shards/pallas_call | solution.py:209
  62.9 0.7 copy-done.3
  63.6 0.8 copy-done.6
  64.4 1.9 %collective-permute-done.9.refs_4_ = bf16[256,768]{1,0:T(8,128)(2,1)S(1)} collective-permute-done((bf16[256,768]{1,0:T(8,128)(2,1)S(1)}, bf16[256,768]{1,0:T(8,128)(2,1)S(1)}, u32[]{:S(2)}, u32[]{:S(2)}) %collective-permute-start.9) | collective-permute-done | bytes 393248 | tf_op jit(solution)/shard_map/ppermute | solution.py:39
  66.3 3.9 %far_sums.1 = bf16[32,4,768]{2,1,0:T(4,128)(2,1)} custom-call(s32[16]{0:T(128)S(1)} %stack.118.table, bf16[256,768]{1,0:T(8,128)(2,1)S(1)} %get-tuple-element.26.rot_ref, f32[9,4,768]{2,1,0:T(4,128)S(1)} %get-tuple-element.27.near_ref, bf16[128,4096]{1,0:T(8,128)(2,1)S(1)} %copy-done.2, bf16[128,4864]{1,0:T(8,128)(2,1)} %collective-permute-done.other_ref, ...), custom_call_target="tpu_custom_call" | custom-call | flops 704643072 | bytes 3670016 | tf_op jit(solution)/shard_map/far_sums/pallas_call | solution.py:230
  70.1 5.2 %all-to-all-start = ((bf16[32,4,768]{2,1,0:T(4,128)(2,1)}), bf16[32,4,768]{2,1,0:T(4,128)(2,1)S(1)}, u32[]{:S(2)}, u32[]{:S(2)}) async-start(bf16[32,4,768]{2,1,0:T(4,128)(2,1)} %far_sums.1), calls=%async_computation | async-start | bytes 393216 | tf_op jit(solution)/shard_map/all_to_all | solution.py:360
  75.3 2.3 %collective-permute-start.11 = (bf16[128,2304]{1,0:T(8,128)(2,1)}, bf16[128,2304]{1,0:T(8,128)(2,1)}, u32[]{:S(2)}, u32[]{:S(2)}) collective-permute-start(bf16[128,2304]{1,0:T(8,128)(2,1)} %copy-done.6), channel_id=1, source_target_pairs={{0,1},{1,0},{64,65},{65,64},{128,129},{129,128},{192,193},{193,192... | collective-permute-start | bytes 1769480 | tf_op jit(solution)/shard_map/ppermute | solution.py:43
  77.6 3.0 %far_grad.1 = (bf16[128,8192]{1,0:T(8,128)(2,1)}, bf16[128,1792]{1,0:T(8,128)(2,1)S(1)}) custom-call(s32[16]{0:T(128)S(1)} %stack.118.table, bf16[256,768]{1,0:T(8,128)(2,1)S(1)} %copy-done.4, bf16[256,768]{1,0:T(8,128)(2,1)S(1)} %collective-permute-done.5.refs_0_, ...), custom_call_target="tpu_custom_call", output_to_operand_aliasing={{0}: (7, {})} | custom-call | flops 704643072 | bytes 3670016 | tf_op jit(solution)/shard_map/far_grad/pallas_call | solution.py:246
  80.6 0.8 copy-done.7
  81.4 3.7 %all-to-all-done = bf16[32,4,768]{2,1,0:T(4,128)(2,1)S(1)} async-done(((bf16[32,4,768]{2,1,0:T(4,128)(2,1)}), bf16[32,4,768]{2,1,0:T(4,128)(2,1)S(1)}, u32[]{:S(2)}, u32[]{:S(2)}) %all-to-all-start) | async-done | bytes 196640 | tf_op jit(solution)/shard_map/all_to_all | solution.py:360
  85.1 0.1 reduce_sum.31
  85.2 0.7 broadcast_in_dim.43
  85.9 2.2 %collective-permute-start.10 = (bf16[128,1792]{1,0:T(8,128)(2,1)}, bf16[128,1792]{1,0:T(8,128)(2,1)S(1)}, u32[]{:S(2)}, u32[]{:S(2)}) collective-permute-start(bf16[128,1792]{1,0:T(8,128)(2,1)} %copy-done.7), channel_id=1, source_target_pairs={{0,1},{1,0},{64,65},{65,64},{128,129},{129,128},{192,193},{193,192... | collective-permute-start | bytes 1376264 | tf_op jit(solution)/shard_map/ppermute | solution.py:43
  88.1 11.5 %all-to-all-start.1 = ((bf16[16,4,768]{2,1,0:T(4,128)(2,1)}), bf16[16,4,768]{2,1,0:T(4,128)(2,1)S(1)}, u32[]{:S(2)}, u32[]{:S(2)}) async-start(bf16[16,4,768]{2,1,0:T(4,128)(2,1)} %broadcast_in_dim.43), calls=%async_computation.1 | async-start | bytes 196608 | tf_op jit(solution)/shard_map/all_to_all | solution.py:367
  99.6 2.0 %place.2.grad_in = bf16[128,8192]{1,0:T(8,128)(2,1)} custom-call(s32[16]{0:T(128)S(1)} %stack.135.theirs.table, bf16[128,2304]{1,0:T(8,128)(2,1)} %collective-permute-done.11.blocks_ref, bf16[128,8192]{1,0:T(8,128)(2,1)} %get-tuple-element.35.grad_in), custom_call_target="tpu_custom_call", output_to_operand_aliasing={{}: (2, {})} | custom-call | bytes 1179648 | tf_op jit(solution)/shard_map/place/pallas_call | solution.py:280
  101.6 0.0 copy-start.10
  101.6 1.4 %place.3 = bf16[128,8192]{1,0:T(8,128)(2,1)} custom-call(s32[16]{0:T(128)S(1)} %stack.135.theirs.table, bf16[128,1792]{1,0:T(8,128)(2,1)S(1)} %collective-permute-done.10.blocks_ref, bf16[128,8192]{1,0:T(8,128)(2,1)} %place.2.grad_in), custom_call_target="tpu_custom_call", output_to_operand_aliasing={{}: (2, {})} | custom-call | bytes 917504 | tf_op jit(solution)/shard_map/place/pallas_call | solution.py:280
  103.0 8.4 %all-to-all-done.1 = bf16[16,4,768]{2,1,0:T(4,128)(2,1)S(1)} async-done(((bf16[16,4,768]{2,1,0:T(4,128)(2,1)}), bf16[16,4,768]{2,1,0:T(4,128)(2,1)S(1)}, u32[]{:S(2)}, u32[]{:S(2)}) %all-to-all-start.1) | async-done | bytes 98336 | tf_op jit(solution)/shard_map/all_to_all | solution.py:367
  111.4 0.1 convert_reduce_fusion
  111.4 0.6 multiply_divide_fusion
  (28 shorter events, 0.1 us)
Async XLA Ops:
  0.6 14.7 %copy-start.11 = (s32[1,8]{1,0:T(1,128)S(1)}, s32[1,8]{1,0:T(1,128)}, u32[]{:S(2)}) copy-start(s32[1,8]{1,0:T(1,128)} %param.8) | copy-start | bytes 100
  0.6 15.6 %copy-start.5 = (bf16[128,768]{1,0:T(8,128)(2,1)S(1)}, bf16[128,768]{1,0:T(8,128)(2,1)}, u32[]{:S(2)}) copy-start(bf16[128,768]{1,0:T(8,128)(2,1)} %cot_ref.1) | copy-start | bytes 589828
  0.7 15.6 %copy-start = (bf16[128,8192]{1,0:T(8,128)(2,1)S(1)}, bf16[128,8192]{1,0:T(8,128)(2,1)}, u32[]{:S(2)}) copy-start(bf16[128,8192]{1,0:T(8,128)(2,1)} %feats_ref.1) | copy-start | bytes 6291460
  10.9 13.1 %collective-permute-start.1 = (bf16[512,768]{1,0:T(8,128)(2,1)S(1)}, bf16[512,768]{1,0:T(8,128)(2,1)}, u32[]{:S(2)}, u32[]{:S(2)}) collective-permute-start(bf16[512,768]{1,0:T(8,128)(2,1)S(1)} %all_gather.3), channel_id=1, source_target_pairs={{0,2},{1,7},{64,66},{65,71},{128,130},{129,135},{192,194},{193,199... | collective-permute-start | bytes 2359304 | tf_op jit(solution)/shard_map/ppermute | solution.py:39
  12.9 13.1 %collective-permute-start.2 = (bf16[512,768]{1,0:T(8,128)(2,1)S(1)}, bf16[512,768]{1,0:T(8,128)(2,1)}, u32[]{:S(2)}, u32[]{:S(2)}) collective-permute-start(bf16[512,768]{1,0:T(8,128)(2,1)S(1)} %all_gather.3), channel_id=1, source_target_pairs={{0,8},{1,57},{64,72},{65,121},{128,136},{129,185},{192,200},{193,2... | collective-permute-start | bytes 2359304 | tf_op jit(solution)/shard_map/ppermute | solution.py:39
  18.2 1.0 copy-start.1
  19.1 0.7 copy-start.8
  24.1 32.8 %copy-start.9 = (bf16[128,768]{1,0:T(8,128)(2,1)S(1)}, bf16[128,768]{1,0:T(8,128)(2,1)}, u32[]{:S(2)}) copy-start(bf16[128,768]{1,0:T(8,128)(2,1)} %copy-done.8) | copy-start | bytes 589828
  26.0 19.7 %collective-permute-start.3 = (bf16[512,768]{1,0:T(8,128)(2,1)}, bf16[512,768]{1,0:T(8,128)(2,1)}, u32[]{:S(2)}, u32[]{:S(2)}) collective-permute-start(bf16[512,768]{1,0:T(8,128)(2,1)} %collective-permute-done.2.refs_2_), channel_id=1, source_target_pairs={{0,2},{1,7},{64,66},{65,71},{128,130},{129,135},{192,194},{193,199... | collective-permute-start | bytes 2359304 | tf_op jit(solution)/shard_map/ppermute | solution.py:39
  27.9 21.5 %collective-permute-start.4 = (bf16[512,768]{1,0:T(8,128)(2,1)}, bf16[512,768]{1,0:T(8,128)(2,1)}, u32[]{:S(2)}, u32[]{:S(2)}) collective-permute-start(bf16[512,768]{1,0:T(8,128)(2,1)} %collective-permute-done.1.refs_1_), channel_id=1, source_target_pairs={{0,57},{1,8},{64,121},{65,72},{128,185},{129,136},{192,249},{193,2... | collective-permute-start | bytes 2359304 | tf_op jit(solution)/shard_map/ppermute | solution.py:39
  30.7 26.2 %collective-permute-start = (bf16[128,4864]{1,0:T(8,128)(2,1)}, bf16[128,4864]{1,0:T(8,128)(2,1)}, u32[]{:S(2)}, u32[]{:S(2)}) collective-permute-start(bf16[128,4864]{1,0:T(8,128)(2,1)} %get-tuple-element.22), channel_id=1, source_target_pairs={{0,1},{1,0},{64,65},{65,64},{128,129},{129,128},{192,193},{193,192... | collective-permute-start | bytes 3735560 | tf_op jit(solution)/shard_map/ppermute | solution.py:43
  34.2 22.7 %copy-start.2 = (bf16[128,4096]{1,0:T(8,128)(2,1)S(1)}, bf16[128,4096]{1,0:T(8,128)(2,1)}, u32[]{:S(2)}) copy-start(bf16[128,4096]{1,0:T(8,128)(2,1)} %copy-done.1) | copy-start | bytes 3145732
  35.3 17.0 %collective-permute-start.5 = (bf16[256,768]{1,0:T(8,128)(2,1)S(1)}, bf16[256,768]{1,0:T(8,128)(2,1)S(1)}, u32[]{:S(2)}, u32[]{:S(2)}) collective-permute-start(bf16[256,768]{1,0:T(8,128)(2,1)S(1)} %constant_dynamic-slice_fusion.1), channel_id=1, source_target_pairs={{0,2},{1,7},{64,66},{65,71},{128,130},{129,135},{192,194},{193,199... | collective-permute-start | bytes 1179656 | tf_op jit(solution)/shard_map/ppermute | solution.py:39
  41.2 11.1 %collective-permute-start.6 = (bf16[256,768]{1,0:T(8,128)(2,1)S(1)}, bf16[256,768]{1,0:T(8,128)(2,1)S(1)}, u32[]{:S(2)}, u32[]{:S(2)}) collective-permute-start(bf16[256,768]{1,0:T(8,128)(2,1)S(1)} %constant_dynamic-slice_fusion), channel_id=1, source_target_pairs={{0,8},{1,57},{64,72},{65,121},{128,136},{129,185},{192,200},{193,2... | collective-permute-start | bytes 1179656 | tf_op jit(solution)/shard_map/ppermute | solution.py:39
  45.7 20.6 %collective-permute-start.7 = (bf16[512,768]{1,0:T(8,128)(2,1)}, bf16[512,768]{1,0:T(8,128)(2,1)S(1)}, u32[]{:S(2)}, u32[]{:S(2)}) collective-permute-start(bf16[512,768]{1,0:T(8,128)(2,1)} %collective-permute-done.3.refs_3_), channel_id=1, source_target_pairs={{0,2},{1,7},{64,66},{65,71},{128,130},{129,135},{192,194},{193,199... | collective-permute-start | bytes 2359304 | tf_op jit(solution)/shard_map/ppermute | solution.py:39
  49.4 16.9 %collective-permute-start.8 = (bf16[512,768]{1,0:T(8,128)(2,1)}, bf16[512,768]{1,0:T(8,128)(2,1)S(1)}, u32[]{:S(2)}, u32[]{:S(2)}) collective-permute-start(bf16[512,768]{1,0:T(8,128)(2,1)} %collective-permute-done.4.refs_4_), channel_id=1, source_target_pairs={{0,8},{1,57},{64,72},{65,121},{128,136},{129,185},{192,200},{193,2... | collective-permute-start | bytes 2359304 | tf_op jit(solution)/shard_map/ppermute | solution.py:39
  52.3 13.9 %collective-permute-start.9 = (bf16[256,768]{1,0:T(8,128)(2,1)S(1)}, bf16[256,768]{1,0:T(8,128)(2,1)S(1)}, u32[]{:S(2)}, u32[]{:S(2)}) collective-permute-start(bf16[256,768]{1,0:T(8,128)(2,1)S(1)} %constant_dynamic-slice_fusion.2), channel_id=1, source_target_pairs={{0,10},{1,63},{64,74},{65,127},{128,138},{129,191},{192,202},{193,... | collective-permute-start | bytes 1179656 | tf_op jit(solution)/shard_map/ppermute | solution.py:39
  62.9 0.7 copy-start.3
  63.6 0.8 copy-start.6
  66.3 11.3 %copy-start.4 = (bf16[256,768]{1,0:T(8,128)(2,1)S(1)}, bf16[256,768]{1,0:T(8,128)(2,1)}, u32[]{:S(2)}) copy-start(bf16[256,768]{1,0:T(8,128)(2,1)} %copy-done.3) | copy-start | bytes 1179652
  70.1 14.9 %all-to-all-start = ((bf16[32,4,768]{2,1,0:T(4,128)(2,1)}), bf16[32,4,768]{2,1,0:T(4,128)(2,1)S(1)}, u32[]{:S(2)}, u32[]{:S(2)}) async-start(bf16[32,4,768]{2,1,0:T(4,128)(2,1)} %far_sums.1), calls=%async_computation | async-start | bytes 393216 | tf_op jit(solution)/shard_map/all_to_all | solution.py:360
  75.3 24.3 %collective-permute-start.11 = (bf16[128,2304]{1,0:T(8,128)(2,1)}, bf16[128,2304]{1,0:T(8,128)(2,1)}, u32[]{:S(2)}, u32[]{:S(2)}) collective-permute-start(bf16[128,2304]{1,0:T(8,128)(2,1)} %copy-done.6), channel_id=1, source_target_pairs={{0,1},{1,0},{64,65},{65,64},{128,129},{129,128},{192,193},{193,192... | collective-permute-start | bytes 1769480 | tf_op jit(solution)/shard_map/ppermute | solution.py:43
  80.6 0.8 copy-start.7
  85.9 15.7 %collective-permute-start.10 = (bf16[128,1792]{1,0:T(8,128)(2,1)}, bf16[128,1792]{1,0:T(8,128)(2,1)S(1)}, u32[]{:S(2)}, u32[]{:S(2)}) collective-permute-start(bf16[128,1792]{1,0:T(8,128)(2,1)} %copy-done.7), channel_id=1, source_target_pairs={{0,1},{1,0},{64,65},{65,64},{128,129},{129,128},{192,193},{193,192... | collective-permute-start | bytes 1376264 | tf_op jit(solution)/shard_map/ppermute | solution.py:43
  88.1 23.3 %all-to-all-start.1 = ((bf16[16,4,768]{2,1,0:T(4,128)(2,1)}), bf16[16,4,768]{2,1,0:T(4,128)(2,1)S(1)}, u32[]{:S(2)}, u32[]{:S(2)}) async-start(bf16[16,4,768]{2,1,0:T(4,128)(2,1)} %broadcast_in_dim.43), calls=%async_computation.1 | async-start | bytes 196608 | tf_op jit(solution)/shard_map/all_to_all | solution.py:367
  101.6 9.8 %copy-start.10 = (f32[4,768]{1,0:T(4,128)S(1)}, f32[4,768]{1,0:T(4,128)}, u32[]{:S(2)}) copy-start(f32[4,768]{1,0:T(4,128)} %param.11) | copy-start | bytes 36868

commit v9 on v8

--- a/solution.py
+++ b/solution.py
@@ -12,7 +12,7 @@
 GROUP = 64
 AXES = ("dp", "tensor")
 NX, NY, NYL, NZ = 4, 8, 4, 8
-VMEM = 12 * 1024 * 1024
+VMEM = 48 * 1024 * 1024
 
 
 def device_at(x, y, z, core):
@@ -340,7 +340,7 @@
 
     from_xy = send(from_y, 1, 0)
     from_yx = send(from_x, 0, 1, cross=True)
-    half_x, half_y = my_half(from_x), my_half(from_y)
+    half_x, half_y, _ = lax.optimization_barrier((my_half(from_x), my_half(from_y), feats[1]))
     from_xy, _, _ = lax.optimization_barrier((from_xy, half_x, half_y))
 
     far_x = send(from_xy, 1, 0)

time: 113 us -> 112 us (level)
  starting transfers between devices: 52.9 us -> 55.6 us
  waiting for transfers between devices: 20.1 us -> 17.6 us
    all_to_all x1, starting transfers between devices: 5.19 us -> 8.87 us  [per_device(): lax.all_to_all(sums, 'tensor', split_axis=0, concat_axis=0, tiled=True)]
    ppermute x9, waiting for transfers between devices: 8.03 us -> 5.52 us  [send(): return lax.ppermute(value, AXES, permutation(target))]
    ppermute x9, starting transfers between devices: 28.2 us -> 29.7 us  [send(): return lax.ppermute(value, AXES, permutation(target))]
    ppermute x3, starting transfers between devices: 7.98 us -> 6.6 us  [swap(): lax.ppermute(value, AXES, permutation(lambda x, y, z, core: (x, y, z, cor...]
    all_to_all x1, starting transfers between devices: 11.5 us -> 10.4 us  [per_device(): lax.all_to_all(share, 'dp', split_axis=0, concat_axis=0, tiled=True)]
    unnamed x24 -> x28, local copies, waits for them, and re-layouts: 4 us -> 4.02 us
where the time goes in v9:
time: 112 us; the launch traced here: 111 us
  starting transfers between devices  55.6 us (50%)
  waiting for transfers between devices  17.6 us (16%)
  Pallas kernels  17.2 us (15%)
  blocking collectives  8.87 us (8%)
  local copies, waits for them, and re-layouts  8 us (7%)
  other arithmetic  2.77 us (2%)
  between operations  1.35 us (1%)
    ppermute x9, starting transfers between devices, send(): return lax.ppermute(value, AXES, permutation(target))  29.7 us
    all_to_all x1, starting transfers between devices, per_device(): lax.all_to_all(share, 'dp', split_axis=0, concat_axis=0, tiled=True)  10.4 us
    all_gather x1, blocking collectives, per_device(): lax.all_gather(weight, 'tensor', axis=0, tiled=True, axis_index_groups=pa...  8.87 us
    all_to_all x1, starting transfers between devices, per_device(): lax.all_to_all(sums, 'tensor', split_axis=0, concat_axis=0, tiled=True)  8.87 us
    all_to_all x1, waiting for transfers between devices, per_device(): lax.all_to_all(share, 'dp', split_axis=0, concat_axis=0, tiled=True)  8.39 us
    ppermute x3, starting transfers between devices, swap(): lax.ppermute(value, AXES, permutation(lambda x, y, z, core: (x, y, z, cor...  6.6 us
    pallas_call x1, Pallas kernels, near_shards(): pl.pallas_call(functools.partial(near_kernel, rows, len(weights)), out_sh...  6.03 us
    ppermute x9, waiting for transfers between devices, send(): return lax.ppermute(value, AXES, permutation(target))  5.52 us
  transfers between devices with their start and end apart: 14, of which 5 were waited for; matrix products, arithmetic and copies ran while one was open for 4% of the time, Pallas kernels for 13%

profile of v9, /device:TPU:1, one launch (start us, length us, event | category | flops | bytes accessed | tf_op | source)
XLA Modules:
  0.0 111.4 jit_solution(18112249468742441668)
XLA Ops:
  0.7 1.4 %fusion.2.refs_0_ = bf16[256,768]{1,0:T(8,128)(2,1)S(1)} fusion(s32[256,768]{1,0:T(8,128)} %param.9, s32[4,768]{1,0:T(4,128)} %param.10, f32[4,768]{1,0:T(4,128)} %param.11), kind=kLoop, calls=%fused_computation.3 | loop fusion | flops 786432 | bytes 1204224 | tf_op jit(solution)/shard_map/convert_element_type | solution.py:66
  2.1 8.9 %all_gather.3 = bf16[512,768]{1,0:T(8,128)(2,1)S(1)} all-gather(bf16[256,768]{1,0:T(8,128)(2,1)S(1)} %fusion.2.refs_0_), channel_id=1, replica_groups={{0,1},{2,3},{4,5},{6,7},{8,9},{10,11},{12,13},{14,15},{16,17},{18,19},{..., dimensions={0}, use_global_device_ids=true | all-gather | bytes 1179648 | tf_op jit(solution)/shard_map/all_gather | solution.py:327
  10.9 1.9 %collective-permute-start.1 = (bf16[512,768]{1,0:T(8,128)(2,1)S(1)}, bf16[512,768]{1,0:T(8,128)(2,1)}, u32[]{:S(2)}, u32[]{:S(2)}) collective-permute-start(bf16[512,768]{1,0:T(8,128)(2,1)S(1)} %all_gather.3), channel_id=1, source_target_pairs={{0,2},{1,7},{64,66},{65,71},{128,130},{129,135},{192,194},{193,199... | collective-permute-start | bytes 2359304 | tf_op jit(solution)/shard_map/ppermute | solution.py:39
  12.9 2.2 %collective-permute-start.2 = (bf16[512,768]{1,0:T(8,128)(2,1)S(1)}, bf16[512,768]{1,0:T(8,128)(2,1)}, u32[]{:S(2)}, u32[]{:S(2)}) collective-permute-start(bf16[512,768]{1,0:T(8,128)(2,1)S(1)} %all_gather.3), channel_id=1, source_target_pairs={{0,8},{1,57},{64,72},{65,121},{128,136},{129,185},{192,200},{193,2... | collective-permute-start | bytes 2359304 | tf_op jit(solution)/shard_map/ppermute | solution.py:39
  15.4 0.1 select_reduce_fusion.1
  15.5 0.1 select_reduce_fusion
  15.6 0.1 stack.118.table
  15.7 0.1 stack.135.theirs.table
  15.8 0.3 multiply_sine_fusion
  16.1 0.1 pad_maximum_fusion
  16.2 1.9 %pack.1 = (bf16[128,768]{1,0:T(8,128)(2,1)S(1)}, bf16[128,4096]{1,0:T(8,128)(2,1)S(1)}, bf16[128,4864]{1,0:T(8,128)(2,1)}) custom-call(s32[16]{0:T(128)S(1)} %stack.118.table, s32[16]{0:T(128)S(1)} %stack.135.theirs.table, f32[128,128]{1,0:T(8,128)S(1)} %get-tuple-element.45.even_ref, f32[128,128]{1,0:T(8,128)S(1)} %get-tuple-element.46.odd_ref, ...), custom_call_target="tpu_custom_call" | custom-call | bytes 6291456 | tf_op jit(solution)/shard_map/pack/pallas_call | solution.py:189
  18.2 1.0 copy-done.3
  19.1 0.7 copy-done.10
  19.8 2.1 %collective-permute-start = (bf16[128,4864]{1,0:T(8,128)(2,1)}, bf16[128,4864]{1,0:T(8,128)(2,1)S(1)}, u32[]{:S(2)}, u32[]{:S(2)}) collective-permute-start(bf16[128,4864]{1,0:T(8,128)(2,1)} %get-tuple-element.24), channel_id=1, source_target_pairs={{0,1},{1,0},{64,65},{65,64},{128,129},{129,128},{192,193},{193,192... | collective-permute-start | bytes 3735560 | tf_op jit(solution)/shard_map/ppermute | solution.py:43
  22.0 2.1 %collective-permute-done.1.refs_1_ = bf16[512,768]{1,0:T(8,128)(2,1)} collective-permute-done((bf16[512,768]{1,0:T(8,128)(2,1)S(1)}, bf16[512,768]{1,0:T(8,128)(2,1)}, u32[]{:S(2)}, u32[]{:S(2)}) %collective-permute-start.1) | collective-permute-done | bytes 786464 | tf_op jit(solution)/shard_map/ppermute | solution.py:39
  24.1 1.9 %collective-permute-done.2.refs_2_ = bf16[512,768]{1,0:T(8,128)(2,1)} collective-permute-done((bf16[512,768]{1,0:T(8,128)(2,1)S(1)}, bf16[512,768]{1,0:T(8,128)(2,1)}, u32[]{:S(2)}, u32[]{:S(2)}) %collective-permute-start.2) | collective-permute-done | bytes 786464 | tf_op jit(solution)/shard_map/ppermute | solution.py:39
  26.0 1.9 %collective-permute-start.3 = (bf16[512,768]{1,0:T(8,128)(2,1)}, bf16[512,768]{1,0:T(8,128)(2,1)}, u32[]{:S(2)}, u32[]{:S(2)}) collective-permute-start(bf16[512,768]{1,0:T(8,128)(2,1)} %collective-permute-done.2.refs_2_), channel_id=1, source_target_pairs={{0,2},{1,7},{64,66},{65,71},{128,130},{129,135},{192,194},{193,199... | collective-permute-start | bytes 2359304 | tf_op jit(solution)/shard_map/ppermute | solution.py:39
  27.9 2.8 %collective-permute-start.4 = (bf16[512,768]{1,0:T(8,128)(2,1)}, bf16[512,768]{1,0:T(8,128)(2,1)}, u32[]{:S(2)}, u32[]{:S(2)}) collective-permute-start(bf16[512,768]{1,0:T(8,128)(2,1)} %collective-permute-done.1.refs_1_), channel_id=1, source_target_pairs={{0,57},{1,8},{64,121},{65,72},{128,185},{129,136},{192,249},{193,2... | collective-permute-start | bytes 2359304 | tf_op jit(solution)/shard_map/ppermute | solution.py:39
  30.7 1.1 constant_dynamic-slice_fusion.1
  31.7 1.0 constant_dynamic-slice_fusion
  32.8 4.9 %collective-permute-start.5 = (bf16[256,768]{1,0:T(8,128)(2,1)S(1)}, bf16[256,768]{1,0:T(8,128)(2,1)S(1)}, u32[]{:S(2)}, u32[]{:S(2)}) collective-permute-start(bf16[256,768]{1,0:T(8,128)(2,1)S(1)} %constant_dynamic-slice_fusion.1), channel_id=1, source_target_pairs={{0,2},{1,7},{64,66},{65,71},{128,130},{129,135},{192,194},{193,199... | collective-permute-start | bytes 1179656 | tf_op jit(solution)/shard_map/ppermute | solution.py:39
  37.7 6.1 %collective-permute-start.6 = (bf16[256,768]{1,0:T(8,128)(2,1)S(1)}, bf16[256,768]{1,0:T(8,128)(2,1)S(1)}, u32[]{:S(2)}, u32[]{:S(2)}) collective-permute-start(bf16[256,768]{1,0:T(8,128)(2,1)S(1)} %constant_dynamic-slice_fusion), channel_id=1, source_target_pairs={{0,8},{1,57},{64,72},{65,121},{128,136},{129,185},{192,200},{193,2... | collective-permute-start | bytes 1179656 | tf_op jit(solution)/shard_map/ppermute | solution.py:39
  43.7 0.0 collective-permute-done.3.refs_3_
  43.7 3.6 %collective-permute-start.7 = (bf16[512,768]{1,0:T(8,128)(2,1)}, bf16[512,768]{1,0:T(8,128)(2,1)S(1)}, u32[]{:S(2)}, u32[]{:S(2)}) collective-permute-start(bf16[512,768]{1,0:T(8,128)(2,1)} %collective-permute-done.3.refs_3_), channel_id=1, source_target_pairs={{0,2},{1,7},{64,66},{65,71},{128,130},{129,135},{192,194},{193,199... | collective-permute-start | bytes 2359304 | tf_op jit(solution)/shard_map/ppermute | solution.py:39
  47.4 0.0 collective-permute-done.4.refs_4_
  47.4 1.9 %collective-permute-start.8 = (bf16[512,768]{1,0:T(8,128)(2,1)}, bf16[512,768]{1,0:T(8,128)(2,1)S(1)}, u32[]{:S(2)}, u32[]{:S(2)}) collective-permute-start(bf16[512,768]{1,0:T(8,128)(2,1)} %collective-permute-done.4.refs_4_), channel_id=1, source_target_pairs={{0,8},{1,57},{64,72},{65,121},{128,136},{129,185},{192,200},{193,2... | collective-permute-start | bytes 2359304 | tf_op jit(solution)/shard_map/ppermute | solution.py:39
  49.3 1.0 constant_dynamic-slice_fusion.2
  50.4 4.5 %collective-permute-start.9 = (bf16[256,768]{1,0:T(8,128)(2,1)S(1)}, bf16[256,768]{1,0:T(8,128)(2,1)S(1)}, u32[]{:S(2)}, u32[]{:S(2)}) collective-permute-start(bf16[256,768]{1,0:T(8,128)(2,1)S(1)} %constant_dynamic-slice_fusion.2), channel_id=1, source_target_pairs={{0,10},{1,63},{64,74},{65,127},{128,138},{129,191},{192,202},{193,... | collective-permute-start | bytes 1179656 | tf_op jit(solution)/shard_map/ppermute | solution.py:39
  54.9 6.0 %near_shards.1 = (bf16[128,8192]{1,0:T(8,128)(2,1)}, bf16[128,2304]{1,0:T(8,128)(2,1)S(1)}, f32[9,4,768]{2,1,0:T(4,128)S(1)}, bf16[256,768]{1,0:T(8,128)(2,1)S(1)}, bf16[256,768]{1,0:T(8,128)(2,1)S(1)}) custom-call(s32[16]{0:T(128)S(1)} %stack.118.table, bf16[128,768]{1,0:T(8,128)(2,1)S(1)} %copy-done.11, bf16[128,4096]{1,0:T(8,128)(2,1)} %copy-done.3, ...), custom_call_target="tpu_custom_call" | custom-call | flops 1811939328 | bytes 4718592 | tf_op jit(solution)/shard_map/near_shards/pallas_call | solution.py:209
  61.0 0.7 copy-done.5
  61.7 0.8 copy-done.8
  62.5 1.5 %collective-permute-done.9.refs_4_ = bf16[256,768]{1,0:T(8,128)(2,1)S(1)} collective-permute-done((bf16[256,768]{1,0:T(8,128)(2,1)S(1)}, bf16[256,768]{1,0:T(8,128)(2,1)S(1)}, u32[]{:S(2)}, u32[]{:S(2)}) %collective-permute-start.9) | collective-permute-done | bytes 393248 | tf_op jit(solution)/shard_map/ppermute | solution.py:39
  64.0 2.9 %far_sums.1 = bf16[32,4,768]{2,1,0:T(4,128)(2,1)} custom-call(s32[16]{0:T(128)S(1)} %stack.118.table, bf16[256,768]{1,0:T(8,128)(2,1)S(1)} %get-tuple-element.30.rot_ref, f32[9,4,768]{2,1,0:T(4,128)S(1)} %get-tuple-element.31.near_ref, bf16[128,4096]{1,0:T(8,128)(2,1)S(1)} %copy-done.4, bf16[128,4864]{1,0:T(8,128)(2,1)S(1)} %copy-done.2, ...), custom_call_target="tpu_custom_call" | custom-call | flops 704643072 | bytes 3670016 | tf_op jit(solution)/shard_map/far_sums/pallas_call | solution.py:230
  67.0 8.9 %all-to-all-start = ((bf16[32,4,768]{2,1,0:T(4,128)(2,1)}), bf16[32,4,768]{2,1,0:T(4,128)(2,1)S(1)}, u32[]{:S(2)}, u32[]{:S(2)}) async-start(bf16[32,4,768]{2,1,0:T(4,128)(2,1)} %far_sums.1), calls=%async_computation | async-start | bytes 393216 | tf_op jit(solution)/shard_map/all_to_all | solution.py:360
  75.9 2.3 %collective-permute-start.11 = (bf16[128,2304]{1,0:T(8,128)(2,1)}, bf16[128,2304]{1,0:T(8,128)(2,1)}, u32[]{:S(2)}, u32[]{:S(2)}) collective-permute-start(bf16[128,2304]{1,0:T(8,128)(2,1)} %copy-done.8), channel_id=1, source_target_pairs={{0,1},{1,0},{64,65},{65,64},{128,129},{129,128},{192,193},{193,192... | collective-permute-start | bytes 1769480 | tf_op jit(solution)/shard_map/ppermute | solution.py:43
  78.2 3.0 %far_grad.1 = (bf16[128,8192]{1,0:T(8,128)(2,1)}, bf16[128,1792]{1,0:T(8,128)(2,1)S(1)}) custom-call(s32[16]{0:T(128)S(1)} %stack.118.table, bf16[256,768]{1,0:T(8,128)(2,1)S(1)} %copy-done.6, bf16[256,768]{1,0:T(8,128)(2,1)S(1)} %collective-permute-done.5.refs_0_, ...), custom_call_target="tpu_custom_call", output_to_operand_aliasing={{0}: (7, {})} | custom-call | flops 704643072 | bytes 3670016 | tf_op jit(solution)/shard_map/far_grad/pallas_call | solution.py:246
  81.2 0.8 copy-done.9
  81.9 3.7 %all-to-all-done = bf16[32,4,768]{2,1,0:T(4,128)(2,1)S(1)} async-done(((bf16[32,4,768]{2,1,0:T(4,128)(2,1)}), bf16[32,4,768]{2,1,0:T(4,128)(2,1)S(1)}, u32[]{:S(2)}, u32[]{:S(2)}) %all-to-all-start) | async-done | bytes 196640 | tf_op jit(solution)/shard_map/all_to_all | solution.py:360
  85.6 0.1 reduce_sum.31
  85.7 0.7 broadcast_in_dim.43
  86.4 2.2 %collective-permute-start.10 = (bf16[128,1792]{1,0:T(8,128)(2,1)}, bf16[128,1792]{1,0:T(8,128)(2,1)S(1)}, u32[]{:S(2)}, u32[]{:S(2)}) collective-permute-start(bf16[128,1792]{1,0:T(8,128)(2,1)} %copy-done.9), channel_id=1, source_target_pairs={{0,1},{1,0},{64,65},{65,64},{128,129},{129,128},{192,193},{193,192... | collective-permute-start | bytes 1376264 | tf_op jit(solution)/shard_map/ppermute | solution.py:43
  88.6 10.4 %all-to-all-start.1 = ((bf16[16,4,768]{2,1,0:T(4,128)(2,1)}), bf16[16,4,768]{2,1,0:T(4,128)(2,1)S(1)}, u32[]{:S(2)}, u32[]{:S(2)}) async-start(bf16[16,4,768]{2,1,0:T(4,128)(2,1)} %broadcast_in_dim.43), calls=%async_computation.1 | async-start | bytes 196608 | tf_op jit(solution)/shard_map/all_to_all | solution.py:367
  99.0 2.0 %place.2.grad_in = bf16[128,8192]{1,0:T(8,128)(2,1)} custom-call(s32[16]{0:T(128)S(1)} %stack.135.theirs.table, bf16[128,2304]{1,0:T(8,128)(2,1)} %collective-permute-done.11.blocks_ref, bf16[128,8192]{1,0:T(8,128)(2,1)} %get-tuple-element.39.grad_in), custom_call_target="tpu_custom_call", output_to_operand_aliasing={{}: (2, {})} | custom-call | bytes 1179648 | tf_op jit(solution)/shard_map/place/pallas_call | solution.py:280
  101.0 0.0 copy-start.12
  101.0 1.4 %place.3 = bf16[128,8192]{1,0:T(8,128)(2,1)} custom-call(s32[16]{0:T(128)S(1)} %stack.135.theirs.table, bf16[128,1792]{1,0:T(8,128)(2,1)S(1)} %collective-permute-done.10.blocks_ref, bf16[128,8192]{1,0:T(8,128)(2,1)} %place.2.grad_in), custom_call_target="tpu_custom_call", output_to_operand_aliasing={{}: (2, {})} | custom-call | bytes 917504 | tf_op jit(solution)/shard_map/place/pallas_call | solution.py:280
  102.4 8.4 %all-to-all-done.1 = bf16[16,4,768]{2,1,0:T(4,128)(2,1)S(1)} async-done(((bf16[16,4,768]{2,1,0:T(4,128)(2,1)}), bf16[16,4,768]{2,1,0:T(4,128)(2,1)S(1)}, u32[]{:S(2)}, u32[]{:S(2)}) %all-to-all-start.1) | async-done | bytes 98336 | tf_op jit(solution)/shard_map/all_to_all | solution.py:367
  110.7 0.1 convert_reduce_fusion
  110.8 0.6 multiply_divide_fusion
  (32 shorter events, 0.1 us)
Async XLA Ops:
  0.6 14.8 %copy-start.13 = (s32[1,8]{1,0:T(1,128)S(1)}, s32[1,8]{1,0:T(1,128)}, u32[]{:S(2)}) copy-start(s32[1,8]{1,0:T(1,128)} %param.8) | copy-start | bytes 100
  0.6 15.6 %copy-start.7 = (bf16[128,768]{1,0:T(8,128)(2,1)S(1)}, bf16[128,768]{1,0:T(8,128)(2,1)}, u32[]{:S(2)}) copy-start(bf16[128,768]{1,0:T(8,128)(2,1)} %cot_ref.1) | copy-start | bytes 589828
  0.7 15.6 %copy-start = (bf16[128,8192]{1,0:T(8,128)(2,1)S(1)}, bf16[128,8192]{1,0:T(8,128)(2,1)}, u32[]{:S(2)}) copy-start(bf16[128,8192]{1,0:T(8,128)(2,1)} %feats_ref.1) | copy-start | bytes 6291460
  10.9 13.1 %collective-permute-start.1 = (bf16[512,768]{1,0:T(8,128)(2,1)S(1)}, bf16[512,768]{1,0:T(8,128)(2,1)}, u32[]{:S(2)}, u32[]{:S(2)}) collective-permute-start(bf16[512,768]{1,0:T(8,128)(2,1)S(1)} %all_gather.3), channel_id=1, source_target_pairs={{0,2},{1,7},{64,66},{65,71},{128,130},{129,135},{192,194},{193,199... | collective-permute-start | bytes 2359304 | tf_op jit(solution)/shard_map/ppermute | solution.py:39
  12.9 13.1 %collective-permute-start.2 = (bf16[512,768]{1,0:T(8,128)(2,1)S(1)}, bf16[512,768]{1,0:T(8,128)(2,1)}, u32[]{:S(2)}, u32[]{:S(2)}) collective-permute-start(bf16[512,768]{1,0:T(8,128)(2,1)S(1)} %all_gather.3), channel_id=1, source_target_pairs={{0,8},{1,57},{64,72},{65,121},{128,136},{129,185},{192,200},{193,2... | collective-permute-start | bytes 2359304 | tf_op jit(solution)/shard_map/ppermute | solution.py:39
  18.2 1.0 copy-start.3
  19.1 0.7 copy-start.10
  19.8 35.1 %copy-start.11 = (bf16[128,768]{1,0:T(8,128)(2,1)S(1)}, bf16[128,768]{1,0:T(8,128)(2,1)}, u32[]{:S(2)}) copy-start(bf16[128,768]{1,0:T(8,128)(2,1)} %copy-done.10) | copy-start | bytes 589828
  19.8 13.0 %collective-permute-start = (bf16[128,4864]{1,0:T(8,128)(2,1)}, bf16[128,4864]{1,0:T(8,128)(2,1)S(1)}, u32[]{:S(2)}, u32[]{:S(2)}) collective-permute-start(bf16[128,4864]{1,0:T(8,128)(2,1)} %get-tuple-element.24), channel_id=1, source_target_pairs={{0,1},{1,0},{64,65},{65,64},{128,129},{129,128},{192,193},{193,192... | collective-permute-start | bytes 3735560 | tf_op jit(solution)/shard_map/ppermute | solution.py:43
  26.0 17.8 %collective-permute-start.3 = (bf16[512,768]{1,0:T(8,128)(2,1)}, bf16[512,768]{1,0:T(8,128)(2,1)}, u32[]{:S(2)}, u32[]{:S(2)}) collective-permute-start(bf16[512,768]{1,0:T(8,128)(2,1)} %collective-permute-done.2.refs_2_), channel_id=1, source_target_pairs={{0,2},{1,7},{64,66},{65,71},{128,130},{129,135},{192,194},{193,199... | collective-permute-start | bytes 2359304 | tf_op jit(solution)/shard_map/ppermute | solution.py:39
  27.9 19.5 %collective-permute-start.4 = (bf16[512,768]{1,0:T(8,128)(2,1)}, bf16[512,768]{1,0:T(8,128)(2,1)}, u32[]{:S(2)}, u32[]{:S(2)}) collective-permute-start(bf16[512,768]{1,0:T(8,128)(2,1)} %collective-permute-done.1.refs_1_), channel_id=1, source_target_pairs={{0,57},{1,8},{64,121},{65,72},{128,185},{129,136},{192,249},{193,2... | collective-permute-start | bytes 2359304 | tf_op jit(solution)/shard_map/ppermute | solution.py:39
  32.8 10.9 %copy-start.1 = (bf16[128,4864]{1,0:T(8,128)(2,1)}, bf16[128,4864]{1,0:T(8,128)(2,1)S(1)}, u32[]{:S(2)}) copy-start(bf16[128,4864]{1,0:T(8,128)(2,1)S(1)} %collective-permute-done.other_ref) | copy-start | bytes 3735556
  32.8 17.6 %collective-permute-start.5 = (bf16[256,768]{1,0:T(8,128)(2,1)S(1)}, bf16[256,768]{1,0:T(8,128)(2,1)S(1)}, u32[]{:S(2)}, u32[]{:S(2)}) collective-permute-start(bf16[256,768]{1,0:T(8,128)(2,1)S(1)} %constant_dynamic-slice_fusion.1), channel_id=1, source_target_pairs={{0,2},{1,7},{64,66},{65,71},{128,130},{129,135},{192,194},{193,199... | collective-permute-start | bytes 1179656 | tf_op jit(solution)/shard_map/ppermute | solution.py:39
  37.7 12.7 %collective-permute-start.6 = (bf16[256,768]{1,0:T(8,128)(2,1)S(1)}, bf16[256,768]{1,0:T(8,128)(2,1)S(1)}, u32[]{:S(2)}, u32[]{:S(2)}) collective-permute-start(bf16[256,768]{1,0:T(8,128)(2,1)S(1)} %constant_dynamic-slice_fusion), channel_id=1, source_target_pairs={{0,8},{1,57},{64,72},{65,121},{128,136},{129,185},{192,200},{193,2... | collective-permute-start | bytes 1179656 | tf_op jit(solution)/shard_map/ppermute | solution.py:39
  43.7 20.3 %collective-permute-start.7 = (bf16[512,768]{1,0:T(8,128)(2,1)}, bf16[512,768]{1,0:T(8,128)(2,1)S(1)}, u32[]{:S(2)}, u32[]{:S(2)}) collective-permute-start(bf16[512,768]{1,0:T(8,128)(2,1)} %collective-permute-done.3.refs_3_), channel_id=1, source_target_pairs={{0,2},{1,7},{64,66},{65,71},{128,130},{129,135},{192,194},{193,199... | collective-permute-start | bytes 2359304 | tf_op jit(solution)/shard_map/ppermute | solution.py:39
  47.4 16.6 %collective-permute-start.8 = (bf16[512,768]{1,0:T(8,128)(2,1)}, bf16[512,768]{1,0:T(8,128)(2,1)S(1)}, u32[]{:S(2)}, u32[]{:S(2)}) collective-permute-start(bf16[512,768]{1,0:T(8,128)(2,1)} %collective-permute-done.4.refs_4_), channel_id=1, source_target_pairs={{0,8},{1,57},{64,72},{65,121},{128,136},{129,185},{192,200},{193,2... | collective-permute-start | bytes 2359304 | tf_op jit(solution)/shard_map/ppermute | solution.py:39
  50.4 13.6 %collective-permute-start.9 = (bf16[256,768]{1,0:T(8,128)(2,1)S(1)}, bf16[256,768]{1,0:T(8,128)(2,1)S(1)}, u32[]{:S(2)}, u32[]{:S(2)}) collective-permute-start(bf16[256,768]{1,0:T(8,128)(2,1)S(1)} %constant_dynamic-slice_fusion.2), channel_id=1, source_target_pairs={{0,10},{1,63},{64,74},{65,127},{128,138},{129,191},{192,202},{193,... | collective-permute-start | bytes 1179656 | tf_op jit(solution)/shard_map/ppermute | solution.py:39
  54.9 9.1 %copy-start.2 = (bf16[128,4864]{1,0:T(8,128)(2,1)S(1)}, bf16[128,4864]{1,0:T(8,128)(2,1)}, u32[]{:S(2)}) copy-start(bf16[128,4864]{1,0:T(8,128)(2,1)} %copy-done.1) | copy-start | bytes 3735556
  54.9 9.1 %copy-start.4 = (bf16[128,4096]{1,0:T(8,128)(2,1)S(1)}, bf16[128,4096]{1,0:T(8,128)(2,1)}, u32[]{:S(2)}) copy-start(bf16[128,4096]{1,0:T(8,128)(2,1)} %copy-done.3) | copy-start | bytes 3145732
  61.0 0.8 copy-start.5
  61.7 0.8 copy-start.8
  64.0 14.1 %copy-start.6 = (bf16[256,768]{1,0:T(8,128)(2,1)S(1)}, bf16[256,768]{1,0:T(8,128)(2,1)}, u32[]{:S(2)}) copy-start(bf16[256,768]{1,0:T(8,128)(2,1)} %copy-done.5) | copy-start | bytes 1179652
  67.0 18.6 %all-to-all-start = ((bf16[32,4,768]{2,1,0:T(4,128)(2,1)}), bf16[32,4,768]{2,1,0:T(4,128)(2,1)S(1)}, u32[]{:S(2)}, u32[]{:S(2)}) async-start(bf16[32,4,768]{2,1,0:T(4,128)(2,1)} %far_sums.1), calls=%async_computation | async-start | bytes 393216 | tf_op jit(solution)/shard_map/all_to_all | solution.py:360
  75.9 23.1 %collective-permute-start.11 = (bf16[128,2304]{1,0:T(8,128)(2,1)}, bf16[128,2304]{1,0:T(8,128)(2,1)}, u32[]{:S(2)}, u32[]{:S(2)}) collective-permute-start(bf16[128,2304]{1,0:T(8,128)(2,1)} %copy-done.8), channel_id=1, source_target_pairs={{0,1},{1,0},{64,65},{65,64},{128,129},{129,128},{192,193},{193,192... | collective-permute-start | bytes 1769480 | tf_op jit(solution)/shard_map/ppermute | solution.py:43
  81.2 0.8 copy-start.9
  86.4 14.6 %collective-permute-start.10 = (bf16[128,1792]{1,0:T(8,128)(2,1)}, bf16[128,1792]{1,0:T(8,128)(2,1)S(1)}, u32[]{:S(2)}, u32[]{:S(2)}) collective-permute-start(bf16[128,1792]{1,0:T(8,128)(2,1)} %copy-done.9), channel_id=1, source_target_pairs={{0,1},{1,0},{64,65},{65,64},{128,129},{129,128},{192,193},{193,192... | collective-permute-start | bytes 1376264 | tf_op jit(solution)/shard_map/ppermute | solution.py:43
  88.6 22.1 %all-to-all-start.1 = ((bf16[16,4,768]{2,1,0:T(4,128)(2,1)}), bf16[16,4,768]{2,1,0:T(4,128)(2,1)S(1)}, u32[]{:S(2)}, u32[]{:S(2)}) async-start(bf16[16,4,768]{2,1,0:T(4,128)(2,1)} %broadcast_in_dim.43), calls=%async_computation.1 | async-start | bytes 196608 | tf_op jit(solution)/shard_map/all_to_all | solution.py:367
  101.0 9.8 %copy-start.12 = (f32[4,768]{1,0:T(4,128)S(1)}, f32[4,768]{1,0:T(4,128)}, u32[]{:S(2)}) copy-start(f32[4,768]{1,0:T(4,128)} %param.11) | copy-start | bytes 36868

commit v10 on v9

--- a/solution.py
+++ b/solution.py
@@ -202,6 +202,36 @@
     )(table, theirs, *turn, cotangent, feats)
 
 
+def halves_kernel(core, *refs):
+    count = len(refs) // 2
+    sems = refs[-1]
+    copies = []
+    for at, (whole, half) in enumerate(zip(refs[:count], refs[count:-1])):
+        rows = half.shape[0]
+        mine = pl.ds(pl.multiple_of(core[0] * rows, rows), rows)
+        copies.append(pltpu.make_async_copy(whole.at[mine], half, sems.at[at]))
+    for copy in copies:
+        copy.start()
+    for copy in copies:
+        copy.wait()
+
+
+def halves(core, arrays, rows):
+    half = jax.ShapeDtypeStruct((rows, arrays[0].shape[1]), arrays[0].dtype)
+    return pl.pallas_call(
+        halves_kernel,
+        out_shape=(half,) * len(arrays),
+        in_specs=[SMEM_SPEC] + [ANY_SPEC] * len(arrays),
+        out_specs=(VMEM_SPEC,) * len(arrays),
+        scratch_shapes=[pltpu.SemaphoreType.DMA((len(arrays),))],
+        cost_estimate=pl.CostEstimate(
+            flops=0, bytes_accessed=4 * len(arrays) * half.size, transcendentals=0
+        ),
+        compiler_params=pltpu.CompilerParams(vmem_limit_bytes=VMEM),
+        name="halves",
+    )(core, *arrays)
+
+
 def near_shards(table, mine, other, rot, weights, rows, width):
     tokens = mine.shape[0]
     cols = rot.shape[1]
@@ -303,10 +333,10 @@
         + [owner(1, 0, 0), owner(1, 0, 1)]
         + [owner(0, 1, 0), owner(0, 1, 1)]
         + [owner(1, 1, 0), owner(1, 1, 1)]
-        + [owner(-1, 1, 0), owner(-1, 1, 1)]
+        + [owner(1, -1, 0), owner(1, -1, 1)]
         + [owner(2, 0, core), owner(0, 2, core)]
-        + [owner(2, 1, 0), owner(2, 1, 1)]
-        + [owner(-1, 2, 0), owner(-1, 2, 1)]
+        + [owner(1, 2, 0), owner(1, 2, 1)]
+        + [owner(2, -1, 0), owner(2, -1, 1)]
         + [owner(2, 2, core)]
     )
 
@@ -326,35 +356,34 @@
     pairs = [[2 * chip, 2 * chip + 1] for chip in range(NX * NYL)]
     chip_weight = lax.all_gather(weight, "tensor", axis=0, tiled=True, axis_index_groups=pairs)
 
+    from_y = send(chip_weight, 0, 1)
     from_x = send(chip_weight, 1, 0)
-    from_y = send(chip_weight, 0, 1)
 
     indices = place_in * tokens + jnp.arange(tokens, dtype=jnp.int32)
     turn = rotation(token_positions(doc_lengths[0], indices))
     mine, mine_feats, to_other = pack(table, theirs, turn, key_cotangent, activations, rows)
     feats = (mine_feats, swap(to_other))
-    from_x, from_y, _ = lax.optimization_barrier((from_x, from_y, to_other))
-
-    def my_half(value):
-        return lax.dynamic_slice_in_dim(value, core * rows, rows, axis=0)
-
-    from_xy = send(from_y, 1, 0)
-    from_yx = send(from_x, 0, 1, cross=True)
-    half_x, half_y, _ = lax.optimization_barrier((my_half(from_x), my_half(from_y), feats[1]))
+    from_x, _ = lax.optimization_barrier((from_x, to_other))
+
+    from_xy = send(from_x, 0, 1)
+    from_yx = send(from_y, 1, 0, cross=True)
+    half_x, half_y = halves(core.reshape(1), [from_x, from_y], rows)
+    half_x, half_y, _ = lax.optimization_barrier((half_x, half_y, feats[1]))
     from_xy, _, _ = lax.optimization_barrier((from_xy, half_x, half_y))
 
-    far_x = send(from_xy, 1, 0)
-    far_y = send(from_yx, 0, 1)
+    far_y = send(from_xy, 0, 1)
+    far_x = send(from_yx, 1, 0)
     far_xx = send(half_x, 1, 0)
     far_yy = send(half_y, 0, 1)
-    half_xy, _, _ = lax.optimization_barrier((my_half(from_xy), far_xx, far_yy))
+    half_xy = lax.dynamic_slice_in_dim(from_xy, core * rows, rows, axis=0)
+    half_xy, _, _ = lax.optimization_barrier((half_xy, far_xx, far_yy))
     far = send(half_xy, 1, 1)
 
     near = [weight, from_x, from_y, from_xy, from_yx]
     grad, sent_near, sums_near, rot, rot_again = near_shards(
         table, *feats, mine, near, rows, activations.shape[1]
     )
-    fars = [far_xx, far_yy, far_x, far_y, far]
+    fars = [far_xx, far_yy, far_y, far_x, far]
     at_hand = sums_near.shape[0]
     sums = far_sums(table, *feats, rot, fars, sums_near, rows, devices)
     shares = lax.all_to_all(sums, "tensor", split_axis=0, concat_axis=0, tiled=True)

time: 112 us -> 111 us (level)
  local copies, waits for them, and re-layouts: 8 us -> 5.9 us
    dynamic_slice x3 -> x1, local copies, waits for them, and re-layouts: 3.12 us -> 1.03 us  [per_device(): half_xy = lax.dynamic_slice_in_dim(from_xy, core * rows, rows, axis=0)]
    pallas_call x0 -> x1, Pallas kernels: none -> 1.88 us  [halves(): pl.pallas_call(halves_kernel, out_shape=(half,) * len(arrays), in_specs=[...]
    all_to_all x1, starting transfers between devices: 10.4 us -> 12.1 us  [per_device(): lax.all_to_all(share, 'dp', split_axis=0, concat_axis=0, tiled=True)]
    all_to_all x1, starting transfers between devices: 8.87 us -> 7.47 us  [per_device(): lax.all_to_all(sums, 'tensor', split_axis=0, concat_axis=0, tiled=True)]
  transfers between devices with their start and end apart: 14 -> 14, of which waited for: 5 -> 5; matrix products, arithmetic and copies ran while one was open for 4% -> 2% of each run, Pallas kernels for 13% -> 14%
where the time goes in v10:
time: 111 us; the launch traced here: 110 us
  starting transfers between devices  56.4 us (51%)
  Pallas kernels  18.1 us (16%)
  waiting for transfers between devices  16.6 us (15%)
  blocking collectives  8.87 us (8%)
  local copies, waits for them, and re-layouts  5.9 us (5%)
  other arithmetic  2.77 us (2%)
  between operations  1.37 us (1%)
    ppermute x9, starting transfers between devices, send(): return lax.ppermute(value, AXES, permutation(target))  30.2 us
    all_to_all x1, starting transfers between devices, per_device(): lax.all_to_all(share, 'dp', split_axis=0, concat_axis=0, tiled=True)  12.1 us
    all_gather x1, blocking collectives, per_device(): lax.all_gather(weight, 'tensor', axis=0, tiled=True, axis_index_groups=pa...  8.87 us
    all_to_all x1, waiting for transfers between devices, per_device(): lax.all_to_all(share, 'dp', split_axis=0, concat_axis=0, tiled=True)  8.39 us
    all_to_all x1, starting transfers between devices, per_device(): lax.all_to_all(sums, 'tensor', split_axis=0, concat_axis=0, tiled=True)  7.47 us
    ppermute x3, starting transfers between devices, swap(): lax.ppermute(value, AXES, permutation(lambda x, y, z, core: (x, y, z, cor...  6.6 us
    pallas_call x1, Pallas kernels, near_shards(): pl.pallas_call(functools.partial(near_kernel, rows, len(weights)), out_sh...  6.03 us
    ppermute x9, waiting for transfers between devices, send(): return lax.ppermute(value, AXES, permutation(target))  4.49 us
  transfers between devices with their start and end apart: 14, of which 5 were waited for; matrix products, arithmetic and copies ran while one was open for 2% of the time, Pallas kernels for 14%

profile of v10, /device:TPU:1, one launch (start us, length us, event | category | flops | bytes accessed | tf_op | source)
XLA Modules:
  0.0 109.9 jit_solution(8297512968364724122)
XLA Ops:
  0.7 1.4 %fusion.2.refs_0_ = bf16[256,768]{1,0:T(8,128)(2,1)S(1)} fusion(s32[256,768]{1,0:T(8,128)} %param.9, s32[4,768]{1,0:T(4,128)} %param.10, f32[4,768]{1,0:T(4,128)} %param.11), kind=kLoop, calls=%fused_computation.3 | loop fusion | flops 786432 | bytes 1204224 | tf_op jit(solution)/shard_map/convert_element_type | solution.py:66
  2.1 8.9 %all_gather.3 = bf16[512,768]{1,0:T(8,128)(2,1)S(1)} all-gather(bf16[256,768]{1,0:T(8,128)(2,1)S(1)} %fusion.2.refs_0_), channel_id=1, replica_groups={{0,1},{2,3},{4,5},{6,7},{8,9},{10,11},{12,13},{14,15},{16,17},{18,19},{..., dimensions={0}, use_global_device_ids=true | all-gather | bytes 1179648 | tf_op jit(solution)/shard_map/all_gather | solution.py:357
  10.9 1.9 %collective-permute-start.1 = (bf16[512,768]{1,0:T(8,128)(2,1)S(1)}, bf16[512,768]{1,0:T(8,128)(2,1)}, u32[]{:S(2)}, u32[]{:S(2)}) collective-permute-start(bf16[512,768]{1,0:T(8,128)(2,1)S(1)} %all_gather.3), channel_id=1, source_target_pairs={{0,2},{1,7},{64,66},{65,71},{128,130},{129,135},{192,194},{193,199... | collective-permute-start | bytes 2359304 | tf_op jit(solution)/shard_map/ppermute | solution.py:39
  12.9 2.2 %collective-permute-start.2 = (bf16[512,768]{1,0:T(8,128)(2,1)S(1)}, bf16[512,768]{1,0:T(8,128)(2,1)}, u32[]{:S(2)}, u32[]{:S(2)}) collective-permute-start(bf16[512,768]{1,0:T(8,128)(2,1)S(1)} %all_gather.3), channel_id=1, source_target_pairs={{0,8},{1,57},{64,72},{65,121},{128,136},{129,185},{192,200},{193,2... | collective-permute-start | bytes 2359304 | tf_op jit(solution)/shard_map/ppermute | solution.py:39
  15.4 0.1 select_reduce_fusion.1
  15.5 0.1 select_reduce_fusion
  15.6 0.1 stack.118.table
  15.7 0.1 stack.135.theirs.table
  15.8 0.3 multiply_sine_fusion
  16.1 0.1 pad_maximum_fusion
  16.3 0.9 pack.1
  17.2 0.9 copy-done.3
  18.1 0.7 copy-done.10
  18.8 2.1 %collective-permute-start = (bf16[128,4864]{1,0:T(8,128)(2,1)S(1)}, bf16[128,4864]{1,0:T(8,128)(2,1)S(1)}, u32[]{:S(2)}, u32[]{:S(2)}) collective-permute-start(bf16[128,4864]{1,0:T(8,128)(2,1)S(1)} %get-tuple-element.25), channel_id=1, source_target_pairs={{0,1},{1,0},{64,65},{65,64},{128,129},{129,128},{192,193},{193,192... | collective-permute-start | bytes 3735560 | tf_op jit(solution)/shard_map/ppermute | solution.py:43
  20.9 3.1 %collective-permute-done.1.refs_0_.refs_1_ = bf16[512,768]{1,0:T(8,128)(2,1)} collective-permute-done((bf16[512,768]{1,0:T(8,128)(2,1)S(1)}, bf16[512,768]{1,0:T(8,128)(2,1)}, u32[]{:S(2)}, u32[]{:S(2)}) %collective-permute-start.1) | collective-permute-done | bytes 786464 | tf_op jit(solution)/shard_map/ppermute | solution.py:39
  24.1 1.9 %collective-permute-start.3 = (bf16[512,768]{1,0:T(8,128)(2,1)}, bf16[512,768]{1,0:T(8,128)(2,1)}, u32[]{:S(2)}, u32[]{:S(2)}) collective-permute-start(bf16[512,768]{1,0:T(8,128)(2,1)} %collective-permute-done.1.refs_0_.refs_1_), channel_id=1, source_target_pairs={{0,8},{1,57},{64,72},{65,121},{128,136},{129,185},{192,200},{193,2... | collective-permute-start | bytes 2359304 | tf_op jit(solution)/shard_map/ppermute | solution.py:39
  26.0 0.0 collective-permute-done.2.refs_1_.refs_2_
  26.0 2.8 %collective-permute-start.4 = (bf16[512,768]{1,0:T(8,128)(2,1)}, bf16[512,768]{1,0:T(8,128)(2,1)}, u32[]{:S(2)}, u32[]{:S(2)}) collective-permute-start(bf16[512,768]{1,0:T(8,128)(2,1)} %collective-permute-done.2.refs_1_.refs_2_), channel_id=1, source_target_pairs={{0,7},{1,2},{64,71},{65,66},{128,135},{129,130},{192,199},{193,194... | collective-permute-start | bytes 2359304 | tf_op jit(solution)/shard_map/ppermute | solution.py:39
  28.7 1.9 %halves.1 = (bf16[256,768]{1,0:T(8,128)(2,1)S(1)}, bf16[256,768]{1,0:T(8,128)(2,1)}) custom-call(s32[1]{0:T(128)} %bitcast.35.core, bf16[512,768]{1,0:T(8,128)(2,1)} %collective-permute-done.1.refs_0_.refs_1_, bf16[512,768]{1,0:T(8,128)(2,1)} %collective-permute-done.2.refs_1_.refs_2_), custom_call_target="tpu_custom_call" | custom-call | bytes 1572864 | tf_op jit(solution)/shard_map/halves/pallas_call | solution.py:221
  30.6 0.0 collective-permute-done.other_ref
  30.7 6.1 %collective-permute-start.5 = (bf16[256,768]{1,0:T(8,128)(2,1)S(1)}, bf16[256,768]{1,0:T(8,128)(2,1)S(1)}, u32[]{:S(2)}, u32[]{:S(2)}) collective-permute-start(bf16[256,768]{1,0:T(8,128)(2,1)S(1)} %get-tuple-element.29), channel_id=1, source_target_pairs={{0,2},{1,7},{64,66},{65,71},{128,130},{129,135},{192,194},{193,199... | collective-permute-start | bytes 1179656 | tf_op jit(solution)/shard_map/ppermute | solution.py:39
  36.7 4.9 %collective-permute-start.6 = (bf16[256,768]{1,0:T(8,128)(2,1)}, bf16[256,768]{1,0:T(8,128)(2,1)S(1)}, u32[]{:S(2)}, u32[]{:S(2)}) collective-permute-start(bf16[256,768]{1,0:T(8,128)(2,1)} %get-tuple-element.30), channel_id=1, source_target_pairs={{0,8},{1,57},{64,72},{65,121},{128,136},{129,185},{192,200},{193,2... | collective-permute-start | bytes 1179656 | tf_op jit(solution)/shard_map/ppermute | solution.py:39
  41.6 0.0 collective-permute-done.3.refs_3_
  41.6 1.9 %collective-permute-start.7 = (bf16[512,768]{1,0:T(8,128)(2,1)}, bf16[512,768]{1,0:T(8,128)(2,1)S(1)}, u32[]{:S(2)}, u32[]{:S(2)}) collective-permute-start(bf16[512,768]{1,0:T(8,128)(2,1)} %collective-permute-done.3.refs_3_), channel_id=1, source_target_pairs={{0,8},{1,57},{64,72},{65,121},{128,136},{129,185},{192,200},{193,2... | collective-permute-start | bytes 2359304 | tf_op jit(solution)/shard_map/ppermute | solution.py:39
  43.5 0.6 collective-permute-done.4.refs_4_
  44.1 4.7 %collective-permute-start.8 = (bf16[512,768]{1,0:T(8,128)(2,1)}, bf16[512,768]{1,0:T(8,128)(2,1)S(1)}, u32[]{:S(2)}, u32[]{:S(2)}) collective-permute-start(bf16[512,768]{1,0:T(8,128)(2,1)} %collective-permute-done.4.refs_4_), channel_id=1, source_target_pairs={{0,2},{1,7},{64,66},{65,71},{128,130},{129,135},{192,194},{193,199... | collective-permute-start | bytes 2359304 | tf_op jit(solution)/shard_map/ppermute | solution.py:39
  48.8 1.0 constant_dynamic-slice_fusion
  49.9 4.0 %collective-permute-start.9 = (bf16[256,768]{1,0:T(8,128)(2,1)S(1)}, bf16[256,768]{1,0:T(8,128)(2,1)S(1)}, u32[]{:S(2)}, u32[]{:S(2)}) collective-permute-start(bf16[256,768]{1,0:T(8,128)(2,1)S(1)} %constant_dynamic-slice_fusion), channel_id=1, source_target_pairs={{0,10},{1,63},{64,74},{65,127},{128,138},{129,191},{192,202},{193,... | collective-permute-start | bytes 1179656 | tf_op jit(solution)/shard_map/ppermute | solution.py:39
  53.9 6.0 %near_shards.1 = (bf16[128,8192]{1,0:T(8,128)(2,1)}, bf16[128,2304]{1,0:T(8,128)(2,1)S(1)}, f32[9,4,768]{2,1,0:T(4,128)S(1)}, bf16[256,768]{1,0:T(8,128)(2,1)S(1)}, bf16[256,768]{1,0:T(8,128)(2,1)S(1)}) custom-call(s32[16]{0:T(128)S(1)} %stack.118.table, bf16[128,768]{1,0:T(8,128)(2,1)S(1)} %copy-done.11, bf16[128,4096]{1,0:T(8,128)(2,1)} %copy-done.3, ...), custom_call_target="tpu_custom_call" | custom-call | flops 1811939328 | bytes 4718592 | tf_op jit(solution)/shard_map/near_shards/pallas_call | solution.py:239
  59.9 0.7 copy-done.5
  60.7 0.8 copy-done.8
  61.5 0.8 collective-permute-done.8.refs_3_
  62.3 2.9 %far_sums.1 = bf16[32,4,768]{2,1,0:T(4,128)(2,1)} custom-call(s32[16]{0:T(128)S(1)} %stack.118.table, bf16[256,768]{1,0:T(8,128)(2,1)S(1)} %get-tuple-element.32.rot_ref, f32[9,4,768]{2,1,0:T(4,128)S(1)} %get-tuple-element.33.near_ref, bf16[128,4096]{1,0:T(8,128)(2,1)S(1)} %copy-done.4, bf16[128,4864]{1,0:T(8,128)(2,1)S(1)} %copy-done.2, ...), custom_call_target="tpu_custom_call" | custom-call | flops 704643072 | bytes 3670016 | tf_op jit(solution)/shard_map/far_sums/pallas_call | solution.py:260
  65.2 7.5 %all-to-all-start = ((bf16[32,4,768]{2,1,0:T(4,128)(2,1)}), bf16[32,4,768]{2,1,0:T(4,128)(2,1)S(1)}, u32[]{:S(2)}, u32[]{:S(2)}) async-start(bf16[32,4,768]{2,1,0:T(4,128)(2,1)} %far_sums.1), calls=%async_computation | async-start | bytes 393216 | tf_op jit(solution)/shard_map/all_to_all | solution.py:389
  72.7 2.3 %collective-permute-start.11 = (bf16[128,2304]{1,0:T(8,128)(2,1)}, bf16[128,2304]{1,0:T(8,128)(2,1)}, u32[]{:S(2)}, u32[]{:S(2)}) collective-permute-start(bf16[128,2304]{1,0:T(8,128)(2,1)} %copy-done.8), channel_id=1, source_target_pairs={{0,1},{1,0},{64,65},{65,64},{128,129},{129,128},{192,193},{193,192... | collective-permute-start | bytes 1769480 | tf_op jit(solution)/shard_map/ppermute | solution.py:43
  75.0 3.0 %far_grad.1 = (bf16[128,8192]{1,0:T(8,128)(2,1)}, bf16[128,1792]{1,0:T(8,128)(2,1)S(1)}) custom-call(s32[16]{0:T(128)S(1)} %stack.118.table, bf16[256,768]{1,0:T(8,128)(2,1)S(1)} %copy-done.6, bf16[256,768]{1,0:T(8,128)(2,1)S(1)} %collective-permute-done.5.refs_0_, ...), custom_call_target="tpu_custom_call", output_to_operand_aliasing={{0}: (7, {})} | custom-call | flops 704643072 | bytes 3670016 | tf_op jit(solution)/shard_map/far_grad/pallas_call | solution.py:276
  78.0 0.8 copy-done.9
  78.8 3.7 %all-to-all-done = bf16[32,4,768]{2,1,0:T(4,128)(2,1)S(1)} async-done(((bf16[32,4,768]{2,1,0:T(4,128)(2,1)}), bf16[32,4,768]{2,1,0:T(4,128)(2,1)S(1)}, u32[]{:S(2)}, u32[]{:S(2)}) %all-to-all-start) | async-done | bytes 196640 | tf_op jit(solution)/shard_map/all_to_all | solution.py:389
  82.4 0.1 reduce_sum.31
  82.5 0.7 broadcast_in_dim.43
  83.2 2.2 %collective-permute-start.10 = (bf16[128,1792]{1,0:T(8,128)(2,1)}, bf16[128,1792]{1,0:T(8,128)(2,1)S(1)}, u32[]{:S(2)}, u32[]{:S(2)}) collective-permute-start(bf16[128,1792]{1,0:T(8,128)(2,1)} %copy-done.9), channel_id=1, source_target_pairs={{0,1},{1,0},{64,65},{65,64},{128,129},{129,128},{192,193},{193,192... | collective-permute-start | bytes 1376264 | tf_op jit(solution)/shard_map/ppermute | solution.py:43
  85.4 12.1 %all-to-all-start.1 = ((bf16[16,4,768]{2,1,0:T(4,128)(2,1)}), bf16[16,4,768]{2,1,0:T(4,128)(2,1)S(1)}, u32[]{:S(2)}, u32[]{:S(2)}) async-start(bf16[16,4,768]{2,1,0:T(4,128)(2,1)} %broadcast_in_dim.43), calls=%async_computation.1 | async-start | bytes 196608 | tf_op jit(solution)/shard_map/all_to_all | solution.py:396
  97.5 2.0 %place.2.grad_in = bf16[128,8192]{1,0:T(8,128)(2,1)} custom-call(s32[16]{0:T(128)S(1)} %stack.135.theirs.table, bf16[128,2304]{1,0:T(8,128)(2,1)} %collective-permute-done.11.blocks_ref, bf16[128,8192]{1,0:T(8,128)(2,1)} %get-tuple-element.41.grad_in), custom_call_target="tpu_custom_call", output_to_operand_aliasing={{}: (2, {})} | custom-call | bytes 1179648 | tf_op jit(solution)/shard_map/place/pallas_call | solution.py:310
  99.5 0.0 copy-start.12
  99.5 1.4 %place.3 = bf16[128,8192]{1,0:T(8,128)(2,1)} custom-call(s32[16]{0:T(128)S(1)} %stack.135.theirs.table, bf16[128,1792]{1,0:T(8,128)(2,1)S(1)} %collective-permute-done.10.blocks_ref, bf16[128,8192]{1,0:T(8,128)(2,1)} %place.2.grad_in), custom_call_target="tpu_custom_call", output_to_operand_aliasing={{}: (2, {})} | custom-call | bytes 917504 | tf_op jit(solution)/shard_map/place/pallas_call | solution.py:310
  100.9 8.4 %all-to-all-done.1 = bf16[16,4,768]{2,1,0:T(4,128)(2,1)S(1)} async-done(((bf16[16,4,768]{2,1,0:T(4,128)(2,1)}), bf16[16,4,768]{2,1,0:T(4,128)(2,1)S(1)}, u32[]{:S(2)}, u32[]{:S(2)}) %all-to-all-start.1) | async-done | bytes 98336 | tf_op jit(solution)/shard_map/all_to_all | solution.py:396
  109.3 0.1 convert_reduce_fusion
  109.3 0.6 multiply_divide_fusion
  (31 shorter events, 0.1 us)
Async XLA Ops:
  0.6 14.8 %copy-start.13 = (s32[1,8]{1,0:T(1,128)S(1)}, s32[1,8]{1,0:T(1,128)}, u32[]{:S(2)}) copy-start(s32[1,8]{1,0:T(1,128)} %param.8) | copy-start | bytes 100
  0.6 15.6 %copy-start.7 = (bf16[128,768]{1,0:T(8,128)(2,1)S(1)}, bf16[128,768]{1,0:T(8,128)(2,1)}, u32[]{:S(2)}) copy-start(bf16[128,768]{1,0:T(8,128)(2,1)} %cot_ref.1) | copy-start | bytes 589828
  0.7 15.6 %copy-start = (bf16[128,8192]{1,0:T(8,128)(2,1)S(1)}, bf16[128,8192]{1,0:T(8,128)(2,1)}, u32[]{:S(2)}) copy-start(bf16[128,8192]{1,0:T(8,128)(2,1)} %feats_ref.1) | copy-start | bytes 6291460
  10.9 13.1 %collective-permute-start.1 = (bf16[512,768]{1,0:T(8,128)(2,1)S(1)}, bf16[512,768]{1,0:T(8,128)(2,1)}, u32[]{:S(2)}, u32[]{:S(2)}) collective-permute-start(bf16[512,768]{1,0:T(8,128)(2,1)S(1)} %all_gather.3), channel_id=1, source_target_pairs={{0,2},{1,7},{64,66},{65,71},{128,130},{129,135},{192,194},{193,199... | collective-permute-start | bytes 2359304 | tf_op jit(solution)/shard_map/ppermute | solution.py:39
  12.9 13.1 %collective-permute-start.2 = (bf16[512,768]{1,0:T(8,128)(2,1)S(1)}, bf16[512,768]{1,0:T(8,128)(2,1)}, u32[]{:S(2)}, u32[]{:S(2)}) collective-permute-start(bf16[512,768]{1,0:T(8,128)(2,1)S(1)} %all_gather.3), channel_id=1, source_target_pairs={{0,8},{1,57},{64,72},{65,121},{128,136},{129,185},{192,200},{193,2... | collective-permute-start | bytes 2359304 | tf_op jit(solution)/shard_map/ppermute | solution.py:39
  17.2 1.0 copy-start.3
  18.1 0.7 copy-start.10
  18.8 35.0 %copy-start.11 = (bf16[128,768]{1,0:T(8,128)(2,1)S(1)}, bf16[128,768]{1,0:T(8,128)(2,1)}, u32[]{:S(2)}) copy-start(bf16[128,768]{1,0:T(8,128)(2,1)} %copy-done.10) | copy-start | bytes 589828
  18.8 11.8 %collective-permute-start = (bf16[128,4864]{1,0:T(8,128)(2,1)S(1)}, bf16[128,4864]{1,0:T(8,128)(2,1)S(1)}, u32[]{:S(2)}, u32[]{:S(2)}) collective-permute-start(bf16[128,4864]{1,0:T(8,128)(2,1)S(1)} %get-tuple-element.25), channel_id=1, source_target_pairs={{0,1},{1,0},{64,65},{65,64},{128,129},{129,128},{192,193},{193,192... | collective-permute-start | bytes 3735560 | tf_op jit(solution)/shard_map/ppermute | solution.py:43
  24.1 17.5 %collective-permute-start.3 = (bf16[512,768]{1,0:T(8,128)(2,1)}, bf16[512,768]{1,0:T(8,128)(2,1)}, u32[]{:S(2)}, u32[]{:S(2)}) collective-permute-start(bf16[512,768]{1,0:T(8,128)(2,1)} %collective-permute-done.1.refs_0_.refs_1_), channel_id=1, source_target_pairs={{0,8},{1,57},{64,72},{65,121},{128,136},{129,185},{192,200},{193,2... | collective-permute-start | bytes 2359304 | tf_op jit(solution)/shard_map/ppermute | solution.py:39
  26.0 18.1 %collective-permute-start.4 = (bf16[512,768]{1,0:T(8,128)(2,1)}, bf16[512,768]{1,0:T(8,128)(2,1)}, u32[]{:S(2)}, u32[]{:S(2)}) collective-permute-start(bf16[512,768]{1,0:T(8,128)(2,1)} %collective-permute-done.2.refs_1_.refs_2_), channel_id=1, source_target_pairs={{0,7},{1,2},{64,71},{65,66},{128,135},{129,130},{192,199},{193,194... | collective-permute-start | bytes 2359304 | tf_op jit(solution)/shard_map/ppermute | solution.py:39
  30.6 12.9 %copy-start.1 = (bf16[128,4864]{1,0:T(8,128)(2,1)}, bf16[128,4864]{1,0:T(8,128)(2,1)S(1)}, u32[]{:S(2)}) copy-start(bf16[128,4864]{1,0:T(8,128)(2,1)S(1)} %collective-permute-done.other_ref) | copy-start | bytes 3735556
  30.7 19.2 %collective-permute-start.5 = (bf16[256,768]{1,0:T(8,128)(2,1)S(1)}, bf16[256,768]{1,0:T(8,128)(2,1)S(1)}, u32[]{:S(2)}, u32[]{:S(2)}) collective-permute-start(bf16[256,768]{1,0:T(8,128)(2,1)S(1)} %get-tuple-element.29), channel_id=1, source_target_pairs={{0,2},{1,7},{64,66},{65,71},{128,130},{129,135},{192,194},{193,199... | collective-permute-start | bytes 1179656 | tf_op jit(solution)/shard_map/ppermute | solution.py:39
  36.7 13.1 %collective-permute-start.6 = (bf16[256,768]{1,0:T(8,128)(2,1)}, bf16[256,768]{1,0:T(8,128)(2,1)S(1)}, u32[]{:S(2)}, u32[]{:S(2)}) collective-permute-start(bf16[256,768]{1,0:T(8,128)(2,1)} %get-tuple-element.30), channel_id=1, source_target_pairs={{0,8},{1,57},{64,72},{65,121},{128,136},{129,185},{192,200},{193,2... | collective-permute-start | bytes 1179656 | tf_op jit(solution)/shard_map/ppermute | solution.py:39
  41.6 19.9 %collective-permute-start.7 = (bf16[512,768]{1,0:T(8,128)(2,1)}, bf16[512,768]{1,0:T(8,128)(2,1)S(1)}, u32[]{:S(2)}, u32[]{:S(2)}) collective-permute-start(bf16[512,768]{1,0:T(8,128)(2,1)} %collective-permute-done.3.refs_3_), channel_id=1, source_target_pairs={{0,8},{1,57},{64,72},{65,121},{128,136},{129,185},{192,200},{193,2... | collective-permute-start | bytes 2359304 | tf_op jit(solution)/shard_map/ppermute | solution.py:39
  44.1 18.1 %collective-permute-start.8 = (bf16[512,768]{1,0:T(8,128)(2,1)}, bf16[512,768]{1,0:T(8,128)(2,1)S(1)}, u32[]{:S(2)}, u32[]{:S(2)}) collective-permute-start(bf16[512,768]{1,0:T(8,128)(2,1)} %collective-permute-done.4.refs_4_), channel_id=1, source_target_pairs={{0,2},{1,7},{64,66},{65,71},{128,130},{129,135},{192,194},{193,199... | collective-permute-start | bytes 2359304 | tf_op jit(solution)/shard_map/ppermute | solution.py:39
  49.9 11.6 %collective-permute-start.9 = (bf16[256,768]{1,0:T(8,128)(2,1)S(1)}, bf16[256,768]{1,0:T(8,128)(2,1)S(1)}, u32[]{:S(2)}, u32[]{:S(2)}) collective-permute-start(bf16[256,768]{1,0:T(8,128)(2,1)S(1)} %constant_dynamic-slice_fusion), channel_id=1, source_target_pairs={{0,10},{1,63},{64,74},{65,127},{128,138},{129,191},{192,202},{193,... | collective-permute-start | bytes 1179656 | tf_op jit(solution)/shard_map/ppermute | solution.py:39
  53.8 8.4 %copy-start.2 = (bf16[128,4864]{1,0:T(8,128)(2,1)S(1)}, bf16[128,4864]{1,0:T(8,128)(2,1)}, u32[]{:S(2)}) copy-start(bf16[128,4864]{1,0:T(8,128)(2,1)} %copy-done.1) | copy-start | bytes 3735556
  53.9 8.4 %copy-start.4 = (bf16[128,4096]{1,0:T(8,128)(2,1)S(1)}, bf16[128,4096]{1,0:T(8,128)(2,1)}, u32[]{:S(2)}) copy-start(bf16[128,4096]{1,0:T(8,128)(2,1)} %copy-done.3) | copy-start | bytes 3145732
  59.9 0.7 copy-start.5
  60.7 0.8 copy-start.8
  62.3 12.7 %copy-start.6 = (bf16[256,768]{1,0:T(8,128)(2,1)S(1)}, bf16[256,768]{1,0:T(8,128)(2,1)}, u32[]{:S(2)}) copy-start(bf16[256,768]{1,0:T(8,128)(2,1)} %copy-done.5) | copy-start | bytes 1179652
  65.2 17.2 %all-to-all-start = ((bf16[32,4,768]{2,1,0:T(4,128)(2,1)}), bf16[32,4,768]{2,1,0:T(4,128)(2,1)S(1)}, u32[]{:S(2)}, u32[]{:S(2)}) async-start(bf16[32,4,768]{2,1,0:T(4,128)(2,1)} %far_sums.1), calls=%async_computation | async-start | bytes 393216 | tf_op jit(solution)/shard_map/all_to_all | solution.py:389
  72.7 24.8 %collective-permute-start.11 = (bf16[128,2304]{1,0:T(8,128)(2,1)}, bf16[128,2304]{1,0:T(8,128)(2,1)}, u32[]{:S(2)}, u32[]{:S(2)}) collective-permute-start(bf16[128,2304]{1,0:T(8,128)(2,1)} %copy-done.8), channel_id=1, source_target_pairs={{0,1},{1,0},{64,65},{65,64},{128,129},{129,128},{192,193},{193,192... | collective-permute-start | bytes 1769480 | tf_op jit(solution)/shard_map/ppermute | solution.py:43
  78.0 0.8 copy-start.9
  83.2 16.3 %collective-permute-start.10 = (bf16[128,1792]{1,0:T(8,128)(2,1)}, bf16[128,1792]{1,0:T(8,128)(2,1)S(1)}, u32[]{:S(2)}, u32[]{:S(2)}) collective-permute-start(bf16[128,1792]{1,0:T(8,128)(2,1)} %copy-done.9), channel_id=1, source_target_pairs={{0,1},{1,0},{64,65},{65,64},{128,129},{129,128},{192,193},{193,192... | collective-permute-start | bytes 1376264 | tf_op jit(solution)/shard_map/ppermute | solution.py:43
  85.4 23.9 %all-to-all-start.1 = ((bf16[16,4,768]{2,1,0:T(4,128)(2,1)}), bf16[16,4,768]{2,1,0:T(4,128)(2,1)S(1)}, u32[]{:S(2)}, u32[]{:S(2)}) async-start(bf16[16,4,768]{2,1,0:T(4,128)(2,1)} %broadcast_in_dim.43), calls=%async_computation.1 | async-start | bytes 196608 | tf_op jit(solution)/shard_map/all_to_all | solution.py:396
  99.5 9.8 %copy-start.12 = (f32[4,768]{1,0:T(4,128)S(1)}, f32[4,768]{1,0:T(4,128)}, u32[]{:S(2)}) copy-start(f32[4,768]{1,0:T(4,128)} %param.11) | copy-start | bytes 36868

commit v11 on v10

--- a/solution.py
+++ b/solution.py
@@ -362,21 +362,22 @@
     indices = place_in * tokens + jnp.arange(tokens, dtype=jnp.int32)
     turn = rotation(token_positions(doc_lengths[0], indices))
     mine, mine_feats, to_other = pack(table, theirs, turn, key_cotangent, activations, rows)
+    own, _ = lax.optimization_barrier((weight, to_other))
+    far_xx = send(own, 2, 0)
+    from_x, _ = lax.optimization_barrier((from_x, to_other))
+    to_other, _ = lax.optimization_barrier((to_other, far_xx))
     feats = (mine_feats, swap(to_other))
-    from_x, _ = lax.optimization_barrier((from_x, to_other))
 
     from_xy = send(from_x, 0, 1)
     from_yx = send(from_y, 1, 0, cross=True)
-    half_x, half_y = halves(core.reshape(1), [from_x, from_y], rows)
-    half_x, half_y, _ = lax.optimization_barrier((half_x, half_y, feats[1]))
-    from_xy, _, _ = lax.optimization_barrier((from_xy, half_x, half_y))
+    (half_y,) = halves(core.reshape(1), [from_y], rows)
+    from_xy, _ = lax.optimization_barrier((from_xy, half_y))
 
     far_y = send(from_xy, 0, 1)
     far_x = send(from_yx, 1, 0)
-    far_xx = send(half_x, 1, 0)
     far_yy = send(half_y, 0, 1)
     half_xy = lax.dynamic_slice_in_dim(from_xy, core * rows, rows, axis=0)
-    half_xy, _, _ = lax.optimization_barrier((half_xy, far_xx, far_yy))
+    half_xy, _ = lax.optimization_barrier((half_xy, far_yy))
     far = send(half_xy, 1, 1)
 
     near = [weight, from_x, from_y, from_xy, from_yx]

time: 111 us -> 110 us (level)
  starting transfers between devices: 56.4 us -> 53.2 us
  waiting for transfers between devices: 16.6 us -> 18.7 us
    all_to_all x1, starting transfers between devices: 12.1 us -> 5.4 us  [per_device(): lax.all_to_all(share, 'dp', split_axis=0, concat_axis=0, tiled=True)]
    ppermute x3, starting transfers between devices: 6.6 us -> 12.2 us  [swap(): lax.ppermute(value, AXES, permutation(lambda x, y, z, core: (x, y, z, cor...]
    ppermute x9, starting transfers between devices: 30.2 us -> 27.6 us  [send(): return lax.ppermute(value, AXES, permutation(target))]
    ppermute x9, waiting for transfers between devices: 4.49 us -> 6.57 us  [send(): return lax.ppermute(value, AXES, permutation(target))]
    unnamed x28 -> x24, local copies, waits for them, and re-layouts: 4.01 us -> 3.95 us
  transfers between devices with their start and end apart: 14 -> 14, of which waited for: 5 -> 4; matrix products, arithmetic and copies ran while one was open for 2% -> 2% of each run, Pallas kernels for 14% -> 14%
where the time goes in v11:
time: 110 us
  starting transfers between devices  53.2 us (48%)
  Pallas kernels  19 us (17%)
  waiting for transfers between devices  18.7 us (17%)
  blocking collectives  8.87 us (8%)
  local copies, waits for them, and re-layouts  5.84 us (5%)
  other arithmetic  2.77 us (3%)
  between operations  1.36 us (1%)
    ppermute x9, starting transfers between devices, send(): return lax.ppermute(value, AXES, permutation(target))  27.6 us
    ppermute x3, starting transfers between devices, swap(): lax.ppermute(value, AXES, permutation(lambda x, y, z, core: (x, y, z, cor...  12.2 us
    all_gather x1, blocking collectives, per_device(): lax.all_gather(weight, 'tensor', axis=0, tiled=True, axis_index_groups=pa...  8.87 us
    all_to_all x1, waiting for transfers between devices, per_device(): lax.all_to_all(share, 'dp', split_axis=0, concat_axis=0, tiled=True)  8.39 us
    all_to_all x1, starting transfers between devices, per_device(): lax.all_to_all(sums, 'tensor', split_axis=0, concat_axis=0, tiled=True)  7.95 us
    ppermute x9, waiting for transfers between devices, send(): return lax.ppermute(value, AXES, permutation(target))  6.57 us
    pallas_call x1, Pallas kernels, near_shards(): pl.pallas_call(functools.partial(near_kernel, rows, len(weights)), out_sh...  5.96 us
    all_to_all x1, starting transfers between devices, per_device(): lax.all_to_all(share, 'dp', split_axis=0, concat_axis=0, tiled=True)  5.4 us
  transfers between devices with their start and end apart: 14, of which 4 were waited for; matrix products, arithmetic and copies ran while one was open for 2% of the time, Pallas kernels for 14%

profile of v11, /device:TPU:1, one launch (start us, length us, event | category | flops | bytes accessed | tf_op | source)
XLA Modules:
  0.0 109.6 jit_solution(14836146459217414026)
XLA Ops:
  0.7 1.4 %fusion.2.refs_0_ = bf16[256,768]{1,0:T(8,128)(2,1)S(1)} fusion(s32[256,768]{1,0:T(8,128)} %param.9, s32[4,768]{1,0:T(4,128)} %param.10, f32[4,768]{1,0:T(4,128)} %param.11), kind=kLoop, calls=%fused_computation.3 | loop fusion | flops 786432 | bytes 1204224 | tf_op jit(solution)/shard_map/convert_element_type | solution.py:66
  2.1 8.9 %all_gather.3 = bf16[512,768]{1,0:T(8,128)(2,1)S(1)} all-gather(bf16[256,768]{1,0:T(8,128)(2,1)S(1)} %fusion.2.refs_0_), channel_id=1, replica_groups={{0,1},{2,3},{4,5},{6,7},{8,9},{10,11},{12,13},{14,15},{16,17},{18,19},{..., dimensions={0}, use_global_device_ids=true | all-gather | bytes 1179648 | tf_op jit(solution)/shard_map/all_gather | solution.py:357
  10.9 1.9 %collective-permute-start.2 = (bf16[512,768]{1,0:T(8,128)(2,1)S(1)}, bf16[512,768]{1,0:T(8,128)(2,1)}, u32[]{:S(2)}, u32[]{:S(2)}) collective-permute-start(bf16[512,768]{1,0:T(8,128)(2,1)S(1)} %all_gather.3), channel_id=1, source_target_pairs={{0,2},{1,7},{64,66},{65,71},{128,130},{129,135},{192,194},{193,199... | collective-permute-start | bytes 2359304 | tf_op jit(solution)/shard_map/ppermute | solution.py:39
  12.9 2.2 %collective-permute-start.3 = (bf16[512,768]{1,0:T(8,128)(2,1)S(1)}, bf16[512,768]{1,0:T(8,128)(2,1)}, u32[]{:S(2)}, u32[]{:S(2)}) collective-permute-start(bf16[512,768]{1,0:T(8,128)(2,1)S(1)} %all_gather.3), channel_id=1, source_target_pairs={{0,8},{1,57},{64,72},{65,121},{128,136},{129,185},{192,200},{193,2... | collective-permute-start | bytes 2359304 | tf_op jit(solution)/shard_map/ppermute | solution.py:39
  15.4 0.1 select_reduce_fusion.1
  15.5 0.1 select_reduce_fusion
  15.6 0.1 stack.118.table
  15.7 0.1 stack.135.theirs.table
  15.8 0.3 multiply_sine_fusion
  16.1 0.1 pad_maximum_fusion
  16.3 1.9 %pack.1 = (bf16[128,768]{1,0:T(8,128)(2,1)S(1)}, bf16[128,4096]{1,0:T(8,128)(2,1)S(1)}, bf16[128,4864]{1,0:T(8,128)(2,1)}) custom-call(s32[16]{0:T(128)S(1)} %stack.118.table, s32[16]{0:T(128)S(1)} %stack.135.theirs.table, f32[128,128]{1,0:T(8,128)S(1)} %get-tuple-element.43.even_ref, f32[128,128]{1,0:T(8,128)S(1)} %get-tuple-element.44.odd_ref, ...), custom_call_target="tpu_custom_call" | custom-call | bytes 6291456 | tf_op jit(solution)/shard_map/pack/pallas_call | solution.py:189
  18.2 0.7 copy-done.8
  18.9 2.4 %collective-permute-start = (bf16[256,768]{1,0:T(8,128)(2,1)S(1)}, bf16[256,768]{1,0:T(8,128)(2,1)S(1)}, u32[]{:S(2)}, u32[]{:S(2)}) collective-permute-start(bf16[256,768]{1,0:T(8,128)(2,1)S(1)} %fusion.2.refs_0_), channel_id=1, source_target_pairs={{0,4},{1,5},{64,68},{65,69},{128,132},{129,133},{192,196},{193,197... | collective-permute-start | bytes 1179656 | tf_op jit(solution)/shard_map/ppermute | solution.py:39
  21.3 2.7 %collective-permute-done.2.refs_1_ = bf16[512,768]{1,0:T(8,128)(2,1)} collective-permute-done((bf16[512,768]{1,0:T(8,128)(2,1)S(1)}, bf16[512,768]{1,0:T(8,128)(2,1)}, u32[]{:S(2)}, u32[]{:S(2)}) %collective-permute-start.2) | collective-permute-done | bytes 786464 | tf_op jit(solution)/shard_map/ppermute | solution.py:39
  24.1 1.9 %collective-permute-start.4 = (bf16[512,768]{1,0:T(8,128)(2,1)}, bf16[512,768]{1,0:T(8,128)(2,1)}, u32[]{:S(2)}, u32[]{:S(2)}) collective-permute-start(bf16[512,768]{1,0:T(8,128)(2,1)} %collective-permute-done.2.refs_1_), channel_id=1, source_target_pairs={{0,8},{1,57},{64,72},{65,121},{128,136},{129,185},{192,200},{193,2... | collective-permute-start | bytes 2359304 | tf_op jit(solution)/shard_map/ppermute | solution.py:39
  26.0 0.0 collective-permute-done.3.refs_0_.refs_2_
  26.0 3.2 %collective-permute-start.5 = (bf16[512,768]{1,0:T(8,128)(2,1)}, bf16[512,768]{1,0:T(8,128)(2,1)}, u32[]{:S(2)}, u32[]{:S(2)}) collective-permute-start(bf16[512,768]{1,0:T(8,128)(2,1)} %collective-permute-done.3.refs_0_.refs_2_), channel_id=1, source_target_pairs={{0,7},{1,2},{64,71},{65,66},{128,135},{129,130},{192,199},{193,194... | collective-permute-start | bytes 2359304 | tf_op jit(solution)/shard_map/ppermute | solution.py:39
  29.2 3.8 %collective-permute-done.refs_0_ = bf16[256,768]{1,0:T(8,128)(2,1)S(1)} collective-permute-done((bf16[256,768]{1,0:T(8,128)(2,1)S(1)}, bf16[256,768]{1,0:T(8,128)(2,1)S(1)}, u32[]{:S(2)}, u32[]{:S(2)}) %collective-permute-start) | collective-permute-done | bytes 393248 | tf_op jit(solution)/shard_map/ppermute | solution.py:39
  33.0 7.7 %collective-permute-start.1 = (bf16[128,4864]{1,0:T(8,128)(2,1)}, bf16[128,4864]{1,0:T(8,128)(2,1)}, u32[]{:S(2)}, u32[]{:S(2)}) collective-permute-start(bf16[128,4864]{1,0:T(8,128)(2,1)} %get-tuple-element.25), channel_id=1, source_target_pairs={{0,1},{1,0},{64,65},{65,64},{128,129},{129,128},{192,193},{193,192... | collective-permute-start | bytes 3735560 | tf_op jit(solution)/shard_map/ppermute | solution.py:43
  40.7 1.0 halves.1
  41.7 4.9 %collective-permute-start.6 = (bf16[256,768]{1,0:T(8,128)(2,1)S(1)}, bf16[256,768]{1,0:T(8,128)(2,1)S(1)}, u32[]{:S(2)}, u32[]{:S(2)}) collective-permute-start(bf16[256,768]{1,0:T(8,128)(2,1)S(1)} %halves.1), channel_id=1, source_target_pairs={{0,8},{1,57},{64,72},{65,121},{128,136},{129,185},{192,200},{193,2... | collective-permute-start | bytes 1179656 | tf_op jit(solution)/shard_map/ppermute | solution.py:39
  46.6 1.9 %collective-permute-start.7 = (bf16[512,768]{1,0:T(8,128)(2,1)}, bf16[512,768]{1,0:T(8,128)(2,1)S(1)}, u32[]{:S(2)}, u32[]{:S(2)}) collective-permute-start(bf16[512,768]{1,0:T(8,128)(2,1)} %collective-permute-done.4.refs_3_), channel_id=1, source_target_pairs={{0,8},{1,57},{64,72},{65,121},{128,136},{129,185},{192,200},{193,2... | collective-permute-start | bytes 2359304 | tf_op jit(solution)/shard_map/ppermute | solution.py:39
  48.5 4.8 %collective-permute-start.8 = (bf16[512,768]{1,0:T(8,128)(2,1)}, bf16[512,768]{1,0:T(8,128)(2,1)S(1)}, u32[]{:S(2)}, u32[]{:S(2)}) collective-permute-start(bf16[512,768]{1,0:T(8,128)(2,1)} %collective-permute-done.5.refs_4_), channel_id=1, source_target_pairs={{0,2},{1,7},{64,66},{65,71},{128,130},{129,135},{192,194},{193,199... | collective-permute-start | bytes 2359304 | tf_op jit(solution)/shard_map/ppermute | solution.py:39
  53.4 1.0 constant_dynamic-slice_fusion
  54.4 0.0 collective-permute-done.6.refs_1_
  54.4 4.4 %collective-permute-start.9 = (bf16[256,768]{1,0:T(8,128)(2,1)S(1)}, bf16[256,768]{1,0:T(8,128)(2,1)S(1)}, u32[]{:S(2)}, u32[]{:S(2)}) collective-permute-start(bf16[256,768]{1,0:T(8,128)(2,1)S(1)} %constant_dynamic-slice_fusion), channel_id=1, source_target_pairs={{0,10},{1,63},{64,74},{65,127},{128,138},{129,191},{192,202},{193,... | collective-permute-start | bytes 1179656 | tf_op jit(solution)/shard_map/ppermute | solution.py:39
  58.8 0.0 collective-permute-done.1.other_ref
  58.9 0.9 copy-done.9
  59.8 6.0 %near_shards.1 = (bf16[128,8192]{1,0:T(8,128)(2,1)}, bf16[128,2304]{1,0:T(8,128)(2,1)S(1)}, f32[9,4,768]{2,1,0:T(4,128)S(1)}, bf16[256,768]{1,0:T(8,128)(2,1)S(1)}, bf16[256,768]{1,0:T(8,128)(2,1)S(1)}) custom-call(s32[16]{0:T(128)S(1)} %stack.118.table, bf16[128,768]{1,0:T(8,128)(2,1)S(1)} %copy-done.9, bf16[128,4096]{1,0:T(8,128)(2,1)} %copy-done.1, ...), custom_call_target="tpu_custom_call" | custom-call | flops 1811939328 | bytes 4718592 | tf_op jit(solution)/shard_map/near_shards/pallas_call | solution.py:239
  65.8 0.7 copy-done.3
  66.5 0.8 copy-done.6
  67.4 3.7 %far_sums.1 = bf16[32,4,768]{2,1,0:T(4,128)(2,1)} custom-call(s32[16]{0:T(128)S(1)} %stack.118.table, bf16[256,768]{1,0:T(8,128)(2,1)S(1)} %get-tuple-element.28.rot_ref, f32[9,4,768]{2,1,0:T(4,128)S(1)} %get-tuple-element.29.near_ref, bf16[128,4096]{1,0:T(8,128)(2,1)S(1)} %copy-done.2, bf16[128,4864]{1,0:T(8,128)(2,1)} %collective-permute-done.1.other_ref, ...), custom_call_target="tpu_custom_call" | custom-call | flops 704643072 | bytes 3670016 | tf_op jit(solution)/shard_map/far_sums/pallas_call | solution.py:260
  71.1 8.0 %all-to-all-start = ((bf16[32,4,768]{2,1,0:T(4,128)(2,1)}), bf16[32,4,768]{2,1,0:T(4,128)(2,1)S(1)}, u32[]{:S(2)}, u32[]{:S(2)}) async-start(bf16[32,4,768]{2,1,0:T(4,128)(2,1)} %far_sums.1), calls=%async_computation | async-start | bytes 393216 | tf_op jit(solution)/shard_map/all_to_all | solution.py:390
  79.1 2.3 %collective-permute-start.11 = (bf16[128,2304]{1,0:T(8,128)(2,1)}, bf16[128,2304]{1,0:T(8,128)(2,1)}, u32[]{:S(2)}, u32[]{:S(2)}) collective-permute-start(bf16[128,2304]{1,0:T(8,128)(2,1)} %copy-done.6), channel_id=1, source_target_pairs={{0,1},{1,0},{64,65},{65,64},{128,129},{129,128},{192,193},{193,192... | collective-permute-start | bytes 1769480 | tf_op jit(solution)/shard_map/ppermute | solution.py:43
  81.3 3.0 %far_grad.1 = (bf16[128,8192]{1,0:T(8,128)(2,1)}, bf16[128,1792]{1,0:T(8,128)(2,1)S(1)}) custom-call(s32[16]{0:T(128)S(1)} %stack.118.table, bf16[256,768]{1,0:T(8,128)(2,1)S(1)} %copy-done.4, bf16[256,768]{1,0:T(8,128)(2,1)S(1)} %collective-permute-done.refs_0_, ...), custom_call_target="tpu_custom_call", output_to_operand_aliasing={{0}: (7, {})} | custom-call | flops 704643072 | bytes 3670016 | tf_op jit(solution)/shard_map/far_grad/pallas_call | solution.py:276
  84.4 0.8 copy-done.7
  85.1 3.7 %all-to-all-done = bf16[32,4,768]{2,1,0:T(4,128)(2,1)S(1)} async-done(((bf16[32,4,768]{2,1,0:T(4,128)(2,1)}), bf16[32,4,768]{2,1,0:T(4,128)(2,1)S(1)}, u32[]{:S(2)}, u32[]{:S(2)}) %all-to-all-start) | async-done | bytes 196640 | tf_op jit(solution)/shard_map/all_to_all | solution.py:390
  88.8 0.1 reduce_sum.31
  88.9 0.7 broadcast_in_dim.43
  89.6 2.2 %collective-permute-start.10 = (bf16[128,1792]{1,0:T(8,128)(2,1)}, bf16[128,1792]{1,0:T(8,128)(2,1)S(1)}, u32[]{:S(2)}, u32[]{:S(2)}) collective-permute-start(bf16[128,1792]{1,0:T(8,128)(2,1)} %copy-done.7), channel_id=1, source_target_pairs={{0,1},{1,0},{64,65},{65,64},{128,129},{129,128},{192,193},{193,192... | collective-permute-start | bytes 1376264 | tf_op jit(solution)/shard_map/ppermute | solution.py:43
  91.8 5.4 %all-to-all-start.1 = ((bf16[16,4,768]{2,1,0:T(4,128)(2,1)}), bf16[16,4,768]{2,1,0:T(4,128)(2,1)S(1)}, u32[]{:S(2)}, u32[]{:S(2)}) async-start(bf16[16,4,768]{2,1,0:T(4,128)(2,1)} %broadcast_in_dim.43), calls=%async_computation.1 | async-start | bytes 196608 | tf_op jit(solution)/shard_map/all_to_all | solution.py:397
  97.2 0.0 collective-permute-done.11.blocks_ref
  97.2 2.0 %place.2.grad_in = bf16[128,8192]{1,0:T(8,128)(2,1)} custom-call(s32[16]{0:T(128)S(1)} %stack.135.theirs.table, bf16[128,2304]{1,0:T(8,128)(2,1)} %collective-permute-done.11.blocks_ref, bf16[128,8192]{1,0:T(8,128)(2,1)} %get-tuple-element.37.grad_in), custom_call_target="tpu_custom_call", output_to_operand_aliasing={{}: (2, {})} | custom-call | bytes 1179648 | tf_op jit(solution)/shard_map/place/pallas_call | solution.py:310
  99.2 0.0 copy-start.10
  99.2 1.4 %place.3 = bf16[128,8192]{1,0:T(8,128)(2,1)} custom-call(s32[16]{0:T(128)S(1)} %stack.135.theirs.table, bf16[128,1792]{1,0:T(8,128)(2,1)S(1)} %collective-permute-done.10.blocks_ref, bf16[128,8192]{1,0:T(8,128)(2,1)} %place.2.grad_in), custom_call_target="tpu_custom_call", output_to_operand_aliasing={{}: (2, {})} | custom-call | bytes 917504 | tf_op jit(solution)/shard_map/place/pallas_call | solution.py:310
  100.6 8.4 %all-to-all-done.1 = bf16[16,4,768]{2,1,0:T(4,128)(2,1)S(1)} async-done(((bf16[16,4,768]{2,1,0:T(4,128)(2,1)}), bf16[16,4,768]{2,1,0:T(4,128)(2,1)S(1)}, u32[]{:S(2)}, u32[]{:S(2)}) %all-to-all-start.1) | async-done | bytes 98336 | tf_op jit(solution)/shard_map/all_to_all | solution.py:397
  109.0 0.1 convert_reduce_fusion
  109.0 0.6 multiply_divide_fusion
  (27 shorter events, 0.1 us)
Async XLA Ops:
  0.6 14.8 %copy-start.11 = (s32[1,8]{1,0:T(1,128)S(1)}, s32[1,8]{1,0:T(1,128)}, u32[]{:S(2)}) copy-start(s32[1,8]{1,0:T(1,128)} %param.8) | copy-start | bytes 100
  0.6 15.6 %copy-start.5 = (bf16[128,768]{1,0:T(8,128)(2,1)S(1)}, bf16[128,768]{1,0:T(8,128)(2,1)}, u32[]{:S(2)}) copy-start(bf16[128,768]{1,0:T(8,128)(2,1)} %cot_ref.1) | copy-start | bytes 589828
  0.7 15.6 %copy-start = (bf16[128,8192]{1,0:T(8,128)(2,1)S(1)}, bf16[128,8192]{1,0:T(8,128)(2,1)}, u32[]{:S(2)}) copy-start(bf16[128,8192]{1,0:T(8,128)(2,1)} %feats_ref.1) | copy-start | bytes 6291460
  10.9 13.1 %collective-permute-start.2 = (bf16[512,768]{1,0:T(8,128)(2,1)S(1)}, bf16[512,768]{1,0:T(8,128)(2,1)}, u32[]{:S(2)}, u32[]{:S(2)}) collective-permute-start(bf16[512,768]{1,0:T(8,128)(2,1)S(1)} %all_gather.3), channel_id=1, source_target_pairs={{0,2},{1,7},{64,66},{65,71},{128,130},{129,135},{192,194},{193,199... | collective-permute-start | bytes 2359304 | tf_op jit(solution)/shard_map/ppermute | solution.py:39
  12.9 13.1 %collective-permute-start.3 = (bf16[512,768]{1,0:T(8,128)(2,1)S(1)}, bf16[512,768]{1,0:T(8,128)(2,1)}, u32[]{:S(2)}, u32[]{:S(2)}) collective-permute-start(bf16[512,768]{1,0:T(8,128)(2,1)S(1)} %all_gather.3), channel_id=1, source_target_pairs={{0,8},{1,57},{64,72},{65,121},{128,136},{129,185},{192,200},{193,2... | collective-permute-start | bytes 2359304 | tf_op jit(solution)/shard_map/ppermute | solution.py:39
  18.2 0.7 copy-start.8
  18.9 29.6 %copy-start.1 = (bf16[128,4096]{1,0:T(8,128)(2,1)}, bf16[128,4096]{1,0:T(8,128)(2,1)S(1)}, u32[]{:S(2)}) copy-start(bf16[128,4096]{1,0:T(8,128)(2,1)S(1)} %get-tuple-element.22.mine_ref) | copy-start | bytes 3145732
  18.9 14.1 %collective-permute-start = (bf16[256,768]{1,0:T(8,128)(2,1)S(1)}, bf16[256,768]{1,0:T(8,128)(2,1)S(1)}, u32[]{:S(2)}, u32[]{:S(2)}) collective-permute-start(bf16[256,768]{1,0:T(8,128)(2,1)S(1)} %fusion.2.refs_0_), channel_id=1, source_target_pairs={{0,4},{1,5},{64,68},{65,69},{128,132},{129,133},{192,196},{193,197... | collective-permute-start | bytes 1179656 | tf_op jit(solution)/shard_map/ppermute | solution.py:39
  24.1 22.5 %collective-permute-start.4 = (bf16[512,768]{1,0:T(8,128)(2,1)}, bf16[512,768]{1,0:T(8,128)(2,1)}, u32[]{:S(2)}, u32[]{:S(2)}) collective-permute-start(bf16[512,768]{1,0:T(8,128)(2,1)} %collective-permute-done.2.refs_1_), channel_id=1, source_target_pairs={{0,8},{1,57},{64,72},{65,121},{128,136},{129,185},{192,200},{193,2... | collective-permute-start | bytes 2359304 | tf_op jit(solution)/shard_map/ppermute | solution.py:39
  26.0 22.6 %collective-permute-start.5 = (bf16[512,768]{1,0:T(8,128)(2,1)}, bf16[512,768]{1,0:T(8,128)(2,1)}, u32[]{:S(2)}, u32[]{:S(2)}) collective-permute-start(bf16[512,768]{1,0:T(8,128)(2,1)} %collective-permute-done.3.refs_0_.refs_2_), channel_id=1, source_target_pairs={{0,7},{1,2},{64,71},{65,66},{128,135},{129,130},{192,199},{193,194... | collective-permute-start | bytes 2359304 | tf_op jit(solution)/shard_map/ppermute | solution.py:39
  33.0 25.8 %collective-permute-start.1 = (bf16[128,4864]{1,0:T(8,128)(2,1)}, bf16[128,4864]{1,0:T(8,128)(2,1)}, u32[]{:S(2)}, u32[]{:S(2)}) collective-permute-start(bf16[128,4864]{1,0:T(8,128)(2,1)} %get-tuple-element.25), channel_id=1, source_target_pairs={{0,1},{1,0},{64,65},{65,64},{128,129},{129,128},{192,193},{193,192... | collective-permute-start | bytes 3735560 | tf_op jit(solution)/shard_map/ppermute | solution.py:43
  41.7 12.7 %collective-permute-start.6 = (bf16[256,768]{1,0:T(8,128)(2,1)S(1)}, bf16[256,768]{1,0:T(8,128)(2,1)S(1)}, u32[]{:S(2)}, u32[]{:S(2)}) collective-permute-start(bf16[256,768]{1,0:T(8,128)(2,1)S(1)} %halves.1), channel_id=1, source_target_pairs={{0,8},{1,57},{64,72},{65,121},{128,136},{129,185},{192,200},{193,2... | collective-permute-start | bytes 1179656 | tf_op jit(solution)/shard_map/ppermute | solution.py:39
  46.6 20.7 %collective-permute-start.7 = (bf16[512,768]{1,0:T(8,128)(2,1)}, bf16[512,768]{1,0:T(8,128)(2,1)S(1)}, u32[]{:S(2)}, u32[]{:S(2)}) collective-permute-start(bf16[512,768]{1,0:T(8,128)(2,1)} %collective-permute-done.4.refs_3_), channel_id=1, source_target_pairs={{0,8},{1,57},{64,72},{65,121},{128,136},{129,185},{192,200},{193,2... | collective-permute-start | bytes 2359304 | tf_op jit(solution)/shard_map/ppermute | solution.py:39
  48.5 18.8 %collective-permute-start.8 = (bf16[512,768]{1,0:T(8,128)(2,1)}, bf16[512,768]{1,0:T(8,128)(2,1)S(1)}, u32[]{:S(2)}, u32[]{:S(2)}) collective-permute-start(bf16[512,768]{1,0:T(8,128)(2,1)} %collective-permute-done.5.refs_4_), channel_id=1, source_target_pairs={{0,2},{1,7},{64,66},{65,71},{128,130},{129,135},{192,194},{193,199... | collective-permute-start | bytes 2359304 | tf_op jit(solution)/shard_map/ppermute | solution.py:39
  54.4 12.9 %collective-permute-start.9 = (bf16[256,768]{1,0:T(8,128)(2,1)S(1)}, bf16[256,768]{1,0:T(8,128)(2,1)S(1)}, u32[]{:S(2)}, u32[]{:S(2)}) collective-permute-start(bf16[256,768]{1,0:T(8,128)(2,1)S(1)} %constant_dynamic-slice_fusion), channel_id=1, source_target_pairs={{0,10},{1,63},{64,74},{65,127},{128,138},{129,191},{192,202},{193,... | collective-permute-start | bytes 1179656 | tf_op jit(solution)/shard_map/ppermute | solution.py:39
  58.9 0.9 copy-start.9
  59.8 7.6 %copy-start.2 = (bf16[128,4096]{1,0:T(8,128)(2,1)S(1)}, bf16[128,4096]{1,0:T(8,128)(2,1)}, u32[]{:S(2)}) copy-start(bf16[128,4096]{1,0:T(8,128)(2,1)} %copy-done.1) | copy-start | bytes 3145732
  65.8 0.7 copy-start.3
  66.5 0.8 copy-start.6
  67.3 14.0 %copy-start.4 = (bf16[256,768]{1,0:T(8,128)(2,1)S(1)}, bf16[256,768]{1,0:T(8,128)(2,1)}, u32[]{:S(2)}) copy-start(bf16[256,768]{1,0:T(8,128)(2,1)} %copy-done.3) | copy-start | bytes 1179652
  71.1 17.7 %all-to-all-start = ((bf16[32,4,768]{2,1,0:T(4,128)(2,1)}), bf16[32,4,768]{2,1,0:T(4,128)(2,1)S(1)}, u32[]{:S(2)}, u32[]{:S(2)}) async-start(bf16[32,4,768]{2,1,0:T(4,128)(2,1)} %far_sums.1), calls=%async_computation | async-start | bytes 393216 | tf_op jit(solution)/shard_map/all_to_all | solution.py:390
  79.1 18.1 %collective-permute-start.11 = (bf16[128,2304]{1,0:T(8,128)(2,1)}, bf16[128,2304]{1,0:T(8,128)(2,1)}, u32[]{:S(2)}, u32[]{:S(2)}) collective-permute-start(bf16[128,2304]{1,0:T(8,128)(2,1)} %copy-done.6), channel_id=1, source_target_pairs={{0,1},{1,0},{64,65},{65,64},{128,129},{129,128},{192,193},{193,192... | collective-permute-start | bytes 1769480 | tf_op jit(solution)/shard_map/ppermute | solution.py:43
  84.4 0.8 copy-start.7
  89.6 9.6 %collective-permute-start.10 = (bf16[128,1792]{1,0:T(8,128)(2,1)}, bf16[128,1792]{1,0:T(8,128)(2,1)S(1)}, u32[]{:S(2)}, u32[]{:S(2)}) collective-permute-start(bf16[128,1792]{1,0:T(8,128)(2,1)} %copy-done.7), channel_id=1, source_target_pairs={{0,1},{1,0},{64,65},{65,64},{128,129},{129,128},{192,193},{193,192... | collective-permute-start | bytes 1376264 | tf_op jit(solution)/shard_map/ppermute | solution.py:43
  91.8 17.2 %all-to-all-start.1 = ((bf16[16,4,768]{2,1,0:T(4,128)(2,1)}), bf16[16,4,768]{2,1,0:T(4,128)(2,1)S(1)}, u32[]{:S(2)}, u32[]{:S(2)}) async-start(bf16[16,4,768]{2,1,0:T(4,128)(2,1)} %broadcast_in_dim.43), calls=%async_computation.1 | async-start | bytes 196608 | tf_op jit(solution)/shard_map/all_to_all | solution.py:397
  99.2 9.8 %copy-start.10 = (f32[4,768]{1,0:T(4,128)S(1)}, f32[4,768]{1,0:T(4,128)}, u32[]{:S(2)}) copy-start(f32[4,768]{1,0:T(4,128)} %param.11) | copy-start | bytes 36868

commit v12 on v11

--- a/solution.py
+++ b/solution.py
@@ -395,9 +395,9 @@
     share = jnp.broadcast_to(share[None], (lax.axis_size("dp"), *share.shape))
     share, sent_far = lax.optimization_barrier((share, sent_far))
     totals = lax.all_to_all(share, "dp", split_axis=0, concat_axis=0, tiled=True)
+    sent_far, got_near = lax.optimization_barrier((sent_far, got_near))
     grad = place(theirs, got_near, grad, rows, 0)
     grad = place(theirs, swap(sent_far), grad, rows, at_hand)
-    totals, grad = lax.optimization_barrier((totals, grad))
     seq_tokens = tokens * devices
     total = jnp.sum(totals.astype(jnp.float32), axis=0)
     step_grad = total / (seq_tokens * step_sizes)

time: 110 us -> 114 us (1.036)
  starting transfers between devices: 53.2 us -> 57.5 us
  local copies, waits for them, and re-layouts: 5.84 us -> 3.42 us
    all_to_all x1, starting transfers between devices: 5.4 us -> 8.91 us  [per_device(): lax.all_to_all(share, 'dp', split_axis=0, concat_axis=0, tiled=True)]
    unnamed x24 -> x18, local copies, waits for them, and re-layouts: 3.95 us -> 1.53 us
    all_to_all x1, waiting for transfers between devices: 3.68 us -> 5.94 us  [per_device(): lax.all_to_all(sums, 'tensor', split_axis=0, concat_axis=0, tiled=True)]
  transfers between devices with their start and end apart: 14 -> 14, of which waited for: 4 -> 4; matrix products, arithmetic and copies ran while one was open for 2% -> 3% of each run, Pallas kernels for 14% -> 16%
where the time goes in v12:
time: 114 us; the launch traced here: 113 us
  starting transfers between devices  57.5 us (50%)
  Pallas kernels  19.9 us (17%)
  waiting for transfers between devices  18.9 us (17%)
  blocking collectives  9.01 us (8%)
  local copies, waits for them, and re-layouts  3.42 us (3%)
  other arithmetic  2.75 us (2%)
  between operations  1.3 us (1%)
    ppermute x9, starting transfers between devices, send(): return lax.ppermute(value, AXES, permutation(target))  28.6 us
    ppermute x3, starting transfers between devices, swap(): lax.ppermute(value, AXES, permutation(lambda x, y, z, core: (x, y, z, cor...  13.1 us
    all_gather x1, blocking collectives, per_device(): lax.all_gather(weight, 'tensor', axis=0, tiled=True, axis_index_groups=pa...  9.01 us
    all_to_all x1, starting transfers between devices, per_device(): lax.all_to_all(share, 'dp', split_axis=0, concat_axis=0, tiled=True)  8.91 us
    all_to_all x1, waiting for transfers between devices, per_device(): lax.all_to_all(share, 'dp', split_axis=0, concat_axis=0, tiled=True)  7.38 us
    all_to_all x1, starting transfers between devices, per_device(): lax.all_to_all(sums, 'tensor', split_axis=0, concat_axis=0, tiled=True)  6.93 us
    pallas_call x1, Pallas kernels, near_shards(): pl.pallas_call(functools.partial(near_kernel, rows, len(weights)), out_sh...  6.79 us
    all_to_all x1, waiting for transfers between devices, per_device(): lax.all_to_all(sums, 'tensor', split_axis=0, concat_axis=0, tiled=True)  5.94 us
  transfers between devices with their start and end apart: 14, of which 4 were waited for; matrix products, arithmetic and copies ran while one was open for 3% of the time, Pallas kernels for 16%

profile of v12, /device:TPU:1, one launch (start us, length us, event | category | flops | bytes accessed | tf_op | source)
XLA Modules:
  0.0 112.9 jit_solution(14234218986237727148)
XLA Ops:
  0.7 1.4 %fusion.2.refs_0_ = bf16[256,768]{1,0:T(8,128)(2,1)S(1)} fusion(s32[256,768]{1,0:T(8,128)} %param.9, s32[4,768]{1,0:T(4,128)} %param.10, f32[4,768]{1,0:T(4,128)} %param.11), kind=kLoop, calls=%fused_computation.3 | loop fusion | flops 786432 | bytes 1204224 | tf_op jit(solution)/shard_map/convert_element_type | solution.py:66
  2.1 9.0 %all_gather.3 = bf16[512,768]{1,0:T(8,128)(2,1)} all-gather(bf16[256,768]{1,0:T(8,128)(2,1)S(1)} %fusion.2.refs_0_), channel_id=1, replica_groups={{0,1},{2,3},{4,5},{6,7},{8,9},{10,11},{12,13},{14,15},{16,17},{18,19},{..., dimensions={0}, use_global_device_ids=true | all-gather | bytes 1179648 | tf_op jit(solution)/shard_map/all_gather | solution.py:357
  11.1 1.9 %collective-permute-start.2 = (bf16[512,768]{1,0:T(8,128)(2,1)}, bf16[512,768]{1,0:T(8,128)(2,1)}, u32[]{:S(2)}, u32[]{:S(2)}) collective-permute-start(bf16[512,768]{1,0:T(8,128)(2,1)} %all_gather.3), channel_id=1, source_target_pairs={{0,2},{1,7},{64,66},{65,71},{128,130},{129,135},{192,194},{193,199... | collective-permute-start | bytes 2359304 | tf_op jit(solution)/shard_map/ppermute | solution.py:39
  13.0 2.2 %collective-permute-start.3 = (bf16[512,768]{1,0:T(8,128)(2,1)}, bf16[512,768]{1,0:T(8,128)(2,1)}, u32[]{:S(2)}, u32[]{:S(2)}) collective-permute-start(bf16[512,768]{1,0:T(8,128)(2,1)} %all_gather.3), channel_id=1, source_target_pairs={{0,8},{1,57},{64,72},{65,121},{128,136},{129,185},{192,200},{193,2... | collective-permute-start | bytes 2359304 | tf_op jit(solution)/shard_map/ppermute | solution.py:39
  15.2 0.1 select_reduce_fusion.1
  15.3 0.1 select_reduce_fusion
  15.7 0.1 stack.118.theirs.table
  15.8 0.1 stack.135.table
  15.9 0.3 multiply_sine_fusion
  16.2 0.1 pad_maximum_fusion
  16.3 1.9 %pack.1 = (bf16[128,768]{1,0:T(8,128)(2,1)S(1)}, bf16[128,4096]{1,0:T(8,128)(2,1)S(1)}, bf16[128,4864]{1,0:T(8,128)(2,1)}) custom-call(s32[16]{0:T(128)S(1)} %stack.135.table, s32[16]{0:T(128)S(1)} %stack.118.theirs.table, f32[128,128]{1,0:T(8,128)S(1)} %get-tuple-element.43.even_ref, f32[128,128]{1,0:T(8,128)S(1)} %get-tuple-element.44.odd_ref, ...), custom_call_target="tpu_custom_call" | custom-call | bytes 6291456 | tf_op jit(solution)/shard_map/pack/pallas_call | solution.py:189
  18.3 2.4 %collective-permute-start = (bf16[256,768]{1,0:T(8,128)(2,1)S(1)}, bf16[256,768]{1,0:T(8,128)(2,1)S(1)}, u32[]{:S(2)}, u32[]{:S(2)}) collective-permute-start(bf16[256,768]{1,0:T(8,128)(2,1)S(1)} %fusion.2.refs_0_), channel_id=1, source_target_pairs={{0,4},{1,5},{64,68},{65,69},{128,132},{129,133},{192,196},{193,197... | collective-permute-start | bytes 1179656 | tf_op jit(solution)/shard_map/ppermute | solution.py:39
  20.7 3.7 %collective-permute-done.2.refs_1_ = bf16[512,768]{1,0:T(8,128)(2,1)} collective-permute-done((bf16[512,768]{1,0:T(8,128)(2,1)}, bf16[512,768]{1,0:T(8,128)(2,1)}, u32[]{:S(2)}, u32[]{:S(2)}) %collective-permute-start.2) | collective-permute-done | bytes 786464 | tf_op jit(solution)/shard_map/ppermute | solution.py:39
  24.4 1.9 %collective-permute-start.4 = (bf16[512,768]{1,0:T(8,128)(2,1)}, bf16[512,768]{1,0:T(8,128)(2,1)}, u32[]{:S(2)}, u32[]{:S(2)}) collective-permute-start(bf16[512,768]{1,0:T(8,128)(2,1)} %collective-permute-done.2.refs_1_), channel_id=1, source_target_pairs={{0,8},{1,57},{64,72},{65,121},{128,136},{129,185},{192,200},{193,2... | collective-permute-start | bytes 2359304 | tf_op jit(solution)/shard_map/ppermute | solution.py:39
  26.3 0.0 collective-permute-done.3.refs_0_.refs_2_
  26.3 4.2 %collective-permute-start.5 = (bf16[512,768]{1,0:T(8,128)(2,1)}, bf16[512,768]{1,0:T(8,128)(2,1)}, u32[]{:S(2)}, u32[]{:S(2)}) collective-permute-start(bf16[512,768]{1,0:T(8,128)(2,1)} %collective-permute-done.3.refs_0_.refs_2_), channel_id=1, source_target_pairs={{0,7},{1,2},{64,71},{65,66},{128,135},{129,130},{192,199},{193,194... | collective-permute-start | bytes 2359304 | tf_op jit(solution)/shard_map/ppermute | solution.py:39
  30.5 1.9 %collective-permute-done.refs_0_ = bf16[256,768]{1,0:T(8,128)(2,1)S(1)} collective-permute-done((bf16[256,768]{1,0:T(8,128)(2,1)S(1)}, bf16[256,768]{1,0:T(8,128)(2,1)S(1)}, u32[]{:S(2)}, u32[]{:S(2)}) %collective-permute-start) | collective-permute-done | bytes 393248 | tf_op jit(solution)/shard_map/ppermute | solution.py:39
  32.4 8.7 %collective-permute-start.1 = (bf16[128,4864]{1,0:T(8,128)(2,1)}, bf16[128,4864]{1,0:T(8,128)(2,1)}, u32[]{:S(2)}, u32[]{:S(2)}) collective-permute-start(bf16[128,4864]{1,0:T(8,128)(2,1)} %get-tuple-element.25), channel_id=1, source_target_pairs={{0,1},{1,0},{64,65},{65,64},{128,129},{129,128},{192,193},{193,192... | collective-permute-start | bytes 3735560 | tf_op jit(solution)/shard_map/ppermute | solution.py:43
  41.1 1.0 halves.1
  42.1 4.9 %collective-permute-start.6 = (bf16[256,768]{1,0:T(8,128)(2,1)S(1)}, bf16[256,768]{1,0:T(8,128)(2,1)S(1)}, u32[]{:S(2)}, u32[]{:S(2)}) collective-permute-start(bf16[256,768]{1,0:T(8,128)(2,1)S(1)} %halves.1), channel_id=1, source_target_pairs={{0,8},{1,57},{64,72},{65,121},{128,136},{129,185},{192,200},{193,2... | collective-permute-start | bytes 1179656 | tf_op jit(solution)/shard_map/ppermute | solution.py:39
  46.9 0.0 collective-permute-done.4.refs_3_
  46.9 1.9 %collective-permute-start.7 = (bf16[512,768]{1,0:T(8,128)(2,1)}, bf16[512,768]{1,0:T(8,128)(2,1)S(1)}, u32[]{:S(2)}, u32[]{:S(2)}) collective-permute-start(bf16[512,768]{1,0:T(8,128)(2,1)} %collective-permute-done.4.refs_3_), channel_id=1, source_target_pairs={{0,8},{1,57},{64,72},{65,121},{128,136},{129,185},{192,200},{193,2... | collective-permute-start | bytes 2359304 | tf_op jit(solution)/shard_map/ppermute | solution.py:39
  48.9 0.0 collective-permute-done.5.refs_4_
  48.9 4.8 %collective-permute-start.8 = (bf16[512,768]{1,0:T(8,128)(2,1)}, bf16[512,768]{1,0:T(8,128)(2,1)S(1)}, u32[]{:S(2)}, u32[]{:S(2)}) collective-permute-start(bf16[512,768]{1,0:T(8,128)(2,1)} %collective-permute-done.5.refs_4_), channel_id=1, source_target_pairs={{0,2},{1,7},{64,66},{65,71},{128,130},{129,135},{192,194},{193,199... | collective-permute-start | bytes 2359304 | tf_op jit(solution)/shard_map/ppermute | solution.py:39
  53.8 1.0 constant_dynamic-slice_fusion
  54.8 0.0 collective-permute-done.6.refs_1_
  54.8 4.4 %collective-permute-start.9 = (bf16[256,768]{1,0:T(8,128)(2,1)S(1)}, bf16[256,768]{1,0:T(8,128)(2,1)S(1)}, u32[]{:S(2)}, u32[]{:S(2)}) collective-permute-start(bf16[256,768]{1,0:T(8,128)(2,1)S(1)} %constant_dynamic-slice_fusion), channel_id=1, source_target_pairs={{0,10},{1,63},{64,74},{65,127},{128,138},{129,191},{192,202},{193,... | collective-permute-start | bytes 1179656 | tf_op jit(solution)/shard_map/ppermute | solution.py:39
  59.2 0.0 collective-permute-done.1.other_ref
  59.2 6.8 %near_shards.1 = (bf16[128,8192]{1,0:T(8,128)(2,1)}, bf16[128,2304]{1,0:T(8,128)(2,1)}, f32[9,4,768]{2,1,0:T(4,128)S(1)}, bf16[256,768]{1,0:T(8,128)(2,1)S(1)}, bf16[256,768]{1,0:T(8,128)(2,1)S(1)}) custom-call(s32[16]{0:T(128)S(1)} %stack.135.table, bf16[128,768]{1,0:T(8,128)(2,1)S(1)} %get-tuple-element.21.rot_ref, bf16[128,4096]{1,0:T(8,128)(2,1)} %copy-done.1, ...), custom_call_target="tpu_custom_call" | custom-call | flops 1811939328 | bytes 4718592 | tf_op jit(solution)/shard_map/near_shards/pallas_call | solution.py:239
  66.0 0.7 copy-done.3
  66.7 1.9 %collective-permute-start.10 = (bf16[128,2304]{1,0:T(8,128)(2,1)}, bf16[128,2304]{1,0:T(8,128)(2,1)}, u32[]{:S(2)}, u32[]{:S(2)}) collective-permute-start(bf16[128,2304]{1,0:T(8,128)(2,1)} %get-tuple-element.35), channel_id=1, source_target_pairs={{0,1},{1,0},{64,65},{65,64},{128,129},{129,128},{192,193},{193,192... | collective-permute-start | bytes 1769480 | tf_op jit(solution)/shard_map/ppermute | solution.py:43
  68.7 0.0 collective-permute-done.9.refs_4_
  68.7 0.0 collective-permute-done.7.refs_2_
  68.7 0.0 collective-permute-done.8.refs_3_
  68.7 3.8 %far_sums.1 = bf16[32,4,768]{2,1,0:T(4,128)(2,1)} custom-call(s32[16]{0:T(128)S(1)} %stack.135.table, bf16[256,768]{1,0:T(8,128)(2,1)S(1)} %get-tuple-element.28.rot_ref, f32[9,4,768]{2,1,0:T(4,128)S(1)} %get-tuple-element.29.near_ref, bf16[128,4096]{1,0:T(8,128)(2,1)S(1)} %copy-done.2, bf16[128,4864]{1,0:T(8,128)(2,1)} %collective-permute-done.1.other_ref, ...), custom_call_target="tpu_custom_call" | custom-call | flops 704643072 | bytes 3670016 | tf_op jit(solution)/shard_map/far_sums/pallas_call | solution.py:260
  72.6 6.9 %all-to-all-start = ((bf16[32,4,768]{2,1,0:T(4,128)(2,1)}), bf16[32,4,768]{2,1,0:T(4,128)(2,1)S(1)}, u32[]{:S(2)}, u32[]{:S(2)}) async-start(bf16[32,4,768]{2,1,0:T(4,128)(2,1)} %far_sums.1), calls=%async_computation | async-start | bytes 393216 | tf_op jit(solution)/shard_map/all_to_all | solution.py:390
  79.5 3.0 %far_grad.1 = (bf16[128,8192]{1,0:T(8,128)(2,1)}, bf16[128,1792]{1,0:T(8,128)(2,1)S(1)}) custom-call(s32[16]{0:T(128)S(1)} %stack.135.table, bf16[256,768]{1,0:T(8,128)(2,1)S(1)} %copy-done.4, bf16[256,768]{1,0:T(8,128)(2,1)S(1)} %collective-permute-done.refs_0_, ...), custom_call_target="tpu_custom_call", output_to_operand_aliasing={{0}: (7, {})} | custom-call | flops 704643072 | bytes 3670016 | tf_op jit(solution)/shard_map/far_grad/pallas_call | solution.py:276
  82.6 0.8 copy-done.6
  83.3 5.9 %all-to-all-done = bf16[32,4,768]{2,1,0:T(4,128)(2,1)S(1)} async-done(((bf16[32,4,768]{2,1,0:T(4,128)(2,1)}), bf16[32,4,768]{2,1,0:T(4,128)(2,1)S(1)}, u32[]{:S(2)}, u32[]{:S(2)}) %all-to-all-start) | async-done | bytes 196640 | tf_op jit(solution)/shard_map/all_to_all | solution.py:390
  89.3 0.1 reduce_sum.31
  89.4 0.7 broadcast_in_dim.43
  90.0 8.9 %all-to-all-start.1 = ((bf16[16,4,768]{2,1,0:T(4,128)(2,1)}), bf16[16,4,768]{2,1,0:T(4,128)(2,1)S(1)}, u32[]{:S(2)}, u32[]{:S(2)}) async-start(bf16[16,4,768]{2,1,0:T(4,128)(2,1)} %broadcast_in_dim.43), calls=%async_computation.1 | async-start | bytes 196608 | tf_op jit(solution)/shard_map/all_to_all | solution.py:397
  99.0 2.5 %collective-permute-start.11 = (bf16[128,1792]{1,0:T(8,128)(2,1)}, bf16[128,1792]{1,0:T(8,128)(2,1)S(1)}, u32[]{:S(2)}, u32[]{:S(2)}) collective-permute-start(bf16[128,1792]{1,0:T(8,128)(2,1)} %copy-done.6), channel_id=1, source_target_pairs={{0,1},{1,0},{64,65},{65,64},{128,129},{129,128},{192,193},{193,192... | collective-permute-start | bytes 1376264 | tf_op jit(solution)/shard_map/ppermute | solution.py:43
  101.5 0.0 copy-start.7
  101.5 2.0 %place.2.grad_in = bf16[128,8192]{1,0:T(8,128)(2,1)} custom-call(s32[16]{0:T(128)S(1)} %stack.118.theirs.table, bf16[128,2304]{1,0:T(8,128)(2,1)} %collective-permute-done.10.blocks_ref, bf16[128,8192]{1,0:T(8,128)(2,1)} %get-tuple-element.38.grad_in), custom_call_target="tpu_custom_call", output_to_operand_aliasing={{}: (2, {})} | custom-call | bytes 1179648 | tf_op jit(solution)/shard_map/place/pallas_call | solution.py:310
  103.5 7.4 %all-to-all-done.1 = bf16[16,4,768]{2,1,0:T(4,128)(2,1)S(1)} async-done(((bf16[16,4,768]{2,1,0:T(4,128)(2,1)}), bf16[16,4,768]{2,1,0:T(4,128)(2,1)S(1)}, u32[]{:S(2)}, u32[]{:S(2)}) %all-to-all-start.1) | async-done | bytes 98336 | tf_op jit(solution)/shard_map/all_to_all | solution.py:397
  110.9 0.6 multiply_divide_fusion
  111.5 1.4 %place.3 = bf16[128,8192]{1,0:T(8,128)(2,1)} custom-call(s32[16]{0:T(128)S(1)} %stack.118.theirs.table, bf16[128,1792]{1,0:T(8,128)(2,1)S(1)} %collective-permute-done.11.blocks_ref, bf16[128,8192]{1,0:T(8,128)(2,1)} %place.2.grad_in), custom_call_target="tpu_custom_call", output_to_operand_aliasing={{}: (2, {})} | custom-call | bytes 917504 | tf_op jit(solution)/shard_map/place/pallas_call | solution.py:310
  (21 shorter events, 0.1 us)
Async XLA Ops:
  0.6 14.6 %copy-start.8 = (s32[1,8]{1,0:T(1,128)S(1)}, s32[1,8]{1,0:T(1,128)}, u32[]{:S(2)}) copy-start(s32[1,8]{1,0:T(1,128)} %param.8) | copy-start | bytes 100
  0.6 15.7 %copy-start.5 = (bf16[128,768]{1,0:T(8,128)(2,1)S(1)}, bf16[128,768]{1,0:T(8,128)(2,1)}, u32[]{:S(2)}) copy-start(bf16[128,768]{1,0:T(8,128)(2,1)} %cot_ref.1) | copy-start | bytes 589828
  0.7 15.7 %copy-start = (bf16[128,8192]{1,0:T(8,128)(2,1)S(1)}, bf16[128,8192]{1,0:T(8,128)(2,1)}, u32[]{:S(2)}) copy-start(bf16[128,8192]{1,0:T(8,128)(2,1)} %feats_ref.1) | copy-start | bytes 6291460
  11.1 13.3 %collective-permute-start.2 = (bf16[512,768]{1,0:T(8,128)(2,1)}, bf16[512,768]{1,0:T(8,128)(2,1)}, u32[]{:S(2)}, u32[]{:S(2)}) collective-permute-start(bf16[512,768]{1,0:T(8,128)(2,1)} %all_gather.3), channel_id=1, source_target_pairs={{0,2},{1,7},{64,66},{65,71},{128,130},{129,135},{192,194},{193,199... | collective-permute-start | bytes 2359304 | tf_op jit(solution)/shard_map/ppermute | solution.py:39
  13.0 13.3 %collective-permute-start.3 = (bf16[512,768]{1,0:T(8,128)(2,1)}, bf16[512,768]{1,0:T(8,128)(2,1)}, u32[]{:S(2)}, u32[]{:S(2)}) collective-permute-start(bf16[512,768]{1,0:T(8,128)(2,1)} %all_gather.3), channel_id=1, source_target_pairs={{0,8},{1,57},{64,72},{65,121},{128,136},{129,185},{192,200},{193,2... | collective-permute-start | bytes 2359304 | tf_op jit(solution)/shard_map/ppermute | solution.py:39
  18.3 30.6 %copy-start.1 = (bf16[128,4096]{1,0:T(8,128)(2,1)}, bf16[128,4096]{1,0:T(8,128)(2,1)S(1)}, u32[]{:S(2)}) copy-start(bf16[128,4096]{1,0:T(8,128)(2,1)S(1)} %get-tuple-element.22.mine_ref) | copy-start | bytes 3145732
  18.3 14.1 %collective-permute-start = (bf16[256,768]{1,0:T(8,128)(2,1)S(1)}, bf16[256,768]{1,0:T(8,128)(2,1)S(1)}, u32[]{:S(2)}, u32[]{:S(2)}) collective-permute-start(bf16[256,768]{1,0:T(8,128)(2,1)S(1)} %fusion.2.refs_0_), channel_id=1, source_target_pairs={{0,4},{1,5},{64,68},{65,69},{128,132},{129,133},{192,196},{193,197... | collective-permute-start | bytes 1179656 | tf_op jit(solution)/shard_map/ppermute | solution.py:39
  24.4 22.5 %collective-permute-start.4 = (bf16[512,768]{1,0:T(8,128)(2,1)}, bf16[512,768]{1,0:T(8,128)(2,1)}, u32[]{:S(2)}, u32[]{:S(2)}) collective-permute-start(bf16[512,768]{1,0:T(8,128)(2,1)} %collective-permute-done.2.refs_1_), channel_id=1, source_target_pairs={{0,8},{1,57},{64,72},{65,121},{128,136},{129,185},{192,200},{193,2... | collective-permute-start | bytes 2359304 | tf_op jit(solution)/shard_map/ppermute | solution.py:39
  26.3 22.6 %collective-permute-start.5 = (bf16[512,768]{1,0:T(8,128)(2,1)}, bf16[512,768]{1,0:T(8,128)(2,1)}, u32[]{:S(2)}, u32[]{:S(2)}) collective-permute-start(bf16[512,768]{1,0:T(8,128)(2,1)} %collective-permute-done.3.refs_0_.refs_2_), channel_id=1, source_target_pairs={{0,7},{1,2},{64,71},{65,66},{128,135},{129,130},{192,199},{193,194... | collective-permute-start | bytes 2359304 | tf_op jit(solution)/shard_map/ppermute | solution.py:39
  32.4 26.8 %collective-permute-start.1 = (bf16[128,4864]{1,0:T(8,128)(2,1)}, bf16[128,4864]{1,0:T(8,128)(2,1)}, u32[]{:S(2)}, u32[]{:S(2)}) collective-permute-start(bf16[128,4864]{1,0:T(8,128)(2,1)} %get-tuple-element.25), channel_id=1, source_target_pairs={{0,1},{1,0},{64,65},{65,64},{128,129},{129,128},{192,193},{193,192... | collective-permute-start | bytes 3735560 | tf_op jit(solution)/shard_map/ppermute | solution.py:43
  42.1 12.7 %collective-permute-start.6 = (bf16[256,768]{1,0:T(8,128)(2,1)S(1)}, bf16[256,768]{1,0:T(8,128)(2,1)S(1)}, u32[]{:S(2)}, u32[]{:S(2)}) collective-permute-start(bf16[256,768]{1,0:T(8,128)(2,1)S(1)} %halves.1), channel_id=1, source_target_pairs={{0,8},{1,57},{64,72},{65,121},{128,136},{129,185},{192,200},{193,2... | collective-permute-start | bytes 1179656 | tf_op jit(solution)/shard_map/ppermute | solution.py:39
  46.9 21.7 %collective-permute-start.7 = (bf16[512,768]{1,0:T(8,128)(2,1)}, bf16[512,768]{1,0:T(8,128)(2,1)S(1)}, u32[]{:S(2)}, u32[]{:S(2)}) collective-permute-start(bf16[512,768]{1,0:T(8,128)(2,1)} %collective-permute-done.4.refs_3_), channel_id=1, source_target_pairs={{0,8},{1,57},{64,72},{65,121},{128,136},{129,185},{192,200},{193,2... | collective-permute-start | bytes 2359304 | tf_op jit(solution)/shard_map/ppermute | solution.py:39
  48.9 19.8 %collective-permute-start.8 = (bf16[512,768]{1,0:T(8,128)(2,1)}, bf16[512,768]{1,0:T(8,128)(2,1)S(1)}, u32[]{:S(2)}, u32[]{:S(2)}) collective-permute-start(bf16[512,768]{1,0:T(8,128)(2,1)} %collective-permute-done.5.refs_4_), channel_id=1, source_target_pairs={{0,2},{1,7},{64,66},{65,71},{128,130},{129,135},{192,194},{193,199... | collective-permute-start | bytes 2359304 | tf_op jit(solution)/shard_map/ppermute | solution.py:39
  54.8 13.9 %collective-permute-start.9 = (bf16[256,768]{1,0:T(8,128)(2,1)S(1)}, bf16[256,768]{1,0:T(8,128)(2,1)S(1)}, u32[]{:S(2)}, u32[]{:S(2)}) collective-permute-start(bf16[256,768]{1,0:T(8,128)(2,1)S(1)} %constant_dynamic-slice_fusion), channel_id=1, source_target_pairs={{0,10},{1,63},{64,74},{65,127},{128,138},{129,191},{192,202},{193,... | collective-permute-start | bytes 1179656 | tf_op jit(solution)/shard_map/ppermute | solution.py:39
  59.2 9.5 %copy-start.2 = (bf16[128,4096]{1,0:T(8,128)(2,1)S(1)}, bf16[128,4096]{1,0:T(8,128)(2,1)}, u32[]{:S(2)}) copy-start(bf16[128,4096]{1,0:T(8,128)(2,1)} %copy-done.1) | copy-start | bytes 3145732
  66.0 0.7 copy-start.3
  66.7 32.2 %collective-permute-start.10 = (bf16[128,2304]{1,0:T(8,128)(2,1)}, bf16[128,2304]{1,0:T(8,128)(2,1)}, u32[]{:S(2)}, u32[]{:S(2)}) collective-permute-start(bf16[128,2304]{1,0:T(8,128)(2,1)} %get-tuple-element.35), channel_id=1, source_target_pairs={{0,1},{1,0},{64,65},{65,64},{128,129},{129,128},{192,193},{193,192... | collective-permute-start | bytes 1769480 | tf_op jit(solution)/shard_map/ppermute | solution.py:43
  68.7 10.8 %copy-start.4 = (bf16[256,768]{1,0:T(8,128)(2,1)S(1)}, bf16[256,768]{1,0:T(8,128)(2,1)}, u32[]{:S(2)}) copy-start(bf16[256,768]{1,0:T(8,128)(2,1)} %copy-done.3) | copy-start | bytes 1179652
  72.6 16.7 %all-to-all-start = ((bf16[32,4,768]{2,1,0:T(4,128)(2,1)}), bf16[32,4,768]{2,1,0:T(4,128)(2,1)S(1)}, u32[]{:S(2)}, u32[]{:S(2)}) async-start(bf16[32,4,768]{2,1,0:T(4,128)(2,1)} %far_sums.1), calls=%async_computation | async-start | bytes 393216 | tf_op jit(solution)/shard_map/all_to_all | solution.py:390
  82.5 0.8 copy-start.6
  90.0 20.8 %all-to-all-start.1 = ((bf16[16,4,768]{2,1,0:T(4,128)(2,1)}), bf16[16,4,768]{2,1,0:T(4,128)(2,1)S(1)}, u32[]{:S(2)}, u32[]{:S(2)}) async-start(bf16[16,4,768]{2,1,0:T(4,128)(2,1)} %broadcast_in_dim.43), calls=%async_computation.1 | async-start | bytes 196608 | tf_op jit(solution)/shard_map/all_to_all | solution.py:397
  99.0 12.5 %collective-permute-start.11 = (bf16[128,1792]{1,0:T(8,128)(2,1)}, bf16[128,1792]{1,0:T(8,128)(2,1)S(1)}, u32[]{:S(2)}, u32[]{:S(2)}) collective-permute-start(bf16[128,1792]{1,0:T(8,128)(2,1)} %copy-done.6), channel_id=1, source_target_pairs={{0,1},{1,0},{64,65},{65,64},{128,129},{129,128},{192,193},{193,192... | collective-permute-start | bytes 1376264 | tf_op jit(solution)/shard_map/ppermute | solution.py:43
  101.5 9.4 %copy-start.7 = (f32[4,768]{1,0:T(4,128)S(1)}, f32[4,768]{1,0:T(4,128)}, u32[]{:S(2)}) copy-start(f32[4,768]{1,0:T(4,128)} %param.11) | copy-start | bytes 36868

commit v13 on v10

--- a/solution.py
+++ b/solution.py
@@ -396,7 +396,6 @@
     totals = lax.all_to_all(share, "dp", split_axis=0, concat_axis=0, tiled=True)
     grad = place(theirs, got_near, grad, rows, 0)
     grad = place(theirs, swap(sent_far), grad, rows, at_hand)
-    totals, grad = lax.optimization_barrier((totals, grad))
     seq_tokens = tokens * devices
     total = jnp.sum(totals.astype(jnp.float32), axis=0)
     step_grad = total / (seq_tokens * step_sizes)

time: 111 us -> 110 us (level)
  starting transfers between devices: 56.4 us -> 54.8 us
  local copies, waits for them, and re-layouts: 5.9 us -> 4.38 us
  waiting for transfers between devices: 16.6 us -> 18 us
    all_to_all x1, waiting for transfers between devices: 3.67 us -> 5.94 us  [per_device(): lax.all_to_all(sums, 'tensor', split_axis=0, concat_axis=0, tiled=True)]
    unnamed x28 -> x22, local copies, waits for them, and re-layouts: 4.01 us -> 2.49 us
  transfers between devices with their start and end apart: 14 -> 14, of which waited for: 5 -> 4; matrix products, arithmetic and copies ran while one was open for 2% -> 3% of each run, Pallas kernels for 14% -> 16%
where the time goes in v13:
time: 110 us; the launch traced here: 109 us
  starting transfers between devices  54.8 us (50%)
  Pallas kernels  19 us (17%)
  waiting for transfers between devices  18 us (16%)
  blocking collectives  9.01 us (8%)
  local copies, waits for them, and re-layouts  4.38 us (4%)
  other arithmetic  2.75 us (2%)
  between operations  1.4 us (1%)
    ppermute x9, starting transfers between devices, send(): return lax.ppermute(value, AXES, permutation(target))  30 us
    all_to_all x1, starting transfers between devices, per_device(): lax.all_to_all(share, 'dp', split_axis=0, concat_axis=0, tiled=True)  11.3 us
    all_gather x1, blocking collectives, per_device(): lax.all_gather(weight, 'tensor', axis=0, tiled=True, axis_index_groups=pa...  9.01 us
    all_to_all x1, waiting for transfers between devices, per_device(): lax.all_to_all(share, 'dp', split_axis=0, concat_axis=0, tiled=True)  7.34 us
    all_to_all x1, starting transfers between devices, per_device(): lax.all_to_all(sums, 'tensor', split_axis=0, concat_axis=0, tiled=True)  7.02 us
    pallas_call x1, Pallas kernels, near_shards(): pl.pallas_call(functools.partial(near_kernel, rows, len(weights)), out_sh...  6.85 us
    ppermute x3, starting transfers between devices, swap(): lax.ppermute(value, AXES, permutation(lambda x, y, z, core: (x, y, z, cor...  6.41 us
    all_to_all x1, waiting for transfers between devices, per_device(): lax.all_to_all(sums, 'tensor', split_axis=0, concat_axis=0, tiled=True)  5.94 us
  transfers between devices with their start and end apart: 14, of which 4 were waited for; matrix products, arithmetic and copies ran while one was open for 3% of the time, Pallas kernels for 16%

profile of v13, /device:TPU:1, one launch (start us, length us, event | category | flops | bytes accessed | tf_op | source)
XLA Modules:
  0.0 109.4 jit_solution(13710503020030851070)
XLA Ops:
  0.7 1.4 %fusion.2.refs_0_ = bf16[256,768]{1,0:T(8,128)(2,1)S(1)} fusion(s32[256,768]{1,0:T(8,128)} %param.9, s32[4,768]{1,0:T(4,128)} %param.10, f32[4,768]{1,0:T(4,128)} %param.11), kind=kLoop, calls=%fused_computation.3 | loop fusion | flops 786432 | bytes 1204224 | tf_op jit(solution)/shard_map/convert_element_type | solution.py:66
  2.1 9.0 %all_gather.3 = bf16[512,768]{1,0:T(8,128)(2,1)} all-gather(bf16[256,768]{1,0:T(8,128)(2,1)S(1)} %fusion.2.refs_0_), channel_id=1, replica_groups={{0,1},{2,3},{4,5},{6,7},{8,9},{10,11},{12,13},{14,15},{16,17},{18,19},{..., dimensions={0}, use_global_device_ids=true | all-gather | bytes 1179648 | tf_op jit(solution)/shard_map/all_gather | solution.py:357
  11.1 1.9 %collective-permute-start.1 = (bf16[512,768]{1,0:T(8,128)(2,1)}, bf16[512,768]{1,0:T(8,128)(2,1)}, u32[]{:S(2)}, u32[]{:S(2)}) collective-permute-start(bf16[512,768]{1,0:T(8,128)(2,1)} %all_gather.3), channel_id=1, source_target_pairs={{0,2},{1,7},{64,66},{65,71},{128,130},{129,135},{192,194},{193,199... | collective-permute-start | bytes 2359304 | tf_op jit(solution)/shard_map/ppermute | solution.py:39
  13.0 2.2 %collective-permute-start.2 = (bf16[512,768]{1,0:T(8,128)(2,1)}, bf16[512,768]{1,0:T(8,128)(2,1)}, u32[]{:S(2)}, u32[]{:S(2)}) collective-permute-start(bf16[512,768]{1,0:T(8,128)(2,1)} %all_gather.3), channel_id=1, source_target_pairs={{0,8},{1,57},{64,72},{65,121},{128,136},{129,185},{192,200},{193,2... | collective-permute-start | bytes 2359304 | tf_op jit(solution)/shard_map/ppermute | solution.py:39
  15.6 0.1 select_reduce_fusion.1
  15.6 0.1 select_reduce_fusion
  15.7 0.1 stack.118.theirs.table
  15.8 0.1 stack.135.table
  15.9 0.3 multiply_sine_fusion
  16.3 0.1 pad_maximum_fusion
  16.4 0.9 pack.1
  17.3 1.0 copy-done.3
  18.3 2.0 %collective-permute-start = (bf16[128,4864]{1,0:T(8,128)(2,1)S(1)}, bf16[128,4864]{1,0:T(8,128)(2,1)S(1)}, u32[]{:S(2)}, u32[]{:S(2)}) collective-permute-start(bf16[128,4864]{1,0:T(8,128)(2,1)S(1)} %get-tuple-element.23), channel_id=1, source_target_pairs={{0,1},{1,0},{64,65},{65,64},{128,129},{129,128},{192,193},{193,192... | collective-permute-start | bytes 3735560 | tf_op jit(solution)/shard_map/ppermute | solution.py:43
  20.3 4.1 %collective-permute-done.1.refs_0_.refs_1_ = bf16[512,768]{1,0:T(8,128)(2,1)} collective-permute-done((bf16[512,768]{1,0:T(8,128)(2,1)}, bf16[512,768]{1,0:T(8,128)(2,1)}, u32[]{:S(2)}, u32[]{:S(2)}) %collective-permute-start.1) | collective-permute-done | bytes 786464 | tf_op jit(solution)/shard_map/ppermute | solution.py:39
  24.4 1.9 %collective-permute-start.3 = (bf16[512,768]{1,0:T(8,128)(2,1)}, bf16[512,768]{1,0:T(8,128)(2,1)}, u32[]{:S(2)}, u32[]{:S(2)}) collective-permute-start(bf16[512,768]{1,0:T(8,128)(2,1)} %collective-permute-done.1.refs_0_.refs_1_), channel_id=1, source_target_pairs={{0,8},{1,57},{64,72},{65,121},{128,136},{129,185},{192,200},{193,2... | collective-permute-start | bytes 2359304 | tf_op jit(solution)/shard_map/ppermute | solution.py:39
  26.3 0.0 collective-permute-done.2.refs_1_.refs_2_
  26.3 2.8 %collective-permute-start.4 = (bf16[512,768]{1,0:T(8,128)(2,1)}, bf16[512,768]{1,0:T(8,128)(2,1)}, u32[]{:S(2)}, u32[]{:S(2)}) collective-permute-start(bf16[512,768]{1,0:T(8,128)(2,1)} %collective-permute-done.2.refs_1_.refs_2_), channel_id=1, source_target_pairs={{0,7},{1,2},{64,71},{65,66},{128,135},{129,130},{192,199},{193,194... | collective-permute-start | bytes 2359304 | tf_op jit(solution)/shard_map/ppermute | solution.py:39
  29.1 1.9 %halves.1 = (bf16[256,768]{1,0:T(8,128)(2,1)}, bf16[256,768]{1,0:T(8,128)(2,1)S(1)}) custom-call(s32[1]{0:T(128)} %bitcast.35.core, bf16[512,768]{1,0:T(8,128)(2,1)} %collective-permute-done.1.refs_0_.refs_1_, bf16[512,768]{1,0:T(8,128)(2,1)} %collective-permute-done.2.refs_1_.refs_2_), custom_call_target="tpu_custom_call" | custom-call | bytes 1572864 | tf_op jit(solution)/shard_map/halves/pallas_call | solution.py:221
  31.0 0.0 collective-permute-done.other_ref
  31.0 6.1 %collective-permute-start.5 = (bf16[256,768]{1,0:T(8,128)(2,1)}, bf16[256,768]{1,0:T(8,128)(2,1)S(1)}, u32[]{:S(2)}, u32[]{:S(2)}) collective-permute-start(bf16[256,768]{1,0:T(8,128)(2,1)} %get-tuple-element.27), channel_id=1, source_target_pairs={{0,2},{1,7},{64,66},{65,71},{128,130},{129,135},{192,194},{193,199... | collective-permute-start | bytes 1179656 | tf_op jit(solution)/shard_map/ppermute | solution.py:39
  37.1 4.9 %collective-permute-start.6 = (bf16[256,768]{1,0:T(8,128)(2,1)S(1)}, bf16[256,768]{1,0:T(8,128)(2,1)S(1)}, u32[]{:S(2)}, u32[]{:S(2)}) collective-permute-start(bf16[256,768]{1,0:T(8,128)(2,1)S(1)} %get-tuple-element.28), channel_id=1, source_target_pairs={{0,8},{1,57},{64,72},{65,121},{128,136},{129,185},{192,200},{193,2... | collective-permute-start | bytes 1179656 | tf_op jit(solution)/shard_map/ppermute | solution.py:39
  41.9 0.0 collective-permute-done.3.refs_3_
  41.9 1.9 %collective-permute-start.7 = (bf16[512,768]{1,0:T(8,128)(2,1)}, bf16[512,768]{1,0:T(8,128)(2,1)S(1)}, u32[]{:S(2)}, u32[]{:S(2)}) collective-permute-start(bf16[512,768]{1,0:T(8,128)(2,1)} %collective-permute-done.3.refs_3_), channel_id=1, source_target_pairs={{0,8},{1,57},{64,72},{65,121},{128,136},{129,185},{192,200},{193,2... | collective-permute-start | bytes 2359304 | tf_op jit(solution)/shard_map/ppermute | solution.py:39
  43.9 0.6 collective-permute-done.4.refs_4_
  44.5 3.9 %collective-permute-start.8 = (bf16[512,768]{1,0:T(8,128)(2,1)}, bf16[512,768]{1,0:T(8,128)(2,1)S(1)}, u32[]{:S(2)}, u32[]{:S(2)}) collective-permute-start(bf16[512,768]{1,0:T(8,128)(2,1)} %collective-permute-done.4.refs_4_), channel_id=1, source_target_pairs={{0,2},{1,7},{64,66},{65,71},{128,130},{129,135},{192,194},{193,199... | collective-permute-start | bytes 2359304 | tf_op jit(solution)/shard_map/ppermute | solution.py:39
  48.3 1.0 constant_dynamic-slice_fusion
  49.4 0.0 collective-permute-done.6.refs_1_
  49.4 4.6 %collective-permute-start.9 = (bf16[256,768]{1,0:T(8,128)(2,1)S(1)}, bf16[256,768]{1,0:T(8,128)(2,1)S(1)}, u32[]{:S(2)}, u32[]{:S(2)}) collective-permute-start(bf16[256,768]{1,0:T(8,128)(2,1)S(1)} %constant_dynamic-slice_fusion), channel_id=1, source_target_pairs={{0,10},{1,63},{64,74},{65,127},{128,138},{129,191},{192,202},{193,... | collective-permute-start | bytes 1179656 | tf_op jit(solution)/shard_map/ppermute | solution.py:39
  54.0 6.9 %near_shards.1 = (bf16[128,8192]{1,0:T(8,128)(2,1)}, bf16[128,2304]{1,0:T(8,128)(2,1)}, f32[9,4,768]{2,1,0:T(4,128)S(1)}, bf16[256,768]{1,0:T(8,128)(2,1)S(1)}, bf16[256,768]{1,0:T(8,128)(2,1)S(1)}) custom-call(s32[16]{0:T(128)S(1)} %stack.135.table, bf16[128,768]{1,0:T(8,128)(2,1)S(1)} %get-tuple-element.21.rot_ref, bf16[128,4096]{1,0:T(8,128)(2,1)} %copy-done.3, ...), custom_call_target="tpu_custom_call" | custom-call | flops 1811939328 | bytes 4718592 | tf_op jit(solution)/shard_map/near_shards/pallas_call | solution.py:239
  60.9 0.7 copy-done.5
  61.6 1.9 %collective-permute-start.11 = (bf16[128,2304]{1,0:T(8,128)(2,1)}, bf16[128,2304]{1,0:T(8,128)(2,1)}, u32[]{:S(2)}, u32[]{:S(2)}) collective-permute-start(bf16[128,2304]{1,0:T(8,128)(2,1)} %get-tuple-element.37), channel_id=1, source_target_pairs={{0,1},{1,0},{64,65},{65,64},{128,129},{129,128},{192,193},{193,192... | collective-permute-start | bytes 1769480 | tf_op jit(solution)/shard_map/ppermute | solution.py:43
  63.5 0.0 collective-permute-done.9.refs_4_
  63.5 0.0 collective-permute-done.8.refs_3_
  63.6 3.0 %far_sums.1 = bf16[32,4,768]{2,1,0:T(4,128)(2,1)} custom-call(s32[16]{0:T(128)S(1)} %stack.135.table, bf16[256,768]{1,0:T(8,128)(2,1)S(1)} %get-tuple-element.30.rot_ref, f32[9,4,768]{2,1,0:T(4,128)S(1)} %get-tuple-element.31.near_ref, bf16[128,4096]{1,0:T(8,128)(2,1)S(1)} %copy-done.4, bf16[128,4864]{1,0:T(8,128)(2,1)S(1)} %copy-done.2, ...), custom_call_target="tpu_custom_call" | custom-call | flops 704643072 | bytes 3670016 | tf_op jit(solution)/shard_map/far_sums/pallas_call | solution.py:260
  66.6 7.0 %all-to-all-start = ((bf16[32,4,768]{2,1,0:T(4,128)(2,1)}), bf16[32,4,768]{2,1,0:T(4,128)(2,1)S(1)}, u32[]{:S(2)}, u32[]{:S(2)}) async-start(bf16[32,4,768]{2,1,0:T(4,128)(2,1)} %far_sums.1), calls=%async_computation | async-start | bytes 393216 | tf_op jit(solution)/shard_map/all_to_all | solution.py:389
  73.7 3.0 %far_grad.1 = (bf16[128,8192]{1,0:T(8,128)(2,1)}, bf16[128,1792]{1,0:T(8,128)(2,1)S(1)}) custom-call(s32[16]{0:T(128)S(1)} %stack.135.table, bf16[256,768]{1,0:T(8,128)(2,1)S(1)} %copy-done.6, bf16[256,768]{1,0:T(8,128)(2,1)S(1)} %collective-permute-done.5.refs_0_, ...), custom_call_target="tpu_custom_call", output_to_operand_aliasing={{0}: (7, {})} | custom-call | flops 704643072 | bytes 3670016 | tf_op jit(solution)/shard_map/far_grad/pallas_call | solution.py:276
  76.7 0.8 copy-done.8
  77.4 5.9 %all-to-all-done = bf16[32,4,768]{2,1,0:T(4,128)(2,1)S(1)} async-done(((bf16[32,4,768]{2,1,0:T(4,128)(2,1)}), bf16[32,4,768]{2,1,0:T(4,128)(2,1)S(1)}, u32[]{:S(2)}, u32[]{:S(2)}) %all-to-all-start) | async-done | bytes 196640 | tf_op jit(solution)/shard_map/all_to_all | solution.py:389
  83.4 0.1 reduce_sum.31
  83.5 0.7 broadcast_in_dim.43
  84.2 11.3 %all-to-all-start.1 = ((bf16[16,4,768]{2,1,0:T(4,128)(2,1)}), bf16[16,4,768]{2,1,0:T(4,128)(2,1)S(1)}, u32[]{:S(2)}, u32[]{:S(2)}) async-start(bf16[16,4,768]{2,1,0:T(4,128)(2,1)} %broadcast_in_dim.43), calls=%async_computation.1 | async-start | bytes 196608 | tf_op jit(solution)/shard_map/all_to_all | solution.py:396
  95.5 2.5 %collective-permute-start.10 = (bf16[128,1792]{1,0:T(8,128)(2,1)}, bf16[128,1792]{1,0:T(8,128)(2,1)S(1)}, u32[]{:S(2)}, u32[]{:S(2)}) collective-permute-start(bf16[128,1792]{1,0:T(8,128)(2,1)} %copy-done.8), channel_id=1, source_target_pairs={{0,1},{1,0},{64,65},{65,64},{128,129},{129,128},{192,193},{193,192... | collective-permute-start | bytes 1376264 | tf_op jit(solution)/shard_map/ppermute | solution.py:43
  98.0 0.0 collective-permute-done.11.blocks_ref
  98.0 0.0 copy-start.9
  98.0 2.0 %place.2.grad_in = bf16[128,8192]{1,0:T(8,128)(2,1)} custom-call(s32[16]{0:T(128)S(1)} %stack.118.theirs.table, bf16[128,2304]{1,0:T(8,128)(2,1)} %collective-permute-done.11.blocks_ref, bf16[128,8192]{1,0:T(8,128)(2,1)} %get-tuple-element.38.grad_in), custom_call_target="tpu_custom_call", output_to_operand_aliasing={{}: (2, {})} | custom-call | bytes 1179648 | tf_op jit(solution)/shard_map/place/pallas_call | solution.py:310
  100.0 7.3 %all-to-all-done.1 = bf16[16,4,768]{2,1,0:T(4,128)(2,1)S(1)} async-done(((bf16[16,4,768]{2,1,0:T(4,128)(2,1)}), bf16[16,4,768]{2,1,0:T(4,128)(2,1)S(1)}, u32[]{:S(2)}, u32[]{:S(2)}) %all-to-all-start.1) | async-done | bytes 98336 | tf_op jit(solution)/shard_map/all_to_all | solution.py:396
  107.4 0.6 multiply_divide_fusion
  108.0 1.4 %place.3 = bf16[128,8192]{1,0:T(8,128)(2,1)} custom-call(s32[16]{0:T(128)S(1)} %stack.118.theirs.table, bf16[128,1792]{1,0:T(8,128)(2,1)S(1)} %collective-permute-done.10.blocks_ref, bf16[128,8192]{1,0:T(8,128)(2,1)} %place.2.grad_in), custom_call_target="tpu_custom_call", output_to_operand_aliasing={{}: (2, {})} | custom-call | bytes 917504 | tf_op jit(solution)/shard_map/place/pallas_call | solution.py:310
  (25 shorter events, 0.1 us)
Async XLA Ops:
  0.6 14.9 %copy-start.10 = (s32[1,8]{1,0:T(1,128)S(1)}, s32[1,8]{1,0:T(1,128)}, u32[]{:S(2)}) copy-start(s32[1,8]{1,0:T(1,128)} %param.8) | copy-start | bytes 100
  0.6 15.7 %copy-start.7 = (bf16[128,768]{1,0:T(8,128)(2,1)S(1)}, bf16[128,768]{1,0:T(8,128)(2,1)}, u32[]{:S(2)}) copy-start(bf16[128,768]{1,0:T(8,128)(2,1)} %cot_ref.1) | copy-start | bytes 589828
  0.7 15.7 %copy-start = (bf16[128,8192]{1,0:T(8,128)(2,1)S(1)}, bf16[128,8192]{1,0:T(8,128)(2,1)}, u32[]{:S(2)}) copy-start(bf16[128,8192]{1,0:T(8,128)(2,1)} %feats_ref.1) | copy-start | bytes 6291460
  11.1 13.3 %collective-permute-start.1 = (bf16[512,768]{1,0:T(8,128)(2,1)}, bf16[512,768]{1,0:T(8,128)(2,1)}, u32[]{:S(2)}, u32[]{:S(2)}) collective-permute-start(bf16[512,768]{1,0:T(8,128)(2,1)} %all_gather.3), channel_id=1, source_target_pairs={{0,2},{1,7},{64,66},{65,71},{128,130},{129,135},{192,194},{193,199... | collective-permute-start | bytes 2359304 | tf_op jit(solution)/shard_map/ppermute | solution.py:39
  13.0 13.3 %collective-permute-start.2 = (bf16[512,768]{1,0:T(8,128)(2,1)}, bf16[512,768]{1,0:T(8,128)(2,1)}, u32[]{:S(2)}, u32[]{:S(2)}) collective-permute-start(bf16[512,768]{1,0:T(8,128)(2,1)} %all_gather.3), channel_id=1, source_target_pairs={{0,8},{1,57},{64,72},{65,121},{128,136},{129,185},{192,200},{193,2... | collective-permute-start | bytes 2359304 | tf_op jit(solution)/shard_map/ppermute | solution.py:39
  17.3 1.0 copy-start.3
  18.3 12.7 %collective-permute-start = (bf16[128,4864]{1,0:T(8,128)(2,1)S(1)}, bf16[128,4864]{1,0:T(8,128)(2,1)S(1)}, u32[]{:S(2)}, u32[]{:S(2)}) collective-permute-start(bf16[128,4864]{1,0:T(8,128)(2,1)S(1)} %get-tuple-element.23), channel_id=1, source_target_pairs={{0,1},{1,0},{64,65},{65,64},{128,129},{129,128},{192,193},{193,192... | collective-permute-start | bytes 3735560 | tf_op jit(solution)/shard_map/ppermute | solution.py:43
  24.4 17.5 %collective-permute-start.3 = (bf16[512,768]{1,0:T(8,128)(2,1)}, bf16[512,768]{1,0:T(8,128)(2,1)}, u32[]{:S(2)}, u32[]{:S(2)}) collective-permute-start(bf16[512,768]{1,0:T(8,128)(2,1)} %collective-permute-done.1.refs_0_.refs_1_), channel_id=1, source_target_pairs={{0,8},{1,57},{64,72},{65,121},{128,136},{129,185},{192,200},{193,2... | collective-permute-start | bytes 2359304 | tf_op jit(solution)/shard_map/ppermute | solution.py:39
  26.3 18.1 %collective-permute-start.4 = (bf16[512,768]{1,0:T(8,128)(2,1)}, bf16[512,768]{1,0:T(8,128)(2,1)}, u32[]{:S(2)}, u32[]{:S(2)}) collective-permute-start(bf16[512,768]{1,0:T(8,128)(2,1)} %collective-permute-done.2.refs_1_.refs_2_), channel_id=1, source_target_pairs={{0,7},{1,2},{64,71},{65,66},{128,135},{129,130},{192,199},{193,194... | collective-permute-start | bytes 2359304 | tf_op jit(solution)/shard_map/ppermute | solution.py:39
  31.0 12.9 %copy-start.1 = (bf16[128,4864]{1,0:T(8,128)(2,1)}, bf16[128,4864]{1,0:T(8,128)(2,1)S(1)}, u32[]{:S(2)}) copy-start(bf16[128,4864]{1,0:T(8,128)(2,1)S(1)} %collective-permute-done.other_ref) | copy-start | bytes 3735556
  31.0 18.4 %collective-permute-start.5 = (bf16[256,768]{1,0:T(8,128)(2,1)}, bf16[256,768]{1,0:T(8,128)(2,1)S(1)}, u32[]{:S(2)}, u32[]{:S(2)}) collective-permute-start(bf16[256,768]{1,0:T(8,128)(2,1)} %get-tuple-element.27), channel_id=1, source_target_pairs={{0,2},{1,7},{64,66},{65,71},{128,130},{129,135},{192,194},{193,199... | collective-permute-start | bytes 1179656 | tf_op jit(solution)/shard_map/ppermute | solution.py:39
  37.1 12.3 %collective-permute-start.6 = (bf16[256,768]{1,0:T(8,128)(2,1)S(1)}, bf16[256,768]{1,0:T(8,128)(2,1)S(1)}, u32[]{:S(2)}, u32[]{:S(2)}) collective-permute-start(bf16[256,768]{1,0:T(8,128)(2,1)S(1)} %get-tuple-element.28), channel_id=1, source_target_pairs={{0,8},{1,57},{64,72},{65,121},{128,136},{129,185},{192,200},{193,2... | collective-permute-start | bytes 1179656 | tf_op jit(solution)/shard_map/ppermute | solution.py:39
  41.9 21.6 %collective-permute-start.7 = (bf16[512,768]{1,0:T(8,128)(2,1)}, bf16[512,768]{1,0:T(8,128)(2,1)S(1)}, u32[]{:S(2)}, u32[]{:S(2)}) collective-permute-start(bf16[512,768]{1,0:T(8,128)(2,1)} %collective-permute-done.3.refs_3_), channel_id=1, source_target_pairs={{0,8},{1,57},{64,72},{65,121},{128,136},{129,185},{192,200},{193,2... | collective-permute-start | bytes 2359304 | tf_op jit(solution)/shard_map/ppermute | solution.py:39
  44.5 19.1 %collective-permute-start.8 = (bf16[512,768]{1,0:T(8,128)(2,1)}, bf16[512,768]{1,0:T(8,128)(2,1)S(1)}, u32[]{:S(2)}, u32[]{:S(2)}) collective-permute-start(bf16[512,768]{1,0:T(8,128)(2,1)} %collective-permute-done.4.refs_4_), channel_id=1, source_target_pairs={{0,2},{1,7},{64,66},{65,71},{128,130},{129,135},{192,194},{193,199... | collective-permute-start | bytes 2359304 | tf_op jit(solution)/shard_map/ppermute | solution.py:39
  49.4 14.1 %collective-permute-start.9 = (bf16[256,768]{1,0:T(8,128)(2,1)S(1)}, bf16[256,768]{1,0:T(8,128)(2,1)S(1)}, u32[]{:S(2)}, u32[]{:S(2)}) collective-permute-start(bf16[256,768]{1,0:T(8,128)(2,1)S(1)} %constant_dynamic-slice_fusion), channel_id=1, source_target_pairs={{0,10},{1,63},{64,74},{65,127},{128,138},{129,191},{192,202},{193,... | collective-permute-start | bytes 1179656 | tf_op jit(solution)/shard_map/ppermute | solution.py:39
  54.0 9.6 %copy-start.2 = (bf16[128,4864]{1,0:T(8,128)(2,1)S(1)}, bf16[128,4864]{1,0:T(8,128)(2,1)}, u32[]{:S(2)}) copy-start(bf16[128,4864]{1,0:T(8,128)(2,1)} %copy-done.1) | copy-start | bytes 3735556
  54.0 9.6 %copy-start.4 = (bf16[128,4096]{1,0:T(8,128)(2,1)S(1)}, bf16[128,4096]{1,0:T(8,128)(2,1)}, u32[]{:S(2)}) copy-start(bf16[128,4096]{1,0:T(8,128)(2,1)} %copy-done.3) | copy-start | bytes 3145732
  60.9 0.7 copy-start.5
  61.6 36.4 %collective-permute-start.11 = (bf16[128,2304]{1,0:T(8,128)(2,1)}, bf16[128,2304]{1,0:T(8,128)(2,1)}, u32[]{:S(2)}, u32[]{:S(2)}) collective-permute-start(bf16[128,2304]{1,0:T(8,128)(2,1)} %get-tuple-element.37), channel_id=1, source_target_pairs={{0,1},{1,0},{64,65},{65,64},{128,129},{129,128},{192,193},{193,192... | collective-permute-start | bytes 1769480 | tf_op jit(solution)/shard_map/ppermute | solution.py:43
  63.6 10.1 %copy-start.6 = (bf16[256,768]{1,0:T(8,128)(2,1)S(1)}, bf16[256,768]{1,0:T(8,128)(2,1)}, u32[]{:S(2)}) copy-start(bf16[256,768]{1,0:T(8,128)(2,1)} %copy-done.5) | copy-start | bytes 1179652
  66.6 16.8 %all-to-all-start = ((bf16[32,4,768]{2,1,0:T(4,128)(2,1)}), bf16[32,4,768]{2,1,0:T(4,128)(2,1)S(1)}, u32[]{:S(2)}, u32[]{:S(2)}) async-start(bf16[32,4,768]{2,1,0:T(4,128)(2,1)} %far_sums.1), calls=%async_computation | async-start | bytes 393216 | tf_op jit(solution)/shard_map/all_to_all | solution.py:389
  76.7 0.8 copy-start.8
  84.2 23.2 %all-to-all-start.1 = ((bf16[16,4,768]{2,1,0:T(4,128)(2,1)}), bf16[16,4,768]{2,1,0:T(4,128)(2,1)S(1)}, u32[]{:S(2)}, u32[]{:S(2)}) async-start(bf16[16,4,768]{2,1,0:T(4,128)(2,1)} %broadcast_in_dim.43), calls=%async_computation.1 | async-start | bytes 196608 | tf_op jit(solution)/shard_map/all_to_all | solution.py:396
  95.5 12.5 %collective-permute-start.10 = (bf16[128,1792]{1,0:T(8,128)(2,1)}, bf16[128,1792]{1,0:T(8,128)(2,1)S(1)}, u32[]{:S(2)}, u32[]{:S(2)}) collective-permute-start(bf16[128,1792]{1,0:T(8,128)(2,1)} %copy-done.8), channel_id=1, source_target_pairs={{0,1},{1,0},{64,65},{65,64},{128,129},{129,128},{192,193},{193,192... | collective-permute-start | bytes 1376264 | tf_op jit(solution)/shard_map/ppermute | solution.py:43
  98.0 9.4 %copy-start.9 = (f32[4,768]{1,0:T(4,128)S(1)}, f32[4,768]{1,0:T(4,128)}, u32[]{:S(2)}) copy-start(f32[4,768]{1,0:T(4,128)} %param.11) | copy-start | bytes 36868
